TPU v7x, 512 devices: a whole 4x8x8 slice. The times are simulated.
512 devices in a mesh: row: 8 (over y), col: 16 (over z, core), layer: 4 (over x).
Axes of the slice: x: 4, y: 8, z: 8, core: 2. Of those that a mesh axis runs over, the one named last changes fastest.
Arguments:
- matrix: bfloat16 [6144, 6144], P('row', 'col'), may hold values from -2 to 2, as said below
- keep_mask: int32 [96, 96], P('row', 'col'), may hold values 0 or 1
- send_list: int32 [128, 16], P(('row', 'col')), may hold values from -1 to 71, as said below
Outputs:
- owned_blocks: bfloat16 [2048, 4096], P(('row', 'col'))
Inputs may be any that keep to these rules, and one draw needn't show every extreme that they name: matrix is zero outside a block pattern except on its diagonal. send_list[s, e] numbers a block of source s's tile row-major over its 12 x (6) blocks, or is -1; a source names each block at most once; some owner column receives a block from every source of its grid row.
All inputs are finite; a program needn't handle non-finite values. No bound on the sum of `keep_mask` on one device may be relied on, other than what follows from the above.
Results may differ from a plain program's by a relative error of at most 0.0065.
Values may be sent and summed in bfloat16 or wider, within the bound.
No kernel may reach another device: no remote copies, remote signals or barrier semaphores. Data moves between devices by JAX's collectives and lax.ppermute only.
A program may use at most 64 MiB of HBM per device.

v0:
```python
import jax
import jax.numpy as jnp
from jax import lax
from jax.sharding import PartitionSpec as P

BLK = 64


def passed_along(value, axis, by):
    devices = lax.axis_size(axis)
    return lax.ppermute(value, axis, [(i, (i + by) % devices) for i in range(devices)])


def turn_left(piece, amount):
    return passed_along(piece, "col", amount)


def turn_right(piece, amount):
    return passed_along(piece, "row", amount)


def skew_pieces(piece, offset, count, turner):
    for bit in range(count.bit_length() - 1):
        moved = turner(piece, count - (1 << bit))
        piece = jnp.where(offset // (1 << bit) % 2 == 1, moved, piece)
    return piece


def cannon_product(left, right, rows_count, cols_count):
    total = jnp.zeros((left.shape[0], right.shape[1]), jnp.float32)
    for step in range(rows_count):
        total = total + jnp.dot(left, right, preferred_element_type=jnp.float32)
        if step + 1 < rows_count:
            left = turn_left(left, cols_count - 2)
            right = turn_right(right, rows_count - 1)
    return total


def on_device(matrix, keep_mask, send_list):
    rows_count = lax.axis_size("row")
    cols_count = lax.axis_size("col")
    layers = lax.axis_size("layer")
    row_index = lax.axis_index("row")
    col_index = lax.axis_index("col")
    layer_index = lax.axis_index("layer")
    tile_order = matrix.shape[0]
    half_width = matrix.shape[1]
    quarter = tile_order // layers
    start = layer_index * quarter
    half_source = start // half_width
    left_start = start % half_width
    left_piece = lax.dynamic_slice_in_dim(matrix, left_start, quarter, 1)
    right_piece = lax.dynamic_slice_in_dim(matrix, start, quarter, 0)
    left_offset = (2 * row_index + half_source - col_index % 2) % cols_count
    right_offset = col_index // 2 % rows_count
    left_skewed = skew_pieces(left_piece, left_offset, cols_count, turn_left)
    right_skewed = skew_pieces(right_piece, right_offset, rows_count, turn_right)
    square_part = cannon_product(left_skewed, right_skewed, rows_count, cols_count)
    block_keep = jnp.repeat(jnp.repeat(keep_mask.astype(jnp.float32), BLK, 0), BLK, 1)
    square_total = lax.psum(square_part, "layer")
    filtered = (square_total * block_keep).astype(jnp.bfloat16)
    filtered_rows = lax.dynamic_slice_in_dim(filtered, start, quarter, 0)
    filtered_skewed = skew_pieces(filtered_rows, right_offset, rows_count, turn_right)
    cube_part = cannon_product(left_skewed, filtered_skewed, rows_count, cols_count)
    cube = lax.psum(cube_part.astype(jnp.bfloat16), "layer").astype(jnp.float32)
    updated = (1.5 * matrix.astype(jnp.float32) - 0.5 * cube).astype(jnp.bfloat16)
    tile_blocks = tile_order // BLK
    half_blocks = half_width // BLK
    blocks = updated.reshape(tile_blocks, BLK, half_blocks, BLK).transpose(0, 2, 1, 3)
    blocks = blocks.reshape(tile_blocks * half_blocks, BLK * BLK)
    chosen = send_list[0]
    picked = jnp.take(blocks, jnp.maximum(chosen, 0), axis=0)
    outgoing = jnp.where((chosen >= 0)[:, None], picked, jnp.zeros_like(picked))
    return lax.all_to_all(outgoing, "col", split_axis=0, concat_axis=0, tiled=True)


def solution(mesh):
    in_specs = (P("row", "col"), P("row", "col"), P(("row", "col"), None))
    out_specs = P(("row", "col"), None)
    return jax.shard_map(
        on_device, mesh=mesh, in_specs=in_specs, out_specs=out_specs, check_vma=False
    )
```

profile of v0, /device:TPU:1, one launch (start us, length us, event | category | flops | bytes accessed | tf_op | source)
XLA Modules:
  0.0 420.4 jit_solution(14029540660778168437)
XLA Ops:
  7.5 5.9 %collective-permute-start.4 = (bf16[192,384]{1,0:T(8,128)(2,1)S(1)}, bf16[192,384]{1,0:T(8,128)(2,1)S(1)}, u32[]{:S(2)}, u32[]{:S(2)}) collective-permute-start(bf16[192,384]{1,0:T(8,128)(2,1)S(1)} %constant_dynamic-slice_fusion.1), channel_id=1, source_target_pairs={{0,448},{64,0},{128,64},{192,128},{256,192},{320,256},{384,320},{4... | collective-permute-start | bytes 442376 | tf_op jit(solution)/shard_map/ppermute | solution.py:11
  16.5 5.3 %collective-permute-start.5 = (bf16[192,384]{1,0:T(8,128)(2,1)S(1)}, bf16[192,384]{1,0:T(8,128)(2,1)S(1)}, u32[]{:S(2)}, u32[]{:S(2)}) collective-permute-start(bf16[192,384]{1,0:T(8,128)(2,1)S(1)} %broadcast_select_fusion.5), channel_id=1, source_target_pairs={{0,384},{64,448},{128,0},{192,64},{256,128},{320,192},{384,256},{4... | collective-permute-start | bytes 442376 | tf_op jit(solution)/shard_map/ppermute | solution.py:11
  23.1 2.5 collective-permute-start
  25.7 8.4 %collective-permute-start.6 = (bf16[192,384]{1,0:T(8,128)(2,1)S(1)}, bf16[192,384]{1,0:T(8,128)(2,1)S(1)}, u32[]{:S(2)}, u32[]{:S(2)}) collective-permute-start(bf16[192,384]{1,0:T(8,128)(2,1)S(1)} %broadcast_select_fusion.7), channel_id=1, source_target_pairs={{0,256},{64,320},{128,384},{192,448},{256,0},{320,64},{384,128},{4... | collective-permute-start | bytes 442376 | tf_op jit(solution)/shard_map/ppermute | solution.py:11
  34.3 9.7 %collective-permute-start.1 = (bf16[768,192]{1,0:T(8,128)(2,1)S(1)}, bf16[768,192]{1,0:T(8,128)(2,1)S(1)}, u32[]{:S(2)}, u32[]{:S(2)}) collective-permute-start(bf16[768,192]{1,0:T(8,128)(2,1)S(1)} %broadcast_select_fusion), channel_id=1, source_target_pairs={{0,56},{4,60},{8,0},{12,4},{16,8},{20,12},{24,16},{28,20},{32,24},... | collective-permute-start | bytes 884744 | tf_op jit(solution)/shard_map/ppermute | solution.py:11
  44.2 3.5 collective-permute-start.8
  49.6 6.8 %collective-permute-start.2 = (bf16[768,192]{1,0:T(8,128)(2,1)S(1)}, bf16[768,192]{1,0:T(8,128)(2,1)S(1)}, u32[]{:S(2)}, u32[]{:S(2)}) collective-permute-start(bf16[768,192]{1,0:T(8,128)(2,1)S(1)} %broadcast_select_fusion.1), channel_id=1, source_target_pairs={{0,48},{4,52},{8,56},{12,60},{16,0},{20,4},{24,8},{28,12},{32,16},... | collective-permute-start | bytes 884744 | tf_op jit(solution)/shard_map/ppermute | solution.py:11
  58.4 4.2 %collective-permute-done.10 = bf16[192,384]{1,0:T(8,128)(2,1)S(1)} collective-permute-done((bf16[192,384]{1,0:T(8,128)(2,1)S(1)}, bf16[192,384]{1,0:T(8,128)(2,1)S(1)}, u32[]{:S(2)}, u32[]{:S(2)}) %collective-permute-start.10) | collective-permute-done | bytes 147488 | tf_op jit(solution)/shard_map/ppermute | solution.py:11
  62.7 3.0 collective-permute-start.12
  65.6 4.8 %collective-permute-done.2 = bf16[768,192]{1,0:T(8,128)(2,1)S(1)} collective-permute-done((bf16[768,192]{1,0:T(8,128)(2,1)S(1)}, bf16[768,192]{1,0:T(8,128)(2,1)S(1)}, u32[]{:S(2)}, u32[]{:S(2)}) %collective-permute-start.2) | collective-permute-done | bytes 294944 | tf_op jit(solution)/shard_map/ppermute | solution.py:11
  70.4 6.3 %collective-permute-start.3 = (bf16[768,192]{1,0:T(8,128)(2,1)S(1)}, bf16[768,192]{1,0:T(8,128)(2,1)S(1)}, u32[]{:S(2)}, u32[]{:S(2)}) collective-permute-start(bf16[768,192]{1,0:T(8,128)(2,1)S(1)} %broadcast_select_fusion.2), channel_id=1, source_target_pairs={{0,32},{4,36},{8,40},{12,44},{16,48},{20,52},{24,56},{28,60},{32,0... | collective-permute-start | bytes 884744 | tf_op jit(solution)/shard_map/ppermute | solution.py:11
  78.9 4.1 collective-permute-done.14
  83.0 3.2 collective-permute-start.16
  86.7 15.0 %collective-permute-start.7 = (bf16[768,192]{1,0:T(8,128)(2,1)S(1)}, bf16[768,192]{1,0:T(8,128)(2,1)S(1)}, u32[]{:S(2)}, u32[]{:S(2)}) collective-permute-start(bf16[768,192]{1,0:T(8,128)(2,1)S(1)} %broadcast_select_fusion.3), channel_id=1, source_target_pairs={{0,56},{4,60},{8,0},{12,4},{16,8},{20,12},{24,16},{28,20},{32,24},... | collective-permute-start | bytes 884744 | tf_op jit(solution)/shard_map/ppermute | solution.py:11
  103.6 4.4 %collective-permute-done.18 = bf16[192,384]{1,0:T(8,128)(2,1)S(1)} collective-permute-done((bf16[192,384]{1,0:T(8,128)(2,1)S(1)}, bf16[192,384]{1,0:T(8,128)(2,1)S(1)}, u32[]{:S(2)}, u32[]{:S(2)}) %collective-permute-start.18) | collective-permute-done | bytes 147488 | tf_op jit(solution)/shard_map/ppermute | solution.py:11
  108.0 3.4 collective-permute-start.20
  111.8 3.3 collective-permute-start.9
  115.5 7.0 %collective-permute-done.9 = bf16[768,192]{1,0:T(8,128)(2,1)S(1)} collective-permute-done((bf16[768,192]{1,0:T(8,128)(2,1)S(1)}, bf16[768,192]{1,0:T(8,128)(2,1)S(1)}, u32[]{:S(2)}, u32[]{:S(2)}) %collective-permute-start.9) | collective-permute-done | bytes 294944 | tf_op jit(solution)/shard_map/ppermute | solution.py:11
  122.5 4.8 %collective-permute-start.11 = (bf16[768,192]{1,0:T(8,128)(2,1)S(1)}, bf16[768,192]{1,0:T(8,128)(2,1)S(1)}, u32[]{:S(2)}, u32[]{:S(2)}) collective-permute-start(bf16[768,192]{1,0:T(8,128)(2,1)S(1)} %collective-permute-done.9), channel_id=1, source_target_pairs={{0,56},{4,60},{8,0},{12,4},{16,8},{20,12},{24,16},{28,20},{32,24},... | collective-permute-start | bytes 884744 | tf_op jit(solution)/shard_map/ppermute | solution.py:11
  127.7 5.6 %collective-permute-done.11 = bf16[768,192]{1,0:T(8,128)(2,1)S(1)} collective-permute-done((bf16[768,192]{1,0:T(8,128)(2,1)S(1)}, bf16[768,192]{1,0:T(8,128)(2,1)S(1)}, u32[]{:S(2)}, u32[]{:S(2)}) %collective-permute-start.11) | collective-permute-done | bytes 294944 | tf_op jit(solution)/shard_map/ppermute | solution.py:11
  133.3 5.3 %collective-permute-start.13 = (bf16[768,192]{1,0:T(8,128)(2,1)S(1)}, bf16[768,192]{1,0:T(8,128)(2,1)S(1)}, u32[]{:S(2)}, u32[]{:S(2)}) collective-permute-start(bf16[768,192]{1,0:T(8,128)(2,1)S(1)} %collective-permute-done.11), channel_id=1, source_target_pairs={{0,56},{4,60},{8,0},{12,4},{16,8},{20,12},{24,16},{28,20},{32,24},... | collective-permute-start | bytes 884744 | tf_op jit(solution)/shard_map/ppermute | solution.py:11
  139.0 4.7 %collective-permute-done.13 = bf16[768,192]{1,0:T(8,128)(2,1)S(1)} collective-permute-done((bf16[768,192]{1,0:T(8,128)(2,1)S(1)}, bf16[768,192]{1,0:T(8,128)(2,1)S(1)}, u32[]{:S(2)}, u32[]{:S(2)}) %collective-permute-start.13) | collective-permute-done | bytes 294944 | tf_op jit(solution)/shard_map/ppermute | solution.py:11
  143.7 5.3 %collective-permute-start.15 = (bf16[768,192]{1,0:T(8,128)(2,1)S(1)}, bf16[768,192]{1,0:T(8,128)(2,1)S(1)}, u32[]{:S(2)}, u32[]{:S(2)}) collective-permute-start(bf16[768,192]{1,0:T(8,128)(2,1)S(1)} %collective-permute-done.13), channel_id=1, source_target_pairs={{0,56},{4,60},{8,0},{12,4},{16,8},{20,12},{24,16},{28,20},{32,24},... | collective-permute-start | bytes 884744 | tf_op jit(solution)/shard_map/ppermute | solution.py:11
  149.4 4.3 %collective-permute-done.15 = bf16[768,192]{1,0:T(8,128)(2,1)S(1)} collective-permute-done((bf16[768,192]{1,0:T(8,128)(2,1)S(1)}, bf16[768,192]{1,0:T(8,128)(2,1)S(1)}, u32[]{:S(2)}, u32[]{:S(2)}) %collective-permute-start.15) | collective-permute-done | bytes 294944 | tf_op jit(solution)/shard_map/ppermute | solution.py:11
  153.7 5.0 %collective-permute-start.17 = (bf16[768,192]{1,0:T(8,128)(2,1)S(1)}, bf16[768,192]{1,0:T(8,128)(2,1)S(1)}, u32[]{:S(2)}, u32[]{:S(2)}) collective-permute-start(bf16[768,192]{1,0:T(8,128)(2,1)S(1)} %collective-permute-done.15), channel_id=1, source_target_pairs={{0,56},{4,60},{8,0},{12,4},{16,8},{20,12},{24,16},{28,20},{32,24},... | collective-permute-start | bytes 884744 | tf_op jit(solution)/shard_map/ppermute | solution.py:11
  159.1 5.7 %collective-permute-done.17 = bf16[768,192]{1,0:T(8,128)(2,1)S(1)} collective-permute-done((bf16[768,192]{1,0:T(8,128)(2,1)S(1)}, bf16[768,192]{1,0:T(8,128)(2,1)S(1)}, u32[]{:S(2)}, u32[]{:S(2)}) %collective-permute-start.17) | collective-permute-done | bytes 294944 | tf_op jit(solution)/shard_map/ppermute | solution.py:11
  164.8 3.7 collective-permute-start.19
  168.8 8.1 %collective-permute-done.19 = bf16[768,192]{1,0:T(8,128)(2,1)S(1)} collective-permute-done((bf16[768,192]{1,0:T(8,128)(2,1)S(1)}, bf16[768,192]{1,0:T(8,128)(2,1)S(1)}, u32[]{:S(2)}, u32[]{:S(2)}) %collective-permute-start.19) | collective-permute-done | bytes 294944 | tf_op jit(solution)/shard_map/ppermute | solution.py:11
  180.3 61.8 %all-reduce.3.cloned.1.call-done = f32[768,384]{1,0:T(8,128)} async-done(((f32[768,384]{1,0:T(8,128)}), f32[768,384]{1,0:T(8,128)}) %all-reduce.3.cloned.1.call-update) | async-done | bytes 1179664 | tf_op jit(solution)/shard_map/psum | solution.py:60
  243.2 4.5 %collective-permute-start.21 = (bf16[192,384]{1,0:T(8,128)(2,1)S(1)}, bf16[192,384]{1,0:T(8,128)(2,1)S(1)}, u32[]{:S(2)}, u32[]{:S(2)}) collective-permute-start(bf16[192,384]{1,0:T(8,128)(2,1)S(1)} %fusion.1), channel_id=1, source_target_pairs={{0,448},{64,0},{128,64},{192,128},{256,192},{320,256},{384,320},{4... | collective-permute-start | bytes 442376 | tf_op jit(solution)/shard_map/ppermute | solution.py:11
  247.7 2.1 collective-permute-done.21
  249.8 4.7 %collective-permute-start.22 = (bf16[192,384]{1,0:T(8,128)(2,1)S(1)}, bf16[192,384]{1,0:T(8,128)(2,1)S(1)}, u32[]{:S(2)}, u32[]{:S(2)}) collective-permute-start(bf16[192,384]{1,0:T(8,128)(2,1)S(1)} %broadcast_select_fusion.4), channel_id=1, source_target_pairs={{0,384},{64,448},{128,0},{192,64},{256,128},{320,192},{384,256},{4... | collective-permute-start | bytes 442376 | tf_op jit(solution)/shard_map/ppermute | solution.py:11
  254.5 3.4 collective-permute-done.22
  257.9 6.7 %collective-permute-start.23 = (bf16[192,384]{1,0:T(8,128)(2,1)S(1)}, bf16[192,384]{1,0:T(8,128)(2,1)S(1)}, u32[]{:S(2)}, u32[]{:S(2)}) collective-permute-start(bf16[192,384]{1,0:T(8,128)(2,1)S(1)} %broadcast_select_fusion.6), channel_id=1, source_target_pairs={{0,256},{64,320},{128,384},{192,448},{256,0},{320,64},{384,128},{4... | collective-permute-start | bytes 442376 | tf_op jit(solution)/shard_map/ppermute | solution.py:11
  264.6 3.1 collective-permute-done.23
  267.8 7.8 %collective-permute-start.24 = (bf16[192,384]{1,0:T(8,128)(2,1)S(1)}, bf16[192,384]{1,0:T(8,128)(2,1)S(1)}, u32[]{:S(2)}, u32[]{:S(2)}) collective-permute-start(bf16[192,384]{1,0:T(8,128)(2,1)S(1)} %broadcast_select_fusion.8), channel_id=1, source_target_pairs={{0,448},{64,0},{128,64},{192,128},{256,192},{320,256},{384,320},{4... | collective-permute-start | bytes 442376 | tf_op jit(solution)/shard_map/ppermute | solution.py:11
  275.6 2.1 collective-permute-done.24
  278.0 5.1 %collective-permute-start.25 = (bf16[192,384]{1,0:T(8,128)(2,1)S(1)}, bf16[192,384]{1,0:T(8,128)(2,1)S(1)}, u32[]{:S(2)}, u32[]{:S(2)}) collective-permute-start(bf16[192,384]{1,0:T(8,128)(2,1)S(1)} %collective-permute-done.24), channel_id=1, source_target_pairs={{0,448},{64,0},{128,64},{192,128},{256,192},{320,256},{384,320},{4... | collective-permute-start | bytes 442376 | tf_op jit(solution)/shard_map/ppermute | solution.py:11
  285.3 5.0 %collective-permute-start.26 = (bf16[192,384]{1,0:T(8,128)(2,1)S(1)}, bf16[192,384]{1,0:T(8,128)(2,1)S(1)}, u32[]{:S(2)}, u32[]{:S(2)}) collective-permute-start(bf16[192,384]{1,0:T(8,128)(2,1)S(1)} %collective-permute-done.25), channel_id=1, source_target_pairs={{0,448},{64,0},{128,64},{192,128},{256,192},{320,256},{384,320},{4... | collective-permute-start | bytes 442376 | tf_op jit(solution)/shard_map/ppermute | solution.py:11
  292.3 5.0 %collective-permute-start.27 = (bf16[192,384]{1,0:T(8,128)(2,1)S(1)}, bf16[192,384]{1,0:T(8,128)(2,1)S(1)}, u32[]{:S(2)}, u32[]{:S(2)}) collective-permute-start(bf16[192,384]{1,0:T(8,128)(2,1)S(1)} %collective-permute-done.26), channel_id=1, source_target_pairs={{0,448},{64,0},{128,64},{192,128},{256,192},{320,256},{384,320},{4... | collective-permute-start | bytes 442376 | tf_op jit(solution)/shard_map/ppermute | solution.py:11
  297.7 2.2 collective-permute-done.27
  299.9 5.0 %collective-permute-start.28 = (bf16[192,384]{1,0:T(8,128)(2,1)S(1)}, bf16[192,384]{1,0:T(8,128)(2,1)S(1)}, u32[]{:S(2)}, u32[]{:S(2)}) collective-permute-start(bf16[192,384]{1,0:T(8,128)(2,1)S(1)} %collective-permute-done.27), channel_id=1, source_target_pairs={{0,448},{64,0},{128,64},{192,128},{256,192},{320,256},{384,320},{4... | collective-permute-start | bytes 442376 | tf_op jit(solution)/shard_map/ppermute | solution.py:11
  305.3 3.3 collective-permute-done.28
  308.5 5.3 %collective-permute-start.29 = (bf16[192,384]{1,0:T(8,128)(2,1)S(1)}, bf16[192,384]{1,0:T(8,128)(2,1)S(1)}, u32[]{:S(2)}, u32[]{:S(2)}) collective-permute-start(bf16[192,384]{1,0:T(8,128)(2,1)S(1)} %collective-permute-done.28), channel_id=1, source_target_pairs={{0,448},{64,0},{128,64},{192,128},{256,192},{320,256},{384,320},{4... | collective-permute-start | bytes 442376 | tf_op jit(solution)/shard_map/ppermute | solution.py:11
  314.2 2.4 collective-permute-done.29
  316.6 5.3 %collective-permute-start.30 = (bf16[192,384]{1,0:T(8,128)(2,1)S(1)}, bf16[192,384]{1,0:T(8,128)(2,1)S(1)}, u32[]{:S(2)}, u32[]{:S(2)}) collective-permute-start(bf16[192,384]{1,0:T(8,128)(2,1)S(1)} %collective-permute-done.29), channel_id=1, source_target_pairs={{0,448},{64,0},{128,64},{192,128},{256,192},{320,256},{384,320},{4... | collective-permute-start | bytes 442376 | tf_op jit(solution)/shard_map/ppermute | solution.py:11
  325.3 62.9 %all-reduce.5.cloned.1.call-done = bf16[768,384]{1,0:T(8,128)(2,1)} async-done(((bf16[768,384]{1,0:T(8,128)(2,1)}), bf16[768,384]{1,0:T(8,128)(2,1)}) %all-reduce.5.cloned.1.call-update) | async-done | bytes 589840 | tf_op jit(solution)/shard_map/psum | solution.py:65
  393.6 19.1 %all_to_all.9 = bf16[16,2,2048]{2,1,0:T(2,128)(2,1)S(1)} all-to-all(bf16[16,2,2048]{2,1,0:T(2,128)(2,1)S(1)} %reshape.100), channel_id=1, replica_groups=mesh['row'=8,'col'=16,'layer'=4] {'col'}, dimensions={0} | all-to-all | bytes 262144 | tf_op jit(solution)/shard_map/all_to_all | solution.py:74
  (84 shorter events, 36.1 us)
Async XLA Ops:
  6.5 27.6 %copy-start = (bf16[768,384]{1,0:T(8,128)(2,1)S(1)}, bf16[768,384]{1,0:T(8,128)(2,1)}, u32[]{:S(2)}) copy-start(bf16[768,384]{1,0:T(8,128)(2,1)} %param.3) | copy-start | bytes 1769476
  6.5 235.6 %all-reduce.3.cloned.1.call-start = ((), (), s32[]{:S(2)}) async-start(), calls=%async_computation.1 | async-start | bytes 2359296 | tf_op jit(solution)/shard_map/psum | solution.py:60
  7.5 8.0 %collective-permute-start.4 = (bf16[192,384]{1,0:T(8,128)(2,1)S(1)}, bf16[192,384]{1,0:T(8,128)(2,1)S(1)}, u32[]{:S(2)}, u32[]{:S(2)}) collective-permute-start(bf16[192,384]{1,0:T(8,128)(2,1)S(1)} %constant_dynamic-slice_fusion.1), channel_id=1, source_target_pairs={{0,448},{64,0},{128,64},{192,128},{256,192},{320,256},{384,320},{4... | collective-permute-start | bytes 442376 | tf_op jit(solution)/shard_map/ppermute | solution.py:11
  16.5 9.2 %collective-permute-start.5 = (bf16[192,384]{1,0:T(8,128)(2,1)S(1)}, bf16[192,384]{1,0:T(8,128)(2,1)S(1)}, u32[]{:S(2)}, u32[]{:S(2)}) collective-permute-start(bf16[192,384]{1,0:T(8,128)(2,1)S(1)} %broadcast_select_fusion.5), channel_id=1, source_target_pairs={{0,384},{64,448},{128,0},{192,64},{256,128},{320,192},{384,256},{4... | collective-permute-start | bytes 442376 | tf_op jit(solution)/shard_map/ppermute | solution.py:11
  23.1 11.0 %collective-permute-start = (bf16[768,192]{1,0:T(8,128)(2,1)S(1)}, bf16[768,192]{1,0:T(8,128)(2,1)S(1)}, u32[]{:S(2)}, u32[]{:S(2)}) collective-permute-start(bf16[768,192]{1,0:T(8,128)(2,1)S(1)} %constant_dynamic-slice_fusion.2), channel_id=1, source_target_pairs={{0,60},{4,0},{8,4},{12,8},{16,12},{20,16},{24,20},{28,24},{32,28},... | collective-permute-start | bytes 884744 | tf_op jit(solution)/shard_map/ppermute | solution.py:11
  25.7 18.4 %collective-permute-start.6 = (bf16[192,384]{1,0:T(8,128)(2,1)S(1)}, bf16[192,384]{1,0:T(8,128)(2,1)S(1)}, u32[]{:S(2)}, u32[]{:S(2)}) collective-permute-start(bf16[192,384]{1,0:T(8,128)(2,1)S(1)} %broadcast_select_fusion.7), channel_id=1, source_target_pairs={{0,256},{64,320},{128,384},{192,448},{256,0},{320,64},{384,128},{4... | collective-permute-start | bytes 442376 | tf_op jit(solution)/shard_map/ppermute | solution.py:11
  34.3 15.3 %collective-permute-start.1 = (bf16[768,192]{1,0:T(8,128)(2,1)S(1)}, bf16[768,192]{1,0:T(8,128)(2,1)S(1)}, u32[]{:S(2)}, u32[]{:S(2)}) collective-permute-start(bf16[768,192]{1,0:T(8,128)(2,1)S(1)} %broadcast_select_fusion), channel_id=1, source_target_pairs={{0,56},{4,60},{8,0},{12,4},{16,8},{20,12},{24,16},{28,20},{32,24},... | collective-permute-start | bytes 884744 | tf_op jit(solution)/shard_map/ppermute | solution.py:11
  44.2 12.3 %collective-permute-start.8 = (bf16[192,384]{1,0:T(8,128)(2,1)S(1)}, bf16[192,384]{1,0:T(8,128)(2,1)S(1)}, u32[]{:S(2)}, u32[]{:S(2)}) collective-permute-start(bf16[192,384]{1,0:T(8,128)(2,1)S(1)} %broadcast_select_fusion.9), channel_id=1, source_target_pairs={{0,448},{64,0},{128,64},{192,128},{256,192},{320,256},{384,320},{4... | collective-permute-start | bytes 442376 | tf_op jit(solution)/shard_map/ppermute | solution.py:11
  49.6 20.7 %collective-permute-start.2 = (bf16[768,192]{1,0:T(8,128)(2,1)S(1)}, bf16[768,192]{1,0:T(8,128)(2,1)S(1)}, u32[]{:S(2)}, u32[]{:S(2)}) collective-permute-start(bf16[768,192]{1,0:T(8,128)(2,1)S(1)} %broadcast_select_fusion.1), channel_id=1, source_target_pairs={{0,48},{4,52},{8,56},{12,60},{16,0},{20,4},{24,8},{28,12},{32,16},... | collective-permute-start | bytes 884744 | tf_op jit(solution)/shard_map/ppermute | solution.py:11
  56.5 6.2 %collective-permute-start.10 = (bf16[192,384]{1,0:T(8,128)(2,1)S(1)}, bf16[192,384]{1,0:T(8,128)(2,1)S(1)}, u32[]{:S(2)}, u32[]{:S(2)}) collective-permute-start(bf16[192,384]{1,0:T(8,128)(2,1)S(1)} %collective-permute-done.8), channel_id=1, source_target_pairs={{0,448},{64,0},{128,64},{192,128},{256,192},{320,256},{384,320},{4... | collective-permute-start | bytes 442376 | tf_op jit(solution)/shard_map/ppermute | solution.py:11
  62.7 14.1 %collective-permute-start.12 = (bf16[192,384]{1,0:T(8,128)(2,1)S(1)}, bf16[192,384]{1,0:T(8,128)(2,1)S(1)}, u32[]{:S(2)}, u32[]{:S(2)}) collective-permute-start(bf16[192,384]{1,0:T(8,128)(2,1)S(1)} %collective-permute-done.10), channel_id=1, source_target_pairs={{0,448},{64,0},{128,64},{192,128},{256,192},{320,256},{384,320},{4... | collective-permute-start | bytes 442376 | tf_op jit(solution)/shard_map/ppermute | solution.py:11
  70.4 16.2 %collective-permute-start.3 = (bf16[768,192]{1,0:T(8,128)(2,1)S(1)}, bf16[768,192]{1,0:T(8,128)(2,1)S(1)}, u32[]{:S(2)}, u32[]{:S(2)}) collective-permute-start(bf16[768,192]{1,0:T(8,128)(2,1)S(1)} %broadcast_select_fusion.2), channel_id=1, source_target_pairs={{0,32},{4,36},{8,40},{12,44},{16,48},{20,52},{24,56},{28,60},{32,0... | collective-permute-start | bytes 884744 | tf_op jit(solution)/shard_map/ppermute | solution.py:11
  76.8 6.2 %collective-permute-start.14 = (bf16[192,384]{1,0:T(8,128)(2,1)S(1)}, bf16[192,384]{1,0:T(8,128)(2,1)S(1)}, u32[]{:S(2)}, u32[]{:S(2)}) collective-permute-start(bf16[192,384]{1,0:T(8,128)(2,1)S(1)} %collective-permute-done.12), channel_id=1, source_target_pairs={{0,448},{64,0},{128,64},{192,128},{256,192},{320,256},{384,320},{4... | collective-permute-start | bytes 442376 | tf_op jit(solution)/shard_map/ppermute | solution.py:11
  83.0 18.7 %collective-permute-start.16 = (bf16[192,384]{1,0:T(8,128)(2,1)S(1)}, bf16[192,384]{1,0:T(8,128)(2,1)S(1)}, u32[]{:S(2)}, u32[]{:S(2)}) collective-permute-start(bf16[192,384]{1,0:T(8,128)(2,1)S(1)} %collective-permute-done.14), channel_id=1, source_target_pairs={{0,448},{64,0},{128,64},{192,128},{256,192},{320,256},{384,320},{4... | collective-permute-start | bytes 442376 | tf_op jit(solution)/shard_map/ppermute | solution.py:11
  86.7 24.8 %collective-permute-start.7 = (bf16[768,192]{1,0:T(8,128)(2,1)S(1)}, bf16[768,192]{1,0:T(8,128)(2,1)S(1)}, u32[]{:S(2)}, u32[]{:S(2)}) collective-permute-start(bf16[768,192]{1,0:T(8,128)(2,1)S(1)} %broadcast_select_fusion.3), channel_id=1, source_target_pairs={{0,56},{4,60},{8,0},{12,4},{16,8},{20,12},{24,16},{28,20},{32,24},... | collective-permute-start | bytes 884744 | tf_op jit(solution)/shard_map/ppermute | solution.py:11
  101.6 6.4 %collective-permute-start.18 = (bf16[192,384]{1,0:T(8,128)(2,1)S(1)}, bf16[192,384]{1,0:T(8,128)(2,1)S(1)}, u32[]{:S(2)}, u32[]{:S(2)}) collective-permute-start(bf16[192,384]{1,0:T(8,128)(2,1)S(1)} %collective-permute-done.16), channel_id=1, source_target_pairs={{0,448},{64,0},{128,64},{192,128},{256,192},{320,256},{384,320},{4... | collective-permute-start | bytes 442376 | tf_op jit(solution)/shard_map/ppermute | solution.py:11
  108.0 60.8 %collective-permute-start.20 = (bf16[192,384]{1,0:T(8,128)(2,1)S(1)}, bf16[192,384]{1,0:T(8,128)(2,1)S(1)}, u32[]{:S(2)}, u32[]{:S(2)}) collective-permute-start(bf16[192,384]{1,0:T(8,128)(2,1)S(1)} %collective-permute-done.18), channel_id=1, source_target_pairs={{0,448},{64,0},{128,64},{192,128},{256,192},{320,256},{384,320},{4... | collective-permute-start | bytes 442376 | tf_op jit(solution)/shard_map/ppermute | solution.py:11
  111.8 10.7 %collective-permute-start.9 = (bf16[768,192]{1,0:T(8,128)(2,1)S(1)}, bf16[768,192]{1,0:T(8,128)(2,1)S(1)}, u32[]{:S(2)}, u32[]{:S(2)}) collective-permute-start(bf16[768,192]{1,0:T(8,128)(2,1)S(1)} %collective-permute-done.7), channel_id=1, source_target_pairs={{0,56},{4,60},{8,0},{12,4},{16,8},{20,12},{24,16},{28,20},{32,24},... | collective-permute-start | bytes 884744 | tf_op jit(solution)/shard_map/ppermute | solution.py:11
  122.5 5.2 %copy-start.3 = (bf16[768,192]{1,0:T(8,128)(2,1)}, bf16[768,192]{1,0:T(8,128)(2,1)S(1)}, u32[]{:S(2)}) copy-start(bf16[768,192]{1,0:T(8,128)(2,1)S(1)} %collective-permute-done.9) | copy-start | bytes 884740
  122.5 10.8 %collective-permute-start.11 = (bf16[768,192]{1,0:T(8,128)(2,1)S(1)}, bf16[768,192]{1,0:T(8,128)(2,1)S(1)}, u32[]{:S(2)}, u32[]{:S(2)}) collective-permute-start(bf16[768,192]{1,0:T(8,128)(2,1)S(1)} %collective-permute-done.9), channel_id=1, source_target_pairs={{0,56},{4,60},{8,0},{12,4},{16,8},{20,12},{24,16},{28,20},{32,24},... | collective-permute-start | bytes 884744 | tf_op jit(solution)/shard_map/ppermute | solution.py:11
  133.3 5.7 %copy-start.1 = (bf16[768,192]{1,0:T(8,128)(2,1)}, bf16[768,192]{1,0:T(8,128)(2,1)S(1)}, u32[]{:S(2)}) copy-start(bf16[768,192]{1,0:T(8,128)(2,1)S(1)} %collective-permute-done.11) | copy-start | bytes 884740
  133.3 10.4 %collective-permute-start.13 = (bf16[768,192]{1,0:T(8,128)(2,1)S(1)}, bf16[768,192]{1,0:T(8,128)(2,1)S(1)}, u32[]{:S(2)}, u32[]{:S(2)}) collective-permute-start(bf16[768,192]{1,0:T(8,128)(2,1)S(1)} %collective-permute-done.11), channel_id=1, source_target_pairs={{0,56},{4,60},{8,0},{12,4},{16,8},{20,12},{24,16},{28,20},{32,24},... | collective-permute-start | bytes 884744 | tf_op jit(solution)/shard_map/ppermute | solution.py:11
  143.7 10.0 %collective-permute-start.15 = (bf16[768,192]{1,0:T(8,128)(2,1)S(1)}, bf16[768,192]{1,0:T(8,128)(2,1)S(1)}, u32[]{:S(2)}, u32[]{:S(2)}) collective-permute-start(bf16[768,192]{1,0:T(8,128)(2,1)S(1)} %collective-permute-done.13), channel_id=1, source_target_pairs={{0,56},{4,60},{8,0},{12,4},{16,8},{20,12},{24,16},{28,20},{32,24},... | collective-permute-start | bytes 884744 | tf_op jit(solution)/shard_map/ppermute | solution.py:11
  153.7 11.1 %collective-permute-start.17 = (bf16[768,192]{1,0:T(8,128)(2,1)S(1)}, bf16[768,192]{1,0:T(8,128)(2,1)S(1)}, u32[]{:S(2)}, u32[]{:S(2)}) collective-permute-start(bf16[768,192]{1,0:T(8,128)(2,1)S(1)} %collective-permute-done.15), channel_id=1, source_target_pairs={{0,56},{4,60},{8,0},{12,4},{16,8},{20,12},{24,16},{28,20},{32,24},... | collective-permute-start | bytes 884744 | tf_op jit(solution)/shard_map/ppermute | solution.py:11
  164.8 12.1 %collective-permute-start.19 = (bf16[768,192]{1,0:T(8,128)(2,1)S(1)}, bf16[768,192]{1,0:T(8,128)(2,1)S(1)}, u32[]{:S(2)}, u32[]{:S(2)}) collective-permute-start(bf16[768,192]{1,0:T(8,128)(2,1)S(1)} %collective-permute-done.17), channel_id=1, source_target_pairs={{0,56},{4,60},{8,0},{12,4},{16,8},{20,12},{24,16},{28,20},{32,24},... | collective-permute-start | bytes 884744 | tf_op jit(solution)/shard_map/ppermute | solution.py:11
  178.3 0.7 copy-start.5
  178.3 209.9 %all-reduce.5.cloned.1.call-start = ((), (), s32[]{:S(2)}) async-start(), calls=%async_computation.2 | async-start | bytes 1179648 | tf_op jit(solution)/shard_map/psum | solution.py:65
  243.2 6.5 %collective-permute-start.21 = (bf16[192,384]{1,0:T(8,128)(2,1)S(1)}, bf16[192,384]{1,0:T(8,128)(2,1)S(1)}, u32[]{:S(2)}, u32[]{:S(2)}) collective-permute-start(bf16[192,384]{1,0:T(8,128)(2,1)S(1)} %fusion.1), channel_id=1, source_target_pairs={{0,448},{64,0},{128,64},{192,128},{256,192},{320,256},{384,320},{4... | collective-permute-start | bytes 442376 | tf_op jit(solution)/shard_map/ppermute | solution.py:11
  249.8 8.1 %collective-permute-start.22 = (bf16[192,384]{1,0:T(8,128)(2,1)S(1)}, bf16[192,384]{1,0:T(8,128)(2,1)S(1)}, u32[]{:S(2)}, u32[]{:S(2)}) collective-permute-start(bf16[192,384]{1,0:T(8,128)(2,1)S(1)} %broadcast_select_fusion.4), channel_id=1, source_target_pairs={{0,384},{64,448},{128,0},{192,64},{256,128},{320,192},{384,256},{4... | collective-permute-start | bytes 442376 | tf_op jit(solution)/shard_map/ppermute | solution.py:11
  257.9 9.9 %collective-permute-start.23 = (bf16[192,384]{1,0:T(8,128)(2,1)S(1)}, bf16[192,384]{1,0:T(8,128)(2,1)S(1)}, u32[]{:S(2)}, u32[]{:S(2)}) collective-permute-start(bf16[192,384]{1,0:T(8,128)(2,1)S(1)} %broadcast_select_fusion.6), channel_id=1, source_target_pairs={{0,256},{64,320},{128,384},{192,448},{256,0},{320,64},{384,128},{4... | collective-permute-start | bytes 442376 | tf_op jit(solution)/shard_map/ppermute | solution.py:11
  267.8 9.9 %collective-permute-start.24 = (bf16[192,384]{1,0:T(8,128)(2,1)S(1)}, bf16[192,384]{1,0:T(8,128)(2,1)S(1)}, u32[]{:S(2)}, u32[]{:S(2)}) collective-permute-start(bf16[192,384]{1,0:T(8,128)(2,1)S(1)} %broadcast_select_fusion.8), channel_id=1, source_target_pairs={{0,448},{64,0},{128,64},{192,128},{256,192},{320,256},{384,320},{4... | collective-permute-start | bytes 442376 | tf_op jit(solution)/shard_map/ppermute | solution.py:11
  278.0 12.2 %copy-start.4 = (bf16[768,192]{1,0:T(8,128)(2,1)S(1)}, bf16[768,192]{1,0:T(8,128)(2,1)}, u32[]{:S(2)}) copy-start(bf16[768,192]{1,0:T(8,128)(2,1)} %copy-done.3) | copy-start | bytes 884740
  278.0 7.2 %collective-permute-start.25 = (bf16[192,384]{1,0:T(8,128)(2,1)S(1)}, bf16[192,384]{1,0:T(8,128)(2,1)S(1)}, u32[]{:S(2)}, u32[]{:S(2)}) collective-permute-start(bf16[192,384]{1,0:T(8,128)(2,1)S(1)} %collective-permute-done.24), channel_id=1, source_target_pairs={{0,448},{64,0},{128,64},{192,128},{256,192},{320,256},{384,320},{4... | collective-permute-start | bytes 442376 | tf_op jit(solution)/shard_map/ppermute | solution.py:11
  283.5 13.8 %copy-start.2 = (bf16[768,192]{1,0:T(8,128)(2,1)S(1)}, bf16[768,192]{1,0:T(8,128)(2,1)}, u32[]{:S(2)}) copy-start(bf16[768,192]{1,0:T(8,128)(2,1)} %copy-done.1) | copy-start | bytes 884740
  285.3 7.1 %collective-permute-start.26 = (bf16[192,384]{1,0:T(8,128)(2,1)S(1)}, bf16[192,384]{1,0:T(8,128)(2,1)S(1)}, u32[]{:S(2)}, u32[]{:S(2)}) collective-permute-start(bf16[192,384]{1,0:T(8,128)(2,1)S(1)} %collective-permute-done.25), channel_id=1, source_target_pairs={{0,448},{64,0},{128,64},{192,128},{256,192},{320,256},{384,320},{4... | collective-permute-start | bytes 442376 | tf_op jit(solution)/shard_map/ppermute | solution.py:11
  292.3 7.5 %collective-permute-start.27 = (bf16[192,384]{1,0:T(8,128)(2,1)S(1)}, bf16[192,384]{1,0:T(8,128)(2,1)S(1)}, u32[]{:S(2)}, u32[]{:S(2)}) collective-permute-start(bf16[192,384]{1,0:T(8,128)(2,1)S(1)} %collective-permute-done.26), channel_id=1, source_target_pairs={{0,448},{64,0},{128,64},{192,128},{256,192},{320,256},{384,320},{4... | collective-permute-start | bytes 442376 | tf_op jit(solution)/shard_map/ppermute | solution.py:11
  299.9 8.6 %collective-permute-start.28 = (bf16[192,384]{1,0:T(8,128)(2,1)S(1)}, bf16[192,384]{1,0:T(8,128)(2,1)S(1)}, u32[]{:S(2)}, u32[]{:S(2)}) collective-permute-start(bf16[192,384]{1,0:T(8,128)(2,1)S(1)} %collective-permute-done.27), channel_id=1, source_target_pairs={{0,448},{64,0},{128,64},{192,128},{256,192},{320,256},{384,320},{4... | collective-permute-start | bytes 442376 | tf_op jit(solution)/shard_map/ppermute | solution.py:11
  308.5 8.1 %collective-permute-start.29 = (bf16[192,384]{1,0:T(8,128)(2,1)S(1)}, bf16[192,384]{1,0:T(8,128)(2,1)S(1)}, u32[]{:S(2)}, u32[]{:S(2)}) collective-permute-start(bf16[192,384]{1,0:T(8,128)(2,1)S(1)} %collective-permute-done.28), channel_id=1, source_target_pairs={{0,448},{64,0},{128,64},{192,128},{256,192},{320,256},{384,320},{4... | collective-permute-start | bytes 442376 | tf_op jit(solution)/shard_map/ppermute | solution.py:11
  316.6 7.4 %collective-permute-start.30 = (bf16[192,384]{1,0:T(8,128)(2,1)S(1)}, bf16[192,384]{1,0:T(8,128)(2,1)S(1)}, u32[]{:S(2)}, u32[]{:S(2)}) collective-permute-start(bf16[192,384]{1,0:T(8,128)(2,1)S(1)} %collective-permute-done.29), channel_id=1, source_target_pairs={{0,448},{64,0},{128,64},{192,128},{256,192},{320,256},{384,320},{4... | collective-permute-start | bytes 442376 | tf_op jit(solution)/shard_map/ppermute | solution.py:11
  322.3 2.9 copy-start.6
Sparse Core Ops, SparseCore 0:
  178.5 63.6 all-reduce.2
  325.4 62.7 all-reduce.4
where the time goes:
time: 422 us; the launch traced here: 420 us
  waiting for transfers between devices  206 us (49%)
  starting transfers between devices  161 us (38%)
  blocking collectives  19.1 us (5%)
  between operations  14.3 us (3%)
  local copies, waits for them, and re-layouts  8.42 us (2%)
  matrix products  7.56 us (2%)
  other arithmetic  4.53 us (1%)
    ppermute x31, starting transfers between devices, passed_along(): lax.ppermute(value, axis, [(i, (i + by) % devices) for i in range(devices)])  161 us
    ppermute x31, waiting for transfers between devices, passed_along(): lax.ppermute(value, axis, [(i, (i + by) % devices) for i in range(devices)])  81.1 us
    psum x1, waiting for transfers between devices, on_device(): cube = lax.psum(cube_part.astype(jnp.bfloat16), 'layer').astype(jnp.float32)  62.9 us
    psum x1, waiting for transfers between devices, on_device(): square_total = lax.psum(square_part, 'layer')  61.8 us
    all_to_all x1, blocking collectives, on_device(): lax.all_to_all(outgoing, 'col', split_axis=0, concat_axis=0, tiled=True)  19.1 us
  transfers between devices with their start and end apart: 33, of which 26 were waited for; matrix products, arithmetic and copies ran while one was open for 2% of the time, Pallas kernels for 0%

commit v1 on v0

v1 whole, which is shorter than its diff:
```python
import jax
import jax.numpy as jnp
from jax import lax
from jax.sharding import PartitionSpec as P

BLK = 64


def on_device(matrix, keep_mask, send_list):
    layers = lax.axis_size("layer")
    layer_index = lax.axis_index("layer")
    tile_rows, width = matrix.shape
    part = width // layers
    halves = tile_rows // width
    left_piece = lax.dynamic_slice_in_dim(matrix, layer_index * part, part, 1).T
    right_piece = lax.dynamic_slice_in_dim(
        matrix.reshape(halves, layers, part, width), layer_index, 1, 1
    ).reshape(halves * part, width)
    left_t = lax.all_gather(left_piece, "col", axis=0, tiled=True)
    right = lax.all_gather(right_piece, "row", axis=0, tiled=True)
    contract = (((0,), (0,)), ((), ()))
    square_part = lax.dot_general(left_t, right, contract, preferred_element_type=jnp.float32)
    square_part = square_part.reshape(halves, layers, part, width).transpose(1, 0, 2, 3)
    square_part = square_part.reshape(layers, halves * part, width).astype(jnp.bfloat16)
    parts = lax.all_to_all(square_part, "layer", split_axis=0, concat_axis=0, tiled=True)
    square = parts.astype(jnp.float32).sum(0)
    block_keep = jnp.repeat(jnp.repeat(keep_mask.astype(jnp.float32), BLK, 0), BLK, 1)
    block_keep = lax.dynamic_slice_in_dim(
        block_keep.reshape(halves, layers, part, width), layer_index, 1, 1
    ).reshape(halves * part, width)
    filtered_piece = (square * block_keep).astype(jnp.bfloat16)
    filtered = lax.all_gather(filtered_piece, "row", axis=0, tiled=True)
    cube_part = lax.dot_general(left_t, filtered, contract, preferred_element_type=jnp.float32)
    own = jnp.where(layer_index == 0, 1.5, 0.0) * matrix.astype(jnp.float32)
    updated = (own - 0.5 * cube_part).astype(jnp.bfloat16)
    tile_blocks = tile_rows // BLK
    half_blocks = width // BLK
    blocks = updated.reshape(tile_blocks, BLK, half_blocks, BLK).transpose(0, 2, 1, 3)
    blocks = blocks.reshape(tile_blocks * half_blocks, BLK * BLK // 128, 128)
    chosen = send_list[0]
    picked = jnp.take(blocks, jnp.maximum(chosen, 0), axis=0)
    outgoing = jnp.where((chosen >= 0)[:, None, None], picked, jnp.zeros_like(picked))
    arrived = lax.all_to_all(outgoing, "col", split_axis=0, concat_axis=0, tiled=True)
    everyone = lax.all_gather(arrived, "layer", axis=0)
    total = everyone.astype(jnp.float32).sum(0).astype(jnp.bfloat16)
    return total.reshape(total.shape[0], BLK * BLK)


def solution(mesh):
    in_specs = (P("row", "col"), P("row", "col"), P(("row", "col"), None))
    out_specs = P(("row", "col"), None)
    return jax.shard_map(
        on_device, mesh=mesh, in_specs=in_specs, out_specs=out_specs, check_vma=False
    )
```

time: 422 us -> 201 us (0.48)
  starting transfers between devices: 161 us -> 4.17 us
  waiting for transfers between devices: 206 us -> 132 us
  blocking collectives: 19.1 us -> 32.6 us
    ppermute x31 -> x0, starting transfers between devices: 161 us -> none  [passed_along(): lax.ppermute(value, axis, [(i, (i + by) % devices) for i in range(devices)])]
    all_gather x0 -> x3, waiting for transfers between devices: none -> 125 us  [the longest x1 48.8 us: on_device(): left_t = lax.all_gather(left_piece, 'col', axis=0, tiled=True)]
    psum x2 -> x0, waiting for transfers between devices: 125 us -> none  [the longest x1 62.9 us: on_device(): cube = lax.psum(cube_part.astype(jnp.bfloat16), 'layer').astype(jnp.float32)]
    ppermute x31 -> x0, waiting for transfers between devices: 81.1 us -> none  [passed_along(): lax.ppermute(value, axis, [(i, (i + by) % devices) for i in range(devices)])]
    all_gather x0 -> x1, blocking collectives: none -> 11.4 us  [on_device(): everyone = lax.all_gather(arrived, 'layer', axis=0)]
    all_to_all x0 -> x1, waiting for transfers between devices: none -> 6.94 us  [on_device(): lax.all_to_all(square_part, 'layer', split_axis=0, concat_axis=0, tiled=T...]
  transfers between devices with their start and end apart: 33 -> 4, of which waited for: 26 -> 4; matrix products, arithmetic and copies ran while one was open for 2% -> 2% of each run, Pallas kernels for 0% -> 0%
where the time goes in v1:
time: 201 us; the launch traced here: 200 us
  waiting for transfers between devices  132 us (66%)
  blocking collectives  32.6 us (16%)
  between operations  13.3 us (7%)
  local copies, waits for them, and re-layouts  10.2 us (5%)
  matrix products  6.78 us (3%)
  starting transfers between devices  4.17 us (2%)
    all_gather x1, waiting for transfers between devices, on_device(): left_t = lax.all_gather(left_piece, 'col', axis=0, tiled=True)  48.8 us
    all_gather x1, waiting for transfers between devices, on_device(): right = lax.all_gather(right_piece, 'row', axis=0, tiled=True)  42 us
    all_gather x1, waiting for transfers between devices, on_device(): filtered = lax.all_gather(filtered_piece, 'row', axis=0, tiled=True)  34.3 us
    all_to_all x1, blocking collectives, on_device(): lax.all_to_all(outgoing, 'col', split_axis=0, concat_axis=0, tiled=True)  21.2 us
    all_gather x1, blocking collectives, on_device(): everyone = lax.all_gather(arrived, 'layer', axis=0)  11.4 us
    all_to_all x1, waiting for transfers between devices, on_device(): lax.all_to_all(square_part, 'layer', split_axis=0, concat_axis=0, tiled=T...  6.94 us
    all_to_all x1, starting transfers between devices, on_device(): lax.all_to_all(square_part, 'layer', split_axis=0, concat_axis=0, tiled=T...  4.12 us
  transfers between devices with their start and end apart: 4, of which 4 were waited for; matrix products, arithmetic and copies ran while one was open for 2% of the time, Pallas kernels for 0%

profile of v1, /device:TPU:1, one launch (start us, length us, event | category | flops | bytes accessed | tf_op | source)
XLA Modules:
  0.0 200.0 jit_solution(17258176501160128025)
XLA Ops:
  6.5 0.0 all-gather.7.cloned.1.call-start
  6.5 1.6 constant_dynamic-slice_fusion.1
  8.1 0.0 all-gather.7.cloned.1.call-update
  8.1 0.0 all-gather.5.cloned.1.call-start
  8.2 1.1 constant_dynamic-slice_fusion.2
  9.3 0.8 copy.14
  10.1 0.0 all-gather.5.cloned.1.call-update
  10.1 42.0 %all-gather.7.cloned.1.call-done = bf16[1536,384]{1,0:T(8,128)(2,1)} async-done(((bf16[192,384]{1,0:T(8,128)(2,1)}), bf16[1536,384]{1,0:T(8,128)(2,1)}) %all-gather.7.cloned.1.call-update) | async-done | bytes 1179664 | tf_op jit(solution)/shard_map/all_gather | solution.py:20
  52.1 48.8 %all-gather.5.cloned.1.call-done = bf16[1536,768]{1,0:T(8,128)(2,1)} async-done(((bf16[96,768]{1,0:T(8,128)(2,1)}), bf16[1536,768]{1,0:T(8,128)(2,1)}) %all-gather.5.cloned.1.call-update) | async-done | bytes 2359312 | tf_op jit(solution)/shard_map/all_gather | solution.py:19
  101.0 3.4 %convolution_convert_fusion = bf16[768,384]{1,0:T(8,128)(2,1)S(1)} fusion(bf16[1536,768]{1,0:T(8,128)(2,1)} %all-gather.5.cloned.1.call-done, bf16[1536,384]{1,0:T(8,128)(2,1)} %all-gather.7.cloned.1.call-done), kind=kOutput, calls=%fused_computation.3 | convolution fusion | flops 906264576 | bytes 4128768 | tf_op jit(solution)/shard_map/dot_general | solution.py:22
  104.4 0.0 copy-start.1
  104.4 0.9 copy.11
  105.3 4.1 %all-to-all-start = ((bf16[4,192,384]{2,1,0:T(8,128)(2,1)}), bf16[4,192,384]{2,1,0:T(8,128)(2,1)S(1)}, u32[]{:S(2)}, u32[]{:S(2)}) async-start(bf16[4,192,384]{2,1,0:T(8,128)(2,1)} %bitcast.7), calls=%async_computation | async-start | bytes 1179648 | tf_op jit(solution)/shard_map/all_to_all | solution.py:25
  109.4 0.0 all-gather.9.cloned.1.call-start
  109.4 0.0 copy-done.1
  109.4 0.1 broadcast_in_dim.30
  109.5 0.1 reshape.56
  109.5 0.1 broadcast_in_dim.31
  109.6 1.6 reshape_reshape.3
  111.2 0.3 constant_dynamic-slice_fusion
  111.6 0.0 copy-start.2
  111.6 0.0 copy-start
  111.6 0.6 copy.12
  112.2 6.9 %all-to-all-done = bf16[4,192,384]{2,1,0:T(8,128)(2,1)S(1)} async-done(((bf16[4,192,384]{2,1,0:T(8,128)(2,1)}), bf16[4,192,384]{2,1,0:T(8,128)(2,1)S(1)}, u32[]{:S(2)}, u32[]{:S(2)}) %all-to-all-start) | async-done | bytes 589856 | tf_op jit(solution)/shard_map/all_to_all | solution.py:25
  119.1 0.1 convert_reduce_fusion
  119.2 0.7 fusion.2
  119.9 0.0 all-gather.9.cloned.1.call-update
  119.9 0.0 copy-done.2
  120.0 34.3 %all-gather.9.cloned.1.call-done = bf16[1536,384]{1,0:T(8,128)(2,1)} async-done(((bf16[192,384]{1,0:T(8,128)(2,1)}), bf16[1536,384]{1,0:T(8,128)(2,1)}) %all-gather.9.cloned.1.call-update) | async-done | bytes 1179664 | tf_op jit(solution)/shard_map/all_gather | solution.py:32
  154.3 0.0 copy-done
  154.3 3.4 %fusion.1 = bf16[768,384]{1,0:T(8,128)(2,1)S(1)} fusion(bf16[1536,768]{1,0:T(8,128)(2,1)} %all-gather.5.cloned.1.call-done, bf16[1536,384]{1,0:T(8,128)(2,1)} %all-gather.9.cloned.1.call-done, bf16[768,384]{1,0:T(8,128)(2,1)S(1)} %copy-done, f32[]{:T(128)S(6)} %select_n.22), kind=kOutput, calls=%fused_computation.4 | convolution fusion | flops 907444224 | bytes 4718596 | tf_op jit(solution)/shard_map/dot_general | solution.py:33
  157.7 0.9 reshape.58
  158.6 0.3 copy.13
  158.9 0.6 reshape.59
  159.5 0.6 gather_fusion
  160.0 0.1 select_select_fusion
  160.1 21.2 %all_to_all.10 = bf16[16,32,128]{2,1,0:T(8,128)(2,1)S(1)} all-to-all(bf16[16,32,128]{2,1,0:T(8,128)(2,1)S(1)} %select_select_fusion), channel_id=1, replica_groups=mesh['row'=8,'col'=16,'layer'=4] {'col'}, dimensions={0} | all-to-all | bytes 262144 | tf_op jit(solution)/shard_map/all_to_all | solution.py:43
  181.3 11.4 %all-gather = bf16[64,32,128]{2,1,0:T(8,128)(2,1)S(1)} all-gather(bf16[16,32,128]{2,1,0:T(8,128)(2,1)S(1)} %all_to_all.10), channel_id=2, replica_groups=mesh['row'=8,'col'=16,'layer'=4] {'layer'}, dimensions={0}, use_global_device_ids=true | all-gather | bytes 655360 | tf_op jit(solution)/shard_map/all_gather | solution.py:44
  192.7 0.1 reduce_sum.22
  192.8 0.7 copy.17
  (4 shorter events, 0.0 us)
Async XLA Ops:
  6.5 45.6 %all-gather.7.cloned.1.call-start = ((), (), s32[]{:S(2)}) async-start(), calls=%async_computation.3 | async-start | bytes 1327104 | tf_op jit(solution)/shard_map/all_gather | solution.py:20
  8.1 92.8 %all-gather.5.cloned.1.call-start = ((), (), s32[]{:S(2)}) async-start(), calls=%async_computation.2 | async-start | bytes 2506752 | tf_op jit(solution)/shard_map/all_gather | solution.py:19
  104.4 5.0 %copy-start.1 = (s32[12,6]{0,1:T(8,128)S(1)}, s32[12,6]{0,1:T(8,128)}, u32[]{:S(2)}) copy-start(s32[12,6]{0,1:T(8,128)} %param.4) | copy-start | bytes 868
  105.3 13.9 %all-to-all-start = ((bf16[4,192,384]{2,1,0:T(8,128)(2,1)}), bf16[4,192,384]{2,1,0:T(8,128)(2,1)S(1)}, u32[]{:S(2)}, u32[]{:S(2)}) async-start(bf16[4,192,384]{2,1,0:T(8,128)(2,1)} %bitcast.7), calls=%async_computation | async-start | bytes 1179648 | tf_op jit(solution)/shard_map/all_to_all | solution.py:25
  109.4 44.9 %all-gather.9.cloned.1.call-start = ((), (), s32[]{:S(2)}) async-start(), calls=%async_computation.4 | async-start | bytes 1327104 | tf_op jit(solution)/shard_map/all_gather | solution.py:32
  111.6 8.3 %copy-start.2 = (s32[1,16]{1,0:T(1,128)S(1)}, s32[1,16]{1,0:T(1,128)}, u32[]{:S(2)}) copy-start(s32[1,16]{1,0:T(1,128)} %param.5) | copy-start | bytes 196
  111.6 42.7 %copy-start = (bf16[768,384]{1,0:T(8,128)(2,1)S(1)}, bf16[768,384]{1,0:T(8,128)(2,1)}, u32[]{:S(2)}) copy-start(bf16[768,384]{1,0:T(8,128)(2,1)} %param.3) | copy-start | bytes 1769476
Sparse Core Ops, SparseCore 0:
  9.4 42.6 all-gather.6
  54.3 46.6 all-gather.4
  120.0 34.1 all-gather.8

commit v2 on v1

v2 whole, which is shorter than its diff:
```python
import functools

import jax
import jax.numpy as jnp
from jax import lax
from jax.experimental import pallas as pl
from jax.experimental.pallas import tpu as pltpu
from jax.sharding import Mesh, PartitionSpec as P

BLK = 64
CONTRACT = (((0,), (0,)), ((), ()))


def to_all(piece, axis):
    copies = jnp.broadcast_to(piece[None], (lax.axis_size(axis),) + piece.shape)
    return lax.all_to_all(copies, axis, split_axis=0, concat_axis=0, tiled=True)


def product(left_ref, right_ref):
    _, depth, _ = left_ref.shape
    columns = right_ref.shape[-1]
    total = None
    for side in range(2):
        right = right_ref[:, side].reshape(depth, columns)
        term = lax.dot_general(left_ref[side], right, CONTRACT, preferred_element_type=jnp.float32)
        total = term if total is None else total + term
    return total


def square_kernel(left_ref, right_ref, out_ref):
    layers, halves, part, columns = out_ref.shape
    total = product(left_ref, right_ref).astype(out_ref.dtype)
    for half in range(halves):
        for layer in range(layers):
            start = (half * layers + layer) * part
            out_ref[layer, half] = total[start : start + part]


def cube_kernel(chosen_ref, left_ref, right_ref, matrix_ref, own_ref, out_ref, total_ref, block_ref):
    owners, pairs, lanes = out_ref.shape
    half_blocks = matrix_ref.shape[1] // BLK
    total_ref[...] = own_ref[0] * matrix_ref[...].astype(jnp.float32) - 0.5 * product(left_ref, right_ref)
    low = lax.broadcasted_iota(jnp.int32, (pairs, lanes), 1) < BLK

    def one(owner, carry):
        index = chosen_ref[owner]
        live = jnp.where(index >= 0, 1.0, 0.0)
        index = jnp.maximum(index, 0)
        row = index // half_blocks
        column = index % half_blocks
        start = pl.multiple_of(row * BLK, BLK)
        lane = pl.multiple_of(column // 2 * lanes, lanes)
        block = total_ref[pl.ds(start, BLK), pl.ds(lane, lanes)] * live
        turned = pltpu.roll(block, BLK, 1)
        odd = column % 2 == 1
        block_ref[0] = jnp.where(odd, turned, block)
        block_ref[1] = jnp.where(odd, block, turned)
        even_rows = block_ref[0, pl.ds(0, pairs, stride=2), :]
        odd_rows = block_ref[1, pl.ds(1, pairs, stride=2), :]
        out_ref[owner] = jnp.where(low, even_rows, odd_rows).astype(out_ref.dtype)
        return carry

    lax.fori_loop(0, owners, one, 0)


def on_device(matrix, keep_mask, send_list):
    layers = lax.axis_size("layer")
    rows_count = lax.axis_size("row")
    layer_index = lax.axis_index("layer")
    core_index = lax.axis_index("core")
    tile_rows, width = matrix.shape
    part = width // layers
    halves = tile_rows // width
    depth = rows_count * part
    vmem = pl.BlockSpec(memory_space=pltpu.VMEM)
    smem = pl.BlockSpec(memory_space=pltpu.SMEM)
    params = pltpu.CompilerParams(vmem_limit_bytes=40 * 2**20)

    left_piece = lax.dynamic_slice_in_dim(matrix, layer_index * part, part, 1).T
    right_piece = lax.dynamic_slice_in_dim(
        matrix.reshape(halves, layers, part, width), layer_index, 1, 1
    ).reshape(halves, part, width)
    left_own = to_all(left_piece, "z").reshape(depth, tile_rows)
    right = to_all(right_piece, "row")
    left_other = lax.ppermute(left_own, "core", [(0, 1), (1, 0)])
    first = core_index == 0
    left = jnp.stack([jnp.where(first, left_own, left_other), jnp.where(first, left_other, left_own)])

    square_part = pl.pallas_call(
        square_kernel,
        out_shape=jax.ShapeDtypeStruct((layers, halves, part, width), jnp.bfloat16),
        in_specs=[vmem, vmem],
        out_specs=vmem,
        compiler_params=params,
    )(left, right)
    parts = lax.all_to_all(square_part, "layer", split_axis=0, concat_axis=0, tiled=True)
    square = parts.astype(jnp.float32).sum(0)
    block_keep = jnp.repeat(jnp.repeat(keep_mask.astype(jnp.float32), BLK, 0), BLK, 1)
    block_keep = lax.dynamic_slice_in_dim(
        block_keep.reshape(halves, layers, part, width), layer_index, 1, 1
    ).reshape(halves, part, width)
    filtered_piece = (square * block_keep).astype(jnp.bfloat16)
    filtered = to_all(filtered_piece, "row")

    own = jnp.where(layer_index == 0, 1.5, 0.0).astype(jnp.float32).reshape(1)
    chosen = send_list[0]
    pairs = BLK * BLK // 128
    outgoing = pl.pallas_call(
        cube_kernel,
        out_shape=jax.ShapeDtypeStruct((chosen.shape[0], pairs, 128), jnp.bfloat16),
        in_specs=[smem, vmem, vmem, vmem, smem],
        out_specs=vmem,
        scratch_shapes=[
            pltpu.VMEM((tile_rows, width), jnp.float32),
            pltpu.VMEM((2, BLK, 128), jnp.float32),
        ],
        compiler_params=params,
    )(chosen, left, filtered, matrix, own)
    arrived = lax.all_to_all(outgoing, ("z", "core"), split_axis=0, concat_axis=0, tiled=True)
    everyone = to_all(arrived, "layer")
    total = everyone.astype(jnp.float32).sum(0).astype(jnp.bfloat16)
    return total.reshape(total.shape[0], BLK * BLK)


def solution(mesh):
    sizes = mesh.shape
    cores = 2
    shape = (sizes["row"], sizes["col"] // cores, cores, sizes["layer"])
    split = Mesh(mesh.devices.reshape(shape), ("row", "z", "core", "layer"))
    column = ("z", "core")
    in_specs = (P("row", column), P("row", column), P(("row",) + column, None))
    out_specs = P(("row",) + column, None)
    return jax.shard_map(
        on_device, mesh=split, in_specs=in_specs, out_specs=out_specs, check_vma=False
    )
```

time: 201 us -> 170 us (0.85)
  waiting for transfers between devices: 132 us -> 92.7 us
  starting transfers between devices: 4.17 us -> 28.3 us
  between operations: 13.3 us -> 0.14 us
  matrix products: 6.78 us -> 0 us
  blocking collectives: 32.6 us -> 26.5 us
  Pallas kernels: 0 us -> 4.94 us
  local copies, waits for them, and re-layouts: 10.2 us -> 14.9 us
    all_gather x3 -> x0, waiting for transfers between devices: 125 us -> none  [the longest x1 48.8 us: on_device(): left_t = lax.all_gather(left_piece, 'col', axis=0, tiled=True)]
    all_to_all x0 -> x3, waiting for transfers between devices: none -> 87.3 us  [to_all(): return lax.all_to_all(copies, axis, split_axis=0, concat_axis=0, tiled=True)]
    all_to_all x0 -> x3, starting transfers between devices: none -> 21.4 us  [to_all(): return lax.all_to_all(copies, axis, split_axis=0, concat_axis=0, tiled=True)]
    all_gather x1 -> x0, blocking collectives: 11.4 us -> none  [on_device(): everyone = lax.all_gather(arrived, 'layer', axis=0)]
    dot_general x2 -> x0, matrix products: 6.78 us -> none  [the longest x1 3.39 us: on_device(): lax.dot_general(left_t, filtered, contract, preferred_element_type=jnp.fl...]
    all_to_all x1 -> x2, blocking collectives: 21.2 us -> 26.5 us  [the longest x1 14.3 us: on_device(): lax.all_to_all(outgoing, ('z', 'core'), split_axis=0, concat_axis=0, tile...]
    pallas_call x0 -> x2, Pallas kernels: none -> 4.94 us  [the longest x1 3.53 us: on_device(): pl.pallas_call(cube_kernel, out_shape=jax.ShapeDtypeStruct((chosen.shape[...]
    broadcast_in_dim x0 -> x5, local copies, waits for them, and re-layouts: none -> 4.44 us  [to_all(): copies = jnp.broadcast_to(piece[None], (lax.axis_size(axis),) + piece.shape)]
  transfers between devices with their start and end apart: 4 -> 5, of which waited for: 4 -> 5; matrix products, arithmetic and copies ran while one was open for 2% -> 5% of each run, Pallas kernels for 0% -> 0%
where the time goes in v2:
time: 170 us; the launch traced here: 169 us
  waiting for transfers between devices  92.7 us (55%)
  starting transfers between devices  28.3 us (17%)
  blocking collectives  26.5 us (16%)
  local copies, waits for them, and re-layouts  14.9 us (9%)
  Pallas kernels  4.94 us (3%)
  other arithmetic  1.75 us (1%)
    all_to_all x3, waiting for transfers between devices, to_all(): return lax.all_to_all(copies, axis, split_axis=0, concat_axis=0, tiled=True)  87.3 us
    all_to_all x3, starting transfers between devices, to_all(): return lax.all_to_all(copies, axis, split_axis=0, concat_axis=0, tiled=True)  21.4 us
    all_to_all x1, blocking collectives, on_device(): lax.all_to_all(outgoing, ('z', 'core'), split_axis=0, concat_axis=0, tile...  14.3 us
    all_to_all x1, blocking collectives, to_all(): return lax.all_to_all(copies, axis, split_axis=0, concat_axis=0, tiled=True)  12.3 us
    broadcast_in_dim x5, local copies, waits for them, and re-layouts, to_all(): copies = jnp.broadcast_to(piece[None], (lax.axis_size(axis),) + piece.shape)  4.44 us
    all_to_all x1, starting transfers between devices, on_device(): lax.all_to_all(square_part, 'layer', split_axis=0, concat_axis=0, tiled=T...  4.29 us
    pallas_call x1, Pallas kernels, on_device(): pl.pallas_call(cube_kernel, out_shape=jax.ShapeDtypeStruct((chosen.shape[...  3.53 us
  transfers between devices with their start and end apart: 5, of which 5 were waited for; matrix products, arithmetic and copies ran while one was open for 5% of the time, Pallas kernels for 0%

profile of v2, /device:TPU:1, one launch (start us, length us, event | category | flops | bytes accessed | tf_op | source)
XLA Modules:
  0.0 169.4 jit_solution(8420335209056723131)
XLA Ops:
  0.0 1.1 dynamic-slice_bitcast_fusion
  1.1 0.1 copy.9
  1.3 1.1 broadcast_in_dim.14
  2.4 10.9 %all-to-all-start = ((bf16[8,96,768]{2,1,0:T(8,128)(2,1)}), bf16[8,96,768]{2,1,0:T(8,128)(2,1)S(1)}, u32[]{:S(2)}, u32[]{:S(2)}) async-start(bf16[8,96,768]{2,1,0:T(8,128)(2,1)} %broadcast_in_dim.14), calls=%async_computation | async-start | bytes 2359296 | tf_op jit(solution)/shard_map/all_to_all | solution.py:16
  13.2 0.9 dynamic-slice_bitcast_fusion.1
  14.2 31.1 %all-to-all-done = bf16[8,96,768]{2,1,0:T(8,128)(2,1)S(1)} async-done(((bf16[8,96,768]{2,1,0:T(8,128)(2,1)}), bf16[8,96,768]{2,1,0:T(8,128)(2,1)S(1)}, u32[]{:S(2)}, u32[]{:S(2)}) %all-to-all-start) | async-done | bytes 1179680 | tf_op jit(solution)/shard_map/all_to_all | solution.py:16
  45.3 1.2 broadcast_in_dim.16
  46.5 6.8 %all-to-all-start.1 = ((bf16[8,2,96,384]{3,2,1,0:T(8,128)(2,1)}), bf16[8,2,96,384]{3,2,1,0:T(8,128)(2,1)S(1)}, u32[]{:S(2)}, u32[]{:S(2)}) async-start(bf16[8,2,96,384]{3,2,1,0:T(8,128)(2,1)} %broadcast_in_dim.16), calls=%async_computation.1 | async-start | bytes 2359296 | tf_op jit(solution)/shard_map/all_to_all | solution.py:16
  53.3 2.7 %collective-permute-start = (bf16[768,768]{1,0:T(8,128)(2,1)S(1)}, bf16[768,768]{1,0:T(8,128)(2,1)S(1)}, u32[]{:S(2)}, u32[]{:S(2)}) collective-permute-start(bf16[768,768]{1,0:T(8,128)(2,1)S(1)} %bitcast.28), channel_id=1, source_target_pairs={{0,4},{4,0},{1,5},{5,1},{2,6},{6,2},{3,7},{7,3},{8,12},{12,8},{9,1... | collective-permute-start | bytes 3538952 | tf_op jit(solution)/shard_map/ppermute | solution.py:85
  56.0 2.4 %collective-permute-done = bf16[768,768]{1,0:T(8,128)(2,1)S(1)} collective-permute-done((bf16[768,768]{1,0:T(8,128)(2,1)S(1)}, bf16[768,768]{1,0:T(8,128)(2,1)S(1)}, u32[]{:S(2)}, u32[]{:S(2)}) %collective-permute-start) | collective-permute-done | bytes 1179680 | tf_op jit(solution)/shard_map/ppermute | solution.py:85
  58.4 0.2 select_bitcast_fusion.1
  58.6 0.2 pad_maximum_fusion.left_ref
  58.9 26.5 %all-to-all-done.1.right_ref = bf16[8,2,96,384]{3,2,1,0:T(8,128)(2,1)S(1)} async-done(((bf16[8,2,96,384]{3,2,1,0:T(8,128)(2,1)}), bf16[8,2,96,384]{3,2,1,0:T(8,128)(2,1)S(1)}, u32[]{:S(2)}, u32[]{:S(2)}) %all-to-all-start.1) | async-done | bytes 1179680 | tf_op jit(solution)/shard_map/all_to_all | solution.py:16
  85.3 1.4 shard_map.37
  86.7 0.0 copy-start
  86.7 0.8 copy-done
  87.6 0.0 copy-start.3
  87.6 4.3 %all-to-all-start.2 = ((bf16[4,2,96,384]{3,2,1,0:T(8,128)(2,1)}), bf16[4,2,96,384]{3,2,1,0:T(8,128)(2,1)}, u32[]{:S(2)}, u32[]{:S(2)}) async-start(bf16[4,2,96,384]{3,2,1,0:T(8,128)(2,1)} %copy-done), calls=%async_computation.2 | async-start | bytes 1179648 | tf_op jit(solution)/shard_map/all_to_all | solution.py:96
  91.9 0.0 copy-done.3
  91.9 0.1 broadcast_in_dim.34
  92.0 0.7 reshape.31
  92.7 0.8 broadcast_in_dim.35
  93.5 2.7 %reshape_reshape.3 = f32[2,4,96,384]{2,1,0,3:T(4,128)} reshape(f32[768,6,64]{0,2,1:T(8,128)S(1)} %broadcast_in_dim.35) | data formatting | bytes 2359296 | tf_op jit(solution)/shard_map/reshape;reshape | solution.py:100
  96.2 1.7 %constant_dynamic-slice_fusion = f32[2,1,96,384]{2,1,0,3:T(1,128)S(1)} fusion(f32[2,4,96,384]{2,1,0,3:T(4,128)} %reshape_reshape.3, s32[]{:T(128)S(6)} %select_n.27), kind=kLoop, calls=%fused_computation.9 | loop fusion | bytes 589828 | tf_op jit(solution)/shard_map/dynamic_slice | solution.py:99
  98.0 0.6 copy.10
  98.5 3.0 %all-to-all-done.2 = bf16[4,2,96,384]{3,2,1,0:T(8,128)(2,1)} async-done(((bf16[4,2,96,384]{3,2,1,0:T(8,128)(2,1)}), bf16[4,2,96,384]{3,2,1,0:T(8,128)(2,1)}, u32[]{:S(2)}, u32[]{:S(2)}) %all-to-all-start.2) | async-done | bytes 589856 | tf_op jit(solution)/shard_map/all_to_all | solution.py:96
  101.5 1.2 convert_reduce_fusion
  102.7 1.2 broadcast_in_dim.36
  103.9 0.0 copy-start.2
  103.9 3.7 %all-to-all-start.3 = ((bf16[8,2,96,384]{3,2,1,0:T(8,128)(2,1)}), bf16[8,2,96,384]{3,2,1,0:T(8,128)(2,1)S(1)}, u32[]{:S(2)}, u32[]{:S(2)}) async-start(bf16[8,2,96,384]{3,2,1,0:T(8,128)(2,1)} %broadcast_in_dim.36), calls=%async_computation.3 | async-start | bytes 2359296 | tf_op jit(solution)/shard_map/all_to_all | solution.py:16
  107.6 29.7 %all-to-all-done.3.right_ref = bf16[8,2,96,384]{3,2,1,0:T(8,128)(2,1)S(1)} async-done(((bf16[8,2,96,384]{3,2,1,0:T(8,128)(2,1)}), bf16[8,2,96,384]{3,2,1,0:T(8,128)(2,1)S(1)}, u32[]{:S(2)}, u32[]{:S(2)}) %all-to-all-start.3) | async-done | bytes 1179680 | tf_op jit(solution)/shard_map/all_to_all | solution.py:16
  137.4 0.0 copy-done.2
  137.4 0.0 copy-start.1
  137.4 1.1 copy-done.1
  138.4 3.5 %shard_map.38 = bf16[16,32,128]{2,1,0:T(8,128)(2,1)S(1)} custom-call(s32[16]{0:T(128)S(1)} %bitcast.27, bf16[2,768,768]{2,1,0:T(8,128)(2,1)S(1)} %pad_maximum_fusion.left_ref, bf16[8,2,96,384]{3,2,1,0:T(8,128)(2,1)S(1)} %all-to-all-done.3.right_ref, bf16[768,384]{1,0:T(8,128)(2,1)S(1)} %copy-done.1, f32[1]{0:T(128)} %bitcast.8.own_ref), custom_call_target="tpu_custom_call" | custom-call | tf_op jit(solution)/shard_map/pallas_call | solution.py:108
  142.0 14.3 %all_to_all.30 = bf16[16,32,128]{2,1,0:T(8,128)(2,1)S(1)} all-to-all(bf16[16,32,128]{2,1,0:T(8,128)(2,1)S(1)} %shard_map.38), channel_id=1, replica_groups=mesh['row'=8,'z'=8,'core'=2,'layer'=4] {'z','core'}, dimensions={0} | all-to-all | bytes 262144 | tf_op jit(solution)/shard_map/all_to_all | solution.py:119
  156.2 0.1 broadcast_in_dim.37
  156.3 12.3 %all_to_all.31 = bf16[4,16,32,128]{3,2,1,0:T(8,128)(2,1)S(1)} all-to-all(bf16[4,16,32,128]{3,2,1,0:T(8,128)(2,1)S(1)} %broadcast_in_dim.37), channel_id=1, replica_groups=mesh['row'=8,'z'=8,'core'=2,'layer'=4] {'layer'}, dimensions={0} | all-to-all | bytes 1048576 | tf_op jit(solution)/shard_map/all_to_all | solution.py:16
  168.6 0.1 reduce_sum.22
  168.7 0.7 copy.13
  (2 shorter events, 0.0 us)
Async XLA Ops:
  2.4 42.9 %all-to-all-start = ((bf16[8,96,768]{2,1,0:T(8,128)(2,1)}), bf16[8,96,768]{2,1,0:T(8,128)(2,1)S(1)}, u32[]{:S(2)}, u32[]{:S(2)}) async-start(bf16[8,96,768]{2,1,0:T(8,128)(2,1)} %broadcast_in_dim.14), calls=%async_computation | async-start | bytes 2359296 | tf_op jit(solution)/shard_map/all_to_all | solution.py:16
  46.5 38.9 %all-to-all-start.1 = ((bf16[8,2,96,384]{3,2,1,0:T(8,128)(2,1)}), bf16[8,2,96,384]{3,2,1,0:T(8,128)(2,1)S(1)}, u32[]{:S(2)}, u32[]{:S(2)}) async-start(bf16[8,2,96,384]{3,2,1,0:T(8,128)(2,1)} %broadcast_in_dim.16), calls=%async_computation.1 | async-start | bytes 2359296 | tf_op jit(solution)/shard_map/all_to_all | solution.py:16
  53.3 5.1 %collective-permute-start = (bf16[768,768]{1,0:T(8,128)(2,1)S(1)}, bf16[768,768]{1,0:T(8,128)(2,1)S(1)}, u32[]{:S(2)}, u32[]{:S(2)}) collective-permute-start(bf16[768,768]{1,0:T(8,128)(2,1)S(1)} %bitcast.28), channel_id=1, source_target_pairs={{0,4},{4,0},{1,5},{5,1},{2,6},{6,2},{3,7},{7,3},{8,12},{12,8},{9,1... | collective-permute-start | bytes 3538952 | tf_op jit(solution)/shard_map/ppermute | solution.py:85
  86.7 0.8 copy-start
  87.6 4.3 %copy-start.3 = (s32[12,6]{0,1:T(8,128)S(1)}, s32[12,6]{0,1:T(8,128)}, u32[]{:S(2)}) copy-start(s32[12,6]{0,1:T(8,128)} %param.4) | copy-start | bytes 868
  87.6 13.9 %all-to-all-start.2 = ((bf16[4,2,96,384]{3,2,1,0:T(8,128)(2,1)}), bf16[4,2,96,384]{3,2,1,0:T(8,128)(2,1)}, u32[]{:S(2)}, u32[]{:S(2)}) async-start(bf16[4,2,96,384]{3,2,1,0:T(8,128)(2,1)} %copy-done), calls=%async_computation.2 | async-start | bytes 1179648 | tf_op jit(solution)/shard_map/all_to_all | solution.py:96
  103.9 33.5 %copy-start.2 = (s32[1,16]{1,0:T(1,128)S(1)}, s32[1,16]{1,0:T(1,128)}, u32[]{:S(2)}) copy-start(s32[1,16]{1,0:T(1,128)} %param.5) | copy-start | bytes 196
  103.9 33.5 %all-to-all-start.3 = ((bf16[8,2,96,384]{3,2,1,0:T(8,128)(2,1)}), bf16[8,2,96,384]{3,2,1,0:T(8,128)(2,1)S(1)}, u32[]{:S(2)}, u32[]{:S(2)}) async-start(bf16[8,2,96,384]{3,2,1,0:T(8,128)(2,1)} %broadcast_in_dim.36), calls=%async_computation.3 | async-start | bytes 2359296 | tf_op jit(solution)/shard_map/all_to_all | solution.py:16
  137.4 1.1 copy-start.1

commit v3 on v2

v3 whole, which is shorter than its diff:
```python
import functools

import jax
import jax.numpy as jnp
from jax import lax
from jax.experimental import pallas as pl
from jax.experimental.pallas import tpu as pltpu
from jax.sharding import Mesh, PartitionSpec as P

BLK = 64
CONTRACT = (((0,), (0,)), ((), ()))


def to_all(piece, axis):
    copies = jnp.broadcast_to(piece[None], (lax.axis_size(axis),) + piece.shape)
    return lax.all_to_all(copies, axis, split_axis=0, concat_axis=0, tiled=True)


def shifted(piece, axis, by):
    size = lax.axis_size(axis)
    return lax.ppermute(piece, axis, [(i, (i - by) % size) for i in range(size)])


def ring_of_eight(piece, axis):
    half = piece.shape[0] // 2
    up = shifted(piece, axis, 2)
    down = shifted(piece, axis, -2)
    near_up = shifted(piece, axis, 1)
    near_down = shifted(piece, axis, -1)
    far_up = shifted(up, axis, 1)
    far_down = shifted(down, axis, -1)
    opposite_up = shifted(up[:half], axis, 2)
    opposite_down = shifted(down[half:], axis, -2)
    return piece, near_up, up, far_up, opposite_up, opposite_down, far_down, down, near_down


def product(own_ref, other_ref, right_ref):
    depth = own_ref.shape[0]
    columns = right_ref.shape[-1]
    own = lax.dot_general(
        own_ref[...], right_ref[0].reshape(depth, columns), CONTRACT, preferred_element_type=jnp.float32
    )
    other = lax.dot_general(
        other_ref[...], right_ref[1].reshape(depth, columns), CONTRACT, preferred_element_type=jnp.float32
    )
    return own + other


def square_kernel(place_ref, own_ref, other_ref, right_ref, out_ref, ordered_ref):
    layers, halves, part, columns = out_ref.shape
    tiles = right_ref.shape[0]
    z, core = place_ref[1], place_ref[2]
    for offset in range(tiles):
        tile = lax.rem(z + offset, tiles)
        ordered_ref[0, offset] = right_ref[tile, core]
        ordered_ref[1, offset] = right_ref[tile, 1 - core]
    total = product(own_ref, other_ref, ordered_ref).astype(out_ref.dtype)
    for half in range(halves):
        for layer in range(layers):
            start = (half * layers + layer) * part
            out_ref[layer, half] = total[start : start + part]


def cube_kernel(chosen_ref, place_ref, scale_ref, own_ref, other_ref, matrix_ref, *refs):
    pieces = refs[:9]
    out_ref, ordered_ref, total_ref, block_ref = refs[9:]
    tiles = ordered_ref.shape[1]
    row, z, core = place_ref[0], place_ref[1], place_ref[2]
    for offset, piece in zip((0, 1, 2, 3, 5, 6, 7), pieces[:4] + pieces[6:]):
        tile = lax.rem(row + offset + tiles - z, tiles)
        ordered_ref[0, tile] = piece[core]
        ordered_ref[1, tile] = piece[1 - core]
    tile = lax.rem(row + 4 + tiles - z, tiles)
    ordered_ref[core, tile] = pieces[4][0]
    ordered_ref[1 - core, tile] = pieces[5][0]
    owners, pairs, lanes = out_ref.shape
    half_blocks = matrix_ref.shape[1] // BLK
    total_ref[...] = scale_ref[0] * matrix_ref[...].astype(jnp.float32) - 0.5 * product(
        own_ref, other_ref, ordered_ref
    )
    low = lax.broadcasted_iota(jnp.int32, (pairs, lanes), 1) < BLK

    def one(owner, carry):
        index = chosen_ref[owner]
        live = jnp.where(index >= 0, 1.0, 0.0)
        index = jnp.maximum(index, 0)
        column = index % half_blocks
        start = pl.multiple_of(index // half_blocks * BLK, BLK)
        lane = pl.multiple_of(column // 2 * lanes, lanes)
        block = total_ref[pl.ds(start, BLK), pl.ds(lane, lanes)] * live
        turned = pltpu.roll(block, BLK, 1)
        odd = column % 2 == 1
        block_ref[0] = jnp.where(odd, turned, block)
        block_ref[1] = jnp.where(odd, block, turned)
        even_rows = block_ref[0, pl.ds(0, pairs, stride=2), :]
        odd_rows = block_ref[1, pl.ds(1, pairs, stride=2), :]
        out_ref[owner] = jnp.where(low, even_rows, odd_rows).astype(out_ref.dtype)
        return carry

    lax.fori_loop(0, owners, one, 0)


def on_device(matrix, keep_mask, send_list):
    layers = lax.axis_size("layer")
    rows_count = lax.axis_size("row")
    layer_index = lax.axis_index("layer")
    row_index = lax.axis_index("row")
    z_index = lax.axis_index("z")
    core_index = lax.axis_index("core")
    tile_rows, width = matrix.shape
    part = width // layers
    halves = tile_rows // width
    vmem = pl.BlockSpec(memory_space=pltpu.VMEM)
    smem = pl.BlockSpec(memory_space=pltpu.SMEM)
    params = pltpu.CompilerParams(vmem_limit_bytes=40 * 2**20)

    left_piece = lax.dynamic_slice_in_dim(matrix, layer_index * part, part, 1).T
    right_piece = lax.dynamic_slice_in_dim(
        matrix.reshape(halves, layers, part, width), layer_index, 1, 1
    ).reshape(halves, part, width)
    right = to_all(right_piece, "row")
    left_own = jnp.concatenate(ring_of_eight(left_piece, "z"), axis=0)
    left_other = lax.ppermute(left_own, "core", [(0, 1), (1, 0)])
    place = jnp.stack([row_index, z_index, core_index])

    square_part = pl.pallas_call(
        square_kernel,
        out_shape=jax.ShapeDtypeStruct((layers, halves, part, width), jnp.bfloat16),
        in_specs=[smem, vmem, vmem, vmem],
        out_specs=vmem,
        scratch_shapes=[pltpu.VMEM((halves, rows_count, part, width), jnp.bfloat16)],
        compiler_params=params,
    )(place, left_own, left_other, right)
    parts = lax.all_to_all(square_part, "layer", split_axis=0, concat_axis=0, tiled=True)
    square = parts.astype(jnp.float32).sum(0)
    block_keep = jnp.repeat(jnp.repeat(keep_mask.astype(jnp.float32), BLK, 0), BLK, 1)
    block_keep = lax.dynamic_slice_in_dim(
        block_keep.reshape(halves, layers, part, width), layer_index, 1, 1
    ).reshape(halves, part, width)
    filtered_piece = (square * block_keep).astype(jnp.bfloat16)
    filtered = ring_of_eight(filtered_piece, "row")

    scale = jnp.where(layer_index == 0, 1.5, 0.0).astype(jnp.float32).reshape(1)
    chosen = send_list[0]
    pairs = BLK * BLK // 128
    outgoing = pl.pallas_call(
        cube_kernel,
        out_shape=jax.ShapeDtypeStruct((chosen.shape[0], pairs, 128), jnp.bfloat16),
        in_specs=[smem] * 3 + [vmem] * 12,
        out_specs=vmem,
        scratch_shapes=[
            pltpu.VMEM((halves, rows_count, part, width), jnp.bfloat16),
            pltpu.VMEM((tile_rows, width), jnp.float32),
            pltpu.VMEM((2, BLK, 128), jnp.float32),
        ],
        compiler_params=params,
    )(chosen, place, scale, left_own, left_other, matrix, *filtered)
    arrived = lax.all_to_all(outgoing, ("z", "core"), split_axis=0, concat_axis=0, tiled=True)
    everyone = to_all(arrived, "layer")
    total = everyone.astype(jnp.float32).sum(0).astype(jnp.bfloat16)
    return total.reshape(total.shape[0], BLK * BLK)


def solution(mesh):
    sizes = mesh.shape
    cores = 2
    shape = (sizes["row"], sizes["col"] // cores, cores, sizes["layer"])
    split = Mesh(mesh.devices.reshape(shape), ("row", "z", "core", "layer"))
    column = ("z", "core")
    in_specs = (P("row", column), P("row", column), P(("row",) + column, None))
    out_specs = P(("row",) + column, None)
    return jax.shard_map(
        on_device, mesh=split, in_specs=in_specs, out_specs=out_specs, check_vma=False
    )
```

time: 170 us -> 148 us (0.87)
  waiting for transfers between devices: 92.7 us -> 16.3 us
  starting transfers between devices: 28.3 us -> 77.8 us
  blocking collectives: 26.5 us -> 29.8 us
    all_to_all x3 -> x1, waiting for transfers between devices: 87.3 us -> 7.92 us  [to_all(): return lax.all_to_all(copies, axis, split_axis=0, concat_axis=0, tiled=True)]
    ppermute x0 -> x16, starting transfers between devices: none -> 61.2 us  [shifted(): lax.ppermute(piece, axis, [(i, (i - by) % size) for i in range(size)])]
    all_to_all x3 -> x1, starting transfers between devices: 21.4 us -> 6.82 us  [to_all(): return lax.all_to_all(copies, axis, split_axis=0, concat_axis=0, tiled=True)]
    ppermute x0 -> x16, waiting for transfers between devices: none -> 3.77 us  [shifted(): lax.ppermute(piece, axis, [(i, (i - by) % size) for i in range(size)])]
    all_to_all x1, blocking collectives: 14.3 us -> 17.5 us  [on_device(): lax.all_to_all(outgoing, ('z', 'core'), split_axis=0, concat_axis=0, tile...]
    ppermute x1, starting transfers between devices: 2.67 us -> 5.4 us  [on_device(): left_other = lax.ppermute(left_own, 'core', [(0, 1), (1, 0)])]
    broadcast_in_dim x5 -> x3, local copies, waits for them, and re-layouts: 4.44 us -> 2.19 us  [to_all(): copies = jnp.broadcast_to(piece[None], (lax.axis_size(axis),) + piece.shape)]
  transfers between devices with their start and end apart: 5 -> 19, of which waited for: 5 -> 5; matrix products, arithmetic and copies ran while one was open for 5% -> 7% of each run, Pallas kernels for 0% -> 0%
where the time goes in v3:
time: 148 us; the launch traced here: 147 us
  starting transfers between devices  77.8 us (53%)
  blocking collectives  29.8 us (20%)
  waiting for transfers between devices  16.3 us (11%)
  local copies, waits for them, and re-layouts  13.7 us (9%)
  Pallas kernels  6.23 us (4%)
  other arithmetic  2.32 us (2%)
    ppermute x16, starting transfers between devices, shifted(): lax.ppermute(piece, axis, [(i, (i - by) % size) for i in range(size)])  61.2 us
    all_to_all x1, blocking collectives, on_device(): lax.all_to_all(outgoing, ('z', 'core'), split_axis=0, concat_axis=0, tile...  17.5 us
    all_to_all x1, blocking collectives, to_all(): return lax.all_to_all(copies, axis, split_axis=0, concat_axis=0, tiled=True)  12.3 us
    all_to_all x1, waiting for transfers between devices, to_all(): return lax.all_to_all(copies, axis, split_axis=0, concat_axis=0, tiled=True)  7.92 us
    all_to_all x1, starting transfers between devices, to_all(): return lax.all_to_all(copies, axis, split_axis=0, concat_axis=0, tiled=True)  6.82 us
    ppermute x1, starting transfers between devices, on_device(): left_other = lax.ppermute(left_own, 'core', [(0, 1), (1, 0)])  5.4 us
    all_to_all x1, starting transfers between devices, on_device(): lax.all_to_all(square_part, 'layer', split_axis=0, concat_axis=0, tiled=T...  4.29 us
    pallas_call x1, Pallas kernels, on_device(): pl.pallas_call(cube_kernel, out_shape=jax.ShapeDtypeStruct((chosen.shape[...  4.21 us
  transfers between devices with their start and end apart: 19, of which 5 were waited for; matrix products, arithmetic and copies ran while one was open for 7% of the time, Pallas kernels for 0%

profile of v3, /device:TPU:1, one launch (start us, length us, event | category | flops | bytes accessed | tf_op | source)
XLA Modules:
  0.0 146.6 jit_solution(14228667796054508410)
XLA Ops:
  0.0 1.1 constant_dynamic-slice_fusion.1
  1.1 0.1 copy.10
  1.3 4.8 %collective-permute-start.7 = (bf16[96,768]{1,0:T(8,128)(2,1)S(1)}, bf16[96,768]{1,0:T(8,128)(2,1)S(1)}, u32[]{:S(2)}, u32[]{:S(2)}) collective-permute-start(bf16[96,768]{1,0:T(8,128)(2,1)S(1)} %bitcast.24), channel_id=1, source_target_pairs={{0,8},{8,16},{16,24},{24,32},{32,40},{40,48},{48,56},{56,0},{1,9},... | collective-permute-start | bytes 442376 | tf_op jit(solution)/shard_map/ppermute | solution.py:21
  6.1 5.8 %collective-permute-start.4 = (bf16[96,768]{1,0:T(8,128)(2,1)S(1)}, bf16[96,768]{1,0:T(8,128)(2,1)S(1)}, u32[]{:S(2)}, u32[]{:S(2)}) collective-permute-start(bf16[96,768]{1,0:T(8,128)(2,1)S(1)} %bitcast.25), channel_id=1, source_target_pairs={{0,16},{8,24},{16,32},{24,40},{32,48},{40,56},{48,0},{56,8},{1,17}... | collective-permute-start | bytes 442376 | tf_op jit(solution)/shard_map/ppermute | solution.py:21
  11.9 5.9 %collective-permute-start.1 = (bf16[96,768]{1,0:T(8,128)(2,1)S(1)}, bf16[96,768]{1,0:T(8,128)(2,1)S(1)}, u32[]{:S(2)}, u32[]{:S(2)}) collective-permute-start(bf16[96,768]{1,0:T(8,128)(2,1)S(1)} %bitcast.26), channel_id=1, source_target_pairs={{0,48},{8,56},{16,0},{24,8},{32,16},{40,24},{48,32},{56,40},{1,49}... | collective-permute-start | bytes 442376 | tf_op jit(solution)/shard_map/ppermute | solution.py:21
  17.8 3.1 %collective-permute-start = (bf16[96,768]{1,0:T(8,128)(2,1)S(1)}, bf16[96,768]{1,0:T(8,128)(2,1)S(1)}, u32[]{:S(2)}, u32[]{:S(2)}) collective-permute-start(bf16[96,768]{1,0:T(8,128)(2,1)S(1)} %bitcast.27), channel_id=1, source_target_pairs={{0,56},{8,0},{16,8},{24,16},{32,24},{40,32},{48,40},{56,48},{1,57}... | collective-permute-start | bytes 442376 | tf_op jit(solution)/shard_map/ppermute | solution.py:21
  20.9 0.9 dynamic-slice_bitcast_fusion
  21.8 1.2 broadcast_in_dim.20
  23.0 6.8 %all-to-all-start = ((bf16[8,2,96,384]{3,2,1,0:T(8,128)(2,1)}), bf16[8,2,96,384]{3,2,1,0:T(8,128)(2,1)S(1)}, u32[]{:S(2)}, u32[]{:S(2)}) async-start(bf16[8,2,96,384]{3,2,1,0:T(8,128)(2,1)} %broadcast_in_dim.20), calls=%async_computation | async-start | bytes 2359296 | tf_op jit(solution)/shard_map/all_to_all | solution.py:16
  29.9 1.9 %collective-permute-start.5 = (bf16[48,768]{1,0:T(8,128)(2,1)S(1)}, bf16[48,768]{1,0:T(8,128)(2,1)S(1)}, u32[]{:S(2)}, u32[]{:S(2)}) collective-permute-start(bf16[48,768]{1,0:T(8,128)(2,1)S(1)} %slice.17), channel_id=1, source_target_pairs={{0,16},{8,24},{16,32},{24,40},{32,48},{40,56},{48,0},{56,8},{1,17}... | collective-permute-start | bytes 221192 | tf_op jit(solution)/shard_map/ppermute | solution.py:21
  31.8 5.5 %collective-permute-start.3 = (bf16[48,768]{1,0:T(8,128)(2,1)S(1)}, bf16[48,768]{1,0:T(8,128)(2,1)S(1)}, u32[]{:S(2)}, u32[]{:S(2)}) collective-permute-start(bf16[48,768]{1,0:T(8,128)(2,1)S(1)} %slice.16), channel_id=1, source_target_pairs={{0,48},{8,56},{16,0},{24,8},{32,16},{40,24},{48,32},{56,40},{1,49}... | collective-permute-start | bytes 221192 | tf_op jit(solution)/shard_map/ppermute | solution.py:21
  37.3 2.2 %collective-permute-start.6 = (bf16[96,768]{1,0:T(8,128)(2,1)S(1)}, bf16[96,768]{1,0:T(8,128)(2,1)S(1)}, u32[]{:S(2)}, u32[]{:S(2)}) collective-permute-start(bf16[96,768]{1,0:T(8,128)(2,1)S(1)} %collective-permute-done.4), channel_id=1, source_target_pairs={{0,8},{8,16},{16,24},{24,32},{32,40},{40,48},{48,56},{56,0},{1,9},... | collective-permute-start | bytes 442376 | tf_op jit(solution)/shard_map/ppermute | solution.py:21
  39.5 4.3 %collective-permute-start.2 = (bf16[96,768]{1,0:T(8,128)(2,1)S(1)}, bf16[96,768]{1,0:T(8,128)(2,1)S(1)}, u32[]{:S(2)}, u32[]{:S(2)}) collective-permute-start(bf16[96,768]{1,0:T(8,128)(2,1)S(1)} %collective-permute-done.1), channel_id=1, source_target_pairs={{0,56},{8,0},{16,8},{24,16},{32,24},{40,32},{48,40},{56,48},{1,57}... | collective-permute-start | bytes 442376 | tf_op jit(solution)/shard_map/ppermute | solution.py:21
  43.9 2.0 %collective-permute-done.2 = bf16[96,768]{1,0:T(8,128)(2,1)S(1)} collective-permute-done((bf16[96,768]{1,0:T(8,128)(2,1)S(1)}, bf16[96,768]{1,0:T(8,128)(2,1)S(1)}, u32[]{:S(2)}, u32[]{:S(2)}) %collective-permute-start.2) | collective-permute-done | bytes 147488 | tf_op jit(solution)/shard_map/ppermute | solution.py:21
  46.1 5.4 %collective-permute-start.8 = (bf16[768,768]{1,0:T(8,128)(2,1)S(1)}, bf16[768,768]{1,0:T(8,128)(2,1)S(1)}, u32[]{:S(2)}, u32[]{:S(2)}) collective-permute-start(bf16[768,768]{1,0:T(8,128)(2,1)S(1)} %constant_dynamic-update-slice_fusion.own_ref), channel_id=1, source_target_pairs={{0,4},{4,0},{1,5},{5,1},{2,6},{6,2},{3,7},{7,3},{8,12},{12,8},{9,1... | collective-permute-start | bytes 3538952 | tf_op jit(solution)/shard_map/ppermute | solution.py:123
  51.5 0.1 pad_add_fusion.place_ref
  51.5 2.4 %collective-permute-done.8.other_ref = bf16[768,768]{1,0:T(8,128)(2,1)S(1)} collective-permute-done((bf16[768,768]{1,0:T(8,128)(2,1)S(1)}, bf16[768,768]{1,0:T(8,128)(2,1)S(1)}, u32[]{:S(2)}, u32[]{:S(2)}) %collective-permute-start.8) | collective-permute-done | bytes 1179680 | tf_op jit(solution)/shard_map/ppermute | solution.py:123
  53.9 7.9 %all-to-all-done.right_ref = bf16[8,2,96,384]{3,2,1,0:T(8,128)(2,1)S(1)} async-done(((bf16[8,2,96,384]{3,2,1,0:T(8,128)(2,1)}), bf16[8,2,96,384]{3,2,1,0:T(8,128)(2,1)S(1)}, u32[]{:S(2)}, u32[]{:S(2)}) %all-to-all-start) | async-done | bytes 1179680 | tf_op jit(solution)/shard_map/all_to_all | solution.py:16
  61.8 2.0 %shard_map.37 = bf16[4,2,96,384]{3,2,1,0:T(8,128)(2,1)S(1)} custom-call(s32[3]{0:T(128)S(1)} %pad_add_fusion.place_ref, bf16[768,768]{1,0:T(8,128)(2,1)S(1)} %constant_dynamic-update-slice_fusion.own_ref, bf16[768,768]{1,0:T(8,128)(2,1)S(1)} %collective-permute-done.8.other_ref, bf16[8,2,96,384]{3,2,1,0:T(8,128)(2,1)S(1)} %all-to-all-done.right_ref), custom_call_target="tpu_custom_call" | custom-call | tf_op jit(solution)/shard_map/pallas_call | solution.py:126
  63.9 0.8 copy-done
  64.7 4.3 %all-to-all-start.1 = ((bf16[4,2,96,384]{3,2,1,0:T(8,128)(2,1)}), bf16[4,2,96,384]{3,2,1,0:T(8,128)(2,1)}, u32[]{:S(2)}, u32[]{:S(2)}) async-start(bf16[4,2,96,384]{3,2,1,0:T(8,128)(2,1)} %copy-done), calls=%async_computation.1 | async-start | bytes 1179648 | tf_op jit(solution)/shard_map/all_to_all | solution.py:134
  69.0 0.1 broadcast_in_dim.21
  69.1 0.7 reshape.19
  69.8 0.8 broadcast_in_dim.22
  70.6 2.8 %reshape_reshape.3 = f32[2,4,96,384]{2,1,0,3:T(4,128)} reshape(f32[768,6,64]{0,2,1:T(8,128)S(1)} %broadcast_in_dim.22) | data formatting | bytes 2359296 | tf_op jit(solution)/shard_map/reshape;reshape | solution.py:138
  73.4 1.7 %constant_dynamic-slice_fusion = f32[2,1,96,384]{2,1,0,3:T(1,128)S(1)} fusion(f32[2,4,96,384]{2,1,0,3:T(4,128)} %reshape_reshape.3, s32[]{:T(128)S(6)} %select_n.13), kind=kLoop, calls=%fused_computation.14 | loop fusion | bytes 589828 | tf_op jit(solution)/shard_map/dynamic_slice | solution.py:137
  75.1 0.0 copy-start.1
  75.1 1.2 copy.9
  76.4 2.3 %all-to-all-done.1 = bf16[4,2,96,384]{3,2,1,0:T(8,128)(2,1)} async-done(((bf16[4,2,96,384]{3,2,1,0:T(8,128)(2,1)}), bf16[4,2,96,384]{3,2,1,0:T(8,128)(2,1)}, u32[]{:S(2)}, u32[]{:S(2)}) %all-to-all-start.1) | async-done | bytes 589856 | tf_op jit(solution)/shard_map/all_to_all | solution.py:134
  78.6 1.2 convert_reduce_fusion
  79.8 1.0 fusion.refs_0_
  80.8 1.9 %collective-permute-start.13 = (bf16[2,96,384]{2,1,0:T(8,128)(2,1)S(1)}, bf16[2,96,384]{2,1,0:T(8,128)(2,1)S(1)}, u32[]{:S(2)}, u32[]{:S(2)}) collective-permute-start(bf16[2,96,384]{2,1,0:T(8,128)(2,1)S(1)} %fusion.refs_0_), channel_id=1, source_target_pairs={{0,128},{64,192},{128,256},{192,320},{256,384},{320,448},{384,0},{... | collective-permute-start | bytes 442376 | tf_op jit(solution)/shard_map/ppermute | solution.py:21
  82.7 5.5 %collective-permute-start.10 = (bf16[2,96,384]{2,1,0:T(8,128)(2,1)S(1)}, bf16[2,96,384]{2,1,0:T(8,128)(2,1)S(1)}, u32[]{:S(2)}, u32[]{:S(2)}) collective-permute-start(bf16[2,96,384]{2,1,0:T(8,128)(2,1)S(1)} %fusion.refs_0_), channel_id=1, source_target_pairs={{0,384},{64,448},{128,0},{192,64},{256,128},{320,192},{384,256},{4... | collective-permute-start | bytes 442376 | tf_op jit(solution)/shard_map/ppermute | solution.py:21
  88.2 1.9 %collective-permute-start.16 = (bf16[2,96,384]{2,1,0:T(8,128)(2,1)S(1)}, bf16[2,96,384]{2,1,0:T(8,128)(2,1)S(1)}, u32[]{:S(2)}, u32[]{:S(2)}) collective-permute-start(bf16[2,96,384]{2,1,0:T(8,128)(2,1)S(1)} %fusion.refs_0_), channel_id=1, source_target_pairs={{0,64},{64,128},{128,192},{192,256},{256,320},{320,384},{384,448},... | collective-permute-start | bytes 442376 | tf_op jit(solution)/shard_map/ppermute | solution.py:21
  90.1 4.6 %collective-permute-start.9 = (bf16[2,96,384]{2,1,0:T(8,128)(2,1)S(1)}, bf16[2,96,384]{2,1,0:T(8,128)(2,1)}, u32[]{:S(2)}, u32[]{:S(2)}) collective-permute-start(bf16[2,96,384]{2,1,0:T(8,128)(2,1)S(1)} %fusion.refs_0_), channel_id=1, source_target_pairs={{0,448},{64,0},{128,64},{192,128},{256,192},{320,256},{384,320},{4... | collective-permute-start | bytes 442376 | tf_op jit(solution)/shard_map/ppermute | solution.py:21
  94.7 1.9 %collective-permute-start.15 = (bf16[2,96,384]{2,1,0:T(8,128)(2,1)S(1)}, bf16[2,96,384]{2,1,0:T(8,128)(2,1)}, u32[]{:S(2)}, u32[]{:S(2)}) collective-permute-start(bf16[2,96,384]{2,1,0:T(8,128)(2,1)S(1)} %collective-permute-done.13.refs_7_), channel_id=1, source_target_pairs={{0,64},{64,128},{128,192},{192,256},{256,320},{320,384},{384,448},... | collective-permute-start | bytes 442376 | tf_op jit(solution)/shard_map/ppermute | solution.py:21
  96.7 4.6 %collective-permute-start.11 = (bf16[2,96,384]{2,1,0:T(8,128)(2,1)S(1)}, bf16[2,96,384]{2,1,0:T(8,128)(2,1)}, u32[]{:S(2)}, u32[]{:S(2)}) collective-permute-start(bf16[2,96,384]{2,1,0:T(8,128)(2,1)S(1)} %collective-permute-done.10.refs_2_), channel_id=1, source_target_pairs={{0,448},{64,0},{128,64},{192,128},{256,192},{320,256},{384,320},{4... | collective-permute-start | bytes 442376 | tf_op jit(solution)/shard_map/ppermute | solution.py:21
  101.3 0.6 slice.19
  101.9 1.9 %collective-permute-start.14 = (bf16[1,96,384]{2,1,0:T(8,128)(2,1)}, bf16[1,96,384]{2,1,0:T(8,128)(2,1)}, u32[]{:S(2)}, u32[]{:S(2)}) collective-permute-start(bf16[1,96,384]{2,1,0:T(8,128)(2,1)} %slice.19), channel_id=1, source_target_pairs={{0,128},{64,192},{128,256},{192,320},{256,384},{320,448},{384,0},{... | collective-permute-start | bytes 221192 | tf_op jit(solution)/shard_map/ppermute | solution.py:21
  103.8 0.6 slice.18
  104.5 5.5 %collective-permute-start.12 = (bf16[1,96,384]{2,1,0:T(8,128)(2,1)}, bf16[1,96,384]{2,1,0:T(8,128)(2,1)}, u32[]{:S(2)}, u32[]{:S(2)}) collective-permute-start(bf16[1,96,384]{2,1,0:T(8,128)(2,1)} %slice.18), channel_id=1, source_target_pairs={{0,384},{64,448},{128,0},{192,64},{256,128},{320,192},{384,256},{4... | collective-permute-start | bytes 221192 | tf_op jit(solution)/shard_map/ppermute | solution.py:21
  110.0 1.7 %collective-permute-done.12.refs_4_ = bf16[1,96,384]{2,1,0:T(8,128)(2,1)} collective-permute-done((bf16[1,96,384]{2,1,0:T(8,128)(2,1)}, bf16[1,96,384]{2,1,0:T(8,128)(2,1)}, u32[]{:S(2)}, u32[]{:S(2)}) %collective-permute-start.12) | collective-permute-done | bytes 73760 | tf_op jit(solution)/shard_map/ppermute | solution.py:21
  111.7 4.2 %shard_map.38 = bf16[16,32,128]{2,1,0:T(8,128)(2,1)S(1)} custom-call(s32[16]{0:T(128)S(1)} %bitcast.23, s32[3]{0:T(128)S(1)} %pad_add_fusion.place_ref, f32[1]{0:T(128)} %bitcast.4.scale_ref, bf16[768,768]{1,0:T(8,128)(2,1)S(1)} %constant_dynamic-update-slice_fusion.own_ref, bf16[768,768]{1,0:T(8,128)(2,1)S(1)} %collective-permute-done.8.other_ref, ...), custom_call_target="tpu_custom_call" | custom-call | tf_op jit(solution)/shard_map/pallas_call | solution.py:146
  115.9 17.5 %all_to_all.20 = bf16[16,32,128]{2,1,0:T(8,128)(2,1)S(1)} all-to-all(bf16[16,32,128]{2,1,0:T(8,128)(2,1)S(1)} %shard_map.38), channel_id=1, replica_groups=mesh['row'=8,'z'=8,'core'=2,'layer'=4] {'z','core'}, dimensions={0} | all-to-all | bytes 262144 | tf_op jit(solution)/shard_map/all_to_all | solution.py:158
  133.4 0.1 broadcast_in_dim.23
  133.5 12.3 %all_to_all.21 = bf16[4,16,32,128]{3,2,1,0:T(8,128)(2,1)S(1)} all-to-all(bf16[4,16,32,128]{3,2,1,0:T(8,128)(2,1)S(1)} %broadcast_in_dim.23), channel_id=1, replica_groups=mesh['row'=8,'z'=8,'core'=2,'layer'=4] {'layer'}, dimensions={0} | all-to-all | bytes 1048576 | tf_op jit(solution)/shard_map/all_to_all | solution.py:16
  145.8 0.1 reduce_sum.22
  145.9 0.7 copy.13
  (32 shorter events, 0.2 us)
Async XLA Ops:
  1.3 44.8 %collective-permute-start.7 = (bf16[96,768]{1,0:T(8,128)(2,1)S(1)}, bf16[96,768]{1,0:T(8,128)(2,1)S(1)}, u32[]{:S(2)}, u32[]{:S(2)}) collective-permute-start(bf16[96,768]{1,0:T(8,128)(2,1)S(1)} %bitcast.24), channel_id=1, source_target_pairs={{0,8},{8,16},{16,24},{24,32},{32,40},{40,48},{48,56},{56,0},{1,9},... | collective-permute-start | bytes 442376 | tf_op jit(solution)/shard_map/ppermute | solution.py:21
  6.1 23.8 %collective-permute-start.4 = (bf16[96,768]{1,0:T(8,128)(2,1)S(1)}, bf16[96,768]{1,0:T(8,128)(2,1)S(1)}, u32[]{:S(2)}, u32[]{:S(2)}) collective-permute-start(bf16[96,768]{1,0:T(8,128)(2,1)S(1)} %bitcast.25), channel_id=1, source_target_pairs={{0,16},{8,24},{16,32},{24,40},{32,48},{40,56},{48,0},{56,8},{1,17}... | collective-permute-start | bytes 442376 | tf_op jit(solution)/shard_map/ppermute | solution.py:21
  11.9 19.9 %collective-permute-start.1 = (bf16[96,768]{1,0:T(8,128)(2,1)S(1)}, bf16[96,768]{1,0:T(8,128)(2,1)S(1)}, u32[]{:S(2)}, u32[]{:S(2)}) collective-permute-start(bf16[96,768]{1,0:T(8,128)(2,1)S(1)} %bitcast.26), channel_id=1, source_target_pairs={{0,48},{8,56},{16,0},{24,8},{32,16},{40,24},{48,32},{56,40},{1,49}... | collective-permute-start | bytes 442376 | tf_op jit(solution)/shard_map/ppermute | solution.py:21
  17.8 21.7 %collective-permute-start = (bf16[96,768]{1,0:T(8,128)(2,1)S(1)}, bf16[96,768]{1,0:T(8,128)(2,1)S(1)}, u32[]{:S(2)}, u32[]{:S(2)}) collective-permute-start(bf16[96,768]{1,0:T(8,128)(2,1)S(1)} %bitcast.27), channel_id=1, source_target_pairs={{0,56},{8,0},{16,8},{24,16},{32,24},{40,32},{48,40},{56,48},{1,57}... | collective-permute-start | bytes 442376 | tf_op jit(solution)/shard_map/ppermute | solution.py:21
  23.0 38.8 %all-to-all-start = ((bf16[8,2,96,384]{3,2,1,0:T(8,128)(2,1)}), bf16[8,2,96,384]{3,2,1,0:T(8,128)(2,1)S(1)}, u32[]{:S(2)}, u32[]{:S(2)}) async-start(bf16[8,2,96,384]{3,2,1,0:T(8,128)(2,1)} %broadcast_in_dim.20), calls=%async_computation | async-start | bytes 2359296 | tf_op jit(solution)/shard_map/all_to_all | solution.py:16
  29.9 16.1 %collective-permute-start.5 = (bf16[48,768]{1,0:T(8,128)(2,1)S(1)}, bf16[48,768]{1,0:T(8,128)(2,1)S(1)}, u32[]{:S(2)}, u32[]{:S(2)}) collective-permute-start(bf16[48,768]{1,0:T(8,128)(2,1)S(1)} %slice.17), channel_id=1, source_target_pairs={{0,16},{8,24},{16,32},{24,40},{32,48},{40,56},{48,0},{56,8},{1,17}... | collective-permute-start | bytes 221192 | tf_op jit(solution)/shard_map/ppermute | solution.py:21
  31.8 14.1 %collective-permute-start.3 = (bf16[48,768]{1,0:T(8,128)(2,1)S(1)}, bf16[48,768]{1,0:T(8,128)(2,1)S(1)}, u32[]{:S(2)}, u32[]{:S(2)}) collective-permute-start(bf16[48,768]{1,0:T(8,128)(2,1)S(1)} %slice.16), channel_id=1, source_target_pairs={{0,48},{8,56},{16,0},{24,8},{32,16},{40,24},{48,32},{56,40},{1,49}... | collective-permute-start | bytes 221192 | tf_op jit(solution)/shard_map/ppermute | solution.py:21
  37.3 8.7 %collective-permute-start.6 = (bf16[96,768]{1,0:T(8,128)(2,1)S(1)}, bf16[96,768]{1,0:T(8,128)(2,1)S(1)}, u32[]{:S(2)}, u32[]{:S(2)}) collective-permute-start(bf16[96,768]{1,0:T(8,128)(2,1)S(1)} %collective-permute-done.4), channel_id=1, source_target_pairs={{0,8},{8,16},{16,24},{24,32},{32,40},{40,48},{48,56},{56,0},{1,9},... | collective-permute-start | bytes 442376 | tf_op jit(solution)/shard_map/ppermute | solution.py:21
  39.5 6.4 %collective-permute-start.2 = (bf16[96,768]{1,0:T(8,128)(2,1)S(1)}, bf16[96,768]{1,0:T(8,128)(2,1)S(1)}, u32[]{:S(2)}, u32[]{:S(2)}) collective-permute-start(bf16[96,768]{1,0:T(8,128)(2,1)S(1)} %collective-permute-done.1), channel_id=1, source_target_pairs={{0,56},{8,0},{16,8},{24,16},{32,24},{40,32},{48,40},{56,48},{1,57}... | collective-permute-start | bytes 442376 | tf_op jit(solution)/shard_map/ppermute | solution.py:21
  46.1 7.9 %collective-permute-start.8 = (bf16[768,768]{1,0:T(8,128)(2,1)S(1)}, bf16[768,768]{1,0:T(8,128)(2,1)S(1)}, u32[]{:S(2)}, u32[]{:S(2)}) collective-permute-start(bf16[768,768]{1,0:T(8,128)(2,1)S(1)} %constant_dynamic-update-slice_fusion.own_ref), channel_id=1, source_target_pairs={{0,4},{4,0},{1,5},{5,1},{2,6},{6,2},{3,7},{7,3},{8,12},{12,8},{9,1... | collective-permute-start | bytes 3538952 | tf_op jit(solution)/shard_map/ppermute | solution.py:123
  63.9 0.8 copy-start
  64.7 4.3 %copy-start.3 = (s32[12,6]{0,1:T(8,128)S(1)}, s32[12,6]{0,1:T(8,128)}, u32[]{:S(2)}) copy-start(s32[12,6]{0,1:T(8,128)} %param.4) | copy-start | bytes 868
  64.7 14.0 %all-to-all-start.1 = ((bf16[4,2,96,384]{3,2,1,0:T(8,128)(2,1)}), bf16[4,2,96,384]{3,2,1,0:T(8,128)(2,1)}, u32[]{:S(2)}, u32[]{:S(2)}) async-start(bf16[4,2,96,384]{3,2,1,0:T(8,128)(2,1)} %copy-done), calls=%async_computation.1 | async-start | bytes 1179648 | tf_op jit(solution)/shard_map/all_to_all | solution.py:134
  75.1 36.5 %copy-start.1 = (bf16[768,384]{1,0:T(8,128)(2,1)S(1)}, bf16[768,384]{1,0:T(8,128)(2,1)}, u32[]{:S(2)}) copy-start(bf16[768,384]{1,0:T(8,128)(2,1)} %matrix_ref.1) | copy-start | bytes 1769476
  75.1 36.5 %copy-start.2 = (s32[1,16]{1,0:T(1,128)S(1)}, s32[1,16]{1,0:T(1,128)}, u32[]{:S(2)}) copy-start(s32[1,16]{1,0:T(1,128)} %param.5) | copy-start | bytes 196
  80.8 13.9 %collective-permute-start.13 = (bf16[2,96,384]{2,1,0:T(8,128)(2,1)S(1)}, bf16[2,96,384]{2,1,0:T(8,128)(2,1)S(1)}, u32[]{:S(2)}, u32[]{:S(2)}) collective-permute-start(bf16[2,96,384]{2,1,0:T(8,128)(2,1)S(1)} %fusion.refs_0_), channel_id=1, source_target_pairs={{0,128},{64,192},{128,256},{192,320},{256,384},{320,448},{384,0},{... | collective-permute-start | bytes 442376 | tf_op jit(solution)/shard_map/ppermute | solution.py:21
  82.7 13.9 %collective-permute-start.10 = (bf16[2,96,384]{2,1,0:T(8,128)(2,1)S(1)}, bf16[2,96,384]{2,1,0:T(8,128)(2,1)S(1)}, u32[]{:S(2)}, u32[]{:S(2)}) collective-permute-start(bf16[2,96,384]{2,1,0:T(8,128)(2,1)S(1)} %fusion.refs_0_), channel_id=1, source_target_pairs={{0,384},{64,448},{128,0},{192,64},{256,128},{320,192},{384,256},{4... | collective-permute-start | bytes 442376 | tf_op jit(solution)/shard_map/ppermute | solution.py:21
  88.2 16.2 %collective-permute-start.16 = (bf16[2,96,384]{2,1,0:T(8,128)(2,1)S(1)}, bf16[2,96,384]{2,1,0:T(8,128)(2,1)S(1)}, u32[]{:S(2)}, u32[]{:S(2)}) collective-permute-start(bf16[2,96,384]{2,1,0:T(8,128)(2,1)S(1)} %fusion.refs_0_), channel_id=1, source_target_pairs={{0,64},{64,128},{128,192},{192,256},{256,320},{320,384},{384,448},... | collective-permute-start | bytes 442376 | tf_op jit(solution)/shard_map/ppermute | solution.py:21
  90.1 19.8 %collective-permute-start.9 = (bf16[2,96,384]{2,1,0:T(8,128)(2,1)S(1)}, bf16[2,96,384]{2,1,0:T(8,128)(2,1)}, u32[]{:S(2)}, u32[]{:S(2)}) collective-permute-start(bf16[2,96,384]{2,1,0:T(8,128)(2,1)S(1)} %fusion.refs_0_), channel_id=1, source_target_pairs={{0,448},{64,0},{128,64},{192,128},{256,192},{320,256},{384,320},{4... | collective-permute-start | bytes 442376 | tf_op jit(solution)/shard_map/ppermute | solution.py:21
  94.7 16.9 %collective-permute-start.15 = (bf16[2,96,384]{2,1,0:T(8,128)(2,1)S(1)}, bf16[2,96,384]{2,1,0:T(8,128)(2,1)}, u32[]{:S(2)}, u32[]{:S(2)}) collective-permute-start(bf16[2,96,384]{2,1,0:T(8,128)(2,1)S(1)} %collective-permute-done.13.refs_7_), channel_id=1, source_target_pairs={{0,64},{64,128},{128,192},{192,256},{256,320},{320,384},{384,448},... | collective-permute-start | bytes 442376 | tf_op jit(solution)/shard_map/ppermute | solution.py:21
  96.7 15.0 %collective-permute-start.11 = (bf16[2,96,384]{2,1,0:T(8,128)(2,1)S(1)}, bf16[2,96,384]{2,1,0:T(8,128)(2,1)}, u32[]{:S(2)}, u32[]{:S(2)}) collective-permute-start(bf16[2,96,384]{2,1,0:T(8,128)(2,1)S(1)} %collective-permute-done.10.refs_2_), channel_id=1, source_target_pairs={{0,448},{64,0},{128,64},{192,128},{256,192},{320,256},{384,320},{4... | collective-permute-start | bytes 442376 | tf_op jit(solution)/shard_map/ppermute | solution.py:21
  101.9 8.1 %collective-permute-start.14 = (bf16[1,96,384]{2,1,0:T(8,128)(2,1)}, bf16[1,96,384]{2,1,0:T(8,128)(2,1)}, u32[]{:S(2)}, u32[]{:S(2)}) collective-permute-start(bf16[1,96,384]{2,1,0:T(8,128)(2,1)} %slice.19), channel_id=1, source_target_pairs={{0,128},{64,192},{128,256},{192,320},{256,384},{320,448},{384,0},{... | collective-permute-start | bytes 221192 | tf_op jit(solution)/shard_map/ppermute | solution.py:21
  104.5 7.2 %collective-permute-start.12 = (bf16[1,96,384]{2,1,0:T(8,128)(2,1)}, bf16[1,96,384]{2,1,0:T(8,128)(2,1)}, u32[]{:S(2)}, u32[]{:S(2)}) collective-permute-start(bf16[1,96,384]{2,1,0:T(8,128)(2,1)} %slice.18), channel_id=1, source_target_pairs={{0,384},{64,448},{128,0},{192,64},{256,128},{320,192},{384,256},{4... | collective-permute-start | bytes 221192 | tf_op jit(solution)/shard_map/ppermute | solution.py:21

commit v4 on v3

v4 whole, which is shorter than its diff:
```python
import jax
import jax.numpy as jnp
from jax import lax
from jax.experimental import pallas as pl
from jax.experimental.pallas import tpu as pltpu
from jax.sharding import Mesh, PartitionSpec as P

BLK = 64
CONTRACT = (((0,), (0,)), ((), ()))


def to_all(piece, axis):
    copies = jnp.broadcast_to(piece[None], (lax.axis_size(axis),) + piece.shape)
    return lax.all_to_all(copies, axis, split_axis=0, concat_axis=0, tiled=True)


def shifted(piece, axis, by):
    size = lax.axis_size(axis)
    pairs = []
    for i in range(size):
        pairs.append((2 * i, 2 * ((i - by) % size)))
        pairs.append((2 * i + 1, 2 * ((i + by) % size) + 1))
    return lax.ppermute(piece, (axis, "core"), pairs)


def ring_of_eight(piece, axis):
    up = shifted(piece, axis, 2)
    down = shifted(piece, axis, -2)
    near_up = shifted(piece, axis, 1)
    near_down = shifted(piece, axis, -1)
    far_up = shifted(up, axis, 1)
    far_down = shifted(down, axis, -1)
    opposite = shifted(up, axis, 2)
    return piece, near_up, up, far_up, opposite, far_down, down, near_down


def product(own_ref, other_ref, right_ref, start, count):
    depth = own_ref.shape[0]
    columns = right_ref.shape[-1]
    rows = pl.ds(start, count)
    own = lax.dot_general(
        own_ref[:, rows], right_ref[0].reshape(depth, columns), CONTRACT, preferred_element_type=jnp.float32
    )
    other = lax.dot_general(
        other_ref[:, rows], right_ref[1].reshape(depth, columns), CONTRACT, preferred_element_type=jnp.float32
    )
    return own + other


def square_kernel(place_ref, own_ref, other_ref, right_ref, out_ref, ordered_ref, staged_ref, sems):
    halves, layers, part, columns = staged_ref.shape
    tiles = right_ref.shape[0]
    z, core = place_ref[1], place_ref[2]
    way = 1 - 2 * core
    for offset in range(tiles):
        ordered_ref[0, offset] = right_ref[lax.rem(z + way * offset + tiles, tiles), core]
        ordered_ref[1, offset] = right_ref[lax.rem(z - way * offset + tiles, tiles), 1 - core]
    copies = []
    for half in range(halves):
        count = layers * part
        total = product(own_ref, other_ref, ordered_ref, half * count, count)
        staged_ref[half] = total.astype(staged_ref.dtype).reshape(layers, part, columns)
        copies.append(pltpu.make_async_copy(staged_ref.at[half], out_ref.at[:, half], sems.at[half]))
        copies[-1].start()
    for copy in copies:
        copy.wait()


def filter_kernel(keep_ref, layer_ref, parts_ref, out_ref):
    layers, halves, part, columns = parts_ref.shape
    chunk = BLK // 2
    low = lax.broadcasted_iota(jnp.int32, (chunk, 2 * BLK), 1) < BLK
    for half in range(halves):
        for start in range(0, part, chunk):
            block = (half * layers * part + layer_ref[0] * part + start) // BLK
            rows = pl.ds(start, chunk)
            for lane in range(0, columns, 2 * BLK):
                lanes = pl.ds(lane, 2 * BLK)
                total = parts_ref[0, half, rows, lanes].astype(jnp.float32)
                for layer in range(1, layers):
                    total = total + parts_ref[layer, half, rows, lanes].astype(jnp.float32)
                left = keep_ref[block, lane // BLK].astype(jnp.float32)
                right = keep_ref[block, lane // BLK + 1].astype(jnp.float32)
                out_ref[half, rows, lanes] = (total * jnp.where(low, left, right)).astype(out_ref.dtype)


def cube_kernel(chosen_ref, place_ref, scale_ref, own_ref, other_ref, matrix_ref, *refs):
    pieces = refs[:8]
    out_ref, ordered_ref, total_ref, block_ref = refs[8:]
    owners, pairs, lanes = out_ref.shape
    half_blocks = matrix_ref.shape[1] // BLK
    tiles = ordered_ref.shape[1]
    row, z, core = place_ref[0], place_ref[1], place_ref[2]
    way = 1 - 2 * core
    for offset, piece in enumerate(pieces):
        distance = row + way * offset - z
        own = lax.rem(way * distance + 2 * tiles, tiles)
        ordered_ref[0, own] = piece[core]
        ordered_ref[1, lax.rem(tiles - own, tiles)] = piece[1 - core]
    total_ref[...] = scale_ref[0] * matrix_ref[...].astype(jnp.float32) - 0.5 * product(
        own_ref, other_ref, ordered_ref, 0, matrix_ref.shape[0]
    )
    low = lax.broadcasted_iota(jnp.int32, (pairs, lanes), 1) < BLK

    for owner in range(owners):
        index = chosen_ref[owner]
        live = jnp.where(index >= 0, 1.0, 0.0)
        index = jnp.maximum(index, 0)
        column = index % half_blocks
        start = pl.multiple_of(index // half_blocks * BLK, BLK)
        lane = pl.multiple_of(column // 2 * lanes, lanes)
        block = total_ref[pl.ds(start, BLK), pl.ds(lane, lanes)] * live
        turned = pltpu.roll(block, BLK, 1)
        odd = column % 2 == 1
        slot = 2 * (owner % 2)
        block_ref[slot] = jnp.where(odd, turned, block)
        block_ref[slot + 1] = jnp.where(odd, block, turned)
        even_rows = block_ref[slot, pl.ds(0, pairs, stride=2), :]
        odd_rows = block_ref[slot + 1, pl.ds(1, pairs, stride=2), :]
        out_ref[owner] = jnp.where(low, even_rows, odd_rows).astype(out_ref.dtype)


def on_device(matrix, keep_mask, send_list):
    layers = lax.axis_size("layer")
    rows_count = lax.axis_size("row")
    layer_index = lax.axis_index("layer")
    row_index = lax.axis_index("row")
    z_index = lax.axis_index("z")
    core_index = lax.axis_index("core")
    tile_rows, width = matrix.shape
    part = width // layers
    halves = tile_rows // width
    vmem = pl.BlockSpec(memory_space=pltpu.VMEM)
    smem = pl.BlockSpec(memory_space=pltpu.SMEM)
    params = pltpu.CompilerParams(vmem_limit_bytes=40 * 2**20)

    left_piece = lax.dynamic_slice_in_dim(matrix, layer_index * part, part, 1).T
    right_piece = lax.dynamic_slice_in_dim(
        matrix.reshape(halves, layers, part, width), layer_index, 1, 1
    ).reshape(halves, part, width)
    right = to_all(right_piece, "row")
    left_own = jnp.concatenate(ring_of_eight(left_piece, "z"), axis=0)
    left_own, right = lax.optimization_barrier((left_own, right))
    left_other = lax.ppermute(left_own, "core", [(0, 1), (1, 0)])
    place = jnp.stack([row_index, z_index, core_index])

    square_part = pl.pallas_call(
        square_kernel,
        out_shape=jax.ShapeDtypeStruct((layers, halves, part, width), jnp.bfloat16),
        in_specs=[smem, vmem, vmem, vmem],
        out_specs=pl.BlockSpec(memory_space=pltpu.HBM),
        scratch_shapes=[
            pltpu.VMEM((halves, rows_count, part, width), jnp.bfloat16),
            pltpu.VMEM((halves, layers, part, width), jnp.bfloat16),
            pltpu.SemaphoreType.DMA((halves,)),
        ],
        compiler_params=params,
    )(place, left_own, left_other, right)
    parts = lax.all_to_all(square_part, "layer", split_axis=0, concat_axis=0, tiled=True)
    filtered_piece = pl.pallas_call(
        filter_kernel,
        out_shape=jax.ShapeDtypeStruct((halves, part, width), jnp.bfloat16),
        in_specs=[smem, smem, vmem],
        out_specs=vmem,
        compiler_params=params,
    )(keep_mask, layer_index.reshape(1), parts)
    filtered = ring_of_eight(filtered_piece, "row")

    scale = jnp.where(layer_index == 0, 1.5, 0.0).astype(jnp.float32).reshape(1)
    chosen = send_list[0]
    pairs = BLK * BLK // 128
    outgoing = pl.pallas_call(
        cube_kernel,
        out_shape=jax.ShapeDtypeStruct((chosen.shape[0], pairs, 128), jnp.bfloat16),
        in_specs=[smem] * 3 + [vmem] * 11,
        out_specs=vmem,
        scratch_shapes=[
            pltpu.VMEM((halves, rows_count, part, width), jnp.bfloat16),
            pltpu.VMEM((tile_rows, width), jnp.float32),
            pltpu.VMEM((4, BLK, 128), jnp.float32),
        ],
        compiler_params=params,
    )(chosen, place, scale, left_own, left_other, matrix, *filtered)
    arrived = lax.all_to_all(outgoing, ("z", "core"), split_axis=0, concat_axis=0, tiled=True)
    everyone = to_all(arrived, "layer")
    total = everyone.astype(jnp.float32).sum(0).astype(jnp.bfloat16)
    return total.reshape(total.shape[0], BLK * BLK)


def solution(mesh):
    sizes = mesh.shape
    cores = 2
    shape = (sizes["row"], sizes["col"] // cores, cores, sizes["layer"])
    split = Mesh(mesh.devices.reshape(shape), ("row", "z", "core", "layer"))
    column = ("z", "core")
    in_specs = (P("row", column), P("row", column), P(("row",) + column, None))
    out_specs = P(("row",) + column, None)
    return jax.shard_map(
        on_device, mesh=split, in_specs=in_specs, out_specs=out_specs, check_vma=False
    )
```

time: 148 us -> 133 us (0.90)
  local copies, waits for them, and re-layouts: 13.7 us -> 5.83 us
  starting transfers between devices: 77.8 us -> 72.1 us
  waiting for transfers between devices: 16.3 us -> 20.5 us
  blocking collectives: 29.8 us -> 26.8 us
  other arithmetic: 2.32 us -> 0.16 us
    ppermute x16 -> x14, starting transfers between devices: 61.2 us -> 50.8 us  [shifted(): return lax.ppermute(piece, (axis, 'core'), pairs)]
    all_to_all x1, waiting for transfers between devices: 7.92 us -> 0.01 us  [to_all(): return lax.all_to_all(copies, axis, split_axis=0, concat_axis=0, tiled=True)]
    all_to_all x1, waiting for transfers between devices: 2.28 us -> 8.82 us  [on_device(): lax.all_to_all(square_part, 'layer', split_axis=0, concat_axis=0, tiled=T...]
    ppermute x16 -> x14, waiting for transfers between devices: 3.77 us -> 9.27 us  [shifted(): return lax.ppermute(piece, (axis, 'core'), pairs)]
    ppermute x1, starting transfers between devices: 5.4 us -> 9.55 us  [on_device(): left_other = lax.ppermute(left_own, 'core', [(0, 1), (1, 0)])]
    all_to_all x1, blocking collectives: 17.5 us -> 14.5 us  [on_device(): lax.all_to_all(outgoing, ('z', 'core'), split_axis=0, concat_axis=0, tile...]
    dynamic_slice x2 -> x0, local copies, waits for them, and re-layouts: 2.96 us -> none  [on_device(): lax.dynamic_slice_in_dim(block_keep.reshape(halves, layers, part, width),...]
    another operation x1 -> x0, local copies, waits for them, and re-layouts: 2.77 us -> none  [on_device(): block_keep.reshape(halves, layers, part, width)]
  transfers between devices with their start and end apart: 19 -> 17, of which waited for: 5 -> 6; matrix products, arithmetic and copies ran while one was open for 7% -> 2% of each run, Pallas kernels for 0% -> 0%
where the time goes in v4:
time: 133 us; the launch traced here: 132 us
  starting transfers between devices  72.1 us (54%)
  blocking collectives  26.8 us (20%)
  waiting for transfers between devices  20.5 us (15%)
  Pallas kernels  6.59 us (5%)
  local copies, waits for them, and re-layouts  5.83 us (4%)
    ppermute x14, starting transfers between devices, shifted(): return lax.ppermute(piece, (axis, 'core'), pairs)  50.8 us
    all_to_all x1, blocking collectives, on_device(): lax.all_to_all(outgoing, ('z', 'core'), split_axis=0, concat_axis=0, tile...  14.5 us
    all_to_all x1, blocking collectives, to_all(): return lax.all_to_all(copies, axis, split_axis=0, concat_axis=0, tiled=True)  12.3 us
    ppermute x1, starting transfers between devices, on_device(): left_other = lax.ppermute(left_own, 'core', [(0, 1), (1, 0)])  9.55 us
    ppermute x14, waiting for transfers between devices, shifted(): return lax.ppermute(piece, (axis, 'core'), pairs)  9.27 us
    all_to_all x1, waiting for transfers between devices, on_device(): lax.all_to_all(square_part, 'layer', split_axis=0, concat_axis=0, tiled=T...  8.82 us
    all_to_all x1, starting transfers between devices, to_all(): return lax.all_to_all(copies, axis, split_axis=0, concat_axis=0, tiled=True)  7.65 us
    all_to_all x1, starting transfers between devices, on_device(): lax.all_to_all(square_part, 'layer', split_axis=0, concat_axis=0, tiled=T...  4.15 us
  transfers between devices with their start and end apart: 17, of which 6 were waited for; matrix products, arithmetic and copies ran while one was open for 2% of the time, Pallas kernels for 0%

profile of v4, /device:TPU:1, one launch (start us, length us, event | category | flops | bytes accessed | tf_op | source)
XLA Modules:
  0.0 132.3 jit_solution(15074025816455272007)
XLA Ops:
  0.0 0.9 dynamic-slice_bitcast_fusion
  0.9 1.2 broadcast_in_dim.14
  2.1 7.7 %all-to-all-start = ((bf16[8,2,96,384]{3,2,1,0:T(8,128)(2,1)}), bf16[8,2,96,384]{3,2,1,0:T(8,128)(2,1)S(1)}, u32[]{:S(2)}, u32[]{:S(2)}) async-start(bf16[8,2,96,384]{3,2,1,0:T(8,128)(2,1)} %broadcast_in_dim.14), calls=%async_computation | async-start | bytes 2359296 | tf_op jit(solution)/shard_map/all_to_all | solution.py:14
  9.8 1.1 constant_dynamic-slice_fusion
  10.9 0.1 copy.8
  11.0 4.0 %collective-permute-start = (bf16[96,768]{1,0:T(8,128)(2,1)S(1)}, bf16[96,768]{1,0:T(8,128)(2,1)S(1)}, u32[]{:S(2)}, u32[]{:S(2)}) collective-permute-start(bf16[96,768]{1,0:T(8,128)(2,1)S(1)} %bitcast.17), channel_id=1, source_target_pairs={{0,56},{4,12},{8,0},{12,20},{16,8},{20,28},{24,16},{28,36},{32,24}... | collective-permute-start | bytes 442376 | tf_op jit(solution)/shard_map/ppermute | solution.py:23
  15.0 5.8 %collective-permute-start.1 = (bf16[96,768]{1,0:T(8,128)(2,1)S(1)}, bf16[96,768]{1,0:T(8,128)(2,1)S(1)}, u32[]{:S(2)}, u32[]{:S(2)}) collective-permute-start(bf16[96,768]{1,0:T(8,128)(2,1)S(1)} %bitcast.18), channel_id=1, source_target_pairs={{0,48},{4,20},{8,56},{12,28},{16,0},{20,36},{24,8},{28,44},{32,16}... | collective-permute-start | bytes 442376 | tf_op jit(solution)/shard_map/ppermute | solution.py:23
  20.8 5.9 %collective-permute-start.4 = (bf16[96,768]{1,0:T(8,128)(2,1)S(1)}, bf16[96,768]{1,0:T(8,128)(2,1)S(1)}, u32[]{:S(2)}, u32[]{:S(2)}) collective-permute-start(bf16[96,768]{1,0:T(8,128)(2,1)S(1)} %bitcast.19), channel_id=1, source_target_pairs={{0,16},{4,52},{8,24},{12,60},{16,32},{20,4},{24,40},{28,12},{32,48... | collective-permute-start | bytes 442376 | tf_op jit(solution)/shard_map/ppermute | solution.py:23
  26.7 3.1 %collective-permute-start.6 = (bf16[96,768]{1,0:T(8,128)(2,1)S(1)}, bf16[96,768]{1,0:T(8,128)(2,1)S(1)}, u32[]{:S(2)}, u32[]{:S(2)}) collective-permute-start(bf16[96,768]{1,0:T(8,128)(2,1)S(1)} %bitcast.20), channel_id=1, source_target_pairs={{0,8},{4,60},{8,16},{12,4},{16,24},{20,12},{24,32},{28,20},{32,40}... | collective-permute-start | bytes 442376 | tf_op jit(solution)/shard_map/ppermute | solution.py:23
  29.8 0.0 collective-permute-done.1
  29.9 2.2 %collective-permute-start.2 = (bf16[96,768]{1,0:T(8,128)(2,1)S(1)}, bf16[96,768]{1,0:T(8,128)(2,1)S(1)}, u32[]{:S(2)}, u32[]{:S(2)}) collective-permute-start(bf16[96,768]{1,0:T(8,128)(2,1)S(1)} %collective-permute-done.1), channel_id=1, source_target_pairs={{0,56},{4,12},{8,0},{12,20},{16,8},{20,28},{24,16},{28,36},{32,24}... | collective-permute-start | bytes 442376 | tf_op jit(solution)/shard_map/ppermute | solution.py:23
  32.1 2.2 %collective-permute-start.3 = (bf16[96,768]{1,0:T(8,128)(2,1)S(1)}, bf16[96,768]{1,0:T(8,128)(2,1)S(1)}, u32[]{:S(2)}, u32[]{:S(2)}) collective-permute-start(bf16[96,768]{1,0:T(8,128)(2,1)S(1)} %collective-permute-done.1), channel_id=1, source_target_pairs={{0,48},{4,20},{8,56},{12,28},{16,0},{20,36},{24,8},{28,44},{32,16}... | collective-permute-start | bytes 442376 | tf_op jit(solution)/shard_map/ppermute | solution.py:23
  34.2 0.0 collective-permute-done
  34.3 0.0 collective-permute-done.4
  34.3 4.3 %collective-permute-start.5 = (bf16[96,768]{1,0:T(8,128)(2,1)S(1)}, bf16[96,768]{1,0:T(8,128)(2,1)S(1)}, u32[]{:S(2)}, u32[]{:S(2)}) collective-permute-start(bf16[96,768]{1,0:T(8,128)(2,1)S(1)} %collective-permute-done.4), channel_id=1, source_target_pairs={{0,8},{4,60},{8,16},{12,4},{16,24},{20,12},{24,32},{28,20},{32,40}... | collective-permute-start | bytes 442376 | tf_op jit(solution)/shard_map/ppermute | solution.py:23
  38.6 0.1 collective-permute-done.2
  38.7 1.9 %collective-permute-done.3 = bf16[96,768]{1,0:T(8,128)(2,1)S(1)} collective-permute-done((bf16[96,768]{1,0:T(8,128)(2,1)S(1)}, bf16[96,768]{1,0:T(8,128)(2,1)S(1)}, u32[]{:S(2)}, u32[]{:S(2)}) %collective-permute-start.3) | collective-permute-done | bytes 147488 | tf_op jit(solution)/shard_map/ppermute | solution.py:23
  40.5 1.5 %collective-permute-done.5 = bf16[96,768]{1,0:T(8,128)(2,1)S(1)} collective-permute-done((bf16[96,768]{1,0:T(8,128)(2,1)S(1)}, bf16[96,768]{1,0:T(8,128)(2,1)S(1)}, u32[]{:S(2)}, u32[]{:S(2)}) %collective-permute-start.5) | collective-permute-done | bytes 147488 | tf_op jit(solution)/shard_map/ppermute | solution.py:23
  42.0 0.0 collective-permute-done.6
  42.1 0.0 all-to-all-done.right_ref
  42.1 9.6 %collective-permute-start.7 = (bf16[768,768]{1,0:T(8,128)(2,1)S(1)}, bf16[768,768]{1,0:T(8,128)(2,1)S(1)}, u32[]{:S(2)}, u32[]{:S(2)}) collective-permute-start(bf16[768,768]{1,0:T(8,128)(2,1)S(1)} %constant_dynamic-update-slice_fusion.own_ref), channel_id=1, source_target_pairs={{0,4},{4,0},{1,5},{5,1},{2,6},{6,2},{3,7},{7,3},{8,12},{12,8},{9,1... | collective-permute-start | bytes 3538952 | tf_op jit(solution)/shard_map/ppermute | solution.py:144
  51.6 0.1 pad_add_fusion.place_ref
  51.7 2.4 %collective-permute-done.7.other_ref = bf16[768,768]{1,0:T(8,128)(2,1)S(1)} collective-permute-done((bf16[768,768]{1,0:T(8,128)(2,1)S(1)}, bf16[768,768]{1,0:T(8,128)(2,1)S(1)}, u32[]{:S(2)}, u32[]{:S(2)}) %collective-permute-start.7) | collective-permute-done | bytes 1179680 | tf_op jit(solution)/shard_map/ppermute | solution.py:144
  54.1 2.3 %shard_map.37 = bf16[4,2,96,384]{3,2,1,0:T(8,128)(2,1)S(1)} custom-call(s32[3]{0:T(128)S(1)} %pad_add_fusion.place_ref, bf16[768,768]{1,0:T(8,128)(2,1)S(1)} %constant_dynamic-update-slice_fusion.own_ref, bf16[768,768]{1,0:T(8,128)(2,1)S(1)} %collective-permute-done.7.other_ref, bf16[8,2,96,384]{3,2,1,0:T(8,128)(2,1)S(1)} %all-to-all-done.right_ref), custom_call_target="tpu_custom_call" | custom-call | tf_op jit(solution)/shard_map/pallas_call | solution.py:147
  56.4 0.8 copy-done
  57.2 4.1 %all-to-all-start.1 = ((bf16[4,2,96,384]{3,2,1,0:T(8,128)(2,1)}), bf16[4,2,96,384]{3,2,1,0:T(8,128)(2,1)S(1)}, u32[]{:S(2)}, u32[]{:S(2)}) async-start(bf16[4,2,96,384]{3,2,1,0:T(8,128)(2,1)} %copy-done), calls=%async_computation.1 | async-start | bytes 1179648 | tf_op jit(solution)/shard_map/all_to_all | solution.py:159
  61.3 0.8 copy.7.keep_ref
  62.1 8.8 %all-to-all-done.1.parts_ref = bf16[4,2,96,384]{3,2,1,0:T(8,128)(2,1)S(1)} async-done(((bf16[4,2,96,384]{3,2,1,0:T(8,128)(2,1)}), bf16[4,2,96,384]{3,2,1,0:T(8,128)(2,1)S(1)}, u32[]{:S(2)}, u32[]{:S(2)}) %all-to-all-start.1) | async-done | bytes 589856 | tf_op jit(solution)/shard_map/all_to_all | solution.py:159
  70.9 1.4 %shard_map.38.refs_0_ = bf16[2,96,384]{2,1,0:T(8,128)(2,1)} custom-call(s32[12,6]{1,0:T(8,128)S(1)} %copy.7.keep_ref, s32[1]{0:T(128)} %bitcast.8.layer_ref, bf16[4,2,96,384]{3,2,1,0:T(8,128)(2,1)S(1)} %all-to-all-done.1.parts_ref), custom_call_target="tpu_custom_call" | custom-call | tf_op jit(solution)/shard_map/pallas_call | solution.py:160
  72.3 4.5 %collective-permute-start.9 = (bf16[2,96,384]{2,1,0:T(8,128)(2,1)}, bf16[2,96,384]{2,1,0:T(8,128)(2,1)S(1)}, u32[]{:S(2)}, u32[]{:S(2)}) collective-permute-start(bf16[2,96,384]{2,1,0:T(8,128)(2,1)} %shard_map.38.refs_0_), channel_id=1, source_target_pairs={{0,384},{4,132},{64,448},{68,196},{128,0},{132,260},{192,64},{196,... | collective-permute-start | bytes 442376 | tf_op jit(solution)/shard_map/ppermute | solution.py:23
  76.8 3.1 %collective-permute-start.12 = (bf16[2,96,384]{2,1,0:T(8,128)(2,1)}, bf16[2,96,384]{2,1,0:T(8,128)(2,1)S(1)}, u32[]{:S(2)}, u32[]{:S(2)}) collective-permute-start(bf16[2,96,384]{2,1,0:T(8,128)(2,1)} %shard_map.38.refs_0_), channel_id=1, source_target_pairs={{0,128},{4,388},{64,192},{68,452},{128,256},{132,4},{192,320},{196... | collective-permute-start | bytes 442376 | tf_op jit(solution)/shard_map/ppermute | solution.py:23
  79.9 3.4 %collective-permute-start.14 = (bf16[2,96,384]{2,1,0:T(8,128)(2,1)}, bf16[2,96,384]{2,1,0:T(8,128)(2,1)S(1)}, u32[]{:S(2)}, u32[]{:S(2)}) collective-permute-start(bf16[2,96,384]{2,1,0:T(8,128)(2,1)} %shard_map.38.refs_0_), channel_id=1, source_target_pairs={{0,64},{4,452},{64,128},{68,4},{128,192},{132,68},{192,256},{196,1... | collective-permute-start | bytes 442376 | tf_op jit(solution)/shard_map/ppermute | solution.py:23
  83.3 1.9 %collective-permute-start.8 = (bf16[2,96,384]{2,1,0:T(8,128)(2,1)}, bf16[2,96,384]{2,1,0:T(8,128)(2,1)S(1)}, u32[]{:S(2)}, u32[]{:S(2)}) collective-permute-start(bf16[2,96,384]{2,1,0:T(8,128)(2,1)} %shard_map.38.refs_0_), channel_id=1, source_target_pairs={{0,448},{4,68},{64,0},{68,132},{128,64},{132,196},{192,128},{196,2... | collective-permute-start | bytes 442376 | tf_op jit(solution)/shard_map/ppermute | solution.py:23
  85.2 0.0 collective-permute-done.9.refs_2_
  85.2 3.4 %collective-permute-start.10 = (bf16[2,96,384]{2,1,0:T(8,128)(2,1)S(1)}, bf16[2,96,384]{2,1,0:T(8,128)(2,1)}, u32[]{:S(2)}, u32[]{:S(2)}) collective-permute-start(bf16[2,96,384]{2,1,0:T(8,128)(2,1)S(1)} %collective-permute-done.9.refs_2_), channel_id=1, source_target_pairs={{0,448},{4,68},{64,0},{68,132},{128,64},{132,196},{192,128},{196,2... | collective-permute-start | bytes 442376 | tf_op jit(solution)/shard_map/ppermute | solution.py:23
  88.6 4.9 %collective-permute-start.11 = (bf16[2,96,384]{2,1,0:T(8,128)(2,1)S(1)}, bf16[2,96,384]{2,1,0:T(8,128)(2,1)}, u32[]{:S(2)}, u32[]{:S(2)}) collective-permute-start(bf16[2,96,384]{2,1,0:T(8,128)(2,1)S(1)} %collective-permute-done.9.refs_2_), channel_id=1, source_target_pairs={{0,384},{4,132},{64,448},{68,196},{128,0},{132,260},{192,64},{196,... | collective-permute-start | bytes 442376 | tf_op jit(solution)/shard_map/ppermute | solution.py:23
  93.5 0.0 collective-permute-done.12.refs_6_
  93.6 2.2 %collective-permute-start.13 = (bf16[2,96,384]{2,1,0:T(8,128)(2,1)S(1)}, bf16[2,96,384]{2,1,0:T(8,128)(2,1)}, u32[]{:S(2)}, u32[]{:S(2)}) collective-permute-start(bf16[2,96,384]{2,1,0:T(8,128)(2,1)S(1)} %collective-permute-done.12.refs_6_), channel_id=1, source_target_pairs={{0,64},{4,452},{64,128},{68,4},{128,192},{132,68},{192,256},{196,1... | collective-permute-start | bytes 442376 | tf_op jit(solution)/shard_map/ppermute | solution.py:23
  95.8 0.0 collective-permute-done.14.refs_7_
  95.8 0.0 collective-permute-done.8.refs_1_
  95.8 2.2 %collective-permute-done.11.refs_4_ = bf16[2,96,384]{2,1,0:T(8,128)(2,1)} collective-permute-done((bf16[2,96,384]{2,1,0:T(8,128)(2,1)S(1)}, bf16[2,96,384]{2,1,0:T(8,128)(2,1)}, u32[]{:S(2)}, u32[]{:S(2)}) %collective-permute-start.11) | collective-permute-done | bytes 147488 | tf_op jit(solution)/shard_map/ppermute | solution.py:23
  98.0 3.7 %collective-permute-done.13.refs_5_ = bf16[2,96,384]{2,1,0:T(8,128)(2,1)} collective-permute-done((bf16[2,96,384]{2,1,0:T(8,128)(2,1)S(1)}, bf16[2,96,384]{2,1,0:T(8,128)(2,1)}, u32[]{:S(2)}, u32[]{:S(2)}) %collective-permute-start.13) | collective-permute-done | bytes 147488 | tf_op jit(solution)/shard_map/ppermute | solution.py:23
  101.7 2.9 %shard_map.39 = bf16[16,32,128]{2,1,0:T(8,128)(2,1)S(1)} custom-call(s32[16]{0:T(128)S(1)} %bitcast.16, s32[3]{0:T(128)S(1)} %pad_add_fusion.place_ref, f32[1]{0:T(128)} %bitcast.4.scale_ref, bf16[768,768]{1,0:T(8,128)(2,1)S(1)} %constant_dynamic-update-slice_fusion.own_ref, bf16[768,768]{1,0:T(8,128)(2,1)S(1)} %collective-permute-done.7.other_ref, ...), custom_call_target="tpu_custom_call" | custom-call | tf_op jit(solution)/shard_map/pallas_call | solution.py:172
  104.6 14.5 %all_to_all.20 = bf16[16,32,128]{2,1,0:T(8,128)(2,1)S(1)} all-to-all(bf16[16,32,128]{2,1,0:T(8,128)(2,1)S(1)} %shard_map.39), channel_id=1, replica_groups=mesh['row'=8,'z'=8,'core'=2,'layer'=4] {'z','core'}, dimensions={0} | all-to-all | bytes 262144 | tf_op jit(solution)/shard_map/all_to_all | solution.py:184
  119.1 0.1 broadcast_in_dim.15
  119.2 12.3 %all_to_all.21 = bf16[4,16,32,128]{3,2,1,0:T(8,128)(2,1)S(1)} all-to-all(bf16[4,16,32,128]{3,2,1,0:T(8,128)(2,1)S(1)} %broadcast_in_dim.15), channel_id=1, replica_groups=mesh['row'=8,'z'=8,'core'=2,'layer'=4] {'layer'}, dimensions={0} | all-to-all | bytes 1048576 | tf_op jit(solution)/shard_map/all_to_all | solution.py:14
  131.5 0.1 reduce_sum.12
  131.6 0.7 copy.11
  (14 shorter events, 0.1 us)
Async XLA Ops:
  2.1 40.0 %all-to-all-start = ((bf16[8,2,96,384]{3,2,1,0:T(8,128)(2,1)}), bf16[8,2,96,384]{3,2,1,0:T(8,128)(2,1)S(1)}, u32[]{:S(2)}, u32[]{:S(2)}) async-start(bf16[8,2,96,384]{3,2,1,0:T(8,128)(2,1)} %broadcast_in_dim.14), calls=%async_computation | async-start | bytes 2359296 | tf_op jit(solution)/shard_map/all_to_all | solution.py:14
  11.0 23.2 %collective-permute-start = (bf16[96,768]{1,0:T(8,128)(2,1)S(1)}, bf16[96,768]{1,0:T(8,128)(2,1)S(1)}, u32[]{:S(2)}, u32[]{:S(2)}) collective-permute-start(bf16[96,768]{1,0:T(8,128)(2,1)S(1)} %bitcast.17), channel_id=1, source_target_pairs={{0,56},{4,12},{8,0},{12,20},{16,8},{20,28},{24,16},{28,36},{32,24}... | collective-permute-start | bytes 442376 | tf_op jit(solution)/shard_map/ppermute | solution.py:23
  15.0 14.8 %collective-permute-start.1 = (bf16[96,768]{1,0:T(8,128)(2,1)S(1)}, bf16[96,768]{1,0:T(8,128)(2,1)S(1)}, u32[]{:S(2)}, u32[]{:S(2)}) collective-permute-start(bf16[96,768]{1,0:T(8,128)(2,1)S(1)} %bitcast.18), channel_id=1, source_target_pairs={{0,48},{4,20},{8,56},{12,28},{16,0},{20,36},{24,8},{28,44},{32,16}... | collective-permute-start | bytes 442376 | tf_op jit(solution)/shard_map/ppermute | solution.py:23
  20.8 13.4 %collective-permute-start.4 = (bf16[96,768]{1,0:T(8,128)(2,1)S(1)}, bf16[96,768]{1,0:T(8,128)(2,1)S(1)}, u32[]{:S(2)}, u32[]{:S(2)}) collective-permute-start(bf16[96,768]{1,0:T(8,128)(2,1)S(1)} %bitcast.19), channel_id=1, source_target_pairs={{0,16},{4,52},{8,24},{12,60},{16,32},{20,4},{24,40},{28,12},{32,48... | collective-permute-start | bytes 442376 | tf_op jit(solution)/shard_map/ppermute | solution.py:23
  26.7 15.3 %collective-permute-start.6 = (bf16[96,768]{1,0:T(8,128)(2,1)S(1)}, bf16[96,768]{1,0:T(8,128)(2,1)S(1)}, u32[]{:S(2)}, u32[]{:S(2)}) collective-permute-start(bf16[96,768]{1,0:T(8,128)(2,1)S(1)} %bitcast.20), channel_id=1, source_target_pairs={{0,8},{4,60},{8,16},{12,4},{16,24},{20,12},{24,32},{28,20},{32,40}... | collective-permute-start | bytes 442376 | tf_op jit(solution)/shard_map/ppermute | solution.py:23
  29.9 8.8 %collective-permute-start.2 = (bf16[96,768]{1,0:T(8,128)(2,1)S(1)}, bf16[96,768]{1,0:T(8,128)(2,1)S(1)}, u32[]{:S(2)}, u32[]{:S(2)}) collective-permute-start(bf16[96,768]{1,0:T(8,128)(2,1)S(1)} %collective-permute-done.1), channel_id=1, source_target_pairs={{0,56},{4,12},{8,0},{12,20},{16,8},{20,28},{24,16},{28,36},{32,24}... | collective-permute-start | bytes 442376 | tf_op jit(solution)/shard_map/ppermute | solution.py:23
  32.1 8.5 %collective-permute-start.3 = (bf16[96,768]{1,0:T(8,128)(2,1)S(1)}, bf16[96,768]{1,0:T(8,128)(2,1)S(1)}, u32[]{:S(2)}, u32[]{:S(2)}) collective-permute-start(bf16[96,768]{1,0:T(8,128)(2,1)S(1)} %collective-permute-done.1), channel_id=1, source_target_pairs={{0,48},{4,20},{8,56},{12,28},{16,0},{20,36},{24,8},{28,44},{32,16}... | collective-permute-start | bytes 442376 | tf_op jit(solution)/shard_map/ppermute | solution.py:23
  34.3 7.7 %collective-permute-start.5 = (bf16[96,768]{1,0:T(8,128)(2,1)S(1)}, bf16[96,768]{1,0:T(8,128)(2,1)S(1)}, u32[]{:S(2)}, u32[]{:S(2)}) collective-permute-start(bf16[96,768]{1,0:T(8,128)(2,1)S(1)} %collective-permute-done.4), channel_id=1, source_target_pairs={{0,8},{4,60},{8,16},{12,4},{16,24},{20,12},{24,32},{28,20},{32,40}... | collective-permute-start | bytes 442376 | tf_op jit(solution)/shard_map/ppermute | solution.py:23
  42.1 12.0 %collective-permute-start.7 = (bf16[768,768]{1,0:T(8,128)(2,1)S(1)}, bf16[768,768]{1,0:T(8,128)(2,1)S(1)}, u32[]{:S(2)}, u32[]{:S(2)}) collective-permute-start(bf16[768,768]{1,0:T(8,128)(2,1)S(1)} %constant_dynamic-update-slice_fusion.own_ref), channel_id=1, source_target_pairs={{0,4},{4,0},{1,5},{5,1},{2,6},{6,2},{3,7},{7,3},{8,12},{12,8},{9,1... | collective-permute-start | bytes 3538952 | tf_op jit(solution)/shard_map/ppermute | solution.py:144
  56.3 0.8 copy-start
  57.2 44.5 %copy-start.1 = (bf16[768,384]{1,0:T(8,128)(2,1)S(1)}, bf16[768,384]{1,0:T(8,128)(2,1)}, u32[]{:S(2)}) copy-start(bf16[768,384]{1,0:T(8,128)(2,1)} %matrix_ref.1) | copy-start | bytes 1769476
  57.2 44.5 %copy-start.2 = (s32[1,16]{1,0:T(1,128)S(1)}, s32[1,16]{1,0:T(1,128)}, u32[]{:S(2)}) copy-start(s32[1,16]{1,0:T(1,128)} %param.5) | copy-start | bytes 196
  57.2 13.7 %all-to-all-start.1 = ((bf16[4,2,96,384]{3,2,1,0:T(8,128)(2,1)}), bf16[4,2,96,384]{3,2,1,0:T(8,128)(2,1)S(1)}, u32[]{:S(2)}, u32[]{:S(2)}) async-start(bf16[4,2,96,384]{3,2,1,0:T(8,128)(2,1)} %copy-done), calls=%async_computation.1 | async-start | bytes 1179648 | tf_op jit(solution)/shard_map/all_to_all | solution.py:159
  72.3 12.9 %collective-permute-start.9 = (bf16[2,96,384]{2,1,0:T(8,128)(2,1)}, bf16[2,96,384]{2,1,0:T(8,128)(2,1)S(1)}, u32[]{:S(2)}, u32[]{:S(2)}) collective-permute-start(bf16[2,96,384]{2,1,0:T(8,128)(2,1)} %shard_map.38.refs_0_), channel_id=1, source_target_pairs={{0,384},{4,132},{64,448},{68,196},{128,0},{132,260},{192,64},{196,... | collective-permute-start | bytes 442376 | tf_op jit(solution)/shard_map/ppermute | solution.py:23
  76.8 16.7 %collective-permute-start.12 = (bf16[2,96,384]{2,1,0:T(8,128)(2,1)}, bf16[2,96,384]{2,1,0:T(8,128)(2,1)S(1)}, u32[]{:S(2)}, u32[]{:S(2)}) collective-permute-start(bf16[2,96,384]{2,1,0:T(8,128)(2,1)} %shard_map.38.refs_0_), channel_id=1, source_target_pairs={{0,128},{4,388},{64,192},{68,452},{128,256},{132,4},{192,320},{196... | collective-permute-start | bytes 442376 | tf_op jit(solution)/shard_map/ppermute | solution.py:23
  79.9 15.8 %collective-permute-start.14 = (bf16[2,96,384]{2,1,0:T(8,128)(2,1)}, bf16[2,96,384]{2,1,0:T(8,128)(2,1)S(1)}, u32[]{:S(2)}, u32[]{:S(2)}) collective-permute-start(bf16[2,96,384]{2,1,0:T(8,128)(2,1)} %shard_map.38.refs_0_), channel_id=1, source_target_pairs={{0,64},{4,452},{64,128},{68,4},{128,192},{132,68},{192,256},{196,1... | collective-permute-start | bytes 442376 | tf_op jit(solution)/shard_map/ppermute | solution.py:23
  83.3 12.5 %collective-permute-start.8 = (bf16[2,96,384]{2,1,0:T(8,128)(2,1)}, bf16[2,96,384]{2,1,0:T(8,128)(2,1)S(1)}, u32[]{:S(2)}, u32[]{:S(2)}) collective-permute-start(bf16[2,96,384]{2,1,0:T(8,128)(2,1)} %shard_map.38.refs_0_), channel_id=1, source_target_pairs={{0,448},{4,68},{64,0},{68,132},{128,64},{132,196},{192,128},{196,2... | collective-permute-start | bytes 442376 | tf_op jit(solution)/shard_map/ppermute | solution.py:23
  85.2 10.5 %collective-permute-start.10 = (bf16[2,96,384]{2,1,0:T(8,128)(2,1)S(1)}, bf16[2,96,384]{2,1,0:T(8,128)(2,1)}, u32[]{:S(2)}, u32[]{:S(2)}) collective-permute-start(bf16[2,96,384]{2,1,0:T(8,128)(2,1)S(1)} %collective-permute-done.9.refs_2_), channel_id=1, source_target_pairs={{0,448},{4,68},{64,0},{68,132},{128,64},{132,196},{192,128},{196,2... | collective-permute-start | bytes 442376 | tf_op jit(solution)/shard_map/ppermute | solution.py:23
  88.6 9.4 %collective-permute-start.11 = (bf16[2,96,384]{2,1,0:T(8,128)(2,1)S(1)}, bf16[2,96,384]{2,1,0:T(8,128)(2,1)}, u32[]{:S(2)}, u32[]{:S(2)}) collective-permute-start(bf16[2,96,384]{2,1,0:T(8,128)(2,1)S(1)} %collective-permute-done.9.refs_2_), channel_id=1, source_target_pairs={{0,384},{4,132},{64,448},{68,196},{128,0},{132,260},{192,64},{196,... | collective-permute-start | bytes 442376 | tf_op jit(solution)/shard_map/ppermute | solution.py:23
  93.6 8.1 %collective-permute-start.13 = (bf16[2,96,384]{2,1,0:T(8,128)(2,1)S(1)}, bf16[2,96,384]{2,1,0:T(8,128)(2,1)}, u32[]{:S(2)}, u32[]{:S(2)}) collective-permute-start(bf16[2,96,384]{2,1,0:T(8,128)(2,1)S(1)} %collective-permute-done.12.refs_6_), channel_id=1, source_target_pairs={{0,64},{4,452},{64,128},{68,4},{128,192},{132,68},{192,256},{196,1... | collective-permute-start | bytes 442376 | tf_op jit(solution)/shard_map/ppermute | solution.py:23

commit v5 on v4

--- a/solution.py
+++ b/solution.py
@@ -7,11 +7,6 @@
 
 BLK = 64
 CONTRACT = (((0,), (0,)), ((), ()))
-
-
-def to_all(piece, axis):
-    copies = jnp.broadcast_to(piece[None], (lax.axis_size(axis),) + piece.shape)
-    return lax.all_to_all(copies, axis, split_axis=0, concat_axis=0, tiled=True)
 
 
 def shifted(piece, axis, by):
@@ -23,15 +18,30 @@
     return lax.ppermute(piece, (axis, "core"), pairs)
 
 
-def ring_of_eight(piece, axis):
-    up = shifted(piece, axis, 2)
-    down = shifted(piece, axis, -2)
-    near_up = shifted(piece, axis, 1)
-    near_down = shifted(piece, axis, -1)
-    far_up = shifted(up, axis, 1)
-    far_down = shifted(down, axis, -1)
-    opposite = shifted(up, axis, 2)
-    return piece, near_up, up, far_up, opposite, far_down, down, near_down
+def rings_of_eight(pieces, axes):
+    def step(held, by):
+        got = [shifted(piece, axis, by) for piece, axis in zip(held, axes)]
+        return lax.optimization_barrier(got) if len(got) > 1 else got
+
+    ups = step(pieces, 2)
+    downs = step(pieces, -2)
+    near_ups = step(pieces, 1)
+    near_downs = step(pieces, -1)
+    far_ups = step(ups, 1)
+    opposites = step(ups, 2)
+    far_downs = step(downs, -1)
+    return list(zip(pieces, near_ups, ups, far_ups, opposites, far_downs, downs, near_downs))
+
+
+def put_in_order(place_ref, pieces, ordered_ref):
+    tiles = ordered_ref.shape[1]
+    row, z, core = place_ref[0], place_ref[1], place_ref[2]
+    way = 1 - 2 * core
+    for offset, piece in enumerate(pieces):
+        distance = row + way * offset - z
+        own = lax.rem(way * distance + 2 * tiles, tiles)
+        ordered_ref[0, own] = piece[core]
+        ordered_ref[1, lax.rem(tiles - own, tiles)] = piece[1 - core]
 
 
 def product(own_ref, other_ref, right_ref, start, count):
@@ -47,14 +57,10 @@
     return own + other
 
 
-def square_kernel(place_ref, own_ref, other_ref, right_ref, out_ref, ordered_ref, staged_ref, sems):
+def square_kernel(place_ref, own_ref, other_ref, *refs):
+    out_ref, ordered_ref, staged_ref, sems = refs[8:]
     halves, layers, part, columns = staged_ref.shape
-    tiles = right_ref.shape[0]
-    z, core = place_ref[1], place_ref[2]
-    way = 1 - 2 * core
-    for offset in range(tiles):
-        ordered_ref[0, offset] = right_ref[lax.rem(z + way * offset + tiles, tiles), core]
-        ordered_ref[1, offset] = right_ref[lax.rem(z - way * offset + tiles, tiles), 1 - core]
+    put_in_order(place_ref, refs[:8], ordered_ref)
     copies = []
     for half in range(halves):
         count = layers * part
@@ -89,14 +95,7 @@
     out_ref, ordered_ref, total_ref, block_ref = refs[8:]
     owners, pairs, lanes = out_ref.shape
     half_blocks = matrix_ref.shape[1] // BLK
-    tiles = ordered_ref.shape[1]
-    row, z, core = place_ref[0], place_ref[1], place_ref[2]
-    way = 1 - 2 * core
-    for offset, piece in enumerate(pieces):
-        distance = row + way * offset - z
-        own = lax.rem(way * distance + 2 * tiles, tiles)
-        ordered_ref[0, own] = piece[core]
-        ordered_ref[1, lax.rem(tiles - own, tiles)] = piece[1 - core]
+    put_in_order(place_ref, pieces, ordered_ref)
     total_ref[...] = scale_ref[0] * matrix_ref[...].astype(jnp.float32) - 0.5 * product(
         own_ref, other_ref, ordered_ref, 0, matrix_ref.shape[0]
     )
@@ -138,8 +137,8 @@
     right_piece = lax.dynamic_slice_in_dim(
         matrix.reshape(halves, layers, part, width), layer_index, 1, 1
     ).reshape(halves, part, width)
-    right = to_all(right_piece, "row")
-    left_own = jnp.concatenate(ring_of_eight(left_piece, "z"), axis=0)
+    left_pieces, right = rings_of_eight((left_piece, right_piece), ("z", "row"))
+    left_own = jnp.concatenate(left_pieces, axis=0)
     left_own, right = lax.optimization_barrier((left_own, right))
     left_other = lax.ppermute(left_own, "core", [(0, 1), (1, 0)])
     place = jnp.stack([row_index, z_index, core_index])
@@ -147,7 +146,7 @@
     square_part = pl.pallas_call(
         square_kernel,
         out_shape=jax.ShapeDtypeStruct((layers, halves, part, width), jnp.bfloat16),
-        in_specs=[smem, vmem, vmem, vmem],
+        in_specs=[smem] + [vmem] * 10,
         out_specs=pl.BlockSpec(memory_space=pltpu.HBM),
         scratch_shapes=[
             pltpu.VMEM((halves, rows_count, part, width), jnp.bfloat16),
@@ -155,7 +154,7 @@
             pltpu.SemaphoreType.DMA((halves,)),
         ],
         compiler_params=params,
-    )(place, left_own, left_other, right)
+    )(place, left_own, left_other, *right)
     parts = lax.all_to_all(square_part, "layer", split_axis=0, concat_axis=0, tiled=True)
     filtered_piece = pl.pallas_call(
         filter_kernel,
@@ -164,7 +163,7 @@
         out_specs=vmem,
         compiler_params=params,
     )(keep_mask, layer_index.reshape(1), parts)
-    filtered = ring_of_eight(filtered_piece, "row")
+    filtered = rings_of_eight((filtered_piece,), ("row",))[0]
 
     scale = jnp.where(layer_index == 0, 1.5, 0.0).astype(jnp.float32).reshape(1)
     chosen = send_list[0]
@@ -181,9 +180,11 @@
         ],
         compiler_params=params,
     )(chosen, place, scale, left_own, left_other, matrix, *filtered)
-    arrived = lax.all_to_all(outgoing, ("z", "core"), split_axis=0, concat_axis=0, tiled=True)
-    everyone = to_all(arrived, "layer")
-    total = everyone.astype(jnp.float32).sum(0).astype(jnp.bfloat16)
+    copies = jnp.broadcast_to(outgoing[:, None], outgoing.shape[:1] + (layers,) + outgoing.shape[1:])
+    copies = copies.reshape((-1,) + outgoing.shape[1:])
+    everyone = lax.all_to_all(copies, ("z", "core", "layer"), split_axis=0, concat_axis=0, tiled=True)
+    everyone = everyone.reshape(outgoing.shape[:1] + (layers,) + outgoing.shape[1:])
+    total = everyone.astype(jnp.float32).sum(1).astype(jnp.bfloat16)
     return total.reshape(total.shape[0], BLK * BLK)
 
 

time: 133 us -> 143 us (1.075)
  starting transfers between devices: 72.1 us -> 84.9 us
  blocking collectives: 26.8 us -> 23.7 us
  local copies, waits for them, and re-layouts: 5.83 us -> 3.85 us
  waiting for transfers between devices: 20.5 us -> 22 us
    ppermute x14 -> x21, starting transfers between devices: 50.8 us -> 73.7 us  [shifted(): return lax.ppermute(piece, (axis, 'core'), pairs)]
    all_to_all x1 -> x0, starting transfers between devices: 7.65 us -> none  [to_all(): return lax.all_to_all(copies, axis, split_axis=0, concat_axis=0, tiled=True)]
    all_to_all x2 -> x1, blocking collectives: 26.8 us -> 23.7 us  [on_device(): lax.all_to_all(copies, ('z', 'core', 'layer'), split_axis=0, concat_axis=...]
    ppermute x1, starting transfers between devices: 9.55 us -> 7.03 us  [on_device(): left_other = lax.ppermute(left_own, 'core', [(0, 1), (1, 0)])]
    broadcast_in_dim x3 -> x1, local copies, waits for them, and re-layouts: 2.18 us -> 0.08 us  [on_device(): jnp.broadcast_to(outgoing[:, None], outgoing.shape[:1] + (layers,) + outg...]
    ppermute x14 -> x21, waiting for transfers between devices: 9.27 us -> 10.8 us  [shifted(): return lax.ppermute(piece, (axis, 'core'), pairs)]
  transfers between devices with their start and end apart: 17 -> 23, of which waited for: 6 -> 5; matrix products, arithmetic and copies ran while one was open for 2% -> 1% of each run, Pallas kernels for 0% -> 0%
where the time goes in v5:
time: 143 us; the launch traced here: 142 us
  starting transfers between devices  84.9 us (59%)
  blocking collectives  23.7 us (17%)
  waiting for transfers between devices  22 us (15%)
  Pallas kernels  7.11 us (5%)
  local copies, waits for them, and re-layouts  3.85 us (3%)
    ppermute x21, starting transfers between devices, shifted(): return lax.ppermute(piece, (axis, 'core'), pairs)  73.7 us
    all_to_all x1, blocking collectives, on_device(): lax.all_to_all(copies, ('z', 'core', 'layer'), split_axis=0, concat_axis=...  23.7 us
    ppermute x21, waiting for transfers between devices, shifted(): return lax.ppermute(piece, (axis, 'core'), pairs)  10.8 us
    all_to_all x1, waiting for transfers between devices, on_device(): lax.all_to_all(square_part, 'layer', split_axis=0, concat_axis=0, tiled=T...  8.83 us
    ppermute x1, starting transfers between devices, on_device(): left_other = lax.ppermute(left_own, 'core', [(0, 1), (1, 0)])  7.03 us
    all_to_all x1, starting transfers between devices, on_device(): lax.all_to_all(square_part, 'layer', split_axis=0, concat_axis=0, tiled=T...  4.15 us
    pallas_call x1, Pallas kernels, on_device(): pl.pallas_call(cube_kernel, out_shape=jax.ShapeDtypeStruct((chosen.shape[...  2.92 us
  transfers between devices with their start and end apart: 23, of which 5 were waited for; matrix products, arithmetic and copies ran while one was open for 1% of the time, Pallas kernels for 0%

profile of v5, /device:TPU:1, one launch (start us, length us, event | category | flops | bytes accessed | tf_op | source)
XLA Modules:
  0.0 142.1 jit_solution(10310085918841657635)
XLA Ops:
  0.0 1.1 constant_dynamic-slice_fusion
  1.1 0.1 copy.10
  1.3 6.6 %collective-permute-start.2 = (bf16[96,768]{1,0:T(8,128)(2,1)S(1)}, bf16[96,768]{1,0:T(8,128)(2,1)S(1)}, u32[]{:S(2)}, u32[]{:S(2)}) collective-permute-start(bf16[96,768]{1,0:T(8,128)(2,1)S(1)} %bitcast.23), channel_id=1, source_target_pairs={{0,48},{4,20},{8,56},{12,28},{16,0},{20,36},{24,8},{28,44},{32,16}... | collective-permute-start | bytes 442376 | tf_op jit(solution)/shard_map/ppermute | solution.py:18
  7.9 0.9 dynamic-slice_bitcast_fusion.refs_0_
  8.8 4.2 %collective-permute-start.3 = (bf16[2,96,384]{2,1,0:T(8,128)(2,1)S(1)}, bf16[2,96,384]{2,1,0:T(8,128)(2,1)S(1)}, u32[]{:S(2)}, u32[]{:S(2)}) collective-permute-start(bf16[2,96,384]{2,1,0:T(8,128)(2,1)S(1)} %dynamic-slice_bitcast_fusion.refs_0_), channel_id=1, source_target_pairs={{0,384},{4,132},{64,448},{68,196},{128,0},{132,260},{192,64},{196,... | collective-permute-start | bytes 442376 | tf_op jit(solution)/shard_map/ppermute | solution.py:18
  13.1 4.0 %collective-permute-start = (bf16[96,768]{1,0:T(8,128)(2,1)S(1)}, bf16[96,768]{1,0:T(8,128)(2,1)S(1)}, u32[]{:S(2)}, u32[]{:S(2)}) collective-permute-start(bf16[96,768]{1,0:T(8,128)(2,1)S(1)} %bitcast.24), channel_id=1, source_target_pairs={{0,56},{4,12},{8,0},{12,20},{16,8},{20,28},{24,16},{28,36},{32,24}... | collective-permute-start | bytes 442376 | tf_op jit(solution)/shard_map/ppermute | solution.py:18
  17.1 3.2 %collective-permute-start.1 = (bf16[2,96,384]{2,1,0:T(8,128)(2,1)S(1)}, bf16[2,96,384]{2,1,0:T(8,128)(2,1)S(1)}, u32[]{:S(2)}, u32[]{:S(2)}) collective-permute-start(bf16[2,96,384]{2,1,0:T(8,128)(2,1)S(1)} %dynamic-slice_bitcast_fusion.refs_0_), channel_id=1, source_target_pairs={{0,448},{4,68},{64,0},{68,132},{128,64},{132,196},{192,128},{196,2... | collective-permute-start | bytes 442376 | tf_op jit(solution)/shard_map/ppermute | solution.py:18
  20.3 5.9 %collective-permute-start.8 = (bf16[96,768]{1,0:T(8,128)(2,1)S(1)}, bf16[96,768]{1,0:T(8,128)(2,1)S(1)}, u32[]{:S(2)}, u32[]{:S(2)}) collective-permute-start(bf16[96,768]{1,0:T(8,128)(2,1)S(1)} %bitcast.25), channel_id=1, source_target_pairs={{0,16},{4,52},{8,24},{12,60},{16,32},{20,4},{24,40},{28,12},{32,48... | collective-permute-start | bytes 442376 | tf_op jit(solution)/shard_map/ppermute | solution.py:18
  26.2 0.0 collective-permute-done.2
  26.2 3.2 %collective-permute-start.9 = (bf16[2,96,384]{2,1,0:T(8,128)(2,1)S(1)}, bf16[2,96,384]{2,1,0:T(8,128)(2,1)S(1)}, u32[]{:S(2)}, u32[]{:S(2)}) collective-permute-start(bf16[2,96,384]{2,1,0:T(8,128)(2,1)S(1)} %dynamic-slice_bitcast_fusion.refs_0_), channel_id=1, source_target_pairs={{0,128},{4,388},{64,192},{68,452},{128,256},{132,4},{192,320},{196... | collective-permute-start | bytes 442376 | tf_op jit(solution)/shard_map/ppermute | solution.py:18
  29.4 0.0 collective-permute-done.3.refs_2_
  29.4 3.1 %collective-permute-start.12 = (bf16[96,768]{1,0:T(8,128)(2,1)S(1)}, bf16[96,768]{1,0:T(8,128)(2,1)S(1)}, u32[]{:S(2)}, u32[]{:S(2)}) collective-permute-start(bf16[96,768]{1,0:T(8,128)(2,1)S(1)} %bitcast.26), channel_id=1, source_target_pairs={{0,8},{4,60},{8,16},{12,4},{16,24},{20,12},{24,32},{28,20},{32,40}... | collective-permute-start | bytes 442376 | tf_op jit(solution)/shard_map/ppermute | solution.py:18
  32.5 2.6 %collective-permute-start.13 = (bf16[2,96,384]{2,1,0:T(8,128)(2,1)S(1)}, bf16[2,96,384]{2,1,0:T(8,128)(2,1)S(1)}, u32[]{:S(2)}, u32[]{:S(2)}) collective-permute-start(bf16[2,96,384]{2,1,0:T(8,128)(2,1)S(1)} %dynamic-slice_bitcast_fusion.refs_0_), channel_id=1, source_target_pairs={{0,64},{4,452},{64,128},{68,4},{128,192},{132,68},{192,256},{196,1... | collective-permute-start | bytes 442376 | tf_op jit(solution)/shard_map/ppermute | solution.py:18
  35.1 0.0 collective-permute-done.1.refs_1_
  35.1 2.2 %collective-permute-start.4 = (bf16[96,768]{1,0:T(8,128)(2,1)S(1)}, bf16[96,768]{1,0:T(8,128)(2,1)S(1)}, u32[]{:S(2)}, u32[]{:S(2)}) collective-permute-start(bf16[96,768]{1,0:T(8,128)(2,1)S(1)} %collective-permute-done.2), channel_id=1, source_target_pairs={{0,56},{4,12},{8,0},{12,20},{16,8},{20,28},{24,16},{28,36},{32,24}... | collective-permute-start | bytes 442376 | tf_op jit(solution)/shard_map/ppermute | solution.py:18
  37.3 0.0 collective-permute-done.8
  37.3 2.2 %collective-permute-start.6 = (bf16[96,768]{1,0:T(8,128)(2,1)S(1)}, bf16[96,768]{1,0:T(8,128)(2,1)S(1)}, u32[]{:S(2)}, u32[]{:S(2)}) collective-permute-start(bf16[96,768]{1,0:T(8,128)(2,1)S(1)} %collective-permute-done.2), channel_id=1, source_target_pairs={{0,48},{4,20},{8,56},{12,28},{16,0},{20,36},{24,8},{28,44},{32,16}... | collective-permute-start | bytes 442376 | tf_op jit(solution)/shard_map/ppermute | solution.py:18
  39.5 0.0 collective-permute-done.9.refs_6_
  39.5 2.7 %collective-permute-start.5 = (bf16[2,96,384]{2,1,0:T(8,128)(2,1)S(1)}, bf16[2,96,384]{2,1,0:T(8,128)(2,1)S(1)}, u32[]{:S(2)}, u32[]{:S(2)}) collective-permute-start(bf16[2,96,384]{2,1,0:T(8,128)(2,1)S(1)} %collective-permute-done.3.refs_2_), channel_id=1, source_target_pairs={{0,448},{4,68},{64,0},{68,132},{128,64},{132,196},{192,128},{196,2... | collective-permute-start | bytes 442376 | tf_op jit(solution)/shard_map/ppermute | solution.py:18
  42.2 0.0 collective-permute-done.12
  42.2 4.1 %collective-permute-start.7 = (bf16[2,96,384]{2,1,0:T(8,128)(2,1)S(1)}, bf16[2,96,384]{2,1,0:T(8,128)(2,1)S(1)}, u32[]{:S(2)}, u32[]{:S(2)}) collective-permute-start(bf16[2,96,384]{2,1,0:T(8,128)(2,1)S(1)} %collective-permute-done.3.refs_2_), channel_id=1, source_target_pairs={{0,384},{4,132},{64,448},{68,196},{128,0},{132,260},{192,64},{196,... | collective-permute-start | bytes 442376 | tf_op jit(solution)/shard_map/ppermute | solution.py:18
  46.3 4.1 %collective-permute-start.10 = (bf16[96,768]{1,0:T(8,128)(2,1)S(1)}, bf16[96,768]{1,0:T(8,128)(2,1)S(1)}, u32[]{:S(2)}, u32[]{:S(2)}) collective-permute-start(bf16[96,768]{1,0:T(8,128)(2,1)S(1)} %collective-permute-done.8), channel_id=1, source_target_pairs={{0,8},{4,60},{8,16},{12,4},{16,24},{20,12},{24,32},{28,20},{32,40}... | collective-permute-start | bytes 442376 | tf_op jit(solution)/shard_map/ppermute | solution.py:18
  50.4 3.4 %collective-permute-start.11 = (bf16[2,96,384]{2,1,0:T(8,128)(2,1)S(1)}, bf16[2,96,384]{2,1,0:T(8,128)(2,1)S(1)}, u32[]{:S(2)}, u32[]{:S(2)}) collective-permute-start(bf16[2,96,384]{2,1,0:T(8,128)(2,1)S(1)} %collective-permute-done.9.refs_6_), channel_id=1, source_target_pairs={{0,64},{4,452},{64,128},{68,4},{128,192},{132,68},{192,256},{196,1... | collective-permute-start | bytes 442376 | tf_op jit(solution)/shard_map/ppermute | solution.py:18
  53.9 6.9 %collective-permute-done.11.refs_5_ = bf16[2,96,384]{2,1,0:T(8,128)(2,1)S(1)} collective-permute-done((bf16[2,96,384]{2,1,0:T(8,128)(2,1)S(1)}, bf16[2,96,384]{2,1,0:T(8,128)(2,1)S(1)}, u32[]{:S(2)}, u32[]{:S(2)}) %collective-permute-start.11) | collective-permute-done | bytes 147488 | tf_op jit(solution)/shard_map/ppermute | solution.py:18
  60.9 7.0 %collective-permute-start.14 = (bf16[768,768]{1,0:T(8,128)(2,1)S(1)}, bf16[768,768]{1,0:T(8,128)(2,1)S(1)}, u32[]{:S(2)}, u32[]{:S(2)}) collective-permute-start(bf16[768,768]{1,0:T(8,128)(2,1)S(1)} %constant_dynamic-update-slice_fusion.own_ref), channel_id=1, source_target_pairs={{0,4},{4,0},{1,5},{5,1},{2,6},{6,2},{3,7},{7,3},{8,12},{12,8},{9,1... | collective-permute-start | bytes 3538952 | tf_op jit(solution)/shard_map/ppermute | solution.py:143
  68.0 0.1 pad_add_fusion.place_ref
  68.1 2.4 %collective-permute-done.14.other_ref = bf16[768,768]{1,0:T(8,128)(2,1)S(1)} collective-permute-done((bf16[768,768]{1,0:T(8,128)(2,1)S(1)}, bf16[768,768]{1,0:T(8,128)(2,1)S(1)}, u32[]{:S(2)}, u32[]{:S(2)}) %collective-permute-start.14) | collective-permute-done | bytes 1179680 | tf_op jit(solution)/shard_map/ppermute | solution.py:143
  70.4 2.8 %shard_map.37 = bf16[4,2,96,384]{3,2,1,0:T(8,128)(2,1)} custom-call(s32[3]{0:T(128)S(1)} %pad_add_fusion.place_ref, bf16[768,768]{1,0:T(8,128)(2,1)S(1)} %constant_dynamic-update-slice_fusion.own_ref, bf16[768,768]{1,0:T(8,128)(2,1)S(1)} %collective-permute-done.14.other_ref, bf16[2,96,384]{2,1,0:T(8,128)(2,1)S(1)} %dynamic-slice_bitcast_fusion.refs_0_, ...), custom_call_target="tpu_custom_call" | custom-call | tf_op jit(solution)/shard_map/pallas_call | solution.py:146
  73.2 0.0 copy-start
  73.2 0.0 copy-start.1
  73.2 4.2 %all-to-all-start = ((bf16[4,2,96,384]{3,2,1,0:T(8,128)(2,1)}), bf16[4,2,96,384]{3,2,1,0:T(8,128)(2,1)S(1)}, u32[]{:S(2)}, u32[]{:S(2)}) async-start(bf16[4,2,96,384]{3,2,1,0:T(8,128)(2,1)} %shard_map.37), calls=%async_computation | async-start | bytes 1179648 | tf_op jit(solution)/shard_map/all_to_all | solution.py:158
  77.4 0.8 copy.9.keep_ref
  78.2 8.8 %all-to-all-done.parts_ref = bf16[4,2,96,384]{3,2,1,0:T(8,128)(2,1)S(1)} async-done(((bf16[4,2,96,384]{3,2,1,0:T(8,128)(2,1)}), bf16[4,2,96,384]{3,2,1,0:T(8,128)(2,1)S(1)}, u32[]{:S(2)}, u32[]{:S(2)}) %all-to-all-start) | async-done | bytes 589856 | tf_op jit(solution)/shard_map/all_to_all | solution.py:158
  87.0 1.4 shard_map.38.refs_0_
  88.4 1.9 %collective-permute-start.16 = (bf16[2,96,384]{2,1,0:T(8,128)(2,1)}, bf16[2,96,384]{2,1,0:T(8,128)(2,1)S(1)}, u32[]{:S(2)}, u32[]{:S(2)}) collective-permute-start(bf16[2,96,384]{2,1,0:T(8,128)(2,1)} %shard_map.38.refs_0_), channel_id=1, source_target_pairs={{0,384},{4,132},{64,448},{68,196},{128,0},{132,260},{192,64},{196,... | collective-permute-start | bytes 442376 | tf_op jit(solution)/shard_map/ppermute | solution.py:18
  90.3 5.5 %collective-permute-start.19 = (bf16[2,96,384]{2,1,0:T(8,128)(2,1)}, bf16[2,96,384]{2,1,0:T(8,128)(2,1)S(1)}, u32[]{:S(2)}, u32[]{:S(2)}) collective-permute-start(bf16[2,96,384]{2,1,0:T(8,128)(2,1)} %shard_map.38.refs_0_), channel_id=1, source_target_pairs={{0,128},{4,388},{64,192},{68,452},{128,256},{132,4},{192,320},{196... | collective-permute-start | bytes 442376 | tf_op jit(solution)/shard_map/ppermute | solution.py:18
  95.8 1.9 %collective-permute-start.15 = (bf16[2,96,384]{2,1,0:T(8,128)(2,1)}, bf16[2,96,384]{2,1,0:T(8,128)(2,1)S(1)}, u32[]{:S(2)}, u32[]{:S(2)}) collective-permute-start(bf16[2,96,384]{2,1,0:T(8,128)(2,1)} %shard_map.38.refs_0_), channel_id=1, source_target_pairs={{0,448},{4,68},{64,0},{68,132},{128,64},{132,196},{192,128},{196,2... | collective-permute-start | bytes 442376 | tf_op jit(solution)/shard_map/ppermute | solution.py:18
  97.7 4.6 %collective-permute-start.21 = (bf16[2,96,384]{2,1,0:T(8,128)(2,1)}, bf16[2,96,384]{2,1,0:T(8,128)(2,1)S(1)}, u32[]{:S(2)}, u32[]{:S(2)}) collective-permute-start(bf16[2,96,384]{2,1,0:T(8,128)(2,1)} %shard_map.38.refs_0_), channel_id=1, source_target_pairs={{0,64},{4,452},{64,128},{68,4},{128,192},{132,68},{192,256},{196,1... | collective-permute-start | bytes 442376 | tf_op jit(solution)/shard_map/ppermute | solution.py:18
  102.3 1.9 %collective-permute-start.17 = (bf16[2,96,384]{2,1,0:T(8,128)(2,1)S(1)}, bf16[2,96,384]{2,1,0:T(8,128)(2,1)}, u32[]{:S(2)}, u32[]{:S(2)}) collective-permute-start(bf16[2,96,384]{2,1,0:T(8,128)(2,1)S(1)} %collective-permute-done.16.refs_2_), channel_id=1, source_target_pairs={{0,448},{4,68},{64,0},{68,132},{128,64},{132,196},{192,128},{196,2... | collective-permute-start | bytes 442376 | tf_op jit(solution)/shard_map/ppermute | solution.py:18
  104.2 1.9 %collective-permute-start.18 = (bf16[2,96,384]{2,1,0:T(8,128)(2,1)S(1)}, bf16[2,96,384]{2,1,0:T(8,128)(2,1)}, u32[]{:S(2)}, u32[]{:S(2)}) collective-permute-start(bf16[2,96,384]{2,1,0:T(8,128)(2,1)S(1)} %collective-permute-done.16.refs_2_), channel_id=1, source_target_pairs={{0,384},{4,132},{64,448},{68,196},{128,0},{132,260},{192,64},{196,... | collective-permute-start | bytes 442376 | tf_op jit(solution)/shard_map/ppermute | solution.py:18
  106.2 4.6 %collective-permute-start.20 = (bf16[2,96,384]{2,1,0:T(8,128)(2,1)S(1)}, bf16[2,96,384]{2,1,0:T(8,128)(2,1)}, u32[]{:S(2)}, u32[]{:S(2)}) collective-permute-start(bf16[2,96,384]{2,1,0:T(8,128)(2,1)S(1)} %collective-permute-done.19.refs_6_), channel_id=1, source_target_pairs={{0,64},{4,452},{64,128},{68,4},{128,192},{132,68},{192,256},{196,1... | collective-permute-start | bytes 442376 | tf_op jit(solution)/shard_map/ppermute | solution.py:18
  110.8 1.6 %collective-permute-done.18.refs_4_ = bf16[2,96,384]{2,1,0:T(8,128)(2,1)} collective-permute-done((bf16[2,96,384]{2,1,0:T(8,128)(2,1)S(1)}, bf16[2,96,384]{2,1,0:T(8,128)(2,1)}, u32[]{:S(2)}, u32[]{:S(2)}) %collective-permute-start.18) | collective-permute-done | bytes 147488 | tf_op jit(solution)/shard_map/ppermute | solution.py:18
  112.4 2.1 %collective-permute-done.20.refs_5_ = bf16[2,96,384]{2,1,0:T(8,128)(2,1)} collective-permute-done((bf16[2,96,384]{2,1,0:T(8,128)(2,1)S(1)}, bf16[2,96,384]{2,1,0:T(8,128)(2,1)}, u32[]{:S(2)}, u32[]{:S(2)}) %collective-permute-start.20) | collective-permute-done | bytes 147488 | tf_op jit(solution)/shard_map/ppermute | solution.py:18
  114.6 2.9 %shard_map.39 = bf16[16,32,128]{2,1,0:T(8,128)(2,1)S(1)} custom-call(s32[16]{0:T(128)S(1)} %bitcast.21, s32[3]{0:T(128)S(1)} %pad_add_fusion.place_ref, f32[1]{0:T(128)} %bitcast.4.scale_ref, bf16[768,768]{1,0:T(8,128)(2,1)S(1)} %constant_dynamic-update-slice_fusion.own_ref, bf16[768,768]{1,0:T(8,128)(2,1)S(1)} %collective-permute-done.14.other_ref, ...), custom_call_target="tpu_custom_call" | custom-call | tf_op jit(solution)/shard_map/pallas_call | solution.py:171
  117.5 0.1 broadcast_in_dim.2
  117.6 23.7 %all_to_all.10 = bf16[64,32,128]{2,1,0:T(8,128)(2,1)S(1)} all-to-all(bf16[64,32,128]{2,1,0:T(8,128)(2,1)S(1)} %bitcast.22), channel_id=1, replica_groups=mesh['row'=8,'z'=8,'core'=2,'layer'=4] {'z','core','layer'}, dimensions={0} | all-to-all | bytes 1048576 | tf_op jit(solution)/shard_map/all_to_all | solution.py:185
  141.3 0.1 bitcast_reduce_fusion
  141.4 0.7 copy.14
  (22 shorter events, 0.1 us)
Async XLA Ops:
  1.3 24.9 %collective-permute-start.2 = (bf16[96,768]{1,0:T(8,128)(2,1)S(1)}, bf16[96,768]{1,0:T(8,128)(2,1)S(1)}, u32[]{:S(2)}, u32[]{:S(2)}) collective-permute-start(bf16[96,768]{1,0:T(8,128)(2,1)S(1)} %bitcast.23), channel_id=1, source_target_pairs={{0,48},{4,20},{8,56},{12,28},{16,0},{20,36},{24,8},{28,44},{32,16}... | collective-permute-start | bytes 442376 | tf_op jit(solution)/shard_map/ppermute | solution.py:18
  8.8 20.5 %collective-permute-start.3 = (bf16[2,96,384]{2,1,0:T(8,128)(2,1)S(1)}, bf16[2,96,384]{2,1,0:T(8,128)(2,1)S(1)}, u32[]{:S(2)}, u32[]{:S(2)}) collective-permute-start(bf16[2,96,384]{2,1,0:T(8,128)(2,1)S(1)} %dynamic-slice_bitcast_fusion.refs_0_), channel_id=1, source_target_pairs={{0,384},{4,132},{64,448},{68,196},{128,0},{132,260},{192,64},{196,... | collective-permute-start | bytes 442376 | tf_op jit(solution)/shard_map/ppermute | solution.py:18
  13.1 19.4 %collective-permute-start = (bf16[96,768]{1,0:T(8,128)(2,1)S(1)}, bf16[96,768]{1,0:T(8,128)(2,1)S(1)}, u32[]{:S(2)}, u32[]{:S(2)}) collective-permute-start(bf16[96,768]{1,0:T(8,128)(2,1)S(1)} %bitcast.24), channel_id=1, source_target_pairs={{0,56},{4,12},{8,0},{12,20},{16,8},{20,28},{24,16},{28,36},{32,24}... | collective-permute-start | bytes 442376 | tf_op jit(solution)/shard_map/ppermute | solution.py:18
  17.1 18.0 %collective-permute-start.1 = (bf16[2,96,384]{2,1,0:T(8,128)(2,1)S(1)}, bf16[2,96,384]{2,1,0:T(8,128)(2,1)S(1)}, u32[]{:S(2)}, u32[]{:S(2)}) collective-permute-start(bf16[2,96,384]{2,1,0:T(8,128)(2,1)S(1)} %dynamic-slice_bitcast_fusion.refs_0_), channel_id=1, source_target_pairs={{0,448},{4,68},{64,0},{68,132},{128,64},{132,196},{192,128},{196,2... | collective-permute-start | bytes 442376 | tf_op jit(solution)/shard_map/ppermute | solution.py:18
  20.3 17.0 %collective-permute-start.8 = (bf16[96,768]{1,0:T(8,128)(2,1)S(1)}, bf16[96,768]{1,0:T(8,128)(2,1)S(1)}, u32[]{:S(2)}, u32[]{:S(2)}) collective-permute-start(bf16[96,768]{1,0:T(8,128)(2,1)S(1)} %bitcast.25), channel_id=1, source_target_pairs={{0,16},{4,52},{8,24},{12,60},{16,32},{20,4},{24,40},{28,12},{32,48... | collective-permute-start | bytes 442376 | tf_op jit(solution)/shard_map/ppermute | solution.py:18
  26.2 13.3 %collective-permute-start.9 = (bf16[2,96,384]{2,1,0:T(8,128)(2,1)S(1)}, bf16[2,96,384]{2,1,0:T(8,128)(2,1)S(1)}, u32[]{:S(2)}, u32[]{:S(2)}) collective-permute-start(bf16[2,96,384]{2,1,0:T(8,128)(2,1)S(1)} %dynamic-slice_bitcast_fusion.refs_0_), channel_id=1, source_target_pairs={{0,128},{4,388},{64,192},{68,452},{128,256},{132,4},{192,320},{196... | collective-permute-start | bytes 442376 | tf_op jit(solution)/shard_map/ppermute | solution.py:18
  29.4 12.8 %collective-permute-start.12 = (bf16[96,768]{1,0:T(8,128)(2,1)S(1)}, bf16[96,768]{1,0:T(8,128)(2,1)S(1)}, u32[]{:S(2)}, u32[]{:S(2)}) collective-permute-start(bf16[96,768]{1,0:T(8,128)(2,1)S(1)} %bitcast.26), channel_id=1, source_target_pairs={{0,8},{4,60},{8,16},{12,4},{16,24},{20,12},{24,32},{28,20},{32,40}... | collective-permute-start | bytes 442376 | tf_op jit(solution)/shard_map/ppermute | solution.py:18
  32.5 13.8 %collective-permute-start.13 = (bf16[2,96,384]{2,1,0:T(8,128)(2,1)S(1)}, bf16[2,96,384]{2,1,0:T(8,128)(2,1)S(1)}, u32[]{:S(2)}, u32[]{:S(2)}) collective-permute-start(bf16[2,96,384]{2,1,0:T(8,128)(2,1)S(1)} %dynamic-slice_bitcast_fusion.refs_0_), channel_id=1, source_target_pairs={{0,64},{4,452},{64,128},{68,4},{128,192},{132,68},{192,256},{196,1... | collective-permute-start | bytes 442376 | tf_op jit(solution)/shard_map/ppermute | solution.py:18
  35.1 15.3 %collective-permute-start.4 = (bf16[96,768]{1,0:T(8,128)(2,1)S(1)}, bf16[96,768]{1,0:T(8,128)(2,1)S(1)}, u32[]{:S(2)}, u32[]{:S(2)}) collective-permute-start(bf16[96,768]{1,0:T(8,128)(2,1)S(1)} %collective-permute-done.2), channel_id=1, source_target_pairs={{0,56},{4,12},{8,0},{12,20},{16,8},{20,28},{24,16},{28,36},{32,24}... | collective-permute-start | bytes 442376 | tf_op jit(solution)/shard_map/ppermute | solution.py:18
  37.3 16.5 %collective-permute-start.6 = (bf16[96,768]{1,0:T(8,128)(2,1)S(1)}, bf16[96,768]{1,0:T(8,128)(2,1)S(1)}, u32[]{:S(2)}, u32[]{:S(2)}) collective-permute-start(bf16[96,768]{1,0:T(8,128)(2,1)S(1)} %collective-permute-done.2), channel_id=1, source_target_pairs={{0,48},{4,20},{8,56},{12,28},{16,0},{20,36},{24,8},{28,44},{32,16}... | collective-permute-start | bytes 442376 | tf_op jit(solution)/shard_map/ppermute | solution.py:18
  39.5 14.3 %collective-permute-start.5 = (bf16[2,96,384]{2,1,0:T(8,128)(2,1)S(1)}, bf16[2,96,384]{2,1,0:T(8,128)(2,1)S(1)}, u32[]{:S(2)}, u32[]{:S(2)}) collective-permute-start(bf16[2,96,384]{2,1,0:T(8,128)(2,1)S(1)} %collective-permute-done.3.refs_2_), channel_id=1, source_target_pairs={{0,448},{4,68},{64,0},{68,132},{128,64},{132,196},{192,128},{196,2... | collective-permute-start | bytes 442376 | tf_op jit(solution)/shard_map/ppermute | solution.py:18
  42.2 11.7 %collective-permute-start.7 = (bf16[2,96,384]{2,1,0:T(8,128)(2,1)S(1)}, bf16[2,96,384]{2,1,0:T(8,128)(2,1)S(1)}, u32[]{:S(2)}, u32[]{:S(2)}) collective-permute-start(bf16[2,96,384]{2,1,0:T(8,128)(2,1)S(1)} %collective-permute-done.3.refs_2_), channel_id=1, source_target_pairs={{0,384},{4,132},{64,448},{68,196},{128,0},{132,260},{192,64},{196,... | collective-permute-start | bytes 442376 | tf_op jit(solution)/shard_map/ppermute | solution.py:18
  46.3 7.6 %collective-permute-start.10 = (bf16[96,768]{1,0:T(8,128)(2,1)S(1)}, bf16[96,768]{1,0:T(8,128)(2,1)S(1)}, u32[]{:S(2)}, u32[]{:S(2)}) collective-permute-start(bf16[96,768]{1,0:T(8,128)(2,1)S(1)} %collective-permute-done.8), channel_id=1, source_target_pairs={{0,8},{4,60},{8,16},{12,4},{16,24},{20,12},{24,32},{28,20},{32,40}... | collective-permute-start | bytes 442376 | tf_op jit(solution)/shard_map/ppermute | solution.py:18
  50.4 10.5 %collective-permute-start.11 = (bf16[2,96,384]{2,1,0:T(8,128)(2,1)S(1)}, bf16[2,96,384]{2,1,0:T(8,128)(2,1)S(1)}, u32[]{:S(2)}, u32[]{:S(2)}) collective-permute-start(bf16[2,96,384]{2,1,0:T(8,128)(2,1)S(1)} %collective-permute-done.9.refs_6_), channel_id=1, source_target_pairs={{0,64},{4,452},{64,128},{68,4},{128,192},{132,68},{192,256},{196,1... | collective-permute-start | bytes 442376 | tf_op jit(solution)/shard_map/ppermute | solution.py:18
  60.9 9.5 %collective-permute-start.14 = (bf16[768,768]{1,0:T(8,128)(2,1)S(1)}, bf16[768,768]{1,0:T(8,128)(2,1)S(1)}, u32[]{:S(2)}, u32[]{:S(2)}) collective-permute-start(bf16[768,768]{1,0:T(8,128)(2,1)S(1)} %constant_dynamic-update-slice_fusion.own_ref), channel_id=1, source_target_pairs={{0,4},{4,0},{1,5},{5,1},{2,6},{6,2},{3,7},{7,3},{8,12},{12,8},{9,1... | collective-permute-start | bytes 3538952 | tf_op jit(solution)/shard_map/ppermute | solution.py:143
  73.2 41.4 %copy-start = (bf16[768,384]{1,0:T(8,128)(2,1)S(1)}, bf16[768,384]{1,0:T(8,128)(2,1)}, u32[]{:S(2)}) copy-start(bf16[768,384]{1,0:T(8,128)(2,1)} %matrix_ref.1) | copy-start | bytes 1769476
  73.2 41.4 %copy-start.1 = (s32[1,16]{1,0:T(1,128)S(1)}, s32[1,16]{1,0:T(1,128)}, u32[]{:S(2)}) copy-start(s32[1,16]{1,0:T(1,128)} %param.5) | copy-start | bytes 196
  73.2 13.8 %all-to-all-start = ((bf16[4,2,96,384]{3,2,1,0:T(8,128)(2,1)}), bf16[4,2,96,384]{3,2,1,0:T(8,128)(2,1)S(1)}, u32[]{:S(2)}, u32[]{:S(2)}) async-start(bf16[4,2,96,384]{3,2,1,0:T(8,128)(2,1)} %shard_map.37), calls=%async_computation | async-start | bytes 1179648 | tf_op jit(solution)/shard_map/all_to_all | solution.py:158
  88.4 13.9 %collective-permute-start.16 = (bf16[2,96,384]{2,1,0:T(8,128)(2,1)}, bf16[2,96,384]{2,1,0:T(8,128)(2,1)S(1)}, u32[]{:S(2)}, u32[]{:S(2)}) collective-permute-start(bf16[2,96,384]{2,1,0:T(8,128)(2,1)} %shard_map.38.refs_0_), channel_id=1, source_target_pairs={{0,384},{4,132},{64,448},{68,196},{128,0},{132,260},{192,64},{196,... | collective-permute-start | bytes 442376 | tf_op jit(solution)/shard_map/ppermute | solution.py:18
  90.3 15.9 %collective-permute-start.19 = (bf16[2,96,384]{2,1,0:T(8,128)(2,1)}, bf16[2,96,384]{2,1,0:T(8,128)(2,1)S(1)}, u32[]{:S(2)}, u32[]{:S(2)}) collective-permute-start(bf16[2,96,384]{2,1,0:T(8,128)(2,1)} %shard_map.38.refs_0_), channel_id=1, source_target_pairs={{0,128},{4,388},{64,192},{68,452},{128,256},{132,4},{192,320},{196... | collective-permute-start | bytes 442376 | tf_op jit(solution)/shard_map/ppermute | solution.py:18
  95.8 15.0 %collective-permute-start.15 = (bf16[2,96,384]{2,1,0:T(8,128)(2,1)}, bf16[2,96,384]{2,1,0:T(8,128)(2,1)S(1)}, u32[]{:S(2)}, u32[]{:S(2)}) collective-permute-start(bf16[2,96,384]{2,1,0:T(8,128)(2,1)} %shard_map.38.refs_0_), channel_id=1, source_target_pairs={{0,448},{4,68},{64,0},{68,132},{128,64},{132,196},{192,128},{196,2... | collective-permute-start | bytes 442376 | tf_op jit(solution)/shard_map/ppermute | solution.py:18
  97.7 13.1 %collective-permute-start.21 = (bf16[2,96,384]{2,1,0:T(8,128)(2,1)}, bf16[2,96,384]{2,1,0:T(8,128)(2,1)S(1)}, u32[]{:S(2)}, u32[]{:S(2)}) collective-permute-start(bf16[2,96,384]{2,1,0:T(8,128)(2,1)} %shard_map.38.refs_0_), channel_id=1, source_target_pairs={{0,64},{4,452},{64,128},{68,4},{128,192},{132,68},{192,256},{196,1... | collective-permute-start | bytes 442376 | tf_op jit(solution)/shard_map/ppermute | solution.py:18
  102.3 8.5 %collective-permute-start.17 = (bf16[2,96,384]{2,1,0:T(8,128)(2,1)S(1)}, bf16[2,96,384]{2,1,0:T(8,128)(2,1)}, u32[]{:S(2)}, u32[]{:S(2)}) collective-permute-start(bf16[2,96,384]{2,1,0:T(8,128)(2,1)S(1)} %collective-permute-done.16.refs_2_), channel_id=1, source_target_pairs={{0,448},{4,68},{64,0},{68,132},{128,64},{132,196},{192,128},{196,2... | collective-permute-start | bytes 442376 | tf_op jit(solution)/shard_map/ppermute | solution.py:18
  104.2 8.2 %collective-permute-start.18 = (bf16[2,96,384]{2,1,0:T(8,128)(2,1)S(1)}, bf16[2,96,384]{2,1,0:T(8,128)(2,1)}, u32[]{:S(2)}, u32[]{:S(2)}) collective-permute-start(bf16[2,96,384]{2,1,0:T(8,128)(2,1)S(1)} %collective-permute-done.16.refs_2_), channel_id=1, source_target_pairs={{0,384},{4,132},{64,448},{68,196},{128,0},{132,260},{192,64},{196,... | collective-permute-start | bytes 442376 | tf_op jit(solution)/shard_map/ppermute | solution.py:18
  106.2 8.4 %collective-permute-start.20 = (bf16[2,96,384]{2,1,0:T(8,128)(2,1)S(1)}, bf16[2,96,384]{2,1,0:T(8,128)(2,1)}, u32[]{:S(2)}, u32[]{:S(2)}) collective-permute-start(bf16[2,96,384]{2,1,0:T(8,128)(2,1)S(1)} %collective-permute-done.19.refs_6_), channel_id=1, source_target_pairs={{0,64},{4,452},{64,128},{68,4},{128,192},{132,68},{192,256},{196,1... | collective-permute-start | bytes 442376 | tf_op jit(solution)/shard_map/ppermute | solution.py:18

commit v6 on v4

--- a/solution.py
+++ b/solution.py
@@ -6,6 +6,7 @@
 from jax.sharding import Mesh, PartitionSpec as P
 
 BLK = 64
+LAST = 5
 CONTRACT = (((0,), (0,)), ((), ()))
 
 
@@ -34,31 +35,35 @@
     return piece, near_up, up, far_up, opposite, far_down, down, near_down
 
 
-def product(own_ref, other_ref, right_ref, start, count):
-    depth = own_ref.shape[0]
-    columns = right_ref.shape[-1]
+def product(left_refs, right_ref, start, count):
+    tiles, part, columns = right_ref.shape[1:]
     rows = pl.ds(start, count)
-    own = lax.dot_general(
-        own_ref[:, rows], right_ref[0].reshape(depth, columns), CONTRACT, preferred_element_type=jnp.float32
-    )
-    other = lax.dot_general(
-        other_ref[:, rows], right_ref[1].reshape(depth, columns), CONTRACT, preferred_element_type=jnp.float32
-    )
-    return own + other
-
-
-def square_kernel(place_ref, own_ref, other_ref, right_ref, out_ref, ordered_ref, staged_ref, sems):
+    total = None
+    for side in range(2):
+        for left_ref, tile, many in zip(left_refs[2 * side : 2 * side + 2], (0, tiles - 1), (tiles - 1, 1)):
+            right = right_ref[side, pl.ds(tile, many)].reshape(many * part, columns)
+            term = lax.dot_general(left_ref[:, rows], right, CONTRACT, preferred_element_type=jnp.float32)
+            total = term if total is None else total + term
+    return total
+
+
+def place_of(offset, tiles):
+    return jnp.where(offset == LAST, tiles - 1, offset - jnp.where(offset > LAST, 1, 0))
+
+
+def square_kernel(place_ref, own_ref, last_ref, other_ref, other_last_ref, right_ref, out_ref, ordered_ref, staged_ref, sems):
     halves, layers, part, columns = staged_ref.shape
     tiles = right_ref.shape[0]
     z, core = place_ref[1], place_ref[2]
     way = 1 - 2 * core
-    for offset in range(tiles):
-        ordered_ref[0, offset] = right_ref[lax.rem(z + way * offset + tiles, tiles), core]
-        ordered_ref[1, offset] = right_ref[lax.rem(z - way * offset + tiles, tiles), 1 - core]
+    left_refs = (own_ref, last_ref, other_ref, other_last_ref)
+    for tile, offset in enumerate([at for at in range(tiles) if at != LAST] + [LAST]):
+        ordered_ref[0, tile] = right_ref[lax.rem(z + way * offset + tiles, tiles), core]
+        ordered_ref[1, tile] = right_ref[lax.rem(z - way * offset + tiles, tiles), 1 - core]
     copies = []
     for half in range(halves):
         count = layers * part
-        total = product(own_ref, other_ref, ordered_ref, half * count, count)
+        total = product(left_refs, ordered_ref, half * count, count)
         staged_ref[half] = total.astype(staged_ref.dtype).reshape(layers, part, columns)
         copies.append(pltpu.make_async_copy(staged_ref.at[half], out_ref.at[:, half], sems.at[half]))
         copies[-1].start()
@@ -84,7 +89,7 @@
                 out_ref[half, rows, lanes] = (total * jnp.where(low, left, right)).astype(out_ref.dtype)
 
 
-def cube_kernel(chosen_ref, place_ref, scale_ref, own_ref, other_ref, matrix_ref, *refs):
+def cube_kernel(chosen_ref, place_ref, scale_ref, own_ref, last_ref, other_ref, other_last_ref, matrix_ref, *refs):
     pieces = refs[:8]
     out_ref, ordered_ref, total_ref, block_ref = refs[8:]
     owners, pairs, lanes = out_ref.shape
@@ -95,10 +100,11 @@
     for offset, piece in enumerate(pieces):
         distance = row + way * offset - z
         own = lax.rem(way * distance + 2 * tiles, tiles)
-        ordered_ref[0, own] = piece[core]
-        ordered_ref[1, lax.rem(tiles - own, tiles)] = piece[1 - core]
+        other = lax.rem(tiles - own, tiles)
+        ordered_ref[0, place_of(own, tiles)] = piece[core]
+        ordered_ref[1, place_of(other, tiles)] = piece[1 - core]
     total_ref[...] = scale_ref[0] * matrix_ref[...].astype(jnp.float32) - 0.5 * product(
-        own_ref, other_ref, ordered_ref, 0, matrix_ref.shape[0]
+        (own_ref, last_ref, other_ref, other_last_ref), ordered_ref, 0, matrix_ref.shape[0]
     )
     low = lax.broadcasted_iota(jnp.int32, (pairs, lanes), 1) < BLK
 
@@ -139,15 +145,19 @@
         matrix.reshape(halves, layers, part, width), layer_index, 1, 1
     ).reshape(halves, part, width)
     right = to_all(right_piece, "row")
-    left_own = jnp.concatenate(ring_of_eight(left_piece, "z"), axis=0)
-    left_own, right = lax.optimization_barrier((left_own, right))
-    left_other = lax.ppermute(left_own, "core", [(0, 1), (1, 0)])
+    swap = [(0, 1), (1, 0)]
+    pieces = ring_of_eight(left_piece, "z")
+    pieces, last = pieces[:LAST] + pieces[LAST + 1 :], pieces[LAST]
+    own = jnp.concatenate(pieces, axis=0)
+    other = lax.ppermute(own, "core", swap)
+    last, right = lax.optimization_barrier((last, right))
+    left = (own, last, other, lax.ppermute(last, "core", swap))
     place = jnp.stack([row_index, z_index, core_index])
 
     square_part = pl.pallas_call(
         square_kernel,
         out_shape=jax.ShapeDtypeStruct((layers, halves, part, width), jnp.bfloat16),
-        in_specs=[smem, vmem, vmem, vmem],
+        in_specs=[smem] + [vmem] * 5,
         out_specs=pl.BlockSpec(memory_space=pltpu.HBM),
         scratch_shapes=[
             pltpu.VMEM((halves, rows_count, part, width), jnp.bfloat16),
@@ -155,7 +165,7 @@
             pltpu.SemaphoreType.DMA((halves,)),
         ],
         compiler_params=params,
-    )(place, left_own, left_other, right)
+    )(place, *left, right)
     parts = lax.all_to_all(square_part, "layer", split_axis=0, concat_axis=0, tiled=True)
     filtered_piece = pl.pallas_call(
         filter_kernel,
@@ -172,7 +182,7 @@
     outgoing = pl.pallas_call(
         cube_kernel,
         out_shape=jax.ShapeDtypeStruct((chosen.shape[0], pairs, 128), jnp.bfloat16),
-        in_specs=[smem] * 3 + [vmem] * 11,
+        in_specs=[smem] * 3 + [vmem] * 13,
         out_specs=vmem,
         scratch_shapes=[
             pltpu.VMEM((halves, rows_count, part, width), jnp.bfloat16),
@@ -180,10 +190,12 @@
             pltpu.VMEM((4, BLK, 128), jnp.float32),
         ],
         compiler_params=params,
-    )(chosen, place, scale, left_own, left_other, matrix, *filtered)
-    arrived = lax.all_to_all(outgoing, ("z", "core"), split_axis=0, concat_axis=0, tiled=True)
-    everyone = to_all(arrived, "layer")
-    total = everyone.astype(jnp.float32).sum(0).astype(jnp.bfloat16)
+    )(chosen, place, scale, *left, matrix, *filtered)
+    copies = jnp.broadcast_to(outgoing[:, None], outgoing.shape[:1] + (layers,) + outgoing.shape[1:])
+    copies = copies.reshape((-1,) + outgoing.shape[1:])
+    everyone = lax.all_to_all(copies, ("z", "core", "layer"), split_axis=0, concat_axis=0, tiled=True)
+    everyone = everyone.reshape(outgoing.shape[:1] + (layers,) + outgoing.shape[1:])
+    total = everyone.astype(jnp.float32).sum(1).astype(jnp.bfloat16)
     return total.reshape(total.shape[0], BLK * BLK)
 
 

time: 133 us -> 139 us (1.045)
  the two profiles are of different devices: /device:TPU:1 before, /device:TPU:24 now
where the time goes in v6:
time: 139 us; the launch traced here: 138 us
  starting transfers between devices  69.2 us (50%)
  waiting for transfers between devices  29.2 us (21%)
  blocking collectives  26 us (19%)
  Pallas kernels  7.35 us (5%)
  local copies, waits for them, and re-layouts  5.82 us (4%)
    ppermute x14, starting transfers between devices, shifted(): return lax.ppermute(piece, (axis, 'core'), pairs)  51.9 us
    all_to_all x1, blocking collectives, on_device(): lax.all_to_all(copies, ('z', 'core', 'layer'), split_axis=0, concat_axis=...  26 us
    ppermute x14, waiting for transfers between devices, shifted(): return lax.ppermute(piece, (axis, 'core'), pairs)  18.2 us
    all_to_all x1, waiting for transfers between devices, on_device(): lax.all_to_all(square_part, 'layer', split_axis=0, concat_axis=0, tiled=T...  9.72 us
    all_to_all x1, starting transfers between devices, to_all(): return lax.all_to_all(copies, axis, split_axis=0, concat_axis=0, tiled=True)  9.07 us
    all_to_all x1, starting transfers between devices, on_device(): lax.all_to_all(square_part, 'layer', split_axis=0, concat_axis=0, tiled=T...  4.43 us
    pallas_call x1, Pallas kernels, on_device(): pl.pallas_call(cube_kernel, out_shape=jax.ShapeDtypeStruct((chosen.shape[...  3.25 us
  transfers between devices with their start and end apart: 18, of which 8 were waited for; matrix products, arithmetic and copies ran while one was open for 2% of the time, Pallas kernels for 0%

profile of v6, /device:TPU:24, one launch (start us, length us, event | category | flops | bytes accessed | tf_op | source)
XLA Modules:
  0.0 138.1 jit_solution(15701452405162290604)
XLA Ops:
  0.0 0.9 dynamic-slice_bitcast_fusion
  0.9 1.2 broadcast_in_dim.14
  2.1 9.1 %all-to-all-start = ((bf16[8,2,96,384]{3,2,1,0:T(8,128)(2,1)}), bf16[8,2,96,384]{3,2,1,0:T(8,128)(2,1)S(1)}, u32[]{:S(2)}, u32[]{:S(2)}) async-start(bf16[8,2,96,384]{3,2,1,0:T(8,128)(2,1)} %broadcast_in_dim.14), calls=%async_computation | async-start | bytes 2359296 | tf_op jit(solution)/shard_map/all_to_all | solution.py:15
  11.2 1.1 constant_dynamic-slice_fusion
  12.3 0.1 copy.8
  12.4 2.5 %collective-permute-start.5 = (bf16[96,768]{1,0:T(8,128)(2,1)S(1)}, bf16[96,768]{1,0:T(8,128)(2,1)S(1)}, u32[]{:S(2)}, u32[]{:S(2)}) collective-permute-start(bf16[96,768]{1,0:T(8,128)(2,1)S(1)} %bitcast.21), channel_id=1, source_target_pairs={{0,8},{4,60},{8,16},{12,4},{16,24},{20,12},{24,32},{28,20},{32,40}... | collective-permute-start | bytes 442376 | tf_op jit(solution)/shard_map/ppermute | solution.py:24
  15.0 6.1 %collective-permute-start.4 = (bf16[96,768]{1,0:T(8,128)(2,1)S(1)}, bf16[96,768]{1,0:T(8,128)(2,1)S(1)}, u32[]{:S(2)}, u32[]{:S(2)}) collective-permute-start(bf16[96,768]{1,0:T(8,128)(2,1)S(1)} %bitcast.22), channel_id=1, source_target_pairs={{0,16},{4,52},{8,24},{12,60},{16,32},{20,4},{24,40},{28,12},{32,48... | collective-permute-start | bytes 442376 | tf_op jit(solution)/shard_map/ppermute | solution.py:24
  21.1 5.9 %collective-permute-start.1 = (bf16[96,768]{1,0:T(8,128)(2,1)S(1)}, bf16[96,768]{1,0:T(8,128)(2,1)S(1)}, u32[]{:S(2)}, u32[]{:S(2)}) collective-permute-start(bf16[96,768]{1,0:T(8,128)(2,1)S(1)} %bitcast.23), channel_id=1, source_target_pairs={{0,48},{4,20},{8,56},{12,28},{16,0},{20,36},{24,8},{28,44},{32,16}... | collective-permute-start | bytes 442376 | tf_op jit(solution)/shard_map/ppermute | solution.py:24
  26.9 3.4 %collective-permute-start = (bf16[96,768]{1,0:T(8,128)(2,1)S(1)}, bf16[96,768]{1,0:T(8,128)(2,1)S(1)}, u32[]{:S(2)}, u32[]{:S(2)}) collective-permute-start(bf16[96,768]{1,0:T(8,128)(2,1)S(1)} %bitcast.24), channel_id=1, source_target_pairs={{0,56},{4,12},{8,0},{12,20},{16,8},{20,28},{24,16},{28,36},{32,24}... | collective-permute-start | bytes 442376 | tf_op jit(solution)/shard_map/ppermute | solution.py:24
  30.3 1.9 %collective-permute-done.1 = bf16[96,768]{1,0:T(8,128)(2,1)S(1)} collective-permute-done((bf16[96,768]{1,0:T(8,128)(2,1)S(1)}, bf16[96,768]{1,0:T(8,128)(2,1)S(1)}, u32[]{:S(2)}, u32[]{:S(2)}) %collective-permute-start.1) | collective-permute-done | bytes 147488 | tf_op jit(solution)/shard_map/ppermute | solution.py:24
  32.2 4.1 %collective-permute-start.3 = (bf16[96,768]{1,0:T(8,128)(2,1)S(1)}, bf16[96,768]{1,0:T(8,128)(2,1)S(1)}, u32[]{:S(2)}, u32[]{:S(2)}) collective-permute-start(bf16[96,768]{1,0:T(8,128)(2,1)S(1)} %collective-permute-done.1), channel_id=1, source_target_pairs={{0,48},{4,20},{8,56},{12,28},{16,0},{20,36},{24,8},{28,44},{32,16}... | collective-permute-start | bytes 442376 | tf_op jit(solution)/shard_map/ppermute | solution.py:24
  36.3 3.6 %collective-permute-start.2 = (bf16[96,768]{1,0:T(8,128)(2,1)S(1)}, bf16[96,768]{1,0:T(8,128)(2,1)S(1)}, u32[]{:S(2)}, u32[]{:S(2)}) collective-permute-start(bf16[96,768]{1,0:T(8,128)(2,1)S(1)} %collective-permute-done.1), channel_id=1, source_target_pairs={{0,56},{4,12},{8,0},{12,20},{16,8},{20,28},{24,16},{28,36},{32,24}... | collective-permute-start | bytes 442376 | tf_op jit(solution)/shard_map/ppermute | solution.py:24
  39.9 0.0 collective-permute-done
  39.9 3.7 %collective-permute-done.2 = bf16[96,768]{1,0:T(8,128)(2,1)S(1)} collective-permute-done((bf16[96,768]{1,0:T(8,128)(2,1)S(1)}, bf16[96,768]{1,0:T(8,128)(2,1)S(1)}, u32[]{:S(2)}, u32[]{:S(2)}) %collective-permute-start.2) | collective-permute-done | bytes 147488 | tf_op jit(solution)/shard_map/ppermute | solution.py:24
  43.7 0.0 collective-permute-done.3
  43.7 0.0 collective-permute-done.5
  43.8 1.9 %collective-permute-start.7 = (bf16[672,768]{1,0:T(8,128)(2,1)S(1)}, bf16[672,768]{1,0:T(8,128)(2,1)S(1)}, u32[]{:S(2)}, u32[]{:S(2)}) collective-permute-start(bf16[672,768]{1,0:T(8,128)(2,1)S(1)} %constant_dynamic-update-slice_fusion.own_ref), channel_id=1, source_target_pairs={{0,4},{4,0},{1,5},{5,1},{2,6},{6,2},{3,7},{7,3},{8,12},{12,8},{9,1... | collective-permute-start | bytes 3096584 | tf_op jit(solution)/shard_map/ppermute | solution.py:152
  45.7 3.0 %collective-permute-start.6 = (bf16[96,768]{1,0:T(8,128)(2,1)S(1)}, bf16[96,768]{1,0:T(8,128)(2,1)S(1)}, u32[]{:S(2)}, u32[]{:S(2)}) collective-permute-start(bf16[96,768]{1,0:T(8,128)(2,1)S(1)} %collective-permute-done.4), channel_id=1, source_target_pairs={{0,8},{4,60},{8,16},{12,4},{16,24},{20,12},{24,32},{28,20},{32,40}... | collective-permute-start | bytes 442376 | tf_op jit(solution)/shard_map/ppermute | solution.py:24
  48.7 5.3 %collective-permute-done.6.last_ref = bf16[96,768]{1,0:T(8,128)(2,1)S(1)} collective-permute-done((bf16[96,768]{1,0:T(8,128)(2,1)S(1)}, bf16[96,768]{1,0:T(8,128)(2,1)S(1)}, u32[]{:S(2)}, u32[]{:S(2)}) %collective-permute-start.6) | collective-permute-done | bytes 147488 | tf_op jit(solution)/shard_map/ppermute | solution.py:24
  54.0 0.0 all-to-all-done.right_ref
  54.0 1.9 %collective-permute-start.8 = (bf16[96,768]{1,0:T(8,128)(2,1)S(1)}, bf16[96,768]{1,0:T(8,128)(2,1)S(1)}, u32[]{:S(2)}, u32[]{:S(2)}) collective-permute-start(bf16[96,768]{1,0:T(8,128)(2,1)S(1)} %collective-permute-done.6.last_ref), channel_id=1, source_target_pairs={{0,4},{4,0},{1,5},{5,1},{2,6},{6,2},{3,7},{7,3},{8,12},{12,8},{9,1... | collective-permute-start | bytes 442376 | tf_op jit(solution)/shard_map/ppermute | solution.py:154
  55.9 0.1 pad_add_fusion.place_ref
  56.0 0.0 collective-permute-done.7.other_ref
  56.0 1.3 collective-permute-done.8.other_last_ref
  57.2 2.7 %shard_map.37 = bf16[4,2,96,384]{3,2,1,0:T(8,128)(2,1)S(1)} custom-call(s32[3]{0:T(128)S(1)} %pad_add_fusion.place_ref, bf16[672,768]{1,0:T(8,128)(2,1)S(1)} %constant_dynamic-update-slice_fusion.own_ref, bf16[96,768]{1,0:T(8,128)(2,1)S(1)} %collective-permute-done.6.last_ref, bf16[672,768]{1,0:T(8,128)(2,1)S(1)} %collective-permute-done.7.other_ref, ...), custom_call_target="tpu_custom_call" | custom-call | tf_op jit(solution)/shard_map/pallas_call | solution.py:157
  59.9 0.8 copy-done
  60.7 4.4 %all-to-all-start.1 = ((bf16[4,2,96,384]{3,2,1,0:T(8,128)(2,1)}), bf16[4,2,96,384]{3,2,1,0:T(8,128)(2,1)S(1)}, u32[]{:S(2)}, u32[]{:S(2)}) async-start(bf16[4,2,96,384]{3,2,1,0:T(8,128)(2,1)} %copy-done), calls=%async_computation.1 | async-start | bytes 1179648 | tf_op jit(solution)/shard_map/all_to_all | solution.py:169
  65.2 0.8 copy.7.keep_ref
  65.9 9.7 %all-to-all-done.1.parts_ref = bf16[4,2,96,384]{3,2,1,0:T(8,128)(2,1)S(1)} async-done(((bf16[4,2,96,384]{3,2,1,0:T(8,128)(2,1)}), bf16[4,2,96,384]{3,2,1,0:T(8,128)(2,1)S(1)}, u32[]{:S(2)}, u32[]{:S(2)}) %all-to-all-start.1) | async-done | bytes 589856 | tf_op jit(solution)/shard_map/all_to_all | solution.py:169
  75.7 1.4 %shard_map.38.refs_0_ = bf16[2,96,384]{2,1,0:T(8,128)(2,1)} custom-call(s32[12,6]{1,0:T(8,128)S(1)} %copy.7.keep_ref, s32[1]{0:T(128)} %bitcast.8.layer_ref, bf16[4,2,96,384]{3,2,1,0:T(8,128)(2,1)S(1)} %all-to-all-done.1.parts_ref), custom_call_target="tpu_custom_call" | custom-call | tf_op jit(solution)/shard_map/pallas_call | solution.py:170
  77.1 4.6 %collective-permute-start.13 = (bf16[2,96,384]{2,1,0:T(8,128)(2,1)}, bf16[2,96,384]{2,1,0:T(8,128)(2,1)S(1)}, u32[]{:S(2)}, u32[]{:S(2)}) collective-permute-start(bf16[2,96,384]{2,1,0:T(8,128)(2,1)} %shard_map.38.refs_0_), channel_id=1, source_target_pairs={{0,128},{4,388},{64,192},{68,452},{128,256},{132,4},{192,320},{196... | collective-permute-start | bytes 442376 | tf_op jit(solution)/shard_map/ppermute | solution.py:24
  81.7 2.2 %collective-permute-start.10 = (bf16[2,96,384]{2,1,0:T(8,128)(2,1)}, bf16[2,96,384]{2,1,0:T(8,128)(2,1)S(1)}, u32[]{:S(2)}, u32[]{:S(2)}) collective-permute-start(bf16[2,96,384]{2,1,0:T(8,128)(2,1)} %shard_map.38.refs_0_), channel_id=1, source_target_pairs={{0,384},{4,132},{64,448},{68,196},{128,0},{132,260},{192,64},{196,... | collective-permute-start | bytes 442376 | tf_op jit(solution)/shard_map/ppermute | solution.py:24
  83.8 5.8 %collective-permute-start.15 = (bf16[2,96,384]{2,1,0:T(8,128)(2,1)}, bf16[2,96,384]{2,1,0:T(8,128)(2,1)S(1)}, u32[]{:S(2)}, u32[]{:S(2)}) collective-permute-start(bf16[2,96,384]{2,1,0:T(8,128)(2,1)} %shard_map.38.refs_0_), channel_id=1, source_target_pairs={{0,64},{4,452},{64,128},{68,4},{128,192},{132,68},{192,256},{196,1... | collective-permute-start | bytes 442376 | tf_op jit(solution)/shard_map/ppermute | solution.py:24
  89.6 1.9 %collective-permute-start.9 = (bf16[2,96,384]{2,1,0:T(8,128)(2,1)}, bf16[2,96,384]{2,1,0:T(8,128)(2,1)S(1)}, u32[]{:S(2)}, u32[]{:S(2)}) collective-permute-start(bf16[2,96,384]{2,1,0:T(8,128)(2,1)} %shard_map.38.refs_0_), channel_id=1, source_target_pairs={{0,448},{4,68},{64,0},{68,132},{128,64},{132,196},{192,128},{196,2... | collective-permute-start | bytes 442376 | tf_op jit(solution)/shard_map/ppermute | solution.py:24
  91.5 0.0 collective-permute-done.13.refs_6_
  91.6 5.1 %collective-permute-start.14 = (bf16[2,96,384]{2,1,0:T(8,128)(2,1)S(1)}, bf16[2,96,384]{2,1,0:T(8,128)(2,1)}, u32[]{:S(2)}, u32[]{:S(2)}) collective-permute-start(bf16[2,96,384]{2,1,0:T(8,128)(2,1)S(1)} %collective-permute-done.13.refs_6_), channel_id=1, source_target_pairs={{0,64},{4,452},{64,128},{68,4},{128,192},{132,68},{192,256},{196,1... | collective-permute-start | bytes 442376 | tf_op jit(solution)/shard_map/ppermute | solution.py:24
  96.7 0.0 collective-permute-done.10.refs_2_
  96.7 1.9 %collective-permute-start.12 = (bf16[2,96,384]{2,1,0:T(8,128)(2,1)S(1)}, bf16[2,96,384]{2,1,0:T(8,128)(2,1)}, u32[]{:S(2)}, u32[]{:S(2)}) collective-permute-start(bf16[2,96,384]{2,1,0:T(8,128)(2,1)S(1)} %collective-permute-done.10.refs_2_), channel_id=1, source_target_pairs={{0,384},{4,132},{64,448},{68,196},{128,0},{132,260},{192,64},{196,... | collective-permute-start | bytes 442376 | tf_op jit(solution)/shard_map/ppermute | solution.py:24
  98.7 1.9 %collective-permute-start.11 = (bf16[2,96,384]{2,1,0:T(8,128)(2,1)S(1)}, bf16[2,96,384]{2,1,0:T(8,128)(2,1)}, u32[]{:S(2)}, u32[]{:S(2)}) collective-permute-start(bf16[2,96,384]{2,1,0:T(8,128)(2,1)S(1)} %collective-permute-done.10.refs_2_), channel_id=1, source_target_pairs={{0,448},{4,68},{64,0},{68,132},{128,64},{132,196},{192,128},{196,2... | collective-permute-start | bytes 442376 | tf_op jit(solution)/shard_map/ppermute | solution.py:24
  100.6 0.0 collective-permute-done.15.refs_7_
  100.6 0.9 collective-permute-done.14.refs_5_
  101.5 4.9 %collective-permute-done.12.refs_4_ = bf16[2,96,384]{2,1,0:T(8,128)(2,1)} collective-permute-done((bf16[2,96,384]{2,1,0:T(8,128)(2,1)S(1)}, bf16[2,96,384]{2,1,0:T(8,128)(2,1)}, u32[]{:S(2)}, u32[]{:S(2)}) %collective-permute-start.12) | collective-permute-done | bytes 147488 | tf_op jit(solution)/shard_map/ppermute | solution.py:24
  106.4 1.5 %collective-permute-done.11.refs_3_ = bf16[2,96,384]{2,1,0:T(8,128)(2,1)} collective-permute-done((bf16[2,96,384]{2,1,0:T(8,128)(2,1)S(1)}, bf16[2,96,384]{2,1,0:T(8,128)(2,1)}, u32[]{:S(2)}, u32[]{:S(2)}) %collective-permute-start.11) | collective-permute-done | bytes 147488 | tf_op jit(solution)/shard_map/ppermute | solution.py:24
  107.9 3.3 %shard_map.39 = bf16[16,32,128]{2,1,0:T(8,128)(2,1)S(1)} custom-call(s32[16]{0:T(128)S(1)} %bitcast.19, s32[3]{0:T(128)S(1)} %pad_add_fusion.place_ref, f32[1]{0:T(128)} %bitcast.4.scale_ref, bf16[672,768]{1,0:T(8,128)(2,1)S(1)} %constant_dynamic-update-slice_fusion.own_ref, bf16[96,768]{1,0:T(8,128)(2,1)S(1)} %collective-permute-done.6.last_ref, ...), custom_call_target="tpu_custom_call" | custom-call | tf_op jit(solution)/shard_map/pallas_call | solution.py:182
  111.2 0.1 broadcast_in_dim.15
  111.3 26.0 %all_to_all.15 = bf16[64,32,128]{2,1,0:T(8,128)(2,1)S(1)} all-to-all(bf16[64,32,128]{2,1,0:T(8,128)(2,1)S(1)} %bitcast.20), channel_id=1, replica_groups=mesh['row'=8,'z'=8,'core'=2,'layer'=4] {'z','core','layer'}, dimensions={0} | all-to-all | bytes 1048576 | tf_op jit(solution)/shard_map/all_to_all | solution.py:196
  137.3 0.1 bitcast_reduce_fusion
  137.4 0.7 copy.11
  (14 shorter events, 0.1 us)
Async XLA Ops:
  2.1 51.9 %all-to-all-start = ((bf16[8,2,96,384]{3,2,1,0:T(8,128)(2,1)}), bf16[8,2,96,384]{3,2,1,0:T(8,128)(2,1)S(1)}, u32[]{:S(2)}, u32[]{:S(2)}) async-start(bf16[8,2,96,384]{3,2,1,0:T(8,128)(2,1)} %broadcast_in_dim.14), calls=%async_computation | async-start | bytes 2359296 | tf_op jit(solution)/shard_map/all_to_all | solution.py:15
  12.4 31.3 %collective-permute-start.5 = (bf16[96,768]{1,0:T(8,128)(2,1)S(1)}, bf16[96,768]{1,0:T(8,128)(2,1)S(1)}, u32[]{:S(2)}, u32[]{:S(2)}) collective-permute-start(bf16[96,768]{1,0:T(8,128)(2,1)S(1)} %bitcast.21), channel_id=1, source_target_pairs={{0,8},{4,60},{8,16},{12,4},{16,24},{20,12},{24,32},{28,20},{32,40}... | collective-permute-start | bytes 442376 | tf_op jit(solution)/shard_map/ppermute | solution.py:24
  15.0 28.7 %collective-permute-start.4 = (bf16[96,768]{1,0:T(8,128)(2,1)S(1)}, bf16[96,768]{1,0:T(8,128)(2,1)S(1)}, u32[]{:S(2)}, u32[]{:S(2)}) collective-permute-start(bf16[96,768]{1,0:T(8,128)(2,1)S(1)} %bitcast.22), channel_id=1, source_target_pairs={{0,16},{4,52},{8,24},{12,60},{16,32},{20,4},{24,40},{28,12},{32,48... | collective-permute-start | bytes 442376 | tf_op jit(solution)/shard_map/ppermute | solution.py:24
  21.1 11.1 %collective-permute-start.1 = (bf16[96,768]{1,0:T(8,128)(2,1)S(1)}, bf16[96,768]{1,0:T(8,128)(2,1)S(1)}, u32[]{:S(2)}, u32[]{:S(2)}) collective-permute-start(bf16[96,768]{1,0:T(8,128)(2,1)S(1)} %bitcast.23), channel_id=1, source_target_pairs={{0,48},{4,20},{8,56},{12,28},{16,0},{20,36},{24,8},{28,44},{32,16}... | collective-permute-start | bytes 442376 | tf_op jit(solution)/shard_map/ppermute | solution.py:24
  26.9 12.9 %collective-permute-start = (bf16[96,768]{1,0:T(8,128)(2,1)S(1)}, bf16[96,768]{1,0:T(8,128)(2,1)S(1)}, u32[]{:S(2)}, u32[]{:S(2)}) collective-permute-start(bf16[96,768]{1,0:T(8,128)(2,1)S(1)} %bitcast.24), channel_id=1, source_target_pairs={{0,56},{4,12},{8,0},{12,20},{16,8},{20,28},{24,16},{28,36},{32,24}... | collective-permute-start | bytes 442376 | tf_op jit(solution)/shard_map/ppermute | solution.py:24
  32.2 11.5 %collective-permute-start.3 = (bf16[96,768]{1,0:T(8,128)(2,1)S(1)}, bf16[96,768]{1,0:T(8,128)(2,1)S(1)}, u32[]{:S(2)}, u32[]{:S(2)}) collective-permute-start(bf16[96,768]{1,0:T(8,128)(2,1)S(1)} %collective-permute-done.1), channel_id=1, source_target_pairs={{0,48},{4,20},{8,56},{12,28},{16,0},{20,36},{24,8},{28,44},{32,16}... | collective-permute-start | bytes 442376 | tf_op jit(solution)/shard_map/ppermute | solution.py:24
  36.3 7.4 %collective-permute-start.2 = (bf16[96,768]{1,0:T(8,128)(2,1)S(1)}, bf16[96,768]{1,0:T(8,128)(2,1)S(1)}, u32[]{:S(2)}, u32[]{:S(2)}) collective-permute-start(bf16[96,768]{1,0:T(8,128)(2,1)S(1)} %collective-permute-done.1), channel_id=1, source_target_pairs={{0,56},{4,12},{8,0},{12,20},{16,8},{20,28},{24,16},{28,36},{32,24}... | collective-permute-start | bytes 442376 | tf_op jit(solution)/shard_map/ppermute | solution.py:24
  43.8 12.2 %collective-permute-start.7 = (bf16[672,768]{1,0:T(8,128)(2,1)S(1)}, bf16[672,768]{1,0:T(8,128)(2,1)S(1)}, u32[]{:S(2)}, u32[]{:S(2)}) collective-permute-start(bf16[672,768]{1,0:T(8,128)(2,1)S(1)} %constant_dynamic-update-slice_fusion.own_ref), channel_id=1, source_target_pairs={{0,4},{4,0},{1,5},{5,1},{2,6},{6,2},{3,7},{7,3},{8,12},{12,8},{9,1... | collective-permute-start | bytes 3096584 | tf_op jit(solution)/shard_map/ppermute | solution.py:152
  45.7 8.2 %collective-permute-start.6 = (bf16[96,768]{1,0:T(8,128)(2,1)S(1)}, bf16[96,768]{1,0:T(8,128)(2,1)S(1)}, u32[]{:S(2)}, u32[]{:S(2)}) collective-permute-start(bf16[96,768]{1,0:T(8,128)(2,1)S(1)} %collective-permute-done.4), channel_id=1, source_target_pairs={{0,8},{4,60},{8,16},{12,4},{16,24},{20,12},{24,32},{28,20},{32,40}... | collective-permute-start | bytes 442376 | tf_op jit(solution)/shard_map/ppermute | solution.py:24
  54.0 3.3 %collective-permute-start.8 = (bf16[96,768]{1,0:T(8,128)(2,1)S(1)}, bf16[96,768]{1,0:T(8,128)(2,1)S(1)}, u32[]{:S(2)}, u32[]{:S(2)}) collective-permute-start(bf16[96,768]{1,0:T(8,128)(2,1)S(1)} %collective-permute-done.6.last_ref), channel_id=1, source_target_pairs={{0,4},{4,0},{1,5},{5,1},{2,6},{6,2},{3,7},{7,3},{8,12},{12,8},{9,1... | collective-permute-start | bytes 442376 | tf_op jit(solution)/shard_map/ppermute | solution.py:154
  59.9 0.8 copy-start
  60.7 47.2 %copy-start.1 = (bf16[768,384]{1,0:T(8,128)(2,1)S(1)}, bf16[768,384]{1,0:T(8,128)(2,1)}, u32[]{:S(2)}) copy-start(bf16[768,384]{1,0:T(8,128)(2,1)} %matrix_ref.1) | copy-start | bytes 1769476
  60.7 47.2 %copy-start.2 = (s32[1,16]{1,0:T(1,128)S(1)}, s32[1,16]{1,0:T(1,128)}, u32[]{:S(2)}) copy-start(s32[1,16]{1,0:T(1,128)} %param.5) | copy-start | bytes 196
  60.7 14.9 %all-to-all-start.1 = ((bf16[4,2,96,384]{3,2,1,0:T(8,128)(2,1)}), bf16[4,2,96,384]{3,2,1,0:T(8,128)(2,1)S(1)}, u32[]{:S(2)}, u32[]{:S(2)}) async-start(bf16[4,2,96,384]{3,2,1,0:T(8,128)(2,1)} %copy-done), calls=%async_computation.1 | async-start | bytes 1179648 | tf_op jit(solution)/shard_map/all_to_all | solution.py:169
  77.1 14.5 %collective-permute-start.13 = (bf16[2,96,384]{2,1,0:T(8,128)(2,1)}, bf16[2,96,384]{2,1,0:T(8,128)(2,1)S(1)}, u32[]{:S(2)}, u32[]{:S(2)}) collective-permute-start(bf16[2,96,384]{2,1,0:T(8,128)(2,1)} %shard_map.38.refs_0_), channel_id=1, source_target_pairs={{0,128},{4,388},{64,192},{68,452},{128,256},{132,4},{192,320},{196... | collective-permute-start | bytes 442376 | tf_op jit(solution)/shard_map/ppermute | solution.py:24
  81.7 15.1 %collective-permute-start.10 = (bf16[2,96,384]{2,1,0:T(8,128)(2,1)}, bf16[2,96,384]{2,1,0:T(8,128)(2,1)S(1)}, u32[]{:S(2)}, u32[]{:S(2)}) collective-permute-start(bf16[2,96,384]{2,1,0:T(8,128)(2,1)} %shard_map.38.refs_0_), channel_id=1, source_target_pairs={{0,384},{4,132},{64,448},{68,196},{128,0},{132,260},{192,64},{196,... | collective-permute-start | bytes 442376 | tf_op jit(solution)/shard_map/ppermute | solution.py:24
  83.8 16.8 %collective-permute-start.15 = (bf16[2,96,384]{2,1,0:T(8,128)(2,1)}, bf16[2,96,384]{2,1,0:T(8,128)(2,1)S(1)}, u32[]{:S(2)}, u32[]{:S(2)}) collective-permute-start(bf16[2,96,384]{2,1,0:T(8,128)(2,1)} %shard_map.38.refs_0_), channel_id=1, source_target_pairs={{0,64},{4,452},{64,128},{68,4},{128,192},{132,68},{192,256},{196,1... | collective-permute-start | bytes 442376 | tf_op jit(solution)/shard_map/ppermute | solution.py:24
  89.6 11.0 %collective-permute-start.9 = (bf16[2,96,384]{2,1,0:T(8,128)(2,1)}, bf16[2,96,384]{2,1,0:T(8,128)(2,1)S(1)}, u32[]{:S(2)}, u32[]{:S(2)}) collective-permute-start(bf16[2,96,384]{2,1,0:T(8,128)(2,1)} %shard_map.38.refs_0_), channel_id=1, source_target_pairs={{0,448},{4,68},{64,0},{68,132},{128,64},{132,196},{192,128},{196,2... | collective-permute-start | bytes 442376 | tf_op jit(solution)/shard_map/ppermute | solution.py:24
  91.6 10.0 %collective-permute-start.14 = (bf16[2,96,384]{2,1,0:T(8,128)(2,1)S(1)}, bf16[2,96,384]{2,1,0:T(8,128)(2,1)}, u32[]{:S(2)}, u32[]{:S(2)}) collective-permute-start(bf16[2,96,384]{2,1,0:T(8,128)(2,1)S(1)} %collective-permute-done.13.refs_6_), channel_id=1, source_target_pairs={{0,64},{4,452},{64,128},{68,4},{128,192},{132,68},{192,256},{196,1... | collective-permute-start | bytes 442376 | tf_op jit(solution)/shard_map/ppermute | solution.py:24
  96.7 9.7 %collective-permute-start.12 = (bf16[2,96,384]{2,1,0:T(8,128)(2,1)S(1)}, bf16[2,96,384]{2,1,0:T(8,128)(2,1)}, u32[]{:S(2)}, u32[]{:S(2)}) collective-permute-start(bf16[2,96,384]{2,1,0:T(8,128)(2,1)S(1)} %collective-permute-done.10.refs_2_), channel_id=1, source_target_pairs={{0,384},{4,132},{64,448},{68,196},{128,0},{132,260},{192,64},{196,... | collective-permute-start | bytes 442376 | tf_op jit(solution)/shard_map/ppermute | solution.py:24
  98.7 9.3 %collective-permute-start.11 = (bf16[2,96,384]{2,1,0:T(8,128)(2,1)S(1)}, bf16[2,96,384]{2,1,0:T(8,128)(2,1)}, u32[]{:S(2)}, u32[]{:S(2)}) collective-permute-start(bf16[2,96,384]{2,1,0:T(8,128)(2,1)S(1)} %collective-permute-done.10.refs_2_), channel_id=1, source_target_pairs={{0,448},{4,68},{64,0},{68,132},{128,64},{132,196},{192,128},{196,2... | collective-permute-start | bytes 442376 | tf_op jit(solution)/shard_map/ppermute | solution.py:24

commit v7 on v4

--- a/solution.py
+++ b/solution.py
@@ -18,9 +18,13 @@
     size = lax.axis_size(axis)
     pairs = []
     for i in range(size):
-        pairs.append((2 * i, 2 * ((i - by) % size)))
-        pairs.append((2 * i + 1, 2 * ((i + by) % size) + 1))
-    return lax.ppermute(piece, (axis, "core"), pairs)
+        for core, place in ((0, (i - by) % size), (1, (i + by) % size)):
+            if axis == "layer":
+                pairs.append((core * size + i, core * size + place))
+            else:
+                pairs.append((2 * i + core, 2 * place + core))
+    axes = ("core", axis) if axis == "layer" else (axis, "core")
+    return lax.ppermute(piece, axes, pairs)
 
 
 def ring_of_eight(piece, axis):
@@ -47,38 +51,38 @@
     return own + other
 
 
-def square_kernel(place_ref, own_ref, other_ref, right_ref, out_ref, ordered_ref, staged_ref, sems):
-    halves, layers, part, columns = staged_ref.shape
+def square_kernel(place_ref, own_ref, other_ref, right_ref, *refs):
+    outs, ordered_ref, total_ref = refs[:-2], refs[-2], refs[-1]
+    layers = len(outs)
+    halves, part, _ = outs[0].shape
     tiles = right_ref.shape[0]
     z, core = place_ref[1], place_ref[2]
     way = 1 - 2 * core
     for offset in range(tiles):
         ordered_ref[0, offset] = right_ref[lax.rem(z + way * offset + tiles, tiles), core]
         ordered_ref[1, offset] = right_ref[lax.rem(z - way * offset + tiles, tiles), 1 - core]
-    copies = []
-    for half in range(halves):
-        count = layers * part
-        total = product(own_ref, other_ref, ordered_ref, half * count, count)
-        staged_ref[half] = total.astype(staged_ref.dtype).reshape(layers, part, columns)
-        copies.append(pltpu.make_async_copy(staged_ref.at[half], out_ref.at[:, half], sems.at[half]))
-        copies[-1].start()
-    for copy in copies:
-        copy.wait()
-
-
-def filter_kernel(keep_ref, layer_ref, parts_ref, out_ref):
-    layers, halves, part, columns = parts_ref.shape
+    total_ref[...] = product(own_ref, other_ref, ordered_ref, 0, total_ref.shape[0])
+    for offset, out_ref in enumerate(outs):
+        layer = lax.rem(place_ref[3] + way * offset + layers, layers)
+        for half in range(halves):
+            start = pl.multiple_of((half * layers + layer) * part, part)
+            out_ref[half] = total_ref[pl.ds(start, part), :].astype(out_ref.dtype)
+
+
+def filter_kernel(keep_ref, place_ref, *refs):
+    parts, out_ref = refs[:-1], refs[-1]
+    halves, part, columns = out_ref.shape
     chunk = BLK // 2
     low = lax.broadcasted_iota(jnp.int32, (chunk, 2 * BLK), 1) < BLK
     for half in range(halves):
         for start in range(0, part, chunk):
-            block = (half * layers * part + layer_ref[0] * part + start) // BLK
+            block = (half * columns + place_ref[3] * part + start) // BLK
             rows = pl.ds(start, chunk)
             for lane in range(0, columns, 2 * BLK):
                 lanes = pl.ds(lane, 2 * BLK)
-                total = parts_ref[0, half, rows, lanes].astype(jnp.float32)
-                for layer in range(1, layers):
-                    total = total + parts_ref[layer, half, rows, lanes].astype(jnp.float32)
+                total = parts[0][half, rows, lanes].astype(jnp.float32)
+                for part_ref in parts[1:]:
+                    total = total + part_ref[half, rows, lanes].astype(jnp.float32)
                 left = keep_ref[block, lane // BLK].astype(jnp.float32)
                 right = keep_ref[block, lane // BLK + 1].astype(jnp.float32)
                 out_ref[half, rows, lanes] = (total * jnp.where(low, left, right)).astype(out_ref.dtype)
@@ -132,7 +136,7 @@
     halves = tile_rows // width
     vmem = pl.BlockSpec(memory_space=pltpu.VMEM)
     smem = pl.BlockSpec(memory_space=pltpu.SMEM)
-    params = pltpu.CompilerParams(vmem_limit_bytes=40 * 2**20)
+    params = pltpu.CompilerParams(vmem_limit_bytes=20 * 2**20)
 
     left_piece = lax.dynamic_slice_in_dim(matrix, layer_index * part, part, 1).T
     right_piece = lax.dynamic_slice_in_dim(
@@ -142,28 +146,30 @@
     left_own = jnp.concatenate(ring_of_eight(left_piece, "z"), axis=0)
     left_own, right = lax.optimization_barrier((left_own, right))
     left_other = lax.ppermute(left_own, "core", [(0, 1), (1, 0)])
-    place = jnp.stack([row_index, z_index, core_index])
-
-    square_part = pl.pallas_call(
+    place = jnp.stack([row_index, z_index, core_index, layer_index])
+    ordered = pltpu.VMEM((halves, rows_count, part, width), jnp.bfloat16)
+    total = pltpu.VMEM((tile_rows, width), jnp.float32)
+    piece = jax.ShapeDtypeStruct((halves, part, width), jnp.bfloat16)
+
+    mine, ahead, beyond, behind = pl.pallas_call(
         square_kernel,
-        out_shape=jax.ShapeDtypeStruct((layers, halves, part, width), jnp.bfloat16),
-        in_specs=[smem, vmem, vmem, vmem],
-        out_specs=pl.BlockSpec(memory_space=pltpu.HBM),
-        scratch_shapes=[
-            pltpu.VMEM((halves, rows_count, part, width), jnp.bfloat16),
-            pltpu.VMEM((halves, layers, part, width), jnp.bfloat16),
-            pltpu.SemaphoreType.DMA((halves,)),
-        ],
+        out_shape=[piece] * layers,
+        in_specs=[smem] + [vmem] * 3,
+        out_specs=[vmem] * layers,
+        scratch_shapes=[ordered, total],
         compiler_params=params,
     )(place, left_own, left_other, right)
-    parts = lax.all_to_all(square_part, "layer", split_axis=0, concat_axis=0, tiled=True)
+    passing = shifted(beyond, "layer", -1)
+    from_ahead = shifted(behind, "layer", 1)
+    onward = (passing.astype(jnp.float32) + ahead.astype(jnp.float32)).astype(jnp.bfloat16)
+    from_behind = shifted(onward, "layer", -1)
     filtered_piece = pl.pallas_call(
         filter_kernel,
-        out_shape=jax.ShapeDtypeStruct((halves, part, width), jnp.bfloat16),
-        in_specs=[smem, smem, vmem],
+        out_shape=piece,
+        in_specs=[smem] * 2 + [vmem] * 3,
         out_specs=vmem,
         compiler_params=params,
-    )(keep_mask, layer_index.reshape(1), parts)
+    )(keep_mask, place, mine, from_ahead, from_behind)
     filtered = ring_of_eight(filtered_piece, "row")
 
     scale = jnp.where(layer_index == 0, 1.5, 0.0).astype(jnp.float32).reshape(1)
@@ -174,11 +180,7 @@
         out_shape=jax.ShapeDtypeStruct((chosen.shape[0], pairs, 128), jnp.bfloat16),
         in_specs=[smem] * 3 + [vmem] * 11,
         out_specs=vmem,
-        scratch_shapes=[
-            pltpu.VMEM((halves, rows_count, part, width), jnp.bfloat16),
-            pltpu.VMEM((tile_rows, width), jnp.float32),
-            pltpu.VMEM((4, BLK, 128), jnp.float32),
-        ],
+        scratch_shapes=[ordered, total, pltpu.VMEM((4, BLK, 128), jnp.float32)],
         compiler_params=params,
     )(chosen, place, scale, left_own, left_other, matrix, *filtered)
     arrived = lax.all_to_all(outgoing, ("z", "core"), split_axis=0, concat_axis=0, tiled=True)

time: 133 us -> 135 us (1.015)
  starting transfers between devices: 72.1 us -> 79.4 us
  waiting for transfers between devices: 20.5 us -> 13.2 us
  blocking collectives: 26.8 us -> 29.3 us
    ppermute x14 -> x17, starting transfers between devices: 50.8 us -> 62.2 us  [shifted(): return lax.ppermute(piece, axes, pairs)]
    all_to_all x1 -> x0, waiting for transfers between devices: 8.82 us -> none  [on_device(): lax.all_to_all(square_part, 'layer', split_axis=0, concat_axis=0, tiled=T...]
    all_to_all x1 -> x0, starting transfers between devices: 4.15 us -> none  [on_device(): lax.all_to_all(square_part, 'layer', split_axis=0, concat_axis=0, tiled=T...]
    all_to_all x1, blocking collectives: 14.5 us -> 17 us  [on_device(): lax.all_to_all(outgoing, ('z', 'core'), split_axis=0, concat_axis=0, tile...]
    ppermute x14 -> x17, waiting for transfers between devices: 9.27 us -> 10.9 us  [shifted(): return lax.ppermute(piece, axes, pairs)]
  transfers between devices with their start and end apart: 17 -> 19, of which waited for: 6 -> 7; matrix products, arithmetic and copies ran while one was open for 2% -> 1% of each run, Pallas kernels for 0% -> 0%
where the time goes in v7:
time: 135 us; the launch traced here: 134 us
  starting transfers between devices  79.4 us (59%)
  blocking collectives  29.3 us (22%)
  waiting for transfers between devices  13.2 us (10%)
  Pallas kernels  6.41 us (5%)
  local copies, waits for them, and re-layouts  5.23 us (4%)
    ppermute x17, starting transfers between devices, shifted(): return lax.ppermute(piece, axes, pairs)  62.2 us
    all_to_all x1, blocking collectives, on_device(): lax.all_to_all(outgoing, ('z', 'core'), split_axis=0, concat_axis=0, tile...  17 us
    all_to_all x1, blocking collectives, to_all(): return lax.all_to_all(copies, axis, split_axis=0, concat_axis=0, tiled=True)  12.3 us
    ppermute x17, waiting for transfers between devices, shifted(): return lax.ppermute(piece, axes, pairs)  10.9 us
    ppermute x1, starting transfers between devices, on_device(): left_other = lax.ppermute(left_own, 'core', [(0, 1), (1, 0)])  9.55 us
    all_to_all x1, starting transfers between devices, to_all(): return lax.all_to_all(copies, axis, split_axis=0, concat_axis=0, tiled=True)  7.65 us
    pallas_call x1, Pallas kernels, on_device(): pl.pallas_call(cube_kernel, out_shape=jax.ShapeDtypeStruct((chosen.shape[...  2.92 us
    pallas_call x1, Pallas kernels, on_device(): pl.pallas_call(square_kernel, out_shape=[piece] * layers, in_specs=[smem]...  2.74 us
  transfers between devices with their start and end apart: 19, of which 7 were waited for; matrix products, arithmetic and copies ran while one was open for 1% of the time, Pallas kernels for 0%

profile of v7, /device:TPU:1, one launch (start us, length us, event | category | flops | bytes accessed | tf_op | source)
XLA Modules:
  0.0 134.0 jit_solution(3885821756590573881)
XLA Ops:
  0.0 0.9 dynamic-slice_bitcast_fusion
  0.9 1.2 broadcast_in_dim.14
  2.1 7.7 %all-to-all-start = ((bf16[8,2,96,384]{3,2,1,0:T(8,128)(2,1)}), bf16[8,2,96,384]{3,2,1,0:T(8,128)(2,1)S(1)}, u32[]{:S(2)}, u32[]{:S(2)}) async-start(bf16[8,2,96,384]{3,2,1,0:T(8,128)(2,1)} %broadcast_in_dim.14), calls=%async_computation | async-start | bytes 2359296 | tf_op jit(solution)/shard_map/all_to_all | solution.py:14
  9.7 1.1 constant_dynamic-slice_fusion
  10.9 0.1 copy.8
  11.0 4.0 %collective-permute-start = (bf16[96,768]{1,0:T(8,128)(2,1)S(1)}, bf16[96,768]{1,0:T(8,128)(2,1)S(1)}, u32[]{:S(2)}, u32[]{:S(2)}) collective-permute-start(bf16[96,768]{1,0:T(8,128)(2,1)S(1)} %bitcast.17), channel_id=1, source_target_pairs={{0,56},{4,12},{8,0},{12,20},{16,8},{20,28},{24,16},{28,36},{32,24}... | collective-permute-start | bytes 442376 | tf_op jit(solution)/shard_map/ppermute | solution.py:27
  15.0 5.8 %collective-permute-start.1 = (bf16[96,768]{1,0:T(8,128)(2,1)S(1)}, bf16[96,768]{1,0:T(8,128)(2,1)S(1)}, u32[]{:S(2)}, u32[]{:S(2)}) collective-permute-start(bf16[96,768]{1,0:T(8,128)(2,1)S(1)} %bitcast.18), channel_id=1, source_target_pairs={{0,48},{4,20},{8,56},{12,28},{16,0},{20,36},{24,8},{28,44},{32,16}... | collective-permute-start | bytes 442376 | tf_op jit(solution)/shard_map/ppermute | solution.py:27
  20.8 5.9 %collective-permute-start.4 = (bf16[96,768]{1,0:T(8,128)(2,1)S(1)}, bf16[96,768]{1,0:T(8,128)(2,1)S(1)}, u32[]{:S(2)}, u32[]{:S(2)}) collective-permute-start(bf16[96,768]{1,0:T(8,128)(2,1)S(1)} %bitcast.19), channel_id=1, source_target_pairs={{0,16},{4,52},{8,24},{12,60},{16,32},{20,4},{24,40},{28,12},{32,48... | collective-permute-start | bytes 442376 | tf_op jit(solution)/shard_map/ppermute | solution.py:27
  26.7 3.1 %collective-permute-start.6 = (bf16[96,768]{1,0:T(8,128)(2,1)S(1)}, bf16[96,768]{1,0:T(8,128)(2,1)S(1)}, u32[]{:S(2)}, u32[]{:S(2)}) collective-permute-start(bf16[96,768]{1,0:T(8,128)(2,1)S(1)} %bitcast.20), channel_id=1, source_target_pairs={{0,8},{4,60},{8,16},{12,4},{16,24},{20,12},{24,32},{28,20},{32,40}... | collective-permute-start | bytes 442376 | tf_op jit(solution)/shard_map/ppermute | solution.py:27
  29.8 2.2 %collective-permute-start.2 = (bf16[96,768]{1,0:T(8,128)(2,1)S(1)}, bf16[96,768]{1,0:T(8,128)(2,1)S(1)}, u32[]{:S(2)}, u32[]{:S(2)}) collective-permute-start(bf16[96,768]{1,0:T(8,128)(2,1)S(1)} %collective-permute-done.1), channel_id=1, source_target_pairs={{0,56},{4,12},{8,0},{12,20},{16,8},{20,28},{24,16},{28,36},{32,24}... | collective-permute-start | bytes 442376 | tf_op jit(solution)/shard_map/ppermute | solution.py:27
  32.0 2.2 %collective-permute-start.3 = (bf16[96,768]{1,0:T(8,128)(2,1)S(1)}, bf16[96,768]{1,0:T(8,128)(2,1)S(1)}, u32[]{:S(2)}, u32[]{:S(2)}) collective-permute-start(bf16[96,768]{1,0:T(8,128)(2,1)S(1)} %collective-permute-done.1), channel_id=1, source_target_pairs={{0,48},{4,20},{8,56},{12,28},{16,0},{20,36},{24,8},{28,44},{32,16}... | collective-permute-start | bytes 442376 | tf_op jit(solution)/shard_map/ppermute | solution.py:27
  34.2 0.0 collective-permute-done
  34.3 4.3 %collective-permute-start.5 = (bf16[96,768]{1,0:T(8,128)(2,1)S(1)}, bf16[96,768]{1,0:T(8,128)(2,1)S(1)}, u32[]{:S(2)}, u32[]{:S(2)}) collective-permute-start(bf16[96,768]{1,0:T(8,128)(2,1)S(1)} %collective-permute-done.4), channel_id=1, source_target_pairs={{0,8},{4,60},{8,16},{12,4},{16,24},{20,12},{24,32},{28,20},{32,40}... | collective-permute-start | bytes 442376 | tf_op jit(solution)/shard_map/ppermute | solution.py:27
  38.6 0.1 collective-permute-done.2
  38.6 1.9 %collective-permute-done.3 = bf16[96,768]{1,0:T(8,128)(2,1)S(1)} collective-permute-done((bf16[96,768]{1,0:T(8,128)(2,1)S(1)}, bf16[96,768]{1,0:T(8,128)(2,1)S(1)}, u32[]{:S(2)}, u32[]{:S(2)}) %collective-permute-start.3) | collective-permute-done | bytes 147488 | tf_op jit(solution)/shard_map/ppermute | solution.py:27
  40.5 1.5 %collective-permute-done.5 = bf16[96,768]{1,0:T(8,128)(2,1)S(1)} collective-permute-done((bf16[96,768]{1,0:T(8,128)(2,1)S(1)}, bf16[96,768]{1,0:T(8,128)(2,1)S(1)}, u32[]{:S(2)}, u32[]{:S(2)}) %collective-permute-start.5) | collective-permute-done | bytes 147488 | tf_op jit(solution)/shard_map/ppermute | solution.py:27
  42.0 0.0 collective-permute-done.6
  42.0 9.6 %collective-permute-start.7 = (bf16[768,768]{1,0:T(8,128)(2,1)S(1)}, bf16[768,768]{1,0:T(8,128)(2,1)S(1)}, u32[]{:S(2)}, u32[]{:S(2)}) collective-permute-start(bf16[768,768]{1,0:T(8,128)(2,1)S(1)} %constant_dynamic-update-slice_fusion.own_ref), channel_id=1, source_target_pairs={{0,4},{4,0},{1,5},{5,1},{2,6},{6,2},{3,7},{7,3},{8,12},{12,8},{9,1... | collective-permute-start | bytes 3538952 | tf_op jit(solution)/shard_map/ppermute | solution.py:148
  51.6 0.1 pad_add_fusion.place_ref
  51.7 2.4 %collective-permute-done.7.other_ref = bf16[768,768]{1,0:T(8,128)(2,1)S(1)} collective-permute-done((bf16[768,768]{1,0:T(8,128)(2,1)S(1)}, bf16[768,768]{1,0:T(8,128)(2,1)S(1)}, u32[]{:S(2)}, u32[]{:S(2)}) %collective-permute-start.7) | collective-permute-done | bytes 1179680 | tf_op jit(solution)/shard_map/ppermute | solution.py:148
  54.1 2.7 %shard_map.37 = (bf16[2,96,384]{2,1,0:T(8,128)(2,1)S(1)}, bf16[2,96,384]{2,1,0:T(8,128)(2,1)S(1)}, bf16[2,96,384]{2,1,0:T(8,128)(2,1)S(1)}, bf16[2,96,384]{2,1,0:T(8,128)(2,1)}) custom-call(s32[4]{0:T(128)S(1)} %pad_add_fusion.place_ref, bf16[768,768]{1,0:T(8,128)(2,1)S(1)} %constant_dynamic-update-slice_fusion.own_ref, ...), custom_call_target="tpu_custom_call" | custom-call | tf_op jit(solution)/shard_map/pallas_call | solution.py:154
  56.8 4.4 %collective-permute-start.9 = (bf16[2,96,384]{2,1,0:T(8,128)(2,1)S(1)}, bf16[2,96,384]{2,1,0:T(8,128)(2,1)S(1)}, u32[]{:S(2)}, u32[]{:S(2)}) collective-permute-start(bf16[2,96,384]{2,1,0:T(8,128)(2,1)S(1)} %get-tuple-element.15), channel_id=1, source_target_pairs={{0,1},{4,7},{1,2},{5,4},{2,3},{6,5},{3,0},{7,6},{8,9},{12,15},{9,1... | collective-permute-start | bytes 442376 | tf_op jit(solution)/shard_map/ppermute | solution.py:27
  61.2 1.9 %collective-permute-start.8 = (bf16[2,96,384]{2,1,0:T(8,128)(2,1)}, bf16[2,96,384]{2,1,0:T(8,128)(2,1)S(1)}, u32[]{:S(2)}, u32[]{:S(2)}) collective-permute-start(bf16[2,96,384]{2,1,0:T(8,128)(2,1)} %get-tuple-element.14), channel_id=1, source_target_pairs={{0,3},{4,5},{1,0},{5,6},{2,1},{6,7},{3,2},{7,4},{8,11},{12,13},{9,... | collective-permute-start | bytes 442376 | tf_op jit(solution)/shard_map/ppermute | solution.py:27
  63.2 0.2 collective-permute-done.9
  63.4 5.0 %collective-permute-start.10 = (bf16[2,96,384]{2,1,0:T(8,128)(2,1)S(1)}, bf16[2,96,384]{2,1,0:T(8,128)(2,1)S(1)}, u32[]{:S(2)}, u32[]{:S(2)}) collective-permute-start(bf16[2,96,384]{2,1,0:T(8,128)(2,1)S(1)} %add_convert_fusion), channel_id=1, source_target_pairs={{0,1},{4,7},{1,2},{5,4},{2,3},{6,5},{3,0},{7,6},{8,9},{12,15},{9,1... | collective-permute-start | bytes 442376 | tf_op jit(solution)/shard_map/ppermute | solution.py:27
  68.4 0.1 copy.7.keep_ref
  68.5 0.0 collective-permute-done.8.refs_1_
  68.6 1.9 %collective-permute-done.10.refs_2_ = bf16[2,96,384]{2,1,0:T(8,128)(2,1)S(1)} collective-permute-done((bf16[2,96,384]{2,1,0:T(8,128)(2,1)S(1)}, bf16[2,96,384]{2,1,0:T(8,128)(2,1)S(1)}, u32[]{:S(2)}, u32[]{:S(2)}) %collective-permute-start.10) | collective-permute-done | bytes 147488 | tf_op jit(solution)/shard_map/ppermute | solution.py:27
  70.5 0.9 copy-done.2
  71.4 0.7 shard_map.38.refs_0_
  72.1 4.5 %collective-permute-start.12 = (bf16[2,96,384]{2,1,0:T(8,128)(2,1)S(1)}, bf16[2,96,384]{2,1,0:T(8,128)(2,1)S(1)}, u32[]{:S(2)}, u32[]{:S(2)}) collective-permute-start(bf16[2,96,384]{2,1,0:T(8,128)(2,1)S(1)} %shard_map.38.refs_0_), channel_id=1, source_target_pairs={{0,384},{4,132},{64,448},{68,196},{128,0},{132,260},{192,64},{196,... | collective-permute-start | bytes 442376 | tf_op jit(solution)/shard_map/ppermute | solution.py:27
  76.6 3.1 %collective-permute-start.15 = (bf16[2,96,384]{2,1,0:T(8,128)(2,1)S(1)}, bf16[2,96,384]{2,1,0:T(8,128)(2,1)S(1)}, u32[]{:S(2)}, u32[]{:S(2)}) collective-permute-start(bf16[2,96,384]{2,1,0:T(8,128)(2,1)S(1)} %shard_map.38.refs_0_), channel_id=1, source_target_pairs={{0,128},{4,388},{64,192},{68,452},{128,256},{132,4},{192,320},{196... | collective-permute-start | bytes 442376 | tf_op jit(solution)/shard_map/ppermute | solution.py:27
  79.8 3.4 %collective-permute-start.11 = (bf16[2,96,384]{2,1,0:T(8,128)(2,1)S(1)}, bf16[2,96,384]{2,1,0:T(8,128)(2,1)S(1)}, u32[]{:S(2)}, u32[]{:S(2)}) collective-permute-start(bf16[2,96,384]{2,1,0:T(8,128)(2,1)S(1)} %shard_map.38.refs_0_), channel_id=1, source_target_pairs={{0,448},{4,68},{64,0},{68,132},{128,64},{132,196},{192,128},{196,2... | collective-permute-start | bytes 442376 | tf_op jit(solution)/shard_map/ppermute | solution.py:27
  83.1 3.1 %collective-permute-start.17 = (bf16[2,96,384]{2,1,0:T(8,128)(2,1)S(1)}, bf16[2,96,384]{2,1,0:T(8,128)(2,1)}, u32[]{:S(2)}, u32[]{:S(2)}) collective-permute-start(bf16[2,96,384]{2,1,0:T(8,128)(2,1)S(1)} %shard_map.38.refs_0_), channel_id=1, source_target_pairs={{0,64},{4,452},{64,128},{68,4},{128,192},{132,68},{192,256},{196,1... | collective-permute-start | bytes 442376 | tf_op jit(solution)/shard_map/ppermute | solution.py:27
  86.3 2.1 %collective-permute-start.13 = (bf16[2,96,384]{2,1,0:T(8,128)(2,1)S(1)}, bf16[2,96,384]{2,1,0:T(8,128)(2,1)}, u32[]{:S(2)}, u32[]{:S(2)}) collective-permute-start(bf16[2,96,384]{2,1,0:T(8,128)(2,1)S(1)} %collective-permute-done.12.refs_2_), channel_id=1, source_target_pairs={{0,448},{4,68},{64,0},{68,132},{128,64},{132,196},{192,128},{196,2... | collective-permute-start | bytes 442376 | tf_op jit(solution)/shard_map/ppermute | solution.py:27
  88.4 4.9 %collective-permute-start.14 = (bf16[2,96,384]{2,1,0:T(8,128)(2,1)S(1)}, bf16[2,96,384]{2,1,0:T(8,128)(2,1)}, u32[]{:S(2)}, u32[]{:S(2)}) collective-permute-start(bf16[2,96,384]{2,1,0:T(8,128)(2,1)S(1)} %collective-permute-done.12.refs_2_), channel_id=1, source_target_pairs={{0,384},{4,132},{64,448},{68,196},{128,0},{132,260},{192,64},{196,... | collective-permute-start | bytes 442376 | tf_op jit(solution)/shard_map/ppermute | solution.py:27
  93.4 0.0 collective-permute-done.15.refs_6_
  93.4 2.2 %collective-permute-start.16 = (bf16[2,96,384]{2,1,0:T(8,128)(2,1)S(1)}, bf16[2,96,384]{2,1,0:T(8,128)(2,1)}, u32[]{:S(2)}, u32[]{:S(2)}) collective-permute-start(bf16[2,96,384]{2,1,0:T(8,128)(2,1)S(1)} %collective-permute-done.15.refs_6_), channel_id=1, source_target_pairs={{0,64},{4,452},{64,128},{68,4},{128,192},{132,68},{192,256},{196,1... | collective-permute-start | bytes 442376 | tf_op jit(solution)/shard_map/ppermute | solution.py:27
  95.6 0.0 collective-permute-done.11.refs_1_
  95.6 0.0 collective-permute-done.17.refs_7_
  95.6 3.5 %collective-permute-done.14.refs_4_ = bf16[2,96,384]{2,1,0:T(8,128)(2,1)} collective-permute-done((bf16[2,96,384]{2,1,0:T(8,128)(2,1)S(1)}, bf16[2,96,384]{2,1,0:T(8,128)(2,1)}, u32[]{:S(2)}, u32[]{:S(2)}) %collective-permute-start.14) | collective-permute-done | bytes 147488 | tf_op jit(solution)/shard_map/ppermute | solution.py:27
  99.2 1.8 %collective-permute-done.16.refs_5_ = bf16[2,96,384]{2,1,0:T(8,128)(2,1)} collective-permute-done((bf16[2,96,384]{2,1,0:T(8,128)(2,1)S(1)}, bf16[2,96,384]{2,1,0:T(8,128)(2,1)}, u32[]{:S(2)}, u32[]{:S(2)}) %collective-permute-start.16) | collective-permute-done | bytes 147488 | tf_op jit(solution)/shard_map/ppermute | solution.py:27
  101.0 2.9 %shard_map.39 = bf16[16,32,128]{2,1,0:T(8,128)(2,1)S(1)} custom-call(s32[16]{0:T(128)S(1)} %bitcast.16, s32[4]{0:T(128)S(1)} %pad_add_fusion.place_ref, f32[1]{0:T(128)} %bitcast.5.scale_ref, bf16[768,768]{1,0:T(8,128)(2,1)S(1)} %constant_dynamic-update-slice_fusion.own_ref, bf16[768,768]{1,0:T(8,128)(2,1)S(1)} %collective-permute-done.7.other_ref, ...), custom_call_target="tpu_custom_call" | custom-call | tf_op jit(solution)/shard_map/pallas_call | solution.py:178
  103.9 17.0 %all_to_all.15 = bf16[16,32,128]{2,1,0:T(8,128)(2,1)S(1)} all-to-all(bf16[16,32,128]{2,1,0:T(8,128)(2,1)S(1)} %shard_map.39), channel_id=1, replica_groups=mesh['row'=8,'z'=8,'core'=2,'layer'=4] {'z','core'}, dimensions={0} | all-to-all | bytes 262144 | tf_op jit(solution)/shard_map/all_to_all | solution.py:186
  120.9 0.1 broadcast_in_dim.15
  120.9 12.3 %all_to_all.16 = bf16[4,16,32,128]{3,2,1,0:T(8,128)(2,1)S(1)} all-to-all(bf16[4,16,32,128]{3,2,1,0:T(8,128)(2,1)S(1)} %broadcast_in_dim.15), channel_id=1, replica_groups=mesh['row'=8,'z'=8,'core'=2,'layer'=4] {'layer'}, dimensions={0} | all-to-all | bytes 1048576 | tf_op jit(solution)/shard_map/all_to_all | solution.py:14
  133.2 0.1 reduce_sum.12
  133.3 0.7 copy.11
  (23 shorter events, 0.2 us)
Async XLA Ops:
  2.1 39.9 %all-to-all-start = ((bf16[8,2,96,384]{3,2,1,0:T(8,128)(2,1)}), bf16[8,2,96,384]{3,2,1,0:T(8,128)(2,1)S(1)}, u32[]{:S(2)}, u32[]{:S(2)}) async-start(bf16[8,2,96,384]{3,2,1,0:T(8,128)(2,1)} %broadcast_in_dim.14), calls=%async_computation | async-start | bytes 2359296 | tf_op jit(solution)/shard_map/all_to_all | solution.py:14
  11.0 23.2 %collective-permute-start = (bf16[96,768]{1,0:T(8,128)(2,1)S(1)}, bf16[96,768]{1,0:T(8,128)(2,1)S(1)}, u32[]{:S(2)}, u32[]{:S(2)}) collective-permute-start(bf16[96,768]{1,0:T(8,128)(2,1)S(1)} %bitcast.17), channel_id=1, source_target_pairs={{0,56},{4,12},{8,0},{12,20},{16,8},{20,28},{24,16},{28,36},{32,24}... | collective-permute-start | bytes 442376 | tf_op jit(solution)/shard_map/ppermute | solution.py:27
  15.0 14.8 %collective-permute-start.1 = (bf16[96,768]{1,0:T(8,128)(2,1)S(1)}, bf16[96,768]{1,0:T(8,128)(2,1)S(1)}, u32[]{:S(2)}, u32[]{:S(2)}) collective-permute-start(bf16[96,768]{1,0:T(8,128)(2,1)S(1)} %bitcast.18), channel_id=1, source_target_pairs={{0,48},{4,20},{8,56},{12,28},{16,0},{20,36},{24,8},{28,44},{32,16}... | collective-permute-start | bytes 442376 | tf_op jit(solution)/shard_map/ppermute | solution.py:27
  20.8 13.4 %collective-permute-start.4 = (bf16[96,768]{1,0:T(8,128)(2,1)S(1)}, bf16[96,768]{1,0:T(8,128)(2,1)S(1)}, u32[]{:S(2)}, u32[]{:S(2)}) collective-permute-start(bf16[96,768]{1,0:T(8,128)(2,1)S(1)} %bitcast.19), channel_id=1, source_target_pairs={{0,16},{4,52},{8,24},{12,60},{16,32},{20,4},{24,40},{28,12},{32,48... | collective-permute-start | bytes 442376 | tf_op jit(solution)/shard_map/ppermute | solution.py:27
  26.7 15.3 %collective-permute-start.6 = (bf16[96,768]{1,0:T(8,128)(2,1)S(1)}, bf16[96,768]{1,0:T(8,128)(2,1)S(1)}, u32[]{:S(2)}, u32[]{:S(2)}) collective-permute-start(bf16[96,768]{1,0:T(8,128)(2,1)S(1)} %bitcast.20), channel_id=1, source_target_pairs={{0,8},{4,60},{8,16},{12,4},{16,24},{20,12},{24,32},{28,20},{32,40}... | collective-permute-start | bytes 442376 | tf_op jit(solution)/shard_map/ppermute | solution.py:27
  29.8 8.8 %collective-permute-start.2 = (bf16[96,768]{1,0:T(8,128)(2,1)S(1)}, bf16[96,768]{1,0:T(8,128)(2,1)S(1)}, u32[]{:S(2)}, u32[]{:S(2)}) collective-permute-start(bf16[96,768]{1,0:T(8,128)(2,1)S(1)} %collective-permute-done.1), channel_id=1, source_target_pairs={{0,56},{4,12},{8,0},{12,20},{16,8},{20,28},{24,16},{28,36},{32,24}... | collective-permute-start | bytes 442376 | tf_op jit(solution)/shard_map/ppermute | solution.py:27
  32.0 8.5 %collective-permute-start.3 = (bf16[96,768]{1,0:T(8,128)(2,1)S(1)}, bf16[96,768]{1,0:T(8,128)(2,1)S(1)}, u32[]{:S(2)}, u32[]{:S(2)}) collective-permute-start(bf16[96,768]{1,0:T(8,128)(2,1)S(1)} %collective-permute-done.1), channel_id=1, source_target_pairs={{0,48},{4,20},{8,56},{12,28},{16,0},{20,36},{24,8},{28,44},{32,16}... | collective-permute-start | bytes 442376 | tf_op jit(solution)/shard_map/ppermute | solution.py:27
  34.3 7.7 %collective-permute-start.5 = (bf16[96,768]{1,0:T(8,128)(2,1)S(1)}, bf16[96,768]{1,0:T(8,128)(2,1)S(1)}, u32[]{:S(2)}, u32[]{:S(2)}) collective-permute-start(bf16[96,768]{1,0:T(8,128)(2,1)S(1)} %collective-permute-done.4), channel_id=1, source_target_pairs={{0,8},{4,60},{8,16},{12,4},{16,24},{20,12},{24,32},{28,20},{32,40}... | collective-permute-start | bytes 442376 | tf_op jit(solution)/shard_map/ppermute | solution.py:27
  42.0 12.0 %collective-permute-start.7 = (bf16[768,768]{1,0:T(8,128)(2,1)S(1)}, bf16[768,768]{1,0:T(8,128)(2,1)S(1)}, u32[]{:S(2)}, u32[]{:S(2)}) collective-permute-start(bf16[768,768]{1,0:T(8,128)(2,1)S(1)} %constant_dynamic-update-slice_fusion.own_ref), channel_id=1, source_target_pairs={{0,4},{4,0},{1,5},{5,1},{2,6},{6,2},{3,7},{7,3},{8,12},{12,8},{9,1... | collective-permute-start | bytes 3538952 | tf_op jit(solution)/shard_map/ppermute | solution.py:148
  51.7 16.7 %copy-start.4 = (s32[12,6]{0,1:T(8,128)S(1)}, s32[12,6]{0,1:T(8,128)}, u32[]{:S(2)}) copy-start(s32[12,6]{0,1:T(8,128)} %param.4) | copy-start | bytes 868
  51.7 49.3 %copy-start.3 = (s32[1,16]{1,0:T(1,128)S(1)}, s32[1,16]{1,0:T(1,128)}, u32[]{:S(2)}) copy-start(s32[1,16]{1,0:T(1,128)} %param.5) | copy-start | bytes 196
  56.8 6.6 %copy-start.1 = (bf16[2,96,384]{2,1,0:T(8,128)(2,1)}, bf16[2,96,384]{2,1,0:T(8,128)(2,1)S(1)}, u32[]{:S(2)}) copy-start(bf16[2,96,384]{2,1,0:T(8,128)(2,1)S(1)} %get-tuple-element.13.refs_0_) | copy-start | bytes 442372
  56.8 44.2 %copy-start = (bf16[768,384]{1,0:T(8,128)(2,1)S(1)}, bf16[768,384]{1,0:T(8,128)(2,1)}, u32[]{:S(2)}) copy-start(bf16[768,384]{1,0:T(8,128)(2,1)} %matrix_ref.1) | copy-start | bytes 1769476
  56.8 6.5 %collective-permute-start.9 = (bf16[2,96,384]{2,1,0:T(8,128)(2,1)S(1)}, bf16[2,96,384]{2,1,0:T(8,128)(2,1)S(1)}, u32[]{:S(2)}, u32[]{:S(2)}) collective-permute-start(bf16[2,96,384]{2,1,0:T(8,128)(2,1)S(1)} %get-tuple-element.15), channel_id=1, source_target_pairs={{0,1},{4,7},{1,2},{5,4},{2,3},{6,5},{3,0},{7,6},{8,9},{12,15},{9,1... | collective-permute-start | bytes 442376 | tf_op jit(solution)/shard_map/ppermute | solution.py:27
  61.2 7.3 %collective-permute-start.8 = (bf16[2,96,384]{2,1,0:T(8,128)(2,1)}, bf16[2,96,384]{2,1,0:T(8,128)(2,1)S(1)}, u32[]{:S(2)}, u32[]{:S(2)}) collective-permute-start(bf16[2,96,384]{2,1,0:T(8,128)(2,1)} %get-tuple-element.14), channel_id=1, source_target_pairs={{0,3},{4,5},{1,0},{5,6},{2,1},{6,7},{3,2},{7,4},{8,11},{12,13},{9,... | collective-permute-start | bytes 442376 | tf_op jit(solution)/shard_map/ppermute | solution.py:27
  63.4 7.1 %collective-permute-start.10 = (bf16[2,96,384]{2,1,0:T(8,128)(2,1)S(1)}, bf16[2,96,384]{2,1,0:T(8,128)(2,1)S(1)}, u32[]{:S(2)}, u32[]{:S(2)}) collective-permute-start(bf16[2,96,384]{2,1,0:T(8,128)(2,1)S(1)} %add_convert_fusion), channel_id=1, source_target_pairs={{0,1},{4,7},{1,2},{5,4},{2,3},{6,5},{3,0},{7,6},{8,9},{12,15},{9,1... | collective-permute-start | bytes 442376 | tf_op jit(solution)/shard_map/ppermute | solution.py:27
  70.5 0.9 copy-start.2
  72.1 14.1 %collective-permute-start.12 = (bf16[2,96,384]{2,1,0:T(8,128)(2,1)S(1)}, bf16[2,96,384]{2,1,0:T(8,128)(2,1)S(1)}, u32[]{:S(2)}, u32[]{:S(2)}) collective-permute-start(bf16[2,96,384]{2,1,0:T(8,128)(2,1)S(1)} %shard_map.38.refs_0_), channel_id=1, source_target_pairs={{0,384},{4,132},{64,448},{68,196},{128,0},{132,260},{192,64},{196,... | collective-permute-start | bytes 442376 | tf_op jit(solution)/shard_map/ppermute | solution.py:27
  76.6 16.8 %collective-permute-start.15 = (bf16[2,96,384]{2,1,0:T(8,128)(2,1)S(1)}, bf16[2,96,384]{2,1,0:T(8,128)(2,1)S(1)}, u32[]{:S(2)}, u32[]{:S(2)}) collective-permute-start(bf16[2,96,384]{2,1,0:T(8,128)(2,1)S(1)} %shard_map.38.refs_0_), channel_id=1, source_target_pairs={{0,128},{4,388},{64,192},{68,452},{128,256},{132,4},{192,320},{196... | collective-permute-start | bytes 442376 | tf_op jit(solution)/shard_map/ppermute | solution.py:27
  79.8 15.8 %collective-permute-start.11 = (bf16[2,96,384]{2,1,0:T(8,128)(2,1)S(1)}, bf16[2,96,384]{2,1,0:T(8,128)(2,1)S(1)}, u32[]{:S(2)}, u32[]{:S(2)}) collective-permute-start(bf16[2,96,384]{2,1,0:T(8,128)(2,1)S(1)} %shard_map.38.refs_0_), channel_id=1, source_target_pairs={{0,448},{4,68},{64,0},{68,132},{128,64},{132,196},{192,128},{196,2... | collective-permute-start | bytes 442376 | tf_op jit(solution)/shard_map/ppermute | solution.py:27
  83.1 12.5 %collective-permute-start.17 = (bf16[2,96,384]{2,1,0:T(8,128)(2,1)S(1)}, bf16[2,96,384]{2,1,0:T(8,128)(2,1)}, u32[]{:S(2)}, u32[]{:S(2)}) collective-permute-start(bf16[2,96,384]{2,1,0:T(8,128)(2,1)S(1)} %shard_map.38.refs_0_), channel_id=1, source_target_pairs={{0,64},{4,452},{64,128},{68,4},{128,192},{132,68},{192,256},{196,1... | collective-permute-start | bytes 442376 | tf_op jit(solution)/shard_map/ppermute | solution.py:27
  86.3 9.3 %collective-permute-start.13 = (bf16[2,96,384]{2,1,0:T(8,128)(2,1)S(1)}, bf16[2,96,384]{2,1,0:T(8,128)(2,1)}, u32[]{:S(2)}, u32[]{:S(2)}) collective-permute-start(bf16[2,96,384]{2,1,0:T(8,128)(2,1)S(1)} %collective-permute-done.12.refs_2_), channel_id=1, source_target_pairs={{0,448},{4,68},{64,0},{68,132},{128,64},{132,196},{192,128},{196,2... | collective-permute-start | bytes 442376 | tf_op jit(solution)/shard_map/ppermute | solution.py:27
  88.4 10.7 %collective-permute-start.14 = (bf16[2,96,384]{2,1,0:T(8,128)(2,1)S(1)}, bf16[2,96,384]{2,1,0:T(8,128)(2,1)}, u32[]{:S(2)}, u32[]{:S(2)}) collective-permute-start(bf16[2,96,384]{2,1,0:T(8,128)(2,1)S(1)} %collective-permute-done.12.refs_2_), channel_id=1, source_target_pairs={{0,384},{4,132},{64,448},{68,196},{128,0},{132,260},{192,64},{196,... | collective-permute-start | bytes 442376 | tf_op jit(solution)/shard_map/ppermute | solution.py:27
  93.4 7.6 %collective-permute-start.16 = (bf16[2,96,384]{2,1,0:T(8,128)(2,1)S(1)}, bf16[2,96,384]{2,1,0:T(8,128)(2,1)}, u32[]{:S(2)}, u32[]{:S(2)}) collective-permute-start(bf16[2,96,384]{2,1,0:T(8,128)(2,1)S(1)} %collective-permute-done.15.refs_6_), channel_id=1, source_target_pairs={{0,64},{4,452},{64,128},{68,4},{128,192},{132,68},{192,256},{196,1... | collective-permute-start | bytes 442376 | tf_op jit(solution)/shard_map/ppermute | solution.py:27

commit v8 on v4

--- a/solution.py
+++ b/solution.py
@@ -34,36 +34,39 @@
     return piece, near_up, up, far_up, opposite, far_down, down, near_down
 
 
-def product(own_ref, other_ref, right_ref, start, count):
-    depth = own_ref.shape[0]
-    columns = right_ref.shape[-1]
-    rows = pl.ds(start, count)
-    own = lax.dot_general(
-        own_ref[:, rows], right_ref[0].reshape(depth, columns), CONTRACT, preferred_element_type=jnp.float32
-    )
-    other = lax.dot_general(
-        other_ref[:, rows], right_ref[1].reshape(depth, columns), CONTRACT, preferred_element_type=jnp.float32
-    )
-    return own + other
-
-
-def square_kernel(place_ref, own_ref, other_ref, right_ref, out_ref, ordered_ref, staged_ref, sems):
+def own_kernel(place_ref, own_ref, right_ref, total_ref, ordered_ref):
+    tiles, _, part, columns = right_ref.shape
+    z, core = place_ref[1], place_ref[2]
+    way = 1 - 2 * core
+    for offset in range(tiles):
+        ordered_ref[offset] = right_ref[lax.rem(z + way * offset + tiles, tiles), core]
+    right = ordered_ref[...].reshape(tiles * part, columns)
+    total_ref[...] = lax.dot_general(own_ref[...], right, CONTRACT, preferred_element_type=jnp.float32)
+
+
+def square_kernel(place_ref, total_ref, other_ref, right_ref, out_ref, ordered_ref, staged_ref, sems):
     halves, layers, part, columns = staged_ref.shape
     tiles = right_ref.shape[0]
     z, core = place_ref[1], place_ref[2]
     way = 1 - 2 * core
     for offset in range(tiles):
-        ordered_ref[0, offset] = right_ref[lax.rem(z + way * offset + tiles, tiles), core]
-        ordered_ref[1, offset] = right_ref[lax.rem(z - way * offset + tiles, tiles), 1 - core]
+        ordered_ref[offset] = right_ref[lax.rem(z - way * offset + tiles, tiles), 1 - core]
+    right = ordered_ref[...].reshape(tiles * part, columns)
     copies = []
     for half in range(halves):
-        count = layers * part
-        total = product(own_ref, other_ref, ordered_ref, half * count, count)
-        staged_ref[half] = total.astype(staged_ref.dtype).reshape(layers, part, columns)
+        rows = pl.ds(half * layers * part, layers * part)
+        term = lax.dot_general(other_ref[:, rows], right, CONTRACT, preferred_element_type=jnp.float32)
+        total = (total_ref[rows, :] + term).astype(staged_ref.dtype)
+        staged_ref[half] = total.reshape(layers, part, columns)
         copies.append(pltpu.make_async_copy(staged_ref.at[half], out_ref.at[:, half], sems.at[half]))
         copies[-1].start()
     for copy in copies:
         copy.wait()
+
+
+def turn_kernel(own_ref, other_ref, own_turned_ref, other_turned_ref):
+    own_turned_ref[...] = own_ref[...].T
+    other_turned_ref[...] = other_ref[...].T
 
 
 def filter_kernel(keep_ref, layer_ref, parts_ref, out_ref):
@@ -97,8 +100,11 @@
         own = lax.rem(way * distance + 2 * tiles, tiles)
         ordered_ref[0, own] = piece[core]
         ordered_ref[1, lax.rem(tiles - own, tiles)] = piece[1 - core]
-    total_ref[...] = scale_ref[0] * matrix_ref[...].astype(jnp.float32) - 0.5 * product(
-        own_ref, other_ref, ordered_ref, 0, matrix_ref.shape[0]
+    depth, columns = own_ref.shape[1], matrix_ref.shape[1]
+    total_ref[...] = jnp.dot(
+        own_ref[...], ordered_ref[0].reshape(depth, columns), preferred_element_type=jnp.float32
+    ) + jnp.dot(
+        other_ref[...], ordered_ref[1].reshape(depth, columns), preferred_element_type=jnp.float32
     )
     low = lax.broadcasted_iota(jnp.int32, (pairs, lanes), 1) < BLK
 
@@ -109,7 +115,8 @@
         column = index % half_blocks
         start = pl.multiple_of(index // half_blocks * BLK, BLK)
         lane = pl.multiple_of(column // 2 * lanes, lanes)
-        block = total_ref[pl.ds(start, BLK), pl.ds(lane, lanes)] * live
+        block = matrix_ref[pl.ds(start, BLK), pl.ds(lane, lanes)].astype(jnp.float32) * scale_ref[0]
+        block = (block - 0.5 * total_ref[pl.ds(start, BLK), pl.ds(lane, lanes)]) * live
         turned = pltpu.roll(block, BLK, 1)
         odd = column % 2 == 1
         slot = 2 * (owner % 2)
@@ -144,18 +151,43 @@
     left_other = lax.ppermute(left_own, "core", [(0, 1), (1, 0)])
     place = jnp.stack([row_index, z_index, core_index])
 
+    depth = left_own.shape[0]
+    ordered = pltpu.VMEM((rows_count, part, width), jnp.bfloat16)
+    cost = pl.CostEstimate(
+        flops=2 * tile_rows * width * depth, bytes_accessed=2 * depth * (tile_rows + width), transcendentals=0
+    )
+    own_total = pl.pallas_call(
+        own_kernel,
+        out_shape=jax.ShapeDtypeStruct((tile_rows, width), jnp.float32),
+        in_specs=[smem] + [vmem] * 2,
+        out_specs=vmem,
+        scratch_shapes=[ordered],
+        compiler_params=params,
+        cost_estimate=cost,
+    )(place, left_own, right)
     square_part = pl.pallas_call(
         square_kernel,
         out_shape=jax.ShapeDtypeStruct((layers, halves, part, width), jnp.bfloat16),
-        in_specs=[smem, vmem, vmem, vmem],
+        in_specs=[smem] + [vmem] * 3,
         out_specs=pl.BlockSpec(memory_space=pltpu.HBM),
         scratch_shapes=[
-            pltpu.VMEM((halves, rows_count, part, width), jnp.bfloat16),
+            ordered,
             pltpu.VMEM((halves, layers, part, width), jnp.bfloat16),
             pltpu.SemaphoreType.DMA((halves,)),
         ],
         compiler_params=params,
-    )(place, left_own, left_other, right)
+        cost_estimate=cost,
+    )(place, own_total, left_other, right)
+    left_own, left_other, square_part = lax.optimization_barrier((left_own, left_other, square_part))
+    turned = jax.ShapeDtypeStruct((tile_rows, depth), left_own.dtype)
+    left_own, left_other = pl.pallas_call(
+        turn_kernel,
+        out_shape=[turned] * 2,
+        in_specs=[vmem] * 2,
+        out_specs=[vmem] * 2,
+        compiler_params=params,
+        cost_estimate=cost,
+    )(left_own, left_other)
     parts = lax.all_to_all(square_part, "layer", split_axis=0, concat_axis=0, tiled=True)
     filtered_piece = pl.pallas_call(
         filter_kernel,

time: 133 us -> 131 us (0.985)
    pallas_call x0 -> x2, Pallas kernels: none -> 2.03 us  [the longest x1 1.37 us: on_device(): pl.pallas_call(own_kernel, out_shape=jax.ShapeDtypeStruct((tile_rows, wid...]
    ppermute x1, waiting for transfers between devices: 2.37 us -> 1 us  [on_device(): left_other = lax.ppermute(left_own, 'core', [(0, 1), (1, 0)])]
  transfers between devices with their start and end apart: 17 -> 17, of which waited for: 6 -> 6; matrix products, arithmetic and copies ran while one was open for 2% -> 1% of each run, Pallas kernels for 0% -> 2%
where the time goes in v8:
time: 131 us; the launch traced here: 130 us
  starting transfers between devices  72.1 us (55%)
  blocking collectives  26.5 us (20%)
  waiting for transfers between devices  19.3 us (15%)
  Pallas kernels  6.78 us (5%)
  local copies, waits for them, and re-layouts  5.15 us (4%)
    ppermute x14, starting transfers between devices, shifted(): return lax.ppermute(piece, (axis, 'core'), pairs)  50.8 us
    all_to_all x1, blocking collectives, on_device(): lax.all_to_all(outgoing, ('z', 'core'), split_axis=0, concat_axis=0, tile...  14.2 us
    all_to_all x1, blocking collectives, to_all(): return lax.all_to_all(copies, axis, split_axis=0, concat_axis=0, tiled=True)  12.3 us
    ppermute x1, starting transfers between devices, on_device(): left_other = lax.ppermute(left_own, 'core', [(0, 1), (1, 0)])  9.55 us
    all_to_all x1, waiting for transfers between devices, on_device(): lax.all_to_all(square_part, 'layer', split_axis=0, concat_axis=0, tiled=T...  9.51 us
    ppermute x14, waiting for transfers between devices, shifted(): return lax.ppermute(piece, (axis, 'core'), pairs)  8.78 us
    all_to_all x1, starting transfers between devices, to_all(): return lax.all_to_all(copies, axis, split_axis=0, concat_axis=0, tiled=True)  7.65 us
    all_to_all x1, starting transfers between devices, on_device(): lax.all_to_all(square_part, 'layer', split_axis=0, concat_axis=0, tiled=T...  4.15 us
  transfers between devices with their start and end apart: 17, of which 6 were waited for; matrix products, arithmetic and copies ran while one was open for 1% of the time, Pallas kernels for 2%

profile of v8, /device:TPU:1, one launch (start us, length us, event | category | flops | bytes accessed | tf_op | source)
XLA Modules:
  0.0 130.4 jit_solution(69590456239267735)
XLA Ops:
  0.0 0.9 dynamic-slice_bitcast_fusion
  0.9 1.2 broadcast_in_dim.14
  2.1 7.7 %all-to-all-start = ((bf16[8,2,96,384]{3,2,1,0:T(8,128)(2,1)}), bf16[8,2,96,384]{3,2,1,0:T(8,128)(2,1)S(1)}, u32[]{:S(2)}, u32[]{:S(2)}) async-start(bf16[8,2,96,384]{3,2,1,0:T(8,128)(2,1)} %broadcast_in_dim.14), calls=%async_computation | async-start | bytes 2359296 | tf_op jit(solution)/shard_map/all_to_all | solution.py:14
  9.8 1.1 constant_dynamic-slice_fusion
  10.9 0.1 copy.8
  11.0 4.0 %collective-permute-start = (bf16[96,768]{1,0:T(8,128)(2,1)S(1)}, bf16[96,768]{1,0:T(8,128)(2,1)S(1)}, u32[]{:S(2)}, u32[]{:S(2)}) collective-permute-start(bf16[96,768]{1,0:T(8,128)(2,1)S(1)} %bitcast.17), channel_id=1, source_target_pairs={{0,56},{4,12},{8,0},{12,20},{16,8},{20,28},{24,16},{28,36},{32,24}... | collective-permute-start | bytes 442376 | tf_op jit(solution)/shard_map/ppermute | solution.py:23
  15.0 5.8 %collective-permute-start.1 = (bf16[96,768]{1,0:T(8,128)(2,1)S(1)}, bf16[96,768]{1,0:T(8,128)(2,1)S(1)}, u32[]{:S(2)}, u32[]{:S(2)}) collective-permute-start(bf16[96,768]{1,0:T(8,128)(2,1)S(1)} %bitcast.18), channel_id=1, source_target_pairs={{0,48},{4,20},{8,56},{12,28},{16,0},{20,36},{24,8},{28,44},{32,16}... | collective-permute-start | bytes 442376 | tf_op jit(solution)/shard_map/ppermute | solution.py:23
  20.8 5.9 %collective-permute-start.4 = (bf16[96,768]{1,0:T(8,128)(2,1)S(1)}, bf16[96,768]{1,0:T(8,128)(2,1)S(1)}, u32[]{:S(2)}, u32[]{:S(2)}) collective-permute-start(bf16[96,768]{1,0:T(8,128)(2,1)S(1)} %bitcast.19), channel_id=1, source_target_pairs={{0,16},{4,52},{8,24},{12,60},{16,32},{20,4},{24,40},{28,12},{32,48... | collective-permute-start | bytes 442376 | tf_op jit(solution)/shard_map/ppermute | solution.py:23
  26.7 3.1 %collective-permute-start.6 = (bf16[96,768]{1,0:T(8,128)(2,1)S(1)}, bf16[96,768]{1,0:T(8,128)(2,1)S(1)}, u32[]{:S(2)}, u32[]{:S(2)}) collective-permute-start(bf16[96,768]{1,0:T(8,128)(2,1)S(1)} %bitcast.20), channel_id=1, source_target_pairs={{0,8},{4,60},{8,16},{12,4},{16,24},{20,12},{24,32},{28,20},{32,40}... | collective-permute-start | bytes 442376 | tf_op jit(solution)/shard_map/ppermute | solution.py:23
  29.8 0.0 collective-permute-done.1
  29.8 2.2 %collective-permute-start.2 = (bf16[96,768]{1,0:T(8,128)(2,1)S(1)}, bf16[96,768]{1,0:T(8,128)(2,1)S(1)}, u32[]{:S(2)}, u32[]{:S(2)}) collective-permute-start(bf16[96,768]{1,0:T(8,128)(2,1)S(1)} %collective-permute-done.1), channel_id=1, source_target_pairs={{0,56},{4,12},{8,0},{12,20},{16,8},{20,28},{24,16},{28,36},{32,24}... | collective-permute-start | bytes 442376 | tf_op jit(solution)/shard_map/ppermute | solution.py:23
  32.0 2.2 %collective-permute-start.3 = (bf16[96,768]{1,0:T(8,128)(2,1)S(1)}, bf16[96,768]{1,0:T(8,128)(2,1)S(1)}, u32[]{:S(2)}, u32[]{:S(2)}) collective-permute-start(bf16[96,768]{1,0:T(8,128)(2,1)S(1)} %collective-permute-done.1), channel_id=1, source_target_pairs={{0,48},{4,20},{8,56},{12,28},{16,0},{20,36},{24,8},{28,44},{32,16}... | collective-permute-start | bytes 442376 | tf_op jit(solution)/shard_map/ppermute | solution.py:23
  34.3 0.0 collective-permute-done.4
  34.3 4.3 %collective-permute-start.5 = (bf16[96,768]{1,0:T(8,128)(2,1)S(1)}, bf16[96,768]{1,0:T(8,128)(2,1)S(1)}, u32[]{:S(2)}, u32[]{:S(2)}) collective-permute-start(bf16[96,768]{1,0:T(8,128)(2,1)S(1)} %collective-permute-done.4), channel_id=1, source_target_pairs={{0,8},{4,60},{8,16},{12,4},{16,24},{20,12},{24,32},{28,20},{32,40}... | collective-permute-start | bytes 442376 | tf_op jit(solution)/shard_map/ppermute | solution.py:23
  38.6 0.1 collective-permute-done.2
  38.6 1.9 %collective-permute-done.3 = bf16[96,768]{1,0:T(8,128)(2,1)S(1)} collective-permute-done((bf16[96,768]{1,0:T(8,128)(2,1)S(1)}, bf16[96,768]{1,0:T(8,128)(2,1)S(1)}, u32[]{:S(2)}, u32[]{:S(2)}) %collective-permute-start.3) | collective-permute-done | bytes 147488 | tf_op jit(solution)/shard_map/ppermute | solution.py:23
  40.5 1.5 %collective-permute-done.5 = bf16[96,768]{1,0:T(8,128)(2,1)S(1)} collective-permute-done((bf16[96,768]{1,0:T(8,128)(2,1)S(1)}, bf16[96,768]{1,0:T(8,128)(2,1)S(1)}, u32[]{:S(2)}, u32[]{:S(2)}) %collective-permute-start.5) | collective-permute-done | bytes 147488 | tf_op jit(solution)/shard_map/ppermute | solution.py:23
  42.0 0.0 all-to-all-done.right_ref
  42.1 9.6 %collective-permute-start.7 = (bf16[768,768]{1,0:T(8,128)(2,1)S(1)}, bf16[768,768]{1,0:T(8,128)(2,1)S(1)}, u32[]{:S(2)}, u32[]{:S(2)}) collective-permute-start(bf16[768,768]{1,0:T(8,128)(2,1)S(1)} %constant_dynamic-update-slice_fusion.own_ref), channel_id=1, source_target_pairs={{0,4},{4,0},{1,5},{5,1},{2,6},{6,2},{3,7},{7,3},{8,12},{12,8},{9,1... | collective-permute-start | bytes 3538952 | tf_op jit(solution)/shard_map/ppermute | solution.py:151
  51.6 0.1 pad_add_fusion.place_ref
  51.7 1.4 %shard_map.37.total_ref = f32[768,384]{1,0:T(8,128)S(1)} custom-call(s32[3]{0:T(128)S(1)} %pad_add_fusion.place_ref, bf16[768,768]{1,0:T(8,128)(2,1)S(1)} %constant_dynamic-update-slice_fusion.own_ref, bf16[8,2,96,384]{3,2,1,0:T(8,128)(2,1)S(1)} %all-to-all-done.right_ref), custom_call_target="tpu_custom_call" | custom-call | flops 452984832 | bytes 1769472 | tf_op jit(solution)/shard_map/pallas_call | solution.py:159
  53.1 1.0 collective-permute-done.7.other_ref
  54.1 1.6 %shard_map.38 = bf16[4,2,96,384]{3,2,1,0:T(8,128)(2,1)S(1)} custom-call(s32[3]{0:T(128)S(1)} %pad_add_fusion.place_ref, f32[768,384]{1,0:T(8,128)S(1)} %shard_map.37.total_ref, bf16[768,768]{1,0:T(8,128)(2,1)S(1)} %collective-permute-done.7.other_ref, bf16[8,2,96,384]{3,2,1,0:T(8,128)(2,1)S(1)} %all-to-all-done.right_ref), custom_call_target="tpu_custom_call" | custom-call | flops 452984832 | bytes 1769472 | tf_op jit(solution)/shard_map/pallas_call | solution.py:168
  55.7 0.8 copy-done
  56.5 4.1 %all-to-all-start.1 = ((bf16[4,2,96,384]{3,2,1,0:T(8,128)(2,1)}), bf16[4,2,96,384]{3,2,1,0:T(8,128)(2,1)S(1)}, u32[]{:S(2)}, u32[]{:S(2)}) async-start(bf16[4,2,96,384]{3,2,1,0:T(8,128)(2,1)} %copy-done), calls=%async_computation.1 | async-start | bytes 1179648 | tf_op jit(solution)/shard_map/all_to_all | solution.py:191
  60.7 0.1 copy.7.keep_ref
  60.8 9.5 %all-to-all-done.1.parts_ref = bf16[4,2,96,384]{3,2,1,0:T(8,128)(2,1)S(1)} async-done(((bf16[4,2,96,384]{3,2,1,0:T(8,128)(2,1)}), bf16[4,2,96,384]{3,2,1,0:T(8,128)(2,1)S(1)}, u32[]{:S(2)}, u32[]{:S(2)}) %all-to-all-start.1) | async-done | bytes 589856 | tf_op jit(solution)/shard_map/all_to_all | solution.py:191
  70.3 0.8 shard_map.40.refs_0_
  71.1 4.4 %collective-permute-start.9 = (bf16[2,96,384]{2,1,0:T(8,128)(2,1)S(1)}, bf16[2,96,384]{2,1,0:T(8,128)(2,1)S(1)}, u32[]{:S(2)}, u32[]{:S(2)}) collective-permute-start(bf16[2,96,384]{2,1,0:T(8,128)(2,1)S(1)} %shard_map.40.refs_0_), channel_id=1, source_target_pairs={{0,384},{4,132},{64,448},{68,196},{128,0},{132,260},{192,64},{196,... | collective-permute-start | bytes 442376 | tf_op jit(solution)/shard_map/ppermute | solution.py:23
  75.5 3.1 %collective-permute-start.12 = (bf16[2,96,384]{2,1,0:T(8,128)(2,1)S(1)}, bf16[2,96,384]{2,1,0:T(8,128)(2,1)S(1)}, u32[]{:S(2)}, u32[]{:S(2)}) collective-permute-start(bf16[2,96,384]{2,1,0:T(8,128)(2,1)S(1)} %shard_map.40.refs_0_), channel_id=1, source_target_pairs={{0,128},{4,388},{64,192},{68,452},{128,256},{132,4},{192,320},{196... | collective-permute-start | bytes 442376 | tf_op jit(solution)/shard_map/ppermute | solution.py:23
  78.7 3.3 %collective-permute-start.14 = (bf16[2,96,384]{2,1,0:T(8,128)(2,1)S(1)}, bf16[2,96,384]{2,1,0:T(8,128)(2,1)S(1)}, u32[]{:S(2)}, u32[]{:S(2)}) collective-permute-start(bf16[2,96,384]{2,1,0:T(8,128)(2,1)S(1)} %shard_map.40.refs_0_), channel_id=1, source_target_pairs={{0,64},{4,452},{64,128},{68,4},{128,192},{132,68},{192,256},{196,1... | collective-permute-start | bytes 442376 | tf_op jit(solution)/shard_map/ppermute | solution.py:23
  82.0 1.9 %collective-permute-start.8 = (bf16[2,96,384]{2,1,0:T(8,128)(2,1)S(1)}, bf16[2,96,384]{2,1,0:T(8,128)(2,1)S(1)}, u32[]{:S(2)}, u32[]{:S(2)}) collective-permute-start(bf16[2,96,384]{2,1,0:T(8,128)(2,1)S(1)} %shard_map.40.refs_0_), channel_id=1, source_target_pairs={{0,448},{4,68},{64,0},{68,132},{128,64},{132,196},{192,128},{196,2... | collective-permute-start | bytes 442376 | tf_op jit(solution)/shard_map/ppermute | solution.py:23
  84.0 0.0 collective-permute-done.9.refs_2_
  84.0 3.4 %collective-permute-start.10 = (bf16[2,96,384]{2,1,0:T(8,128)(2,1)S(1)}, bf16[2,96,384]{2,1,0:T(8,128)(2,1)S(1)}, u32[]{:S(2)}, u32[]{:S(2)}) collective-permute-start(bf16[2,96,384]{2,1,0:T(8,128)(2,1)S(1)} %collective-permute-done.9.refs_2_), channel_id=1, source_target_pairs={{0,448},{4,68},{64,0},{68,132},{128,64},{132,196},{192,128},{196,2... | collective-permute-start | bytes 442376 | tf_op jit(solution)/shard_map/ppermute | solution.py:23
  87.3 4.9 %collective-permute-start.11 = (bf16[2,96,384]{2,1,0:T(8,128)(2,1)S(1)}, bf16[2,96,384]{2,1,0:T(8,128)(2,1)S(1)}, u32[]{:S(2)}, u32[]{:S(2)}) collective-permute-start(bf16[2,96,384]{2,1,0:T(8,128)(2,1)S(1)} %collective-permute-done.9.refs_2_), channel_id=1, source_target_pairs={{0,384},{4,132},{64,448},{68,196},{128,0},{132,260},{192,64},{196,... | collective-permute-start | bytes 442376 | tf_op jit(solution)/shard_map/ppermute | solution.py:23
  92.3 2.2 %collective-permute-start.13 = (bf16[2,96,384]{2,1,0:T(8,128)(2,1)S(1)}, bf16[2,96,384]{2,1,0:T(8,128)(2,1)S(1)}, u32[]{:S(2)}, u32[]{:S(2)}) collective-permute-start(bf16[2,96,384]{2,1,0:T(8,128)(2,1)S(1)} %collective-permute-done.12.refs_6_), channel_id=1, source_target_pairs={{0,64},{4,452},{64,128},{68,4},{128,192},{132,68},{192,256},{196,1... | collective-permute-start | bytes 442376 | tf_op jit(solution)/shard_map/ppermute | solution.py:23
  94.5 0.0 copy-start.1
  94.5 0.0 copy-start.2
  94.5 0.7 shard_map.39
  95.2 0.0 collective-permute-done.8.refs_1_
  95.2 1.3 collective-permute-done.11.refs_4_
  96.5 4.1 %collective-permute-done.13.refs_5_ = bf16[2,96,384]{2,1,0:T(8,128)(2,1)S(1)} collective-permute-done((bf16[2,96,384]{2,1,0:T(8,128)(2,1)S(1)}, bf16[2,96,384]{2,1,0:T(8,128)(2,1)S(1)}, u32[]{:S(2)}, u32[]{:S(2)}) %collective-permute-start.13) | collective-permute-done | bytes 147488 | tf_op jit(solution)/shard_map/ppermute | solution.py:23
  100.6 2.4 %shard_map.41 = bf16[16,32,128]{2,1,0:T(8,128)(2,1)S(1)} custom-call(s32[16]{0:T(128)S(1)} %bitcast.16, s32[3]{0:T(128)S(1)} %pad_add_fusion.place_ref, f32[1]{0:T(128)} %bitcast.4.scale_ref, bf16[768,768]{1,0:T(8,128)(2,1)S(1)} %get-tuple-element.16.own_ref, bf16[768,768]{1,0:T(8,128)(2,1)S(1)} %get-tuple-element.17.other_ref, ...), custom_call_target="tpu_custom_call" | custom-call | tf_op jit(solution)/shard_map/pallas_call | solution.py:204
  103.0 14.2 %all_to_all.20 = bf16[16,32,128]{2,1,0:T(8,128)(2,1)S(1)} all-to-all(bf16[16,32,128]{2,1,0:T(8,128)(2,1)S(1)} %shard_map.41), channel_id=1, replica_groups=mesh['row'=8,'z'=8,'core'=2,'layer'=4] {'z','core'}, dimensions={0} | all-to-all | bytes 262144 | tf_op jit(solution)/shard_map/all_to_all | solution.py:216
  117.2 0.1 broadcast_in_dim.15
  117.3 12.3 %all_to_all.21 = bf16[4,16,32,128]{3,2,1,0:T(8,128)(2,1)S(1)} all-to-all(bf16[4,16,32,128]{3,2,1,0:T(8,128)(2,1)S(1)} %broadcast_in_dim.15), channel_id=1, replica_groups=mesh['row'=8,'z'=8,'core'=2,'layer'=4] {'layer'}, dimensions={0} | all-to-all | bytes 1048576 | tf_op jit(solution)/shard_map/all_to_all | solution.py:14
  129.6 0.1 reduce_sum.12
  129.6 0.7 copy.11
  (18 shorter events, 0.1 us)
Async XLA Ops:
  2.1 40.0 %all-to-all-start = ((bf16[8,2,96,384]{3,2,1,0:T(8,128)(2,1)}), bf16[8,2,96,384]{3,2,1,0:T(8,128)(2,1)S(1)}, u32[]{:S(2)}, u32[]{:S(2)}) async-start(bf16[8,2,96,384]{3,2,1,0:T(8,128)(2,1)} %broadcast_in_dim.14), calls=%async_computation | async-start | bytes 2359296 | tf_op jit(solution)/shard_map/all_to_all | solution.py:14
  11.0 23.2 %collective-permute-start = (bf16[96,768]{1,0:T(8,128)(2,1)S(1)}, bf16[96,768]{1,0:T(8,128)(2,1)S(1)}, u32[]{:S(2)}, u32[]{:S(2)}) collective-permute-start(bf16[96,768]{1,0:T(8,128)(2,1)S(1)} %bitcast.17), channel_id=1, source_target_pairs={{0,56},{4,12},{8,0},{12,20},{16,8},{20,28},{24,16},{28,36},{32,24}... | collective-permute-start | bytes 442376 | tf_op jit(solution)/shard_map/ppermute | solution.py:23
  15.0 14.8 %collective-permute-start.1 = (bf16[96,768]{1,0:T(8,128)(2,1)S(1)}, bf16[96,768]{1,0:T(8,128)(2,1)S(1)}, u32[]{:S(2)}, u32[]{:S(2)}) collective-permute-start(bf16[96,768]{1,0:T(8,128)(2,1)S(1)} %bitcast.18), channel_id=1, source_target_pairs={{0,48},{4,20},{8,56},{12,28},{16,0},{20,36},{24,8},{28,44},{32,16}... | collective-permute-start | bytes 442376 | tf_op jit(solution)/shard_map/ppermute | solution.py:23
  20.8 13.4 %collective-permute-start.4 = (bf16[96,768]{1,0:T(8,128)(2,1)S(1)}, bf16[96,768]{1,0:T(8,128)(2,1)S(1)}, u32[]{:S(2)}, u32[]{:S(2)}) collective-permute-start(bf16[96,768]{1,0:T(8,128)(2,1)S(1)} %bitcast.19), channel_id=1, source_target_pairs={{0,16},{4,52},{8,24},{12,60},{16,32},{20,4},{24,40},{28,12},{32,48... | collective-permute-start | bytes 442376 | tf_op jit(solution)/shard_map/ppermute | solution.py:23
  26.7 15.3 %collective-permute-start.6 = (bf16[96,768]{1,0:T(8,128)(2,1)S(1)}, bf16[96,768]{1,0:T(8,128)(2,1)S(1)}, u32[]{:S(2)}, u32[]{:S(2)}) collective-permute-start(bf16[96,768]{1,0:T(8,128)(2,1)S(1)} %bitcast.20), channel_id=1, source_target_pairs={{0,8},{4,60},{8,16},{12,4},{16,24},{20,12},{24,32},{28,20},{32,40}... | collective-permute-start | bytes 442376 | tf_op jit(solution)/shard_map/ppermute | solution.py:23
  29.8 8.8 %collective-permute-start.2 = (bf16[96,768]{1,0:T(8,128)(2,1)S(1)}, bf16[96,768]{1,0:T(8,128)(2,1)S(1)}, u32[]{:S(2)}, u32[]{:S(2)}) collective-permute-start(bf16[96,768]{1,0:T(8,128)(2,1)S(1)} %collective-permute-done.1), channel_id=1, source_target_pairs={{0,56},{4,12},{8,0},{12,20},{16,8},{20,28},{24,16},{28,36},{32,24}... | collective-permute-start | bytes 442376 | tf_op jit(solution)/shard_map/ppermute | solution.py:23
  32.0 8.5 %collective-permute-start.3 = (bf16[96,768]{1,0:T(8,128)(2,1)S(1)}, bf16[96,768]{1,0:T(8,128)(2,1)S(1)}, u32[]{:S(2)}, u32[]{:S(2)}) collective-permute-start(bf16[96,768]{1,0:T(8,128)(2,1)S(1)} %collective-permute-done.1), channel_id=1, source_target_pairs={{0,48},{4,20},{8,56},{12,28},{16,0},{20,36},{24,8},{28,44},{32,16}... | collective-permute-start | bytes 442376 | tf_op jit(solution)/shard_map/ppermute | solution.py:23
  34.3 7.7 %collective-permute-start.5 = (bf16[96,768]{1,0:T(8,128)(2,1)S(1)}, bf16[96,768]{1,0:T(8,128)(2,1)S(1)}, u32[]{:S(2)}, u32[]{:S(2)}) collective-permute-start(bf16[96,768]{1,0:T(8,128)(2,1)S(1)} %collective-permute-done.4), channel_id=1, source_target_pairs={{0,8},{4,60},{8,16},{12,4},{16,24},{20,12},{24,32},{28,20},{32,40}... | collective-permute-start | bytes 442376 | tf_op jit(solution)/shard_map/ppermute | solution.py:23
  42.1 12.0 %collective-permute-start.7 = (bf16[768,768]{1,0:T(8,128)(2,1)S(1)}, bf16[768,768]{1,0:T(8,128)(2,1)S(1)}, u32[]{:S(2)}, u32[]{:S(2)}) collective-permute-start(bf16[768,768]{1,0:T(8,128)(2,1)S(1)} %constant_dynamic-update-slice_fusion.own_ref), channel_id=1, source_target_pairs={{0,4},{4,0},{1,5},{5,1},{2,6},{6,2},{3,7},{7,3},{8,12},{12,8},{9,1... | collective-permute-start | bytes 3538952 | tf_op jit(solution)/shard_map/ppermute | solution.py:151
  55.7 0.8 copy-start
  56.5 4.2 %copy-start.3 = (s32[12,6]{0,1:T(8,128)S(1)}, s32[12,6]{0,1:T(8,128)}, u32[]{:S(2)}) copy-start(s32[12,6]{0,1:T(8,128)} %param.4) | copy-start | bytes 868
  56.5 13.8 %all-to-all-start.1 = ((bf16[4,2,96,384]{3,2,1,0:T(8,128)(2,1)}), bf16[4,2,96,384]{3,2,1,0:T(8,128)(2,1)S(1)}, u32[]{:S(2)}, u32[]{:S(2)}) async-start(bf16[4,2,96,384]{3,2,1,0:T(8,128)(2,1)} %copy-done), calls=%async_computation.1 | async-start | bytes 1179648 | tf_op jit(solution)/shard_map/all_to_all | solution.py:191
  71.1 12.9 %collective-permute-start.9 = (bf16[2,96,384]{2,1,0:T(8,128)(2,1)S(1)}, bf16[2,96,384]{2,1,0:T(8,128)(2,1)S(1)}, u32[]{:S(2)}, u32[]{:S(2)}) collective-permute-start(bf16[2,96,384]{2,1,0:T(8,128)(2,1)S(1)} %shard_map.40.refs_0_), channel_id=1, source_target_pairs={{0,384},{4,132},{64,448},{68,196},{128,0},{132,260},{192,64},{196,... | collective-permute-start | bytes 442376 | tf_op jit(solution)/shard_map/ppermute | solution.py:23
  75.5 16.8 %collective-permute-start.12 = (bf16[2,96,384]{2,1,0:T(8,128)(2,1)S(1)}, bf16[2,96,384]{2,1,0:T(8,128)(2,1)S(1)}, u32[]{:S(2)}, u32[]{:S(2)}) collective-permute-start(bf16[2,96,384]{2,1,0:T(8,128)(2,1)S(1)} %shard_map.40.refs_0_), channel_id=1, source_target_pairs={{0,128},{4,388},{64,192},{68,452},{128,256},{132,4},{192,320},{196... | collective-permute-start | bytes 442376 | tf_op jit(solution)/shard_map/ppermute | solution.py:23
  78.7 16.5 %collective-permute-start.14 = (bf16[2,96,384]{2,1,0:T(8,128)(2,1)S(1)}, bf16[2,96,384]{2,1,0:T(8,128)(2,1)S(1)}, u32[]{:S(2)}, u32[]{:S(2)}) collective-permute-start(bf16[2,96,384]{2,1,0:T(8,128)(2,1)S(1)} %shard_map.40.refs_0_), channel_id=1, source_target_pairs={{0,64},{4,452},{64,128},{68,4},{128,192},{132,68},{192,256},{196,1... | collective-permute-start | bytes 442376 | tf_op jit(solution)/shard_map/ppermute | solution.py:23
  82.0 13.2 %collective-permute-start.8 = (bf16[2,96,384]{2,1,0:T(8,128)(2,1)S(1)}, bf16[2,96,384]{2,1,0:T(8,128)(2,1)S(1)}, u32[]{:S(2)}, u32[]{:S(2)}) collective-permute-start(bf16[2,96,384]{2,1,0:T(8,128)(2,1)S(1)} %shard_map.40.refs_0_), channel_id=1, source_target_pairs={{0,448},{4,68},{64,0},{68,132},{128,64},{132,196},{192,128},{196,2... | collective-permute-start | bytes 442376 | tf_op jit(solution)/shard_map/ppermute | solution.py:23
  84.0 11.2 %collective-permute-start.10 = (bf16[2,96,384]{2,1,0:T(8,128)(2,1)S(1)}, bf16[2,96,384]{2,1,0:T(8,128)(2,1)S(1)}, u32[]{:S(2)}, u32[]{:S(2)}) collective-permute-start(bf16[2,96,384]{2,1,0:T(8,128)(2,1)S(1)} %collective-permute-done.9.refs_2_), channel_id=1, source_target_pairs={{0,448},{4,68},{64,0},{68,132},{128,64},{132,196},{192,128},{196,2... | collective-permute-start | bytes 442376 | tf_op jit(solution)/shard_map/ppermute | solution.py:23
  87.3 9.1 %collective-permute-start.11 = (bf16[2,96,384]{2,1,0:T(8,128)(2,1)S(1)}, bf16[2,96,384]{2,1,0:T(8,128)(2,1)S(1)}, u32[]{:S(2)}, u32[]{:S(2)}) collective-permute-start(bf16[2,96,384]{2,1,0:T(8,128)(2,1)S(1)} %collective-permute-done.9.refs_2_), channel_id=1, source_target_pairs={{0,384},{4,132},{64,448},{68,196},{128,0},{132,260},{192,64},{196,... | collective-permute-start | bytes 442376 | tf_op jit(solution)/shard_map/ppermute | solution.py:23
  92.3 8.3 %collective-permute-start.13 = (bf16[2,96,384]{2,1,0:T(8,128)(2,1)S(1)}, bf16[2,96,384]{2,1,0:T(8,128)(2,1)S(1)}, u32[]{:S(2)}, u32[]{:S(2)}) collective-permute-start(bf16[2,96,384]{2,1,0:T(8,128)(2,1)S(1)} %collective-permute-done.12.refs_6_), channel_id=1, source_target_pairs={{0,64},{4,452},{64,128},{68,4},{128,192},{132,68},{192,256},{196,1... | collective-permute-start | bytes 442376 | tf_op jit(solution)/shard_map/ppermute | solution.py:23
  94.5 6.1 %copy-start.1 = (bf16[768,384]{1,0:T(8,128)(2,1)S(1)}, bf16[768,384]{1,0:T(8,128)(2,1)}, u32[]{:S(2)}) copy-start(bf16[768,384]{1,0:T(8,128)(2,1)} %matrix_ref.1) | copy-start | bytes 1769476
  94.5 6.1 %copy-start.2 = (s32[1,16]{1,0:T(1,128)S(1)}, s32[1,16]{1,0:T(1,128)}, u32[]{:S(2)}) copy-start(s32[1,16]{1,0:T(1,128)} %param.5) | copy-start | bytes 196

commit v9 on v8

--- a/solution.py
+++ b/solution.py
@@ -24,13 +24,13 @@
 
 
 def ring_of_eight(piece, axis):
-    up = shifted(piece, axis, 2)
-    down = shifted(piece, axis, -2)
     near_up = shifted(piece, axis, 1)
     near_down = shifted(piece, axis, -1)
+    up = shifted(near_up, axis, 1)
+    down = shifted(near_down, axis, -1)
     far_up = shifted(up, axis, 1)
     far_down = shifted(down, axis, -1)
-    opposite = shifted(up, axis, 2)
+    opposite = shifted(far_up, axis, 1)
     return piece, near_up, up, far_up, opposite, far_down, down, near_down
 
 

time: 131 us -> 143 us (1.092)
  waiting for transfers between devices: 19.3 us -> 31 us
  blocking collectives: 26.5 us -> 29.2 us
  starting transfers between devices: 72.1 us -> 70.2 us
    ppermute x14, waiting for transfers between devices: 8.78 us -> 20.5 us  [shifted(): return lax.ppermute(piece, (axis, 'core'), pairs)]
    ppermute x14, starting transfers between devices: 50.8 us -> 47.7 us  [shifted(): return lax.ppermute(piece, (axis, 'core'), pairs)]
    all_to_all x1, blocking collectives: 14.2 us -> 16.9 us  [on_device(): lax.all_to_all(outgoing, ('z', 'core'), split_axis=0, concat_axis=0, tile...]
  transfers between devices with their start and end apart: 17 -> 17, of which waited for: 6 -> 12; matrix products, arithmetic and copies ran while one was open for 1% -> 1% of each run, Pallas kernels for 2% -> 1%
where the time goes in v9:
time: 143 us
  starting transfers between devices  70.2 us (49%)
  waiting for transfers between devices  31 us (22%)
  blocking collectives  29.2 us (20%)
  Pallas kernels  6.78 us (5%)
  local copies, waits for them, and re-layouts  5.15 us (4%)
    ppermute x14, starting transfers between devices, shifted(): return lax.ppermute(piece, (axis, 'core'), pairs)  47.7 us
    ppermute x14, waiting for transfers between devices, shifted(): return lax.ppermute(piece, (axis, 'core'), pairs)  20.5 us
    all_to_all x1, blocking collectives, on_device(): lax.all_to_all(outgoing, ('z', 'core'), split_axis=0, concat_axis=0, tile...  16.9 us
    all_to_all x1, blocking collectives, to_all(): return lax.all_to_all(copies, axis, split_axis=0, concat_axis=0, tiled=True)  12.3 us
    ppermute x1, starting transfers between devices, on_device(): left_other = lax.ppermute(left_own, 'core', [(0, 1), (1, 0)])  10.7 us
    all_to_all x1, waiting for transfers between devices, on_device(): lax.all_to_all(square_part, 'layer', split_axis=0, concat_axis=0, tiled=T...  9.5 us
    all_to_all x1, starting transfers between devices, to_all(): return lax.all_to_all(copies, axis, split_axis=0, concat_axis=0, tiled=True)  7.65 us
    all_to_all x1, starting transfers between devices, on_device(): lax.all_to_all(square_part, 'layer', split_axis=0, concat_axis=0, tiled=T...  4.14 us
  transfers between devices with their start and end apart: 17, of which 12 were waited for; matrix products, arithmetic and copies ran while one was open for 1% of the time, Pallas kernels for 1%

profile of v9, /device:TPU:1, one launch (start us, length us, event | category | flops | bytes accessed | tf_op | source)
XLA Modules:
  0.0 142.7 jit_solution(15712776374807664679)
XLA Ops:
  0.0 0.9 dynamic-slice_bitcast_fusion
  0.9 1.2 broadcast_in_dim.14
  2.1 7.7 %all-to-all-start = ((bf16[8,2,96,384]{3,2,1,0:T(8,128)(2,1)}), bf16[8,2,96,384]{3,2,1,0:T(8,128)(2,1)S(1)}, u32[]{:S(2)}, u32[]{:S(2)}) async-start(bf16[8,2,96,384]{3,2,1,0:T(8,128)(2,1)} %broadcast_in_dim.14), calls=%async_computation | async-start | bytes 2359296 | tf_op jit(solution)/shard_map/all_to_all | solution.py:14
  9.8 1.1 constant_dynamic-slice_fusion
  10.9 0.1 copy.8
  11.0 4.0 %collective-permute-start = (bf16[96,768]{1,0:T(8,128)(2,1)S(1)}, bf16[96,768]{1,0:T(8,128)(2,1)S(1)}, u32[]{:S(2)}, u32[]{:S(2)}) collective-permute-start(bf16[96,768]{1,0:T(8,128)(2,1)S(1)} %bitcast.17), channel_id=1, source_target_pairs={{0,56},{4,12},{8,0},{12,20},{16,8},{20,28},{24,16},{28,36},{32,24}... | collective-permute-start | bytes 442376 | tf_op jit(solution)/shard_map/ppermute | solution.py:23
  15.0 9.5 %collective-permute-done = bf16[96,768]{1,0:T(8,128)(2,1)S(1)} collective-permute-done((bf16[96,768]{1,0:T(8,128)(2,1)S(1)}, bf16[96,768]{1,0:T(8,128)(2,1)S(1)}, u32[]{:S(2)}, u32[]{:S(2)}) %collective-permute-start) | collective-permute-done | bytes 147488 | tf_op jit(solution)/shard_map/ppermute | solution.py:23
  24.5 1.9 %collective-permute-start.1 = (bf16[96,768]{1,0:T(8,128)(2,1)S(1)}, bf16[96,768]{1,0:T(8,128)(2,1)S(1)}, u32[]{:S(2)}, u32[]{:S(2)}) collective-permute-start(bf16[96,768]{1,0:T(8,128)(2,1)S(1)} %collective-permute-done), channel_id=1, source_target_pairs={{0,56},{4,12},{8,0},{12,20},{16,8},{20,28},{24,16},{28,36},{32,24}... | collective-permute-start | bytes 442376 | tf_op jit(solution)/shard_map/ppermute | solution.py:23
  26.4 4.6 %collective-permute-start.4 = (bf16[96,768]{1,0:T(8,128)(2,1)S(1)}, bf16[96,768]{1,0:T(8,128)(2,1)S(1)}, u32[]{:S(2)}, u32[]{:S(2)}) collective-permute-start(bf16[96,768]{1,0:T(8,128)(2,1)S(1)} %bitcast.18), channel_id=1, source_target_pairs={{0,8},{4,60},{8,16},{12,4},{16,24},{20,12},{24,32},{28,20},{32,40}... | collective-permute-start | bytes 442376 | tf_op jit(solution)/shard_map/ppermute | solution.py:23
  31.0 0.9 collective-permute-done.1
  31.9 1.9 %collective-permute-start.2 = (bf16[96,768]{1,0:T(8,128)(2,1)S(1)}, bf16[96,768]{1,0:T(8,128)(2,1)S(1)}, u32[]{:S(2)}, u32[]{:S(2)}) collective-permute-start(bf16[96,768]{1,0:T(8,128)(2,1)S(1)} %collective-permute-done.1), channel_id=1, source_target_pairs={{0,56},{4,12},{8,0},{12,20},{16,8},{20,28},{24,16},{28,36},{32,24}... | collective-permute-start | bytes 442376 | tf_op jit(solution)/shard_map/ppermute | solution.py:23
  33.8 0.5 collective-permute-done.4
  34.3 5.3 %collective-permute-start.5 = (bf16[96,768]{1,0:T(8,128)(2,1)S(1)}, bf16[96,768]{1,0:T(8,128)(2,1)S(1)}, u32[]{:S(2)}, u32[]{:S(2)}) collective-permute-start(bf16[96,768]{1,0:T(8,128)(2,1)S(1)} %collective-permute-done.4), channel_id=1, source_target_pairs={{0,8},{4,60},{8,16},{12,4},{16,24},{20,12},{24,32},{28,20},{32,40}... | collective-permute-start | bytes 442376 | tf_op jit(solution)/shard_map/ppermute | solution.py:23
  39.6 1.0 collective-permute-done.2
  40.6 1.9 %collective-permute-start.3 = (bf16[96,768]{1,0:T(8,128)(2,1)S(1)}, bf16[96,768]{1,0:T(8,128)(2,1)S(1)}, u32[]{:S(2)}, u32[]{:S(2)}) collective-permute-start(bf16[96,768]{1,0:T(8,128)(2,1)S(1)} %collective-permute-done.2), channel_id=1, source_target_pairs={{0,56},{4,12},{8,0},{12,20},{16,8},{20,28},{24,16},{28,36},{32,24}... | collective-permute-start | bytes 442376 | tf_op jit(solution)/shard_map/ppermute | solution.py:23
  42.5 4.8 %collective-permute-start.6 = (bf16[96,768]{1,0:T(8,128)(2,1)S(1)}, bf16[96,768]{1,0:T(8,128)(2,1)S(1)}, u32[]{:S(2)}, u32[]{:S(2)}) collective-permute-start(bf16[96,768]{1,0:T(8,128)(2,1)S(1)} %collective-permute-done.5), channel_id=1, source_target_pairs={{0,8},{4,60},{8,16},{12,4},{16,24},{20,12},{24,32},{28,20},{32,40}... | collective-permute-start | bytes 442376 | tf_op jit(solution)/shard_map/ppermute | solution.py:23
  47.4 1.6 %collective-permute-done.3 = bf16[96,768]{1,0:T(8,128)(2,1)S(1)} collective-permute-done((bf16[96,768]{1,0:T(8,128)(2,1)S(1)}, bf16[96,768]{1,0:T(8,128)(2,1)S(1)}, u32[]{:S(2)}, u32[]{:S(2)}) %collective-permute-start.3) | collective-permute-done | bytes 147488 | tf_op jit(solution)/shard_map/ppermute | solution.py:23
  49.0 0.4 collective-permute-done.6
  49.5 10.7 %collective-permute-start.7 = (bf16[768,768]{1,0:T(8,128)(2,1)S(1)}, bf16[768,768]{1,0:T(8,128)(2,1)S(1)}, u32[]{:S(2)}, u32[]{:S(2)}) collective-permute-start(bf16[768,768]{1,0:T(8,128)(2,1)S(1)} %constant_dynamic-update-slice_fusion.own_ref), channel_id=1, source_target_pairs={{0,4},{4,0},{1,5},{5,1},{2,6},{6,2},{3,7},{7,3},{8,12},{12,8},{9,1... | collective-permute-start | bytes 3538952 | tf_op jit(solution)/shard_map/ppermute | solution.py:151
  60.2 0.1 pad_add_fusion.place_ref
  60.2 1.4 shard_map.37.total_ref
  61.6 1.0 collective-permute-done.7.other_ref
  62.6 1.6 %shard_map.38 = bf16[4,2,96,384]{3,2,1,0:T(8,128)(2,1)S(1)} custom-call(s32[3]{0:T(128)S(1)} %pad_add_fusion.place_ref, f32[768,384]{1,0:T(8,128)S(1)} %shard_map.37.total_ref, bf16[768,768]{1,0:T(8,128)(2,1)S(1)} %collective-permute-done.7.other_ref, bf16[8,2,96,384]{3,2,1,0:T(8,128)(2,1)S(1)} %all-to-all-done.right_ref), custom_call_target="tpu_custom_call" | custom-call | flops 452984832 | bytes 1769472 | tf_op jit(solution)/shard_map/pallas_call | solution.py:168
  64.3 0.8 copy-done
  65.1 4.1 %all-to-all-start.1 = ((bf16[4,2,96,384]{3,2,1,0:T(8,128)(2,1)}), bf16[4,2,96,384]{3,2,1,0:T(8,128)(2,1)S(1)}, u32[]{:S(2)}, u32[]{:S(2)}) async-start(bf16[4,2,96,384]{3,2,1,0:T(8,128)(2,1)} %copy-done), calls=%async_computation.1 | async-start | bytes 1179648 | tf_op jit(solution)/shard_map/all_to_all | solution.py:191
  69.2 0.1 copy.7.keep_ref
  69.3 9.5 %all-to-all-done.1.parts_ref = bf16[4,2,96,384]{3,2,1,0:T(8,128)(2,1)S(1)} async-done(((bf16[4,2,96,384]{3,2,1,0:T(8,128)(2,1)}), bf16[4,2,96,384]{3,2,1,0:T(8,128)(2,1)S(1)}, u32[]{:S(2)}, u32[]{:S(2)}) %all-to-all-start.1) | async-done | bytes 589856 | tf_op jit(solution)/shard_map/all_to_all | solution.py:191
  78.8 0.8 shard_map.40.refs_0_
  79.6 3.6 %collective-permute-start.8 = (bf16[2,96,384]{2,1,0:T(8,128)(2,1)S(1)}, bf16[2,96,384]{2,1,0:T(8,128)(2,1)S(1)}, u32[]{:S(2)}, u32[]{:S(2)}) collective-permute-start(bf16[2,96,384]{2,1,0:T(8,128)(2,1)S(1)} %shard_map.40.refs_0_), channel_id=1, source_target_pairs={{0,448},{4,68},{64,0},{68,132},{128,64},{132,196},{192,128},{196,2... | collective-permute-start | bytes 442376 | tf_op jit(solution)/shard_map/ppermute | solution.py:23
  83.2 2.9 %collective-permute-start.12 = (bf16[2,96,384]{2,1,0:T(8,128)(2,1)S(1)}, bf16[2,96,384]{2,1,0:T(8,128)(2,1)S(1)}, u32[]{:S(2)}, u32[]{:S(2)}) collective-permute-start(bf16[2,96,384]{2,1,0:T(8,128)(2,1)S(1)} %shard_map.40.refs_0_), channel_id=1, source_target_pairs={{0,64},{4,452},{64,128},{68,4},{128,192},{132,68},{192,256},{196,1... | collective-permute-start | bytes 442376 | tf_op jit(solution)/shard_map/ppermute | solution.py:23
  86.1 0.6 collective-permute-done.8.refs_1_
  86.7 2.4 %collective-permute-start.9 = (bf16[2,96,384]{2,1,0:T(8,128)(2,1)S(1)}, bf16[2,96,384]{2,1,0:T(8,128)(2,1)S(1)}, u32[]{:S(2)}, u32[]{:S(2)}) collective-permute-start(bf16[2,96,384]{2,1,0:T(8,128)(2,1)S(1)} %collective-permute-done.8.refs_1_), channel_id=1, source_target_pairs={{0,448},{4,68},{64,0},{68,132},{128,64},{132,196},{192,128},{196,2... | collective-permute-start | bytes 442376 | tf_op jit(solution)/shard_map/ppermute | solution.py:23
  89.1 0.7 collective-permute-done.12.refs_7_
  89.8 5.3 %collective-permute-start.13 = (bf16[2,96,384]{2,1,0:T(8,128)(2,1)S(1)}, bf16[2,96,384]{2,1,0:T(8,128)(2,1)S(1)}, u32[]{:S(2)}, u32[]{:S(2)}) collective-permute-start(bf16[2,96,384]{2,1,0:T(8,128)(2,1)S(1)} %collective-permute-done.12.refs_7_), channel_id=1, source_target_pairs={{0,64},{4,452},{64,128},{68,4},{128,192},{132,68},{192,256},{196,1... | collective-permute-start | bytes 442376 | tf_op jit(solution)/shard_map/ppermute | solution.py:23
  95.1 1.9 %collective-permute-start.10 = (bf16[2,96,384]{2,1,0:T(8,128)(2,1)S(1)}, bf16[2,96,384]{2,1,0:T(8,128)(2,1)S(1)}, u32[]{:S(2)}, u32[]{:S(2)}) collective-permute-start(bf16[2,96,384]{2,1,0:T(8,128)(2,1)S(1)} %collective-permute-done.9.refs_2_), channel_id=1, source_target_pairs={{0,448},{4,68},{64,0},{68,132},{128,64},{132,196},{192,128},{196,2... | collective-permute-start | bytes 442376 | tf_op jit(solution)/shard_map/ppermute | solution.py:23
  97.0 0.9 collective-permute-done.13.refs_6_
  97.9 5.3 %collective-permute-start.14 = (bf16[2,96,384]{2,1,0:T(8,128)(2,1)S(1)}, bf16[2,96,384]{2,1,0:T(8,128)(2,1)S(1)}, u32[]{:S(2)}, u32[]{:S(2)}) collective-permute-start(bf16[2,96,384]{2,1,0:T(8,128)(2,1)S(1)} %collective-permute-done.13.refs_6_), channel_id=1, source_target_pairs={{0,64},{4,452},{64,128},{68,4},{128,192},{132,68},{192,256},{196,1... | collective-permute-start | bytes 442376 | tf_op jit(solution)/shard_map/ppermute | solution.py:23
  103.2 1.9 %collective-permute-start.11 = (bf16[2,96,384]{2,1,0:T(8,128)(2,1)S(1)}, bf16[2,96,384]{2,1,0:T(8,128)(2,1)S(1)}, u32[]{:S(2)}, u32[]{:S(2)}) collective-permute-start(bf16[2,96,384]{2,1,0:T(8,128)(2,1)S(1)} %collective-permute-done.10.refs_3_), channel_id=1, source_target_pairs={{0,448},{4,68},{64,0},{68,132},{128,64},{132,196},{192,128},{196,2... | collective-permute-start | bytes 442376 | tf_op jit(solution)/shard_map/ppermute | solution.py:23
  105.1 0.0 copy-start.1
  105.2 0.0 copy-start.2
  105.2 0.7 shard_map.39
  105.8 4.5 %collective-permute-done.11.refs_4_ = bf16[2,96,384]{2,1,0:T(8,128)(2,1)S(1)} collective-permute-done((bf16[2,96,384]{2,1,0:T(8,128)(2,1)S(1)}, bf16[2,96,384]{2,1,0:T(8,128)(2,1)S(1)}, u32[]{:S(2)}, u32[]{:S(2)}) %collective-permute-start.11) | collective-permute-done | bytes 147488 | tf_op jit(solution)/shard_map/ppermute | solution.py:23
  110.3 2.4 %shard_map.41 = bf16[16,32,128]{2,1,0:T(8,128)(2,1)S(1)} custom-call(s32[16]{0:T(128)S(1)} %bitcast.16, s32[3]{0:T(128)S(1)} %pad_add_fusion.place_ref, f32[1]{0:T(128)} %bitcast.4.scale_ref, bf16[768,768]{1,0:T(8,128)(2,1)S(1)} %get-tuple-element.16.own_ref, bf16[768,768]{1,0:T(8,128)(2,1)S(1)} %get-tuple-element.17.other_ref, ...), custom_call_target="tpu_custom_call" | custom-call | tf_op jit(solution)/shard_map/pallas_call | solution.py:204
  112.7 16.9 %all_to_all.20 = bf16[16,32,128]{2,1,0:T(8,128)(2,1)S(1)} all-to-all(bf16[16,32,128]{2,1,0:T(8,128)(2,1)S(1)} %shard_map.41), channel_id=1, replica_groups=mesh['row'=8,'z'=8,'core'=2,'layer'=4] {'z','core'}, dimensions={0} | all-to-all | bytes 262144 | tf_op jit(solution)/shard_map/all_to_all | solution.py:216
  129.6 0.1 broadcast_in_dim.15
  129.7 12.3 %all_to_all.21 = bf16[4,16,32,128]{3,2,1,0:T(8,128)(2,1)S(1)} all-to-all(bf16[4,16,32,128]{3,2,1,0:T(8,128)(2,1)S(1)} %broadcast_in_dim.15), channel_id=1, replica_groups=mesh['row'=8,'z'=8,'core'=2,'layer'=4] {'layer'}, dimensions={0} | all-to-all | bytes 1048576 | tf_op jit(solution)/shard_map/all_to_all | solution.py:14
  141.9 0.1 reduce_sum.12
  142.0 0.7 copy.11
  (18 shorter events, 0.1 us)
Async XLA Ops:
  2.1 47.4 %all-to-all-start = ((bf16[8,2,96,384]{3,2,1,0:T(8,128)(2,1)}), bf16[8,2,96,384]{3,2,1,0:T(8,128)(2,1)S(1)}, u32[]{:S(2)}, u32[]{:S(2)}) async-start(bf16[8,2,96,384]{3,2,1,0:T(8,128)(2,1)} %broadcast_in_dim.14), calls=%async_computation | async-start | bytes 2359296 | tf_op jit(solution)/shard_map/all_to_all | solution.py:14
  11.0 13.5 %collective-permute-start = (bf16[96,768]{1,0:T(8,128)(2,1)S(1)}, bf16[96,768]{1,0:T(8,128)(2,1)S(1)}, u32[]{:S(2)}, u32[]{:S(2)}) collective-permute-start(bf16[96,768]{1,0:T(8,128)(2,1)S(1)} %bitcast.17), channel_id=1, source_target_pairs={{0,56},{4,12},{8,0},{12,20},{16,8},{20,28},{24,16},{28,36},{32,24}... | collective-permute-start | bytes 442376 | tf_op jit(solution)/shard_map/ppermute | solution.py:23
  24.5 7.4 %collective-permute-start.1 = (bf16[96,768]{1,0:T(8,128)(2,1)S(1)}, bf16[96,768]{1,0:T(8,128)(2,1)S(1)}, u32[]{:S(2)}, u32[]{:S(2)}) collective-permute-start(bf16[96,768]{1,0:T(8,128)(2,1)S(1)} %collective-permute-done), channel_id=1, source_target_pairs={{0,56},{4,12},{8,0},{12,20},{16,8},{20,28},{24,16},{28,36},{32,24}... | collective-permute-start | bytes 442376 | tf_op jit(solution)/shard_map/ppermute | solution.py:23
  26.4 7.9 %collective-permute-start.4 = (bf16[96,768]{1,0:T(8,128)(2,1)S(1)}, bf16[96,768]{1,0:T(8,128)(2,1)S(1)}, u32[]{:S(2)}, u32[]{:S(2)}) collective-permute-start(bf16[96,768]{1,0:T(8,128)(2,1)S(1)} %bitcast.18), channel_id=1, source_target_pairs={{0,8},{4,60},{8,16},{12,4},{16,24},{20,12},{24,32},{28,20},{32,40}... | collective-permute-start | bytes 442376 | tf_op jit(solution)/shard_map/ppermute | solution.py:23
  31.9 8.7 %collective-permute-start.2 = (bf16[96,768]{1,0:T(8,128)(2,1)S(1)}, bf16[96,768]{1,0:T(8,128)(2,1)S(1)}, u32[]{:S(2)}, u32[]{:S(2)}) collective-permute-start(bf16[96,768]{1,0:T(8,128)(2,1)S(1)} %collective-permute-done.1), channel_id=1, source_target_pairs={{0,56},{4,12},{8,0},{12,20},{16,8},{20,28},{24,16},{28,36},{32,24}... | collective-permute-start | bytes 442376 | tf_op jit(solution)/shard_map/ppermute | solution.py:23
  34.3 8.2 %collective-permute-start.5 = (bf16[96,768]{1,0:T(8,128)(2,1)S(1)}, bf16[96,768]{1,0:T(8,128)(2,1)S(1)}, u32[]{:S(2)}, u32[]{:S(2)}) collective-permute-start(bf16[96,768]{1,0:T(8,128)(2,1)S(1)} %collective-permute-done.4), channel_id=1, source_target_pairs={{0,8},{4,60},{8,16},{12,4},{16,24},{20,12},{24,32},{28,20},{32,40}... | collective-permute-start | bytes 442376 | tf_op jit(solution)/shard_map/ppermute | solution.py:23
  40.6 8.4 %collective-permute-start.3 = (bf16[96,768]{1,0:T(8,128)(2,1)S(1)}, bf16[96,768]{1,0:T(8,128)(2,1)S(1)}, u32[]{:S(2)}, u32[]{:S(2)}) collective-permute-start(bf16[96,768]{1,0:T(8,128)(2,1)S(1)} %collective-permute-done.2), channel_id=1, source_target_pairs={{0,56},{4,12},{8,0},{12,20},{16,8},{20,28},{24,16},{28,36},{32,24}... | collective-permute-start | bytes 442376 | tf_op jit(solution)/shard_map/ppermute | solution.py:23
  42.5 6.9 %collective-permute-start.6 = (bf16[96,768]{1,0:T(8,128)(2,1)S(1)}, bf16[96,768]{1,0:T(8,128)(2,1)S(1)}, u32[]{:S(2)}, u32[]{:S(2)}) collective-permute-start(bf16[96,768]{1,0:T(8,128)(2,1)S(1)} %collective-permute-done.5), channel_id=1, source_target_pairs={{0,8},{4,60},{8,16},{12,4},{16,24},{20,12},{24,32},{28,20},{32,40}... | collective-permute-start | bytes 442376 | tf_op jit(solution)/shard_map/ppermute | solution.py:23
  49.5 13.1 %collective-permute-start.7 = (bf16[768,768]{1,0:T(8,128)(2,1)S(1)}, bf16[768,768]{1,0:T(8,128)(2,1)S(1)}, u32[]{:S(2)}, u32[]{:S(2)}) collective-permute-start(bf16[768,768]{1,0:T(8,128)(2,1)S(1)} %constant_dynamic-update-slice_fusion.own_ref), channel_id=1, source_target_pairs={{0,4},{4,0},{1,5},{5,1},{2,6},{6,2},{3,7},{7,3},{8,12},{12,8},{9,1... | collective-permute-start | bytes 3538952 | tf_op jit(solution)/shard_map/ppermute | solution.py:151
  64.3 0.8 copy-start
  65.1 4.1 %copy-start.3 = (s32[12,6]{0,1:T(8,128)S(1)}, s32[12,6]{0,1:T(8,128)}, u32[]{:S(2)}) copy-start(s32[12,6]{0,1:T(8,128)} %param.4) | copy-start | bytes 868
  65.1 13.7 %all-to-all-start.1 = ((bf16[4,2,96,384]{3,2,1,0:T(8,128)(2,1)}), bf16[4,2,96,384]{3,2,1,0:T(8,128)(2,1)S(1)}, u32[]{:S(2)}, u32[]{:S(2)}) async-start(bf16[4,2,96,384]{3,2,1,0:T(8,128)(2,1)} %copy-done), calls=%async_computation.1 | async-start | bytes 1179648 | tf_op jit(solution)/shard_map/all_to_all | solution.py:191
  79.6 7.1 %collective-permute-start.8 = (bf16[2,96,384]{2,1,0:T(8,128)(2,1)S(1)}, bf16[2,96,384]{2,1,0:T(8,128)(2,1)S(1)}, u32[]{:S(2)}, u32[]{:S(2)}) collective-permute-start(bf16[2,96,384]{2,1,0:T(8,128)(2,1)S(1)} %shard_map.40.refs_0_), channel_id=1, source_target_pairs={{0,448},{4,68},{64,0},{68,132},{128,64},{132,196},{192,128},{196,2... | collective-permute-start | bytes 442376 | tf_op jit(solution)/shard_map/ppermute | solution.py:23
  83.2 6.6 %collective-permute-start.12 = (bf16[2,96,384]{2,1,0:T(8,128)(2,1)S(1)}, bf16[2,96,384]{2,1,0:T(8,128)(2,1)S(1)}, u32[]{:S(2)}, u32[]{:S(2)}) collective-permute-start(bf16[2,96,384]{2,1,0:T(8,128)(2,1)S(1)} %shard_map.40.refs_0_), channel_id=1, source_target_pairs={{0,64},{4,452},{64,128},{68,4},{128,192},{132,68},{192,256},{196,1... | collective-permute-start | bytes 442376 | tf_op jit(solution)/shard_map/ppermute | solution.py:23
  86.7 8.4 %collective-permute-start.9 = (bf16[2,96,384]{2,1,0:T(8,128)(2,1)S(1)}, bf16[2,96,384]{2,1,0:T(8,128)(2,1)S(1)}, u32[]{:S(2)}, u32[]{:S(2)}) collective-permute-start(bf16[2,96,384]{2,1,0:T(8,128)(2,1)S(1)} %collective-permute-done.8.refs_1_), channel_id=1, source_target_pairs={{0,448},{4,68},{64,0},{68,132},{128,64},{132,196},{192,128},{196,2... | collective-permute-start | bytes 442376 | tf_op jit(solution)/shard_map/ppermute | solution.py:23
  89.8 8.1 %collective-permute-start.13 = (bf16[2,96,384]{2,1,0:T(8,128)(2,1)S(1)}, bf16[2,96,384]{2,1,0:T(8,128)(2,1)S(1)}, u32[]{:S(2)}, u32[]{:S(2)}) collective-permute-start(bf16[2,96,384]{2,1,0:T(8,128)(2,1)S(1)} %collective-permute-done.12.refs_7_), channel_id=1, source_target_pairs={{0,64},{4,452},{64,128},{68,4},{128,192},{132,68},{192,256},{196,1... | collective-permute-start | bytes 442376 | tf_op jit(solution)/shard_map/ppermute | solution.py:23
  95.1 8.1 %collective-permute-start.10 = (bf16[2,96,384]{2,1,0:T(8,128)(2,1)S(1)}, bf16[2,96,384]{2,1,0:T(8,128)(2,1)S(1)}, u32[]{:S(2)}, u32[]{:S(2)}) collective-permute-start(bf16[2,96,384]{2,1,0:T(8,128)(2,1)S(1)} %collective-permute-done.9.refs_2_), channel_id=1, source_target_pairs={{0,448},{4,68},{64,0},{68,132},{128,64},{132,196},{192,128},{196,2... | collective-permute-start | bytes 442376 | tf_op jit(solution)/shard_map/ppermute | solution.py:23
  97.9 8.0 %collective-permute-start.14 = (bf16[2,96,384]{2,1,0:T(8,128)(2,1)S(1)}, bf16[2,96,384]{2,1,0:T(8,128)(2,1)S(1)}, u32[]{:S(2)}, u32[]{:S(2)}) collective-permute-start(bf16[2,96,384]{2,1,0:T(8,128)(2,1)S(1)} %collective-permute-done.13.refs_6_), channel_id=1, source_target_pairs={{0,64},{4,452},{64,128},{68,4},{128,192},{132,68},{192,256},{196,1... | collective-permute-start | bytes 442376 | tf_op jit(solution)/shard_map/ppermute | solution.py:23
  103.2 7.1 %collective-permute-start.11 = (bf16[2,96,384]{2,1,0:T(8,128)(2,1)S(1)}, bf16[2,96,384]{2,1,0:T(8,128)(2,1)S(1)}, u32[]{:S(2)}, u32[]{:S(2)}) collective-permute-start(bf16[2,96,384]{2,1,0:T(8,128)(2,1)S(1)} %collective-permute-done.10.refs_3_), channel_id=1, source_target_pairs={{0,448},{4,68},{64,0},{68,132},{128,64},{132,196},{192,128},{196,2... | collective-permute-start | bytes 442376 | tf_op jit(solution)/shard_map/ppermute | solution.py:23
  105.1 5.2 %copy-start.1 = (bf16[768,384]{1,0:T(8,128)(2,1)S(1)}, bf16[768,384]{1,0:T(8,128)(2,1)}, u32[]{:S(2)}) copy-start(bf16[768,384]{1,0:T(8,128)(2,1)} %matrix_ref.1) | copy-start | bytes 1769476
  105.2 5.2 %copy-start.2 = (s32[1,16]{1,0:T(1,128)S(1)}, s32[1,16]{1,0:T(1,128)}, u32[]{:S(2)}) copy-start(s32[1,16]{1,0:T(1,128)} %param.5) | copy-start | bytes 196

commit v10 on v8

--- a/solution.py
+++ b/solution.py
@@ -28,8 +28,8 @@
     down = shifted(piece, axis, -2)
     near_up = shifted(piece, axis, 1)
     near_down = shifted(piece, axis, -1)
-    far_up = shifted(up, axis, 1)
-    far_down = shifted(down, axis, -1)
+    far_up = shifted(piece, axis, 3)
+    far_down = shifted(piece, axis, -3)
     opposite = shifted(up, axis, 2)
     return piece, near_up, up, far_up, opposite, far_down, down, near_down
 

time: 131 us -> 139 us (1.061)
  waiting for transfers between devices: 19.3 us -> 26.2 us
  starting transfers between devices: 72.1 us -> 68.7 us
  blocking collectives: 26.5 us -> 29.1 us
  Pallas kernels: 6.78 us -> 8.2 us
    ppermute x14, waiting for transfers between devices: 8.78 us -> 15.7 us  [shifted(): return lax.ppermute(piece, (axis, 'core'), pairs)]
    ppermute x1, starting transfers between devices: 9.55 us -> 2.76 us  [on_device(): left_other = lax.ppermute(left_own, 'core', [(0, 1), (1, 0)])]
    ppermute x14, starting transfers between devices: 50.8 us -> 54.2 us  [shifted(): return lax.ppermute(piece, (axis, 'core'), pairs)]
    all_to_all x1, blocking collectives: 14.2 us -> 16.8 us  [on_device(): lax.all_to_all(outgoing, ('z', 'core'), split_axis=0, concat_axis=0, tile...]
  transfers between devices with their start and end apart: 17 -> 17, of which waited for: 6 -> 6; matrix products, arithmetic and copies ran while one was open for 1% -> 1% of each run, Pallas kernels for 2% -> 1%
where the time goes in v10:
time: 139 us
  starting transfers between devices  68.7 us (49%)
  blocking collectives  29.1 us (21%)
  waiting for transfers between devices  26.2 us (19%)
  Pallas kernels  8.2 us (6%)
  local copies, waits for them, and re-layouts  5.81 us (4%)
    ppermute x14, starting transfers between devices, shifted(): return lax.ppermute(piece, (axis, 'core'), pairs)  54.2 us
    all_to_all x1, blocking collectives, on_device(): lax.all_to_all(outgoing, ('z', 'core'), split_axis=0, concat_axis=0, tile...  16.8 us
    ppermute x14, waiting for transfers between devices, shifted(): return lax.ppermute(piece, (axis, 'core'), pairs)  15.7 us
    all_to_all x1, blocking collectives, to_all(): return lax.all_to_all(copies, axis, split_axis=0, concat_axis=0, tiled=True)  12.3 us
    all_to_all x1, waiting for transfers between devices, on_device(): lax.all_to_all(square_part, 'layer', split_axis=0, concat_axis=0, tiled=T...  9.49 us
    all_to_all x1, starting transfers between devices, to_all(): return lax.all_to_all(copies, axis, split_axis=0, concat_axis=0, tiled=True)  7.65 us
    all_to_all x1, starting transfers between devices, on_device(): lax.all_to_all(square_part, 'layer', split_axis=0, concat_axis=0, tiled=T...  4.14 us
    pallas_call x1, Pallas kernels, on_device(): pl.pallas_call(cube_kernel, out_shape=jax.ShapeDtypeStruct((chosen.shape[...  3.12 us
  transfers between devices with their start and end apart: 17, of which 6 were waited for; matrix products, arithmetic and copies ran while one was open for 1% of the time, Pallas kernels for 1%

profile of v10, /device:TPU:1, one launch (start us, length us, event | category | flops | bytes accessed | tf_op | source)
XLA Modules:
  0.0 138.6 jit_solution(6579705385873804173)
XLA Ops:
  0.0 0.9 dynamic-slice_bitcast_fusion
  0.9 1.2 broadcast_in_dim.14
  2.1 7.7 %all-to-all-start = ((bf16[8,2,96,384]{3,2,1,0:T(8,128)(2,1)}), bf16[8,2,96,384]{3,2,1,0:T(8,128)(2,1)S(1)}, u32[]{:S(2)}, u32[]{:S(2)}) async-start(bf16[8,2,96,384]{3,2,1,0:T(8,128)(2,1)} %broadcast_in_dim.14), calls=%async_computation | async-start | bytes 2359296 | tf_op jit(solution)/shard_map/all_to_all | solution.py:14
  9.7 1.1 constant_dynamic-slice_fusion
  10.9 0.1 copy.8
  11.0 4.0 %collective-permute-start = (bf16[96,768]{1,0:T(8,128)(2,1)S(1)}, bf16[96,768]{1,0:T(8,128)(2,1)S(1)}, u32[]{:S(2)}, u32[]{:S(2)}) collective-permute-start(bf16[96,768]{1,0:T(8,128)(2,1)S(1)} %bitcast.17), channel_id=1, source_target_pairs={{0,56},{4,12},{8,0},{12,20},{16,8},{20,28},{24,16},{28,36},{32,24}... | collective-permute-start | bytes 442376 | tf_op jit(solution)/shard_map/ppermute | solution.py:23
  15.0 5.8 %collective-permute-start.1 = (bf16[96,768]{1,0:T(8,128)(2,1)S(1)}, bf16[96,768]{1,0:T(8,128)(2,1)S(1)}, u32[]{:S(2)}, u32[]{:S(2)}) collective-permute-start(bf16[96,768]{1,0:T(8,128)(2,1)S(1)} %bitcast.18), channel_id=1, source_target_pairs={{0,48},{4,20},{8,56},{12,28},{16,0},{20,36},{24,8},{28,44},{32,16}... | collective-permute-start | bytes 442376 | tf_op jit(solution)/shard_map/ppermute | solution.py:23
  20.8 7.0 %collective-permute-start.2 = (bf16[96,768]{1,0:T(8,128)(2,1)S(1)}, bf16[96,768]{1,0:T(8,128)(2,1)S(1)}, u32[]{:S(2)}, u32[]{:S(2)}) collective-permute-start(bf16[96,768]{1,0:T(8,128)(2,1)S(1)} %bitcast.19), channel_id=1, source_target_pairs={{0,40},{4,28},{8,48},{12,36},{16,56},{20,44},{24,0},{28,52},{32,8}... | collective-permute-start | bytes 442376 | tf_op jit(solution)/shard_map/ppermute | solution.py:23
  27.9 1.9 %collective-permute-start.4 = (bf16[96,768]{1,0:T(8,128)(2,1)S(1)}, bf16[96,768]{1,0:T(8,128)(2,1)S(1)}, u32[]{:S(2)}, u32[]{:S(2)}) collective-permute-start(bf16[96,768]{1,0:T(8,128)(2,1)S(1)} %bitcast.20), channel_id=1, source_target_pairs={{0,24},{4,44},{8,32},{12,52},{16,40},{20,60},{24,48},{28,4},{32,56... | collective-permute-start | bytes 442376 | tf_op jit(solution)/shard_map/ppermute | solution.py:23
  29.8 5.2 %collective-permute-start.5 = (bf16[96,768]{1,0:T(8,128)(2,1)S(1)}, bf16[96,768]{1,0:T(8,128)(2,1)S(1)}, u32[]{:S(2)}, u32[]{:S(2)}) collective-permute-start(bf16[96,768]{1,0:T(8,128)(2,1)S(1)} %bitcast.21), channel_id=1, source_target_pairs={{0,16},{4,52},{8,24},{12,60},{16,32},{20,4},{24,40},{28,12},{32,48... | collective-permute-start | bytes 442376 | tf_op jit(solution)/shard_map/ppermute | solution.py:23
  35.0 0.0 collective-permute-done
  35.0 3.1 %collective-permute-start.6 = (bf16[96,768]{1,0:T(8,128)(2,1)S(1)}, bf16[96,768]{1,0:T(8,128)(2,1)S(1)}, u32[]{:S(2)}, u32[]{:S(2)}) collective-permute-start(bf16[96,768]{1,0:T(8,128)(2,1)S(1)} %bitcast.22), channel_id=1, source_target_pairs={{0,8},{4,60},{8,16},{12,4},{16,24},{20,12},{24,32},{28,20},{32,40}... | collective-permute-start | bytes 442376 | tf_op jit(solution)/shard_map/ppermute | solution.py:23
  38.1 0.0 collective-permute-done.1
  38.1 1.9 %collective-permute-start.3 = (bf16[96,768]{1,0:T(8,128)(2,1)S(1)}, bf16[96,768]{1,0:T(8,128)(2,1)S(1)}, u32[]{:S(2)}, u32[]{:S(2)}) collective-permute-start(bf16[96,768]{1,0:T(8,128)(2,1)S(1)} %collective-permute-done.1), channel_id=1, source_target_pairs={{0,48},{4,20},{8,56},{12,28},{16,0},{20,36},{24,8},{28,44},{32,16}... | collective-permute-start | bytes 442376 | tf_op jit(solution)/shard_map/ppermute | solution.py:23
  40.1 9.1 %collective-permute-done.3 = bf16[96,768]{1,0:T(8,128)(2,1)S(1)} collective-permute-done((bf16[96,768]{1,0:T(8,128)(2,1)S(1)}, bf16[96,768]{1,0:T(8,128)(2,1)S(1)}, u32[]{:S(2)}, u32[]{:S(2)}) %collective-permute-start.3) | collective-permute-done | bytes 147488 | tf_op jit(solution)/shard_map/ppermute | solution.py:23
  49.3 0.0 collective-permute-done.6
  49.4 2.8 %collective-permute-start.7 = (bf16[768,768]{1,0:T(8,128)(2,1)S(1)}, bf16[768,768]{1,0:T(8,128)(2,1)S(1)}, u32[]{:S(2)}, u32[]{:S(2)}) collective-permute-start(bf16[768,768]{1,0:T(8,128)(2,1)S(1)} %constant_dynamic-update-slice_fusion.own_ref), channel_id=1, source_target_pairs={{0,4},{4,0},{1,5},{5,1},{2,6},{6,2},{3,7},{7,3},{8,12},{12,8},{9,1... | collective-permute-start | bytes 3538952 | tf_op jit(solution)/shard_map/ppermute | solution.py:151
  52.2 0.1 pad_add_fusion.place_ref
  52.2 1.4 shard_map.37.total_ref
  53.6 1.0 collective-permute-done.7.other_ref
  54.6 1.6 %shard_map.38 = bf16[4,2,96,384]{3,2,1,0:T(8,128)(2,1)S(1)} custom-call(s32[3]{0:T(128)S(1)} %pad_add_fusion.place_ref, f32[768,384]{1,0:T(8,128)S(1)} %shard_map.37.total_ref, bf16[768,768]{1,0:T(8,128)(2,1)S(1)} %collective-permute-done.7.other_ref, bf16[8,2,96,384]{3,2,1,0:T(8,128)(2,1)S(1)} %all-to-all-done.right_ref), custom_call_target="tpu_custom_call" | custom-call | flops 452984832 | bytes 1769472 | tf_op jit(solution)/shard_map/pallas_call | solution.py:168
  56.3 0.8 copy-done
  57.1 4.1 %all-to-all-start.1 = ((bf16[4,2,96,384]{3,2,1,0:T(8,128)(2,1)}), bf16[4,2,96,384]{3,2,1,0:T(8,128)(2,1)S(1)}, u32[]{:S(2)}, u32[]{:S(2)}) async-start(bf16[4,2,96,384]{3,2,1,0:T(8,128)(2,1)} %copy-done), calls=%async_computation.1 | async-start | bytes 1179648 | tf_op jit(solution)/shard_map/all_to_all | solution.py:191
  61.2 0.1 copy.7.keep_ref
  61.3 9.5 %all-to-all-done.1.parts_ref = bf16[4,2,96,384]{3,2,1,0:T(8,128)(2,1)S(1)} async-done(((bf16[4,2,96,384]{3,2,1,0:T(8,128)(2,1)}), bf16[4,2,96,384]{3,2,1,0:T(8,128)(2,1)S(1)}, u32[]{:S(2)}, u32[]{:S(2)}) %all-to-all-start.1) | async-done | bytes 589856 | tf_op jit(solution)/shard_map/all_to_all | solution.py:191
  70.8 1.4 %shard_map.40.refs_0_ = bf16[2,96,384]{2,1,0:T(8,128)(2,1)} custom-call(s32[12,6]{1,0:T(8,128)S(1)} %copy.7.keep_ref, s32[1]{0:T(128)} %bitcast.8.layer_ref, bf16[4,2,96,384]{3,2,1,0:T(8,128)(2,1)S(1)} %all-to-all-done.1.parts_ref), custom_call_target="tpu_custom_call" | custom-call | tf_op jit(solution)/shard_map/pallas_call | solution.py:192
  72.2 4.5 %collective-permute-start.9 = (bf16[2,96,384]{2,1,0:T(8,128)(2,1)}, bf16[2,96,384]{2,1,0:T(8,128)(2,1)}, u32[]{:S(2)}, u32[]{:S(2)}) collective-permute-start(bf16[2,96,384]{2,1,0:T(8,128)(2,1)} %shard_map.40.refs_0_), channel_id=1, source_target_pairs={{0,384},{4,132},{64,448},{68,196},{128,0},{132,260},{192,64},{196,... | collective-permute-start | bytes 442376 | tf_op jit(solution)/shard_map/ppermute | solution.py:23
  76.8 5.2 %collective-permute-start.10 = (bf16[2,96,384]{2,1,0:T(8,128)(2,1)}, bf16[2,96,384]{2,1,0:T(8,128)(2,1)S(1)}, u32[]{:S(2)}, u32[]{:S(2)}) collective-permute-start(bf16[2,96,384]{2,1,0:T(8,128)(2,1)} %shard_map.40.refs_0_), channel_id=1, source_target_pairs={{0,320},{4,196},{64,384},{68,260},{128,448},{132,324},{192,0},{196... | collective-permute-start | bytes 442376 | tf_op jit(solution)/shard_map/ppermute | solution.py:23
  82.0 3.1 %collective-permute-start.12 = (bf16[2,96,384]{2,1,0:T(8,128)(2,1)}, bf16[2,96,384]{2,1,0:T(8,128)(2,1)}, u32[]{:S(2)}, u32[]{:S(2)}) collective-permute-start(bf16[2,96,384]{2,1,0:T(8,128)(2,1)} %shard_map.40.refs_0_), channel_id=1, source_target_pairs={{0,192},{4,324},{64,256},{68,388},{128,320},{132,452},{192,384},{1... | collective-permute-start | bytes 442376 | tf_op jit(solution)/shard_map/ppermute | solution.py:23
  85.1 3.1 %collective-permute-start.13 = (bf16[2,96,384]{2,1,0:T(8,128)(2,1)}, bf16[2,96,384]{2,1,0:T(8,128)(2,1)}, u32[]{:S(2)}, u32[]{:S(2)}) collective-permute-start(bf16[2,96,384]{2,1,0:T(8,128)(2,1)} %shard_map.40.refs_0_), channel_id=1, source_target_pairs={{0,128},{4,388},{64,192},{68,452},{128,256},{132,4},{192,320},{196... | collective-permute-start | bytes 442376 | tf_op jit(solution)/shard_map/ppermute | solution.py:23
  88.2 3.4 %collective-permute-start.14 = (bf16[2,96,384]{2,1,0:T(8,128)(2,1)}, bf16[2,96,384]{2,1,0:T(8,128)(2,1)}, u32[]{:S(2)}, u32[]{:S(2)}) collective-permute-start(bf16[2,96,384]{2,1,0:T(8,128)(2,1)} %shard_map.40.refs_0_), channel_id=1, source_target_pairs={{0,64},{4,452},{64,128},{68,4},{128,192},{132,68},{192,256},{196,1... | collective-permute-start | bytes 442376 | tf_op jit(solution)/shard_map/ppermute | solution.py:23
  91.6 1.9 %collective-permute-start.8 = (bf16[2,96,384]{2,1,0:T(8,128)(2,1)}, bf16[2,96,384]{2,1,0:T(8,128)(2,1)}, u32[]{:S(2)}, u32[]{:S(2)}) collective-permute-start(bf16[2,96,384]{2,1,0:T(8,128)(2,1)} %shard_map.40.refs_0_), channel_id=1, source_target_pairs={{0,448},{4,68},{64,0},{68,132},{128,64},{132,196},{192,128},{196,2... | collective-permute-start | bytes 442376 | tf_op jit(solution)/shard_map/ppermute | solution.py:23
  93.5 0.0 collective-permute-done.10.refs_3_
  93.6 0.7 copy-done.2
  94.2 4.0 %collective-permute-start.11 = (bf16[2,96,384]{2,1,0:T(8,128)(2,1)}, bf16[2,96,384]{2,1,0:T(8,128)(2,1)}, u32[]{:S(2)}, u32[]{:S(2)}) collective-permute-start(bf16[2,96,384]{2,1,0:T(8,128)(2,1)} %collective-permute-done.9.refs_2_), channel_id=1, source_target_pairs={{0,384},{4,132},{64,448},{68,196},{128,0},{132,260},{192,64},{196,... | collective-permute-start | bytes 442376 | tf_op jit(solution)/shard_map/ppermute | solution.py:23
  98.2 0.0 copy-start.1
  98.2 0.0 copy-start.4
  98.2 0.7 shard_map.39
  98.9 0.0 collective-permute-done.12.refs_5_
  98.9 0.8 collective-permute-done.13.refs_6_
  99.7 3.0 %collective-permute-done.14.refs_7_ = bf16[2,96,384]{2,1,0:T(8,128)(2,1)} collective-permute-done((bf16[2,96,384]{2,1,0:T(8,128)(2,1)}, bf16[2,96,384]{2,1,0:T(8,128)(2,1)}, u32[]{:S(2)}, u32[]{:S(2)}) %collective-permute-start.14) | collective-permute-done | bytes 147488 | tf_op jit(solution)/shard_map/ppermute | solution.py:23
  102.7 2.8 %collective-permute-done.11.refs_4_ = bf16[2,96,384]{2,1,0:T(8,128)(2,1)} collective-permute-done((bf16[2,96,384]{2,1,0:T(8,128)(2,1)}, bf16[2,96,384]{2,1,0:T(8,128)(2,1)}, u32[]{:S(2)}, u32[]{:S(2)}) %collective-permute-start.11) | collective-permute-done | bytes 147488 | tf_op jit(solution)/shard_map/ppermute | solution.py:23
  105.4 3.1 %shard_map.41 = bf16[16,32,128]{2,1,0:T(8,128)(2,1)S(1)} custom-call(s32[16]{0:T(128)S(1)} %bitcast.16, s32[3]{0:T(128)S(1)} %pad_add_fusion.place_ref, f32[1]{0:T(128)} %bitcast.4.scale_ref, bf16[768,768]{1,0:T(8,128)(2,1)S(1)} %get-tuple-element.16.own_ref, bf16[768,768]{1,0:T(8,128)(2,1)S(1)} %get-tuple-element.17.other_ref, ...), custom_call_target="tpu_custom_call" | custom-call | tf_op jit(solution)/shard_map/pallas_call | solution.py:204
  108.6 16.8 %all_to_all.20 = bf16[16,32,128]{2,1,0:T(8,128)(2,1)S(1)} all-to-all(bf16[16,32,128]{2,1,0:T(8,128)(2,1)S(1)} %shard_map.41), channel_id=1, replica_groups=mesh['row'=8,'z'=8,'core'=2,'layer'=4] {'z','core'}, dimensions={0} | all-to-all | bytes 262144 | tf_op jit(solution)/shard_map/all_to_all | solution.py:216
  125.4 0.1 broadcast_in_dim.15
  125.5 12.3 %all_to_all.21 = bf16[4,16,32,128]{3,2,1,0:T(8,128)(2,1)S(1)} all-to-all(bf16[4,16,32,128]{3,2,1,0:T(8,128)(2,1)S(1)} %broadcast_in_dim.15), channel_id=1, replica_groups=mesh['row'=8,'z'=8,'core'=2,'layer'=4] {'layer'}, dimensions={0} | all-to-all | bytes 1048576 | tf_op jit(solution)/shard_map/all_to_all | solution.py:14
  137.8 0.1 reduce_sum.12
  137.9 0.7 copy.11
  (22 shorter events, 0.1 us)
Async XLA Ops:
  2.1 47.3 %all-to-all-start = ((bf16[8,2,96,384]{3,2,1,0:T(8,128)(2,1)}), bf16[8,2,96,384]{3,2,1,0:T(8,128)(2,1)S(1)}, u32[]{:S(2)}, u32[]{:S(2)}) async-start(bf16[8,2,96,384]{3,2,1,0:T(8,128)(2,1)} %broadcast_in_dim.14), calls=%async_computation | async-start | bytes 2359296 | tf_op jit(solution)/shard_map/all_to_all | solution.py:14
  11.0 24.0 %collective-permute-start = (bf16[96,768]{1,0:T(8,128)(2,1)S(1)}, bf16[96,768]{1,0:T(8,128)(2,1)S(1)}, u32[]{:S(2)}, u32[]{:S(2)}) collective-permute-start(bf16[96,768]{1,0:T(8,128)(2,1)S(1)} %bitcast.17), channel_id=1, source_target_pairs={{0,56},{4,12},{8,0},{12,20},{16,8},{20,28},{24,16},{28,36},{32,24}... | collective-permute-start | bytes 442376 | tf_op jit(solution)/shard_map/ppermute | solution.py:23
  15.0 23.1 %collective-permute-start.1 = (bf16[96,768]{1,0:T(8,128)(2,1)S(1)}, bf16[96,768]{1,0:T(8,128)(2,1)S(1)}, u32[]{:S(2)}, u32[]{:S(2)}) collective-permute-start(bf16[96,768]{1,0:T(8,128)(2,1)S(1)} %bitcast.18), channel_id=1, source_target_pairs={{0,48},{4,20},{8,56},{12,28},{16,0},{20,36},{24,8},{28,44},{32,16}... | collective-permute-start | bytes 442376 | tf_op jit(solution)/shard_map/ppermute | solution.py:23
  20.8 19.3 %collective-permute-start.2 = (bf16[96,768]{1,0:T(8,128)(2,1)S(1)}, bf16[96,768]{1,0:T(8,128)(2,1)S(1)}, u32[]{:S(2)}, u32[]{:S(2)}) collective-permute-start(bf16[96,768]{1,0:T(8,128)(2,1)S(1)} %bitcast.19), channel_id=1, source_target_pairs={{0,40},{4,28},{8,48},{12,36},{16,56},{20,44},{24,0},{28,52},{32,8}... | collective-permute-start | bytes 442376 | tf_op jit(solution)/shard_map/ppermute | solution.py:23
  27.9 21.4 %collective-permute-start.4 = (bf16[96,768]{1,0:T(8,128)(2,1)S(1)}, bf16[96,768]{1,0:T(8,128)(2,1)S(1)}, u32[]{:S(2)}, u32[]{:S(2)}) collective-permute-start(bf16[96,768]{1,0:T(8,128)(2,1)S(1)} %bitcast.20), channel_id=1, source_target_pairs={{0,24},{4,44},{8,32},{12,52},{16,40},{20,60},{24,48},{28,4},{32,56... | collective-permute-start | bytes 442376 | tf_op jit(solution)/shard_map/ppermute | solution.py:23
  29.8 19.5 %collective-permute-start.5 = (bf16[96,768]{1,0:T(8,128)(2,1)S(1)}, bf16[96,768]{1,0:T(8,128)(2,1)S(1)}, u32[]{:S(2)}, u32[]{:S(2)}) collective-permute-start(bf16[96,768]{1,0:T(8,128)(2,1)S(1)} %bitcast.21), channel_id=1, source_target_pairs={{0,16},{4,52},{8,24},{12,60},{16,32},{20,4},{24,40},{28,12},{32,48... | collective-permute-start | bytes 442376 | tf_op jit(solution)/shard_map/ppermute | solution.py:23
  35.0 14.3 %collective-permute-start.6 = (bf16[96,768]{1,0:T(8,128)(2,1)S(1)}, bf16[96,768]{1,0:T(8,128)(2,1)S(1)}, u32[]{:S(2)}, u32[]{:S(2)}) collective-permute-start(bf16[96,768]{1,0:T(8,128)(2,1)S(1)} %bitcast.22), channel_id=1, source_target_pairs={{0,8},{4,60},{8,16},{12,4},{16,24},{20,12},{24,32},{28,20},{32,40}... | collective-permute-start | bytes 442376 | tf_op jit(solution)/shard_map/ppermute | solution.py:23
  38.1 11.1 %collective-permute-start.3 = (bf16[96,768]{1,0:T(8,128)(2,1)S(1)}, bf16[96,768]{1,0:T(8,128)(2,1)S(1)}, u32[]{:S(2)}, u32[]{:S(2)}) collective-permute-start(bf16[96,768]{1,0:T(8,128)(2,1)S(1)} %collective-permute-done.1), channel_id=1, source_target_pairs={{0,48},{4,20},{8,56},{12,28},{16,0},{20,36},{24,8},{28,44},{32,16}... | collective-permute-start | bytes 442376 | tf_op jit(solution)/shard_map/ppermute | solution.py:23
  49.4 5.2 %collective-permute-start.7 = (bf16[768,768]{1,0:T(8,128)(2,1)S(1)}, bf16[768,768]{1,0:T(8,128)(2,1)S(1)}, u32[]{:S(2)}, u32[]{:S(2)}) collective-permute-start(bf16[768,768]{1,0:T(8,128)(2,1)S(1)} %constant_dynamic-update-slice_fusion.own_ref), channel_id=1, source_target_pairs={{0,4},{4,0},{1,5},{5,1},{2,6},{6,2},{3,7},{7,3},{8,12},{12,8},{9,1... | collective-permute-start | bytes 3538952 | tf_op jit(solution)/shard_map/ppermute | solution.py:151
  56.3 0.8 copy-start
  57.1 4.1 %copy-start.5 = (s32[12,6]{0,1:T(8,128)S(1)}, s32[12,6]{0,1:T(8,128)}, u32[]{:S(2)}) copy-start(s32[12,6]{0,1:T(8,128)} %param.4) | copy-start | bytes 868
  57.1 13.7 %all-to-all-start.1 = ((bf16[4,2,96,384]{3,2,1,0:T(8,128)(2,1)}), bf16[4,2,96,384]{3,2,1,0:T(8,128)(2,1)S(1)}, u32[]{:S(2)}, u32[]{:S(2)}) async-start(bf16[4,2,96,384]{3,2,1,0:T(8,128)(2,1)} %copy-done), calls=%async_computation.1 | async-start | bytes 1179648 | tf_op jit(solution)/shard_map/all_to_all | solution.py:191
  72.2 19.4 %collective-permute-start.9 = (bf16[2,96,384]{2,1,0:T(8,128)(2,1)}, bf16[2,96,384]{2,1,0:T(8,128)(2,1)}, u32[]{:S(2)}, u32[]{:S(2)}) collective-permute-start(bf16[2,96,384]{2,1,0:T(8,128)(2,1)} %shard_map.40.refs_0_), channel_id=1, source_target_pairs={{0,384},{4,132},{64,448},{68,196},{128,0},{132,260},{192,64},{196,... | collective-permute-start | bytes 442376 | tf_op jit(solution)/shard_map/ppermute | solution.py:23
  76.8 16.8 %collective-permute-start.10 = (bf16[2,96,384]{2,1,0:T(8,128)(2,1)}, bf16[2,96,384]{2,1,0:T(8,128)(2,1)S(1)}, u32[]{:S(2)}, u32[]{:S(2)}) collective-permute-start(bf16[2,96,384]{2,1,0:T(8,128)(2,1)} %shard_map.40.refs_0_), channel_id=1, source_target_pairs={{0,320},{4,196},{64,384},{68,260},{128,448},{132,324},{192,0},{196... | collective-permute-start | bytes 442376 | tf_op jit(solution)/shard_map/ppermute | solution.py:23
  82.0 16.9 %collective-permute-start.12 = (bf16[2,96,384]{2,1,0:T(8,128)(2,1)}, bf16[2,96,384]{2,1,0:T(8,128)(2,1)}, u32[]{:S(2)}, u32[]{:S(2)}) collective-permute-start(bf16[2,96,384]{2,1,0:T(8,128)(2,1)} %shard_map.40.refs_0_), channel_id=1, source_target_pairs={{0,192},{4,324},{64,256},{68,388},{128,320},{132,452},{192,384},{1... | collective-permute-start | bytes 442376 | tf_op jit(solution)/shard_map/ppermute | solution.py:23
  85.1 14.6 %collective-permute-start.13 = (bf16[2,96,384]{2,1,0:T(8,128)(2,1)}, bf16[2,96,384]{2,1,0:T(8,128)(2,1)}, u32[]{:S(2)}, u32[]{:S(2)}) collective-permute-start(bf16[2,96,384]{2,1,0:T(8,128)(2,1)} %shard_map.40.refs_0_), channel_id=1, source_target_pairs={{0,128},{4,388},{64,192},{68,452},{128,256},{132,4},{192,320},{196... | collective-permute-start | bytes 442376 | tf_op jit(solution)/shard_map/ppermute | solution.py:23
  88.2 14.4 %collective-permute-start.14 = (bf16[2,96,384]{2,1,0:T(8,128)(2,1)}, bf16[2,96,384]{2,1,0:T(8,128)(2,1)}, u32[]{:S(2)}, u32[]{:S(2)}) collective-permute-start(bf16[2,96,384]{2,1,0:T(8,128)(2,1)} %shard_map.40.refs_0_), channel_id=1, source_target_pairs={{0,64},{4,452},{64,128},{68,4},{128,192},{132,68},{192,256},{196,1... | collective-permute-start | bytes 442376 | tf_op jit(solution)/shard_map/ppermute | solution.py:23
  91.6 11.1 %collective-permute-start.8 = (bf16[2,96,384]{2,1,0:T(8,128)(2,1)}, bf16[2,96,384]{2,1,0:T(8,128)(2,1)}, u32[]{:S(2)}, u32[]{:S(2)}) collective-permute-start(bf16[2,96,384]{2,1,0:T(8,128)(2,1)} %shard_map.40.refs_0_), channel_id=1, source_target_pairs={{0,448},{4,68},{64,0},{68,132},{128,64},{132,196},{192,128},{196,2... | collective-permute-start | bytes 442376 | tf_op jit(solution)/shard_map/ppermute | solution.py:23
  93.6 0.7 copy-start.2
  94.2 11.2 %collective-permute-start.11 = (bf16[2,96,384]{2,1,0:T(8,128)(2,1)}, bf16[2,96,384]{2,1,0:T(8,128)(2,1)}, u32[]{:S(2)}, u32[]{:S(2)}) collective-permute-start(bf16[2,96,384]{2,1,0:T(8,128)(2,1)} %collective-permute-done.9.refs_2_), channel_id=1, source_target_pairs={{0,384},{4,132},{64,448},{68,196},{128,0},{132,260},{192,64},{196,... | collective-permute-start | bytes 442376 | tf_op jit(solution)/shard_map/ppermute | solution.py:23
  98.2 7.2 %copy-start.1 = (bf16[768,384]{1,0:T(8,128)(2,1)S(1)}, bf16[768,384]{1,0:T(8,128)(2,1)}, u32[]{:S(2)}) copy-start(bf16[768,384]{1,0:T(8,128)(2,1)} %matrix_ref.1) | copy-start | bytes 1769476
  98.2 7.2 %copy-start.3 = (bf16[2,96,384]{2,1,0:T(8,128)(2,1)S(1)}, bf16[2,96,384]{2,1,0:T(8,128)(2,1)}, u32[]{:S(2)}) copy-start(bf16[2,96,384]{2,1,0:T(8,128)(2,1)} %copy-done.2) | copy-start | bytes 442372
  98.2 7.2 %copy-start.4 = (s32[1,16]{1,0:T(1,128)S(1)}, s32[1,16]{1,0:T(1,128)}, u32[]{:S(2)}) copy-start(s32[1,16]{1,0:T(1,128)} %param.5) | copy-start | bytes 196

commit v11 on v8

--- a/solution.py
+++ b/solution.py
@@ -23,14 +23,17 @@
     return lax.ppermute(piece, (axis, "core"), pairs)
 
 
-def ring_of_eight(piece, axis):
+def ring_of_eight(piece, axis, near_last=False):
     up = shifted(piece, axis, 2)
     down = shifted(piece, axis, -2)
-    near_up = shifted(piece, axis, 1)
-    near_down = shifted(piece, axis, -1)
+    late = piece
+    if near_last:
+        late, up = lax.optimization_barrier((piece, up))
+    opposite = shifted(up, axis, 2)
     far_up = shifted(up, axis, 1)
     far_down = shifted(down, axis, -1)
-    opposite = shifted(up, axis, 2)
+    near_up = shifted(late, axis, 1)
+    near_down = shifted(late, axis, -1)
     return piece, near_up, up, far_up, opposite, far_down, down, near_down
 
 
@@ -196,7 +199,7 @@
         out_specs=vmem,
         compiler_params=params,
     )(keep_mask, layer_index.reshape(1), parts)
-    filtered = ring_of_eight(filtered_piece, "row")
+    filtered = ring_of_eight(filtered_piece, "row", near_last=True)
 
     scale = jnp.where(layer_index == 0, 1.5, 0.0).astype(jnp.float32).reshape(1)
     chosen = send_list[0]

time: 131 us -> 137 us (1.046)
  blocking collectives: 26.5 us -> 29.5 us
  waiting for transfers between devices: 19.3 us -> 21.8 us
    all_to_all x1, blocking collectives: 14.2 us -> 17.2 us  [on_device(): lax.all_to_all(outgoing, ('z', 'core'), split_axis=0, concat_axis=0, tile...]
    ppermute x14, waiting for transfers between devices: 8.78 us -> 11.3 us  [shifted(): return lax.ppermute(piece, (axis, 'core'), pairs)]
  transfers between devices with their start and end apart: 17 -> 17, of which waited for: 6 -> 7; matrix products, arithmetic and copies ran while one was open for 1% -> 1% of each run, Pallas kernels for 2% -> 1%
where the time goes in v11:
time: 137 us; the launch traced here: 136 us
  starting transfers between devices  72.3 us (53%)
  blocking collectives  29.5 us (22%)
  waiting for transfers between devices  21.8 us (16%)
  Pallas kernels  6.78 us (5%)
  local copies, waits for them, and re-layouts  5.15 us (4%)
    ppermute x14, starting transfers between devices, shifted(): return lax.ppermute(piece, (axis, 'core'), pairs)  50.9 us
    all_to_all x1, blocking collectives, on_device(): lax.all_to_all(outgoing, ('z', 'core'), split_axis=0, concat_axis=0, tile...  17.2 us
    all_to_all x1, blocking collectives, to_all(): return lax.all_to_all(copies, axis, split_axis=0, concat_axis=0, tiled=True)  12.3 us
    ppermute x14, waiting for transfers between devices, shifted(): return lax.ppermute(piece, (axis, 'core'), pairs)  11.3 us
    ppermute x1, starting transfers between devices, on_device(): left_other = lax.ppermute(left_own, 'core', [(0, 1), (1, 0)])  9.55 us
    all_to_all x1, waiting for transfers between devices, on_device(): lax.all_to_all(square_part, 'layer', split_axis=0, concat_axis=0, tiled=T...  9.51 us
    all_to_all x1, starting transfers between devices, to_all(): return lax.all_to_all(copies, axis, split_axis=0, concat_axis=0, tiled=True)  7.65 us
    all_to_all x1, starting transfers between devices, on_device(): lax.all_to_all(square_part, 'layer', split_axis=0, concat_axis=0, tiled=T...  4.15 us
  transfers between devices with their start and end apart: 17, of which 7 were waited for; matrix products, arithmetic and copies ran while one was open for 1% of the time, Pallas kernels for 1%

profile of v11, /device:TPU:1, one launch (start us, length us, event | category | flops | bytes accessed | tf_op | source)
XLA Modules:
  0.0 136.0 jit_solution(5037748270042972715)
XLA Ops:
  0.0 0.9 dynamic-slice_bitcast_fusion
  0.9 1.2 broadcast_in_dim.14
  2.1 7.7 %all-to-all-start = ((bf16[8,2,96,384]{3,2,1,0:T(8,128)(2,1)}), bf16[8,2,96,384]{3,2,1,0:T(8,128)(2,1)S(1)}, u32[]{:S(2)}, u32[]{:S(2)}) async-start(bf16[8,2,96,384]{3,2,1,0:T(8,128)(2,1)} %broadcast_in_dim.14), calls=%async_computation | async-start | bytes 2359296 | tf_op jit(solution)/shard_map/all_to_all | solution.py:14
  9.8 1.1 constant_dynamic-slice_fusion
  10.9 0.1 copy.8
  11.0 4.0 %collective-permute-start = (bf16[96,768]{1,0:T(8,128)(2,1)S(1)}, bf16[96,768]{1,0:T(8,128)(2,1)S(1)}, u32[]{:S(2)}, u32[]{:S(2)}) collective-permute-start(bf16[96,768]{1,0:T(8,128)(2,1)S(1)} %bitcast.17), channel_id=1, source_target_pairs={{0,56},{4,12},{8,0},{12,20},{16,8},{20,28},{24,16},{28,36},{32,24}... | collective-permute-start | bytes 442376 | tf_op jit(solution)/shard_map/ppermute | solution.py:23
  15.0 5.8 %collective-permute-start.1 = (bf16[96,768]{1,0:T(8,128)(2,1)S(1)}, bf16[96,768]{1,0:T(8,128)(2,1)S(1)}, u32[]{:S(2)}, u32[]{:S(2)}) collective-permute-start(bf16[96,768]{1,0:T(8,128)(2,1)S(1)} %bitcast.18), channel_id=1, source_target_pairs={{0,48},{4,20},{8,56},{12,28},{16,0},{20,36},{24,8},{28,44},{32,16}... | collective-permute-start | bytes 442376 | tf_op jit(solution)/shard_map/ppermute | solution.py:23
  20.8 5.9 %collective-permute-start.4 = (bf16[96,768]{1,0:T(8,128)(2,1)S(1)}, bf16[96,768]{1,0:T(8,128)(2,1)S(1)}, u32[]{:S(2)}, u32[]{:S(2)}) collective-permute-start(bf16[96,768]{1,0:T(8,128)(2,1)S(1)} %bitcast.19), channel_id=1, source_target_pairs={{0,16},{4,52},{8,24},{12,60},{16,32},{20,4},{24,40},{28,12},{32,48... | collective-permute-start | bytes 442376 | tf_op jit(solution)/shard_map/ppermute | solution.py:23
  26.7 3.1 %collective-permute-start.6 = (bf16[96,768]{1,0:T(8,128)(2,1)S(1)}, bf16[96,768]{1,0:T(8,128)(2,1)S(1)}, u32[]{:S(2)}, u32[]{:S(2)}) collective-permute-start(bf16[96,768]{1,0:T(8,128)(2,1)S(1)} %bitcast.20), channel_id=1, source_target_pairs={{0,8},{4,60},{8,16},{12,4},{16,24},{20,12},{24,32},{28,20},{32,40}... | collective-permute-start | bytes 442376 | tf_op jit(solution)/shard_map/ppermute | solution.py:23
  29.8 0.0 collective-permute-done.1
  29.8 2.2 %collective-permute-start.2 = (bf16[96,768]{1,0:T(8,128)(2,1)S(1)}, bf16[96,768]{1,0:T(8,128)(2,1)S(1)}, u32[]{:S(2)}, u32[]{:S(2)}) collective-permute-start(bf16[96,768]{1,0:T(8,128)(2,1)S(1)} %collective-permute-done.1), channel_id=1, source_target_pairs={{0,56},{4,12},{8,0},{12,20},{16,8},{20,28},{24,16},{28,36},{32,24}... | collective-permute-start | bytes 442376 | tf_op jit(solution)/shard_map/ppermute | solution.py:23
  32.0 2.2 %collective-permute-start.3 = (bf16[96,768]{1,0:T(8,128)(2,1)S(1)}, bf16[96,768]{1,0:T(8,128)(2,1)S(1)}, u32[]{:S(2)}, u32[]{:S(2)}) collective-permute-start(bf16[96,768]{1,0:T(8,128)(2,1)S(1)} %collective-permute-done.1), channel_id=1, source_target_pairs={{0,48},{4,20},{8,56},{12,28},{16,0},{20,36},{24,8},{28,44},{32,16}... | collective-permute-start | bytes 442376 | tf_op jit(solution)/shard_map/ppermute | solution.py:23
  34.3 0.0 collective-permute-done.4
  34.3 4.3 %collective-permute-start.5 = (bf16[96,768]{1,0:T(8,128)(2,1)S(1)}, bf16[96,768]{1,0:T(8,128)(2,1)S(1)}, u32[]{:S(2)}, u32[]{:S(2)}) collective-permute-start(bf16[96,768]{1,0:T(8,128)(2,1)S(1)} %collective-permute-done.4), channel_id=1, source_target_pairs={{0,8},{4,60},{8,16},{12,4},{16,24},{20,12},{24,32},{28,20},{32,40}... | collective-permute-start | bytes 442376 | tf_op jit(solution)/shard_map/ppermute | solution.py:23
  38.6 0.1 collective-permute-done.2
  38.6 1.9 %collective-permute-done.3 = bf16[96,768]{1,0:T(8,128)(2,1)S(1)} collective-permute-done((bf16[96,768]{1,0:T(8,128)(2,1)S(1)}, bf16[96,768]{1,0:T(8,128)(2,1)S(1)}, u32[]{:S(2)}, u32[]{:S(2)}) %collective-permute-start.3) | collective-permute-done | bytes 147488 | tf_op jit(solution)/shard_map/ppermute | solution.py:23
  40.5 1.5 %collective-permute-done.5 = bf16[96,768]{1,0:T(8,128)(2,1)S(1)} collective-permute-done((bf16[96,768]{1,0:T(8,128)(2,1)S(1)}, bf16[96,768]{1,0:T(8,128)(2,1)S(1)}, u32[]{:S(2)}, u32[]{:S(2)}) %collective-permute-start.5) | collective-permute-done | bytes 147488 | tf_op jit(solution)/shard_map/ppermute | solution.py:23
  42.0 0.0 all-to-all-done.right_ref
  42.1 9.6 %collective-permute-start.7 = (bf16[768,768]{1,0:T(8,128)(2,1)S(1)}, bf16[768,768]{1,0:T(8,128)(2,1)S(1)}, u32[]{:S(2)}, u32[]{:S(2)}) collective-permute-start(bf16[768,768]{1,0:T(8,128)(2,1)S(1)} %constant_dynamic-update-slice_fusion.own_ref), channel_id=1, source_target_pairs={{0,4},{4,0},{1,5},{5,1},{2,6},{6,2},{3,7},{7,3},{8,12},{12,8},{9,1... | collective-permute-start | bytes 3538952 | tf_op jit(solution)/shard_map/ppermute | solution.py:154
  51.6 0.1 pad_add_fusion.place_ref
  51.7 1.4 %shard_map.37.total_ref = f32[768,384]{1,0:T(8,128)S(1)} custom-call(s32[3]{0:T(128)S(1)} %pad_add_fusion.place_ref, bf16[768,768]{1,0:T(8,128)(2,1)S(1)} %constant_dynamic-update-slice_fusion.own_ref, bf16[8,2,96,384]{3,2,1,0:T(8,128)(2,1)S(1)} %all-to-all-done.right_ref), custom_call_target="tpu_custom_call" | custom-call | flops 452984832 | bytes 1769472 | tf_op jit(solution)/shard_map/pallas_call | solution.py:162
  53.1 1.0 collective-permute-done.7.other_ref
  54.1 1.6 %shard_map.38 = bf16[4,2,96,384]{3,2,1,0:T(8,128)(2,1)S(1)} custom-call(s32[3]{0:T(128)S(1)} %pad_add_fusion.place_ref, f32[768,384]{1,0:T(8,128)S(1)} %shard_map.37.total_ref, bf16[768,768]{1,0:T(8,128)(2,1)S(1)} %collective-permute-done.7.other_ref, bf16[8,2,96,384]{3,2,1,0:T(8,128)(2,1)S(1)} %all-to-all-done.right_ref), custom_call_target="tpu_custom_call" | custom-call | flops 452984832 | bytes 1769472 | tf_op jit(solution)/shard_map/pallas_call | solution.py:171
  55.7 0.8 copy-done
  56.5 4.1 %all-to-all-start.1 = ((bf16[4,2,96,384]{3,2,1,0:T(8,128)(2,1)}), bf16[4,2,96,384]{3,2,1,0:T(8,128)(2,1)S(1)}, u32[]{:S(2)}, u32[]{:S(2)}) async-start(bf16[4,2,96,384]{3,2,1,0:T(8,128)(2,1)} %copy-done), calls=%async_computation.1 | async-start | bytes 1179648 | tf_op jit(solution)/shard_map/all_to_all | solution.py:194
  60.7 0.1 copy.7.keep_ref
  60.8 9.5 %all-to-all-done.1.parts_ref = bf16[4,2,96,384]{3,2,1,0:T(8,128)(2,1)S(1)} async-done(((bf16[4,2,96,384]{3,2,1,0:T(8,128)(2,1)}), bf16[4,2,96,384]{3,2,1,0:T(8,128)(2,1)S(1)}, u32[]{:S(2)}, u32[]{:S(2)}) %all-to-all-start.1) | async-done | bytes 589856 | tf_op jit(solution)/shard_map/all_to_all | solution.py:194
  70.3 0.8 shard_map.40.refs_0_
  71.1 4.4 %collective-permute-start.8 = (bf16[2,96,384]{2,1,0:T(8,128)(2,1)S(1)}, bf16[2,96,384]{2,1,0:T(8,128)(2,1)S(1)}, u32[]{:S(2)}, u32[]{:S(2)}) collective-permute-start(bf16[2,96,384]{2,1,0:T(8,128)(2,1)S(1)} %shard_map.40.refs_0_), channel_id=1, source_target_pairs={{0,384},{4,132},{64,448},{68,196},{128,0},{132,260},{192,64},{196,... | collective-permute-start | bytes 442376 | tf_op jit(solution)/shard_map/ppermute | solution.py:23
  75.5 3.1 %collective-permute-start.12 = (bf16[2,96,384]{2,1,0:T(8,128)(2,1)S(1)}, bf16[2,96,384]{2,1,0:T(8,128)(2,1)S(1)}, u32[]{:S(2)}, u32[]{:S(2)}) collective-permute-start(bf16[2,96,384]{2,1,0:T(8,128)(2,1)S(1)} %shard_map.40.refs_0_), channel_id=1, source_target_pairs={{0,128},{4,388},{64,192},{68,452},{128,256},{132,4},{192,320},{196... | collective-permute-start | bytes 442376 | tf_op jit(solution)/shard_map/ppermute | solution.py:23
  78.7 1.6 %collective-permute-done.8.refs_2_ = bf16[2,96,384]{2,1,0:T(8,128)(2,1)S(1)} collective-permute-done((bf16[2,96,384]{2,1,0:T(8,128)(2,1)S(1)}, bf16[2,96,384]{2,1,0:T(8,128)(2,1)S(1)}, u32[]{:S(2)}, u32[]{:S(2)}) %collective-permute-start.8) | collective-permute-done | bytes 147488 | tf_op jit(solution)/shard_map/ppermute | solution.py:23
  80.3 3.6 %collective-permute-start.9 = (bf16[2,96,384]{2,1,0:T(8,128)(2,1)S(1)}, bf16[2,96,384]{2,1,0:T(8,128)(2,1)S(1)}, u32[]{:S(2)}, u32[]{:S(2)}) collective-permute-start(bf16[2,96,384]{2,1,0:T(8,128)(2,1)S(1)} %shard_map.40.refs_0_), channel_id=1, source_target_pairs={{0,448},{4,68},{64,0},{68,132},{128,64},{132,196},{192,128},{196,2... | collective-permute-start | bytes 442376 | tf_op jit(solution)/shard_map/ppermute | solution.py:23
  83.9 2.5 %collective-permute-start.10 = (bf16[2,96,384]{2,1,0:T(8,128)(2,1)S(1)}, bf16[2,96,384]{2,1,0:T(8,128)(2,1)S(1)}, u32[]{:S(2)}, u32[]{:S(2)}) collective-permute-start(bf16[2,96,384]{2,1,0:T(8,128)(2,1)S(1)} %collective-permute-done.8.refs_2_), channel_id=1, source_target_pairs={{0,448},{4,68},{64,0},{68,132},{128,64},{132,196},{192,128},{196,2... | collective-permute-start | bytes 442376 | tf_op jit(solution)/shard_map/ppermute | solution.py:23
  86.5 5.9 %collective-permute-start.11 = (bf16[2,96,384]{2,1,0:T(8,128)(2,1)S(1)}, bf16[2,96,384]{2,1,0:T(8,128)(2,1)S(1)}, u32[]{:S(2)}, u32[]{:S(2)}) collective-permute-start(bf16[2,96,384]{2,1,0:T(8,128)(2,1)S(1)} %collective-permute-done.8.refs_2_), channel_id=1, source_target_pairs={{0,384},{4,132},{64,448},{68,196},{128,0},{132,260},{192,64},{196,... | collective-permute-start | bytes 442376 | tf_op jit(solution)/shard_map/ppermute | solution.py:23
  92.4 0.0 collective-permute-done.12.refs_6_
  92.4 1.9 %collective-permute-start.13 = (bf16[2,96,384]{2,1,0:T(8,128)(2,1)S(1)}, bf16[2,96,384]{2,1,0:T(8,128)(2,1)S(1)}, u32[]{:S(2)}, u32[]{:S(2)}) collective-permute-start(bf16[2,96,384]{2,1,0:T(8,128)(2,1)S(1)} %collective-permute-done.12.refs_6_), channel_id=1, source_target_pairs={{0,64},{4,452},{64,128},{68,4},{128,192},{132,68},{192,256},{196,1... | collective-permute-start | bytes 442376 | tf_op jit(solution)/shard_map/ppermute | solution.py:23
  94.3 1.9 %collective-permute-start.14 = (bf16[2,96,384]{2,1,0:T(8,128)(2,1)S(1)}, bf16[2,96,384]{2,1,0:T(8,128)(2,1)S(1)}, u32[]{:S(2)}, u32[]{:S(2)}) collective-permute-start(bf16[2,96,384]{2,1,0:T(8,128)(2,1)S(1)} %shard_map.40.refs_0_), channel_id=1, source_target_pairs={{0,64},{4,452},{64,128},{68,4},{128,192},{132,68},{192,256},{196,1... | collective-permute-start | bytes 442376 | tf_op jit(solution)/shard_map/ppermute | solution.py:23
  96.3 0.0 copy-start.1
  96.3 0.0 copy-start.2
  96.3 0.7 shard_map.39
  97.0 1.3 collective-permute-done.13.refs_5_
  98.3 5.0 %collective-permute-done.14.refs_7_ = bf16[2,96,384]{2,1,0:T(8,128)(2,1)S(1)} collective-permute-done((bf16[2,96,384]{2,1,0:T(8,128)(2,1)S(1)}, bf16[2,96,384]{2,1,0:T(8,128)(2,1)S(1)}, u32[]{:S(2)}, u32[]{:S(2)}) %collective-permute-start.14) | collective-permute-done | bytes 147488 | tf_op jit(solution)/shard_map/ppermute | solution.py:23
  103.3 2.4 %shard_map.41 = bf16[16,32,128]{2,1,0:T(8,128)(2,1)S(1)} custom-call(s32[16]{0:T(128)S(1)} %bitcast.16, s32[3]{0:T(128)S(1)} %pad_add_fusion.place_ref, f32[1]{0:T(128)} %bitcast.4.scale_ref, bf16[768,768]{1,0:T(8,128)(2,1)S(1)} %get-tuple-element.18.own_ref, bf16[768,768]{1,0:T(8,128)(2,1)S(1)} %get-tuple-element.19.other_ref, ...), custom_call_target="tpu_custom_call" | custom-call | tf_op jit(solution)/shard_map/pallas_call | solution.py:207
  105.6 17.2 %all_to_all.20 = bf16[16,32,128]{2,1,0:T(8,128)(2,1)S(1)} all-to-all(bf16[16,32,128]{2,1,0:T(8,128)(2,1)S(1)} %shard_map.41), channel_id=1, replica_groups=mesh['row'=8,'z'=8,'core'=2,'layer'=4] {'z','core'}, dimensions={0} | all-to-all | bytes 262144 | tf_op jit(solution)/shard_map/all_to_all | solution.py:219
  122.8 0.1 broadcast_in_dim.15
  122.9 12.3 %all_to_all.21 = bf16[4,16,32,128]{3,2,1,0:T(8,128)(2,1)S(1)} all-to-all(bf16[4,16,32,128]{3,2,1,0:T(8,128)(2,1)S(1)} %broadcast_in_dim.15), channel_id=1, replica_groups=mesh['row'=8,'z'=8,'core'=2,'layer'=4] {'layer'}, dimensions={0} | all-to-all | bytes 1048576 | tf_op jit(solution)/shard_map/all_to_all | solution.py:14
  135.2 0.1 reduce_sum.12
  135.2 0.7 copy.11
  (18 shorter events, 0.1 us)
Async XLA Ops:
  2.1 40.0 %all-to-all-start = ((bf16[8,2,96,384]{3,2,1,0:T(8,128)(2,1)}), bf16[8,2,96,384]{3,2,1,0:T(8,128)(2,1)S(1)}, u32[]{:S(2)}, u32[]{:S(2)}) async-start(bf16[8,2,96,384]{3,2,1,0:T(8,128)(2,1)} %broadcast_in_dim.14), calls=%async_computation | async-start | bytes 2359296 | tf_op jit(solution)/shard_map/all_to_all | solution.py:14
  11.0 23.2 %collective-permute-start = (bf16[96,768]{1,0:T(8,128)(2,1)S(1)}, bf16[96,768]{1,0:T(8,128)(2,1)S(1)}, u32[]{:S(2)}, u32[]{:S(2)}) collective-permute-start(bf16[96,768]{1,0:T(8,128)(2,1)S(1)} %bitcast.17), channel_id=1, source_target_pairs={{0,56},{4,12},{8,0},{12,20},{16,8},{20,28},{24,16},{28,36},{32,24}... | collective-permute-start | bytes 442376 | tf_op jit(solution)/shard_map/ppermute | solution.py:23
  15.0 14.8 %collective-permute-start.1 = (bf16[96,768]{1,0:T(8,128)(2,1)S(1)}, bf16[96,768]{1,0:T(8,128)(2,1)S(1)}, u32[]{:S(2)}, u32[]{:S(2)}) collective-permute-start(bf16[96,768]{1,0:T(8,128)(2,1)S(1)} %bitcast.18), channel_id=1, source_target_pairs={{0,48},{4,20},{8,56},{12,28},{16,0},{20,36},{24,8},{28,44},{32,16}... | collective-permute-start | bytes 442376 | tf_op jit(solution)/shard_map/ppermute | solution.py:23
  20.8 13.4 %collective-permute-start.4 = (bf16[96,768]{1,0:T(8,128)(2,1)S(1)}, bf16[96,768]{1,0:T(8,128)(2,1)S(1)}, u32[]{:S(2)}, u32[]{:S(2)}) collective-permute-start(bf16[96,768]{1,0:T(8,128)(2,1)S(1)} %bitcast.19), channel_id=1, source_target_pairs={{0,16},{4,52},{8,24},{12,60},{16,32},{20,4},{24,40},{28,12},{32,48... | collective-permute-start | bytes 442376 | tf_op jit(solution)/shard_map/ppermute | solution.py:23
  26.7 15.3 %collective-permute-start.6 = (bf16[96,768]{1,0:T(8,128)(2,1)S(1)}, bf16[96,768]{1,0:T(8,128)(2,1)S(1)}, u32[]{:S(2)}, u32[]{:S(2)}) collective-permute-start(bf16[96,768]{1,0:T(8,128)(2,1)S(1)} %bitcast.20), channel_id=1, source_target_pairs={{0,8},{4,60},{8,16},{12,4},{16,24},{20,12},{24,32},{28,20},{32,40}... | collective-permute-start | bytes 442376 | tf_op jit(solution)/shard_map/ppermute | solution.py:23
  29.8 8.8 %collective-permute-start.2 = (bf16[96,768]{1,0:T(8,128)(2,1)S(1)}, bf16[96,768]{1,0:T(8,128)(2,1)S(1)}, u32[]{:S(2)}, u32[]{:S(2)}) collective-permute-start(bf16[96,768]{1,0:T(8,128)(2,1)S(1)} %collective-permute-done.1), channel_id=1, source_target_pairs={{0,56},{4,12},{8,0},{12,20},{16,8},{20,28},{24,16},{28,36},{32,24}... | collective-permute-start | bytes 442376 | tf_op jit(solution)/shard_map/ppermute | solution.py:23
  32.0 8.5 %collective-permute-start.3 = (bf16[96,768]{1,0:T(8,128)(2,1)S(1)}, bf16[96,768]{1,0:T(8,128)(2,1)S(1)}, u32[]{:S(2)}, u32[]{:S(2)}) collective-permute-start(bf16[96,768]{1,0:T(8,128)(2,1)S(1)} %collective-permute-done.1), channel_id=1, source_target_pairs={{0,48},{4,20},{8,56},{12,28},{16,0},{20,36},{24,8},{28,44},{32,16}... | collective-permute-start | bytes 442376 | tf_op jit(solution)/shard_map/ppermute | solution.py:23
  34.3 7.7 %collective-permute-start.5 = (bf16[96,768]{1,0:T(8,128)(2,1)S(1)}, bf16[96,768]{1,0:T(8,128)(2,1)S(1)}, u32[]{:S(2)}, u32[]{:S(2)}) collective-permute-start(bf16[96,768]{1,0:T(8,128)(2,1)S(1)} %collective-permute-done.4), channel_id=1, source_target_pairs={{0,8},{4,60},{8,16},{12,4},{16,24},{20,12},{24,32},{28,20},{32,40}... | collective-permute-start | bytes 442376 | tf_op jit(solution)/shard_map/ppermute | solution.py:23
  42.1 12.0 %collective-permute-start.7 = (bf16[768,768]{1,0:T(8,128)(2,1)S(1)}, bf16[768,768]{1,0:T(8,128)(2,1)S(1)}, u32[]{:S(2)}, u32[]{:S(2)}) collective-permute-start(bf16[768,768]{1,0:T(8,128)(2,1)S(1)} %constant_dynamic-update-slice_fusion.own_ref), channel_id=1, source_target_pairs={{0,4},{4,0},{1,5},{5,1},{2,6},{6,2},{3,7},{7,3},{8,12},{12,8},{9,1... | collective-permute-start | bytes 3538952 | tf_op jit(solution)/shard_map/ppermute | solution.py:154
  55.7 0.8 copy-start
  56.5 4.2 %copy-start.3 = (s32[12,6]{0,1:T(8,128)S(1)}, s32[12,6]{0,1:T(8,128)}, u32[]{:S(2)}) copy-start(s32[12,6]{0,1:T(8,128)} %param.4) | copy-start | bytes 868
  56.5 13.8 %all-to-all-start.1 = ((bf16[4,2,96,384]{3,2,1,0:T(8,128)(2,1)}), bf16[4,2,96,384]{3,2,1,0:T(8,128)(2,1)S(1)}, u32[]{:S(2)}, u32[]{:S(2)}) async-start(bf16[4,2,96,384]{3,2,1,0:T(8,128)(2,1)} %copy-done), calls=%async_computation.1 | async-start | bytes 1179648 | tf_op jit(solution)/shard_map/all_to_all | solution.py:194
  71.1 9.2 %collective-permute-start.8 = (bf16[2,96,384]{2,1,0:T(8,128)(2,1)S(1)}, bf16[2,96,384]{2,1,0:T(8,128)(2,1)S(1)}, u32[]{:S(2)}, u32[]{:S(2)}) collective-permute-start(bf16[2,96,384]{2,1,0:T(8,128)(2,1)S(1)} %shard_map.40.refs_0_), channel_id=1, source_target_pairs={{0,384},{4,132},{64,448},{68,196},{128,0},{132,260},{192,64},{196,... | collective-permute-start | bytes 442376 | tf_op jit(solution)/shard_map/ppermute | solution.py:23
  75.5 16.9 %collective-permute-start.12 = (bf16[2,96,384]{2,1,0:T(8,128)(2,1)S(1)}, bf16[2,96,384]{2,1,0:T(8,128)(2,1)S(1)}, u32[]{:S(2)}, u32[]{:S(2)}) collective-permute-start(bf16[2,96,384]{2,1,0:T(8,128)(2,1)S(1)} %shard_map.40.refs_0_), channel_id=1, source_target_pairs={{0,128},{4,388},{64,192},{68,452},{128,256},{132,4},{192,320},{196... | collective-permute-start | bytes 442376 | tf_op jit(solution)/shard_map/ppermute | solution.py:23
  80.3 16.7 %collective-permute-start.9 = (bf16[2,96,384]{2,1,0:T(8,128)(2,1)S(1)}, bf16[2,96,384]{2,1,0:T(8,128)(2,1)S(1)}, u32[]{:S(2)}, u32[]{:S(2)}) collective-permute-start(bf16[2,96,384]{2,1,0:T(8,128)(2,1)S(1)} %shard_map.40.refs_0_), channel_id=1, source_target_pairs={{0,448},{4,68},{64,0},{68,132},{128,64},{132,196},{192,128},{196,2... | collective-permute-start | bytes 442376 | tf_op jit(solution)/shard_map/ppermute | solution.py:23
  83.9 13.0 %collective-permute-start.10 = (bf16[2,96,384]{2,1,0:T(8,128)(2,1)S(1)}, bf16[2,96,384]{2,1,0:T(8,128)(2,1)S(1)}, u32[]{:S(2)}, u32[]{:S(2)}) collective-permute-start(bf16[2,96,384]{2,1,0:T(8,128)(2,1)S(1)} %collective-permute-done.8.refs_2_), channel_id=1, source_target_pairs={{0,448},{4,68},{64,0},{68,132},{128,64},{132,196},{192,128},{196,2... | collective-permute-start | bytes 442376 | tf_op jit(solution)/shard_map/ppermute | solution.py:23
  86.5 10.5 %collective-permute-start.11 = (bf16[2,96,384]{2,1,0:T(8,128)(2,1)S(1)}, bf16[2,96,384]{2,1,0:T(8,128)(2,1)S(1)}, u32[]{:S(2)}, u32[]{:S(2)}) collective-permute-start(bf16[2,96,384]{2,1,0:T(8,128)(2,1)S(1)} %collective-permute-done.8.refs_2_), channel_id=1, source_target_pairs={{0,384},{4,132},{64,448},{68,196},{128,0},{132,260},{192,64},{196,... | collective-permute-start | bytes 442376 | tf_op jit(solution)/shard_map/ppermute | solution.py:23
  92.4 5.9 %collective-permute-start.13 = (bf16[2,96,384]{2,1,0:T(8,128)(2,1)S(1)}, bf16[2,96,384]{2,1,0:T(8,128)(2,1)S(1)}, u32[]{:S(2)}, u32[]{:S(2)}) collective-permute-start(bf16[2,96,384]{2,1,0:T(8,128)(2,1)S(1)} %collective-permute-done.12.refs_6_), channel_id=1, source_target_pairs={{0,64},{4,452},{64,128},{68,4},{128,192},{132,68},{192,256},{196,1... | collective-permute-start | bytes 442376 | tf_op jit(solution)/shard_map/ppermute | solution.py:23
  94.3 8.9 %collective-permute-start.14 = (bf16[2,96,384]{2,1,0:T(8,128)(2,1)S(1)}, bf16[2,96,384]{2,1,0:T(8,128)(2,1)S(1)}, u32[]{:S(2)}, u32[]{:S(2)}) collective-permute-start(bf16[2,96,384]{2,1,0:T(8,128)(2,1)S(1)} %shard_map.40.refs_0_), channel_id=1, source_target_pairs={{0,64},{4,452},{64,128},{68,4},{128,192},{132,68},{192,256},{196,1... | collective-permute-start | bytes 442376 | tf_op jit(solution)/shard_map/ppermute | solution.py:23
  96.3 7.0 %copy-start.1 = (bf16[768,384]{1,0:T(8,128)(2,1)S(1)}, bf16[768,384]{1,0:T(8,128)(2,1)}, u32[]{:S(2)}) copy-start(bf16[768,384]{1,0:T(8,128)(2,1)} %matrix_ref.1) | copy-start | bytes 1769476
  96.3 7.0 %copy-start.2 = (s32[1,16]{1,0:T(1,128)S(1)}, s32[1,16]{1,0:T(1,128)}, u32[]{:S(2)}) copy-start(s32[1,16]{1,0:T(1,128)} %param.5) | copy-start | bytes 196

commit v12 on v8

--- a/solution.py
+++ b/solution.py
@@ -32,6 +32,16 @@
     far_down = shifted(down, axis, -1)
     opposite = shifted(up, axis, 2)
     return piece, near_up, up, far_up, opposite, far_down, down, near_down
+
+
+def ring_with_pair(piece, axis):
+    up = shifted(piece, axis, 2)
+    down = shifted(piece, axis, -2)
+    near_up = shifted(piece, axis, 1)
+    near_down = shifted(piece, axis, -1)
+    pair = shifted(jnp.concatenate([near_up, up]), axis, 2)
+    far_down = shifted(down, axis, -1)
+    return piece, near_up, up, pair, far_down, down, near_down
 
 
 def own_kernel(place_ref, own_ref, right_ref, total_ref, ordered_ref):
@@ -88,8 +98,10 @@
 
 
 def cube_kernel(chosen_ref, place_ref, scale_ref, own_ref, other_ref, matrix_ref, *refs):
-    pieces = refs[:8]
-    out_ref, ordered_ref, total_ref, block_ref = refs[8:]
+    halves = refs[0].shape[0]
+    pair = (refs[3].at[pl.ds(0, halves)], refs[3].at[pl.ds(halves, halves)])
+    pieces = refs[:3] + pair + refs[4:7]
+    out_ref, ordered_ref, total_ref, block_ref = refs[7:]
     owners, pairs, lanes = out_ref.shape
     half_blocks = matrix_ref.shape[1] // BLK
     tiles = ordered_ref.shape[1]
@@ -196,7 +208,7 @@
         out_specs=vmem,
         compiler_params=params,
     )(keep_mask, layer_index.reshape(1), parts)
-    filtered = ring_of_eight(filtered_piece, "row")
+    filtered = ring_with_pair(filtered_piece, "row")
 
     scale = jnp.where(layer_index == 0, 1.5, 0.0).astype(jnp.float32).reshape(1)
     chosen = send_list[0]
@@ -204,7 +216,7 @@
     outgoing = pl.pallas_call(
         cube_kernel,
         out_shape=jax.ShapeDtypeStruct((chosen.shape[0], pairs, 128), jnp.bfloat16),
-        in_specs=[smem] * 3 + [vmem] * 11,
+        in_specs=[smem] * 3 + [vmem] * 10,
         out_specs=vmem,
         scratch_shapes=[
             pltpu.VMEM((halves, rows_count, part, width), jnp.bfloat16),

time: 131 us -> 136 us (1.038)
  blocking collectives: 26.5 us -> 31.8 us
  starting transfers between devices: 72.1 us -> 69.5 us
    all_to_all x1, blocking collectives: 14.2 us -> 19.5 us  [on_device(): lax.all_to_all(outgoing, ('z', 'core'), split_axis=0, concat_axis=0, tile...]
    ppermute x14 -> x13, starting transfers between devices: 50.8 us -> 48.2 us  [shifted(): return lax.ppermute(piece, (axis, 'core'), pairs)]
    ppermute x14 -> x13, waiting for transfers between devices: 8.78 us -> 9.77 us  [shifted(): return lax.ppermute(piece, (axis, 'core'), pairs)]
  transfers between devices with their start and end apart: 17 -> 16, of which waited for: 6 -> 6; matrix products, arithmetic and copies ran while one was open for 1% -> 2% of each run, Pallas kernels for 2% -> 2%
where the time goes in v12:
time: 136 us; the launch traced here: 135 us
  starting transfers between devices  69.5 us (51%)
  blocking collectives  31.8 us (23%)
  waiting for transfers between devices  20.3 us (15%)
  Pallas kernels  6.79 us (5%)
  local copies, waits for them, and re-layouts  5.16 us (4%)
    ppermute x13, starting transfers between devices, shifted(): return lax.ppermute(piece, (axis, 'core'), pairs)  48.2 us
    all_to_all x1, blocking collectives, on_device(): lax.all_to_all(outgoing, ('z', 'core'), split_axis=0, concat_axis=0, tile...  19.5 us
    all_to_all x1, blocking collectives, to_all(): return lax.all_to_all(copies, axis, split_axis=0, concat_axis=0, tiled=True)  12.3 us
    ppermute x13, waiting for transfers between devices, shifted(): return lax.ppermute(piece, (axis, 'core'), pairs)  9.77 us
    ppermute x1, starting transfers between devices, on_device(): left_other = lax.ppermute(left_own, 'core', [(0, 1), (1, 0)])  9.55 us
    all_to_all x1, waiting for transfers between devices, on_device(): lax.all_to_all(square_part, 'layer', split_axis=0, concat_axis=0, tiled=T...  9.49 us
    all_to_all x1, starting transfers between devices, to_all(): return lax.all_to_all(copies, axis, split_axis=0, concat_axis=0, tiled=True)  7.65 us
    all_to_all x1, starting transfers between devices, on_device(): lax.all_to_all(square_part, 'layer', split_axis=0, concat_axis=0, tiled=T...  4.14 us
  transfers between devices with their start and end apart: 16, of which 6 were waited for; matrix products, arithmetic and copies ran while one was open for 2% of the time, Pallas kernels for 2%

profile of v12, /device:TPU:1, one launch (start us, length us, event | category | flops | bytes accessed | tf_op | source)
XLA Modules:
  0.0 134.8 jit_solution(17870035456841995176)
XLA Ops:
  0.0 0.9 dynamic-slice_bitcast_fusion
  0.9 1.2 broadcast_in_dim.14
  2.1 7.7 %all-to-all-start = ((bf16[8,2,96,384]{3,2,1,0:T(8,128)(2,1)}), bf16[8,2,96,384]{3,2,1,0:T(8,128)(2,1)S(1)}, u32[]{:S(2)}, u32[]{:S(2)}) async-start(bf16[8,2,96,384]{3,2,1,0:T(8,128)(2,1)} %broadcast_in_dim.14), calls=%async_computation | async-start | bytes 2359296 | tf_op jit(solution)/shard_map/all_to_all | solution.py:14
  9.8 1.1 constant_dynamic-slice_fusion
  10.9 0.1 copy.8
  11.0 4.0 %collective-permute-start = (bf16[96,768]{1,0:T(8,128)(2,1)S(1)}, bf16[96,768]{1,0:T(8,128)(2,1)S(1)}, u32[]{:S(2)}, u32[]{:S(2)}) collective-permute-start(bf16[96,768]{1,0:T(8,128)(2,1)S(1)} %bitcast.17), channel_id=1, source_target_pairs={{0,56},{4,12},{8,0},{12,20},{16,8},{20,28},{24,16},{28,36},{32,24}... | collective-permute-start | bytes 442376 | tf_op jit(solution)/shard_map/ppermute | solution.py:23
  15.0 5.8 %collective-permute-start.1 = (bf16[96,768]{1,0:T(8,128)(2,1)S(1)}, bf16[96,768]{1,0:T(8,128)(2,1)S(1)}, u32[]{:S(2)}, u32[]{:S(2)}) collective-permute-start(bf16[96,768]{1,0:T(8,128)(2,1)S(1)} %bitcast.18), channel_id=1, source_target_pairs={{0,48},{4,20},{8,56},{12,28},{16,0},{20,36},{24,8},{28,44},{32,16}... | collective-permute-start | bytes 442376 | tf_op jit(solution)/shard_map/ppermute | solution.py:23
  20.8 5.9 %collective-permute-start.4 = (bf16[96,768]{1,0:T(8,128)(2,1)S(1)}, bf16[96,768]{1,0:T(8,128)(2,1)S(1)}, u32[]{:S(2)}, u32[]{:S(2)}) collective-permute-start(bf16[96,768]{1,0:T(8,128)(2,1)S(1)} %bitcast.19), channel_id=1, source_target_pairs={{0,16},{4,52},{8,24},{12,60},{16,32},{20,4},{24,40},{28,12},{32,48... | collective-permute-start | bytes 442376 | tf_op jit(solution)/shard_map/ppermute | solution.py:23
  26.7 3.1 %collective-permute-start.6 = (bf16[96,768]{1,0:T(8,128)(2,1)S(1)}, bf16[96,768]{1,0:T(8,128)(2,1)S(1)}, u32[]{:S(2)}, u32[]{:S(2)}) collective-permute-start(bf16[96,768]{1,0:T(8,128)(2,1)S(1)} %bitcast.20), channel_id=1, source_target_pairs={{0,8},{4,60},{8,16},{12,4},{16,24},{20,12},{24,32},{28,20},{32,40}... | collective-permute-start | bytes 442376 | tf_op jit(solution)/shard_map/ppermute | solution.py:23
  29.8 0.0 collective-permute-done.1
  29.8 2.2 %collective-permute-start.2 = (bf16[96,768]{1,0:T(8,128)(2,1)S(1)}, bf16[96,768]{1,0:T(8,128)(2,1)S(1)}, u32[]{:S(2)}, u32[]{:S(2)}) collective-permute-start(bf16[96,768]{1,0:T(8,128)(2,1)S(1)} %collective-permute-done.1), channel_id=1, source_target_pairs={{0,56},{4,12},{8,0},{12,20},{16,8},{20,28},{24,16},{28,36},{32,24}... | collective-permute-start | bytes 442376 | tf_op jit(solution)/shard_map/ppermute | solution.py:23
  32.0 2.2 %collective-permute-start.3 = (bf16[96,768]{1,0:T(8,128)(2,1)S(1)}, bf16[96,768]{1,0:T(8,128)(2,1)S(1)}, u32[]{:S(2)}, u32[]{:S(2)}) collective-permute-start(bf16[96,768]{1,0:T(8,128)(2,1)S(1)} %collective-permute-done.1), channel_id=1, source_target_pairs={{0,48},{4,20},{8,56},{12,28},{16,0},{20,36},{24,8},{28,44},{32,16}... | collective-permute-start | bytes 442376 | tf_op jit(solution)/shard_map/ppermute | solution.py:23
  34.2 0.0 collective-permute-done
  34.3 4.3 %collective-permute-start.5 = (bf16[96,768]{1,0:T(8,128)(2,1)S(1)}, bf16[96,768]{1,0:T(8,128)(2,1)S(1)}, u32[]{:S(2)}, u32[]{:S(2)}) collective-permute-start(bf16[96,768]{1,0:T(8,128)(2,1)S(1)} %collective-permute-done.4), channel_id=1, source_target_pairs={{0,8},{4,60},{8,16},{12,4},{16,24},{20,12},{24,32},{28,20},{32,40}... | collective-permute-start | bytes 442376 | tf_op jit(solution)/shard_map/ppermute | solution.py:23
  38.6 0.1 collective-permute-done.2
  38.7 1.9 %collective-permute-done.3 = bf16[96,768]{1,0:T(8,128)(2,1)S(1)} collective-permute-done((bf16[96,768]{1,0:T(8,128)(2,1)S(1)}, bf16[96,768]{1,0:T(8,128)(2,1)S(1)}, u32[]{:S(2)}, u32[]{:S(2)}) %collective-permute-start.3) | collective-permute-done | bytes 147488 | tf_op jit(solution)/shard_map/ppermute | solution.py:23
  40.5 1.5 %collective-permute-done.5 = bf16[96,768]{1,0:T(8,128)(2,1)S(1)} collective-permute-done((bf16[96,768]{1,0:T(8,128)(2,1)S(1)}, bf16[96,768]{1,0:T(8,128)(2,1)S(1)}, u32[]{:S(2)}, u32[]{:S(2)}) %collective-permute-start.5) | collective-permute-done | bytes 147488 | tf_op jit(solution)/shard_map/ppermute | solution.py:23
  42.0 0.0 collective-permute-done.6
  42.1 9.6 %collective-permute-start.7 = (bf16[768,768]{1,0:T(8,128)(2,1)S(1)}, bf16[768,768]{1,0:T(8,128)(2,1)S(1)}, u32[]{:S(2)}, u32[]{:S(2)}) collective-permute-start(bf16[768,768]{1,0:T(8,128)(2,1)S(1)} %constant_dynamic-update-slice_fusion.own_ref), channel_id=1, source_target_pairs={{0,4},{4,0},{1,5},{5,1},{2,6},{6,2},{3,7},{7,3},{8,12},{12,8},{9,1... | collective-permute-start | bytes 3538952 | tf_op jit(solution)/shard_map/ppermute | solution.py:163
  51.6 0.1 pad_add_fusion.place_ref
  51.7 1.4 %shard_map.37.total_ref = f32[768,384]{1,0:T(8,128)S(1)} custom-call(s32[3]{0:T(128)S(1)} %pad_add_fusion.place_ref, bf16[768,768]{1,0:T(8,128)(2,1)S(1)} %constant_dynamic-update-slice_fusion.own_ref, bf16[8,2,96,384]{3,2,1,0:T(8,128)(2,1)S(1)} %all-to-all-done.right_ref), custom_call_target="tpu_custom_call" | custom-call | flops 452984832 | bytes 1769472 | tf_op jit(solution)/shard_map/pallas_call | solution.py:171
  53.1 1.0 collective-permute-done.7.other_ref
  54.1 1.6 %shard_map.38 = bf16[4,2,96,384]{3,2,1,0:T(8,128)(2,1)S(1)} custom-call(s32[3]{0:T(128)S(1)} %pad_add_fusion.place_ref, f32[768,384]{1,0:T(8,128)S(1)} %shard_map.37.total_ref, bf16[768,768]{1,0:T(8,128)(2,1)S(1)} %collective-permute-done.7.other_ref, bf16[8,2,96,384]{3,2,1,0:T(8,128)(2,1)S(1)} %all-to-all-done.right_ref), custom_call_target="tpu_custom_call" | custom-call | flops 452984832 | bytes 1769472 | tf_op jit(solution)/shard_map/pallas_call | solution.py:180
  55.7 0.8 copy-done
  56.5 4.1 %all-to-all-start.1 = ((bf16[4,2,96,384]{3,2,1,0:T(8,128)(2,1)}), bf16[4,2,96,384]{3,2,1,0:T(8,128)(2,1)S(1)}, u32[]{:S(2)}, u32[]{:S(2)}) async-start(bf16[4,2,96,384]{3,2,1,0:T(8,128)(2,1)} %copy-done), calls=%async_computation.1 | async-start | bytes 1179648 | tf_op jit(solution)/shard_map/all_to_all | solution.py:203
  60.7 0.1 copy.7.keep_ref
  60.8 9.5 %all-to-all-done.1.parts_ref = bf16[4,2,96,384]{3,2,1,0:T(8,128)(2,1)S(1)} async-done(((bf16[4,2,96,384]{3,2,1,0:T(8,128)(2,1)}), bf16[4,2,96,384]{3,2,1,0:T(8,128)(2,1)S(1)}, u32[]{:S(2)}, u32[]{:S(2)}) %all-to-all-start.1) | async-done | bytes 589856 | tf_op jit(solution)/shard_map/all_to_all | solution.py:203
  70.3 0.8 shard_map.40.refs_0_
  71.1 3.6 %collective-permute-start.8 = (bf16[2,96,384]{2,1,0:T(8,128)(2,1)S(1)}, bf16[2,96,384]{2,1,0:T(8,128)(2,1)S(1)}, u32[]{:S(2)}, u32[]{:S(2)}) collective-permute-start(bf16[2,96,384]{2,1,0:T(8,128)(2,1)S(1)} %shard_map.40.refs_0_), channel_id=1, source_target_pairs={{0,448},{4,68},{64,0},{68,132},{128,64},{132,196},{192,128},{196,2... | collective-permute-start | bytes 442376 | tf_op jit(solution)/shard_map/ppermute | solution.py:23
  74.6 4.0 %collective-permute-start.9 = (bf16[2,96,384]{2,1,0:T(8,128)(2,1)S(1)}, bf16[2,96,384]{2,1,0:T(8,128)(2,1)S(1)}, u32[]{:S(2)}, u32[]{:S(2)}) collective-permute-start(bf16[2,96,384]{2,1,0:T(8,128)(2,1)S(1)} %shard_map.40.refs_0_), channel_id=1, source_target_pairs={{0,384},{4,132},{64,448},{68,196},{128,0},{132,260},{192,64},{196,... | collective-permute-start | bytes 442376 | tf_op jit(solution)/shard_map/ppermute | solution.py:23
  78.6 3.4 %collective-permute-start.11 = (bf16[2,96,384]{2,1,0:T(8,128)(2,1)S(1)}, bf16[2,96,384]{2,1,0:T(8,128)(2,1)S(1)}, u32[]{:S(2)}, u32[]{:S(2)}) collective-permute-start(bf16[2,96,384]{2,1,0:T(8,128)(2,1)S(1)} %shard_map.40.refs_0_), channel_id=1, source_target_pairs={{0,128},{4,388},{64,192},{68,452},{128,256},{132,4},{192,320},{196... | collective-permute-start | bytes 442376 | tf_op jit(solution)/shard_map/ppermute | solution.py:23
  82.1 0.0 collective-permute-done.8.refs_1_
  82.1 1.7 %collective-permute-done.9.refs_2_ = bf16[2,96,384]{2,1,0:T(8,128)(2,1)S(1)} collective-permute-done((bf16[2,96,384]{2,1,0:T(8,128)(2,1)S(1)}, bf16[2,96,384]{2,1,0:T(8,128)(2,1)S(1)}, u32[]{:S(2)}, u32[]{:S(2)}) %collective-permute-start.9) | collective-permute-done | bytes 147488 | tf_op jit(solution)/shard_map/ppermute | solution.py:23
  83.7 0.7 pad_maximum_fusion
  84.5 3.1 %collective-permute-start.10 = (bf16[4,96,384]{2,1,0:T(8,128)(2,1)}, bf16[4,96,384]{2,1,0:T(8,128)(2,1)S(1)}, u32[]{:S(2)}, u32[]{:S(2)}) collective-permute-start(bf16[4,96,384]{2,1,0:T(8,128)(2,1)} %pad_maximum_fusion), channel_id=1, source_target_pairs={{0,384},{4,132},{64,448},{68,196},{128,0},{132,260},{192,64},{196,... | collective-permute-start | bytes 884744 | tf_op jit(solution)/shard_map/ppermute | solution.py:23
  87.5 4.8 %collective-permute-start.13 = (bf16[2,96,384]{2,1,0:T(8,128)(2,1)S(1)}, bf16[2,96,384]{2,1,0:T(8,128)(2,1)S(1)}, u32[]{:S(2)}, u32[]{:S(2)}) collective-permute-start(bf16[2,96,384]{2,1,0:T(8,128)(2,1)S(1)} %shard_map.40.refs_0_), channel_id=1, source_target_pairs={{0,64},{4,452},{64,128},{68,4},{128,192},{132,68},{192,256},{196,1... | collective-permute-start | bytes 442376 | tf_op jit(solution)/shard_map/ppermute | solution.py:23
  92.4 1.9 %collective-permute-start.12 = (bf16[2,96,384]{2,1,0:T(8,128)(2,1)S(1)}, bf16[2,96,384]{2,1,0:T(8,128)(2,1)S(1)}, u32[]{:S(2)}, u32[]{:S(2)}) collective-permute-start(bf16[2,96,384]{2,1,0:T(8,128)(2,1)S(1)} %collective-permute-done.11.refs_5_), channel_id=1, source_target_pairs={{0,64},{4,452},{64,128},{68,4},{128,192},{132,68},{192,256},{196,1... | collective-permute-start | bytes 442376 | tf_op jit(solution)/shard_map/ppermute | solution.py:23
  94.3 0.0 copy-start.1
  94.3 0.0 copy-start.2
  94.3 0.7 shard_map.39
  95.0 0.0 collective-permute-done.13.refs_6_
  95.0 4.7 %collective-permute-done.12.refs_4_ = bf16[2,96,384]{2,1,0:T(8,128)(2,1)S(1)} collective-permute-done((bf16[2,96,384]{2,1,0:T(8,128)(2,1)S(1)}, bf16[2,96,384]{2,1,0:T(8,128)(2,1)S(1)}, u32[]{:S(2)}, u32[]{:S(2)}) %collective-permute-start.12) | collective-permute-done | bytes 147488 | tf_op jit(solution)/shard_map/ppermute | solution.py:23
  99.7 2.4 %shard_map.41 = bf16[16,32,128]{2,1,0:T(8,128)(2,1)S(1)} custom-call(s32[16]{0:T(128)S(1)} %bitcast.16, s32[3]{0:T(128)S(1)} %pad_add_fusion.place_ref, f32[1]{0:T(128)} %bitcast.4.scale_ref, bf16[768,768]{1,0:T(8,128)(2,1)S(1)} %get-tuple-element.16.own_ref, bf16[768,768]{1,0:T(8,128)(2,1)S(1)} %get-tuple-element.17.other_ref, ...), custom_call_target="tpu_custom_call" | custom-call | tf_op jit(solution)/shard_map/pallas_call | solution.py:216
  102.1 19.5 %all_to_all.20 = bf16[16,32,128]{2,1,0:T(8,128)(2,1)S(1)} all-to-all(bf16[16,32,128]{2,1,0:T(8,128)(2,1)S(1)} %shard_map.41), channel_id=1, replica_groups=mesh['row'=8,'z'=8,'core'=2,'layer'=4] {'z','core'}, dimensions={0} | all-to-all | bytes 262144 | tf_op jit(solution)/shard_map/all_to_all | solution.py:228
  121.6 0.1 broadcast_in_dim.15
  121.7 12.3 %all_to_all.21 = bf16[4,16,32,128]{3,2,1,0:T(8,128)(2,1)S(1)} all-to-all(bf16[4,16,32,128]{3,2,1,0:T(8,128)(2,1)S(1)} %broadcast_in_dim.15), channel_id=1, replica_groups=mesh['row'=8,'z'=8,'core'=2,'layer'=4] {'layer'}, dimensions={0} | all-to-all | bytes 1048576 | tf_op jit(solution)/shard_map/all_to_all | solution.py:14
  134.0 0.1 reduce_sum.12
  134.1 0.7 copy.11
  (17 shorter events, 0.1 us)
Async XLA Ops:
  2.1 40.0 %all-to-all-start = ((bf16[8,2,96,384]{3,2,1,0:T(8,128)(2,1)}), bf16[8,2,96,384]{3,2,1,0:T(8,128)(2,1)S(1)}, u32[]{:S(2)}, u32[]{:S(2)}) async-start(bf16[8,2,96,384]{3,2,1,0:T(8,128)(2,1)} %broadcast_in_dim.14), calls=%async_computation | async-start | bytes 2359296 | tf_op jit(solution)/shard_map/all_to_all | solution.py:14
  11.0 23.2 %collective-permute-start = (bf16[96,768]{1,0:T(8,128)(2,1)S(1)}, bf16[96,768]{1,0:T(8,128)(2,1)S(1)}, u32[]{:S(2)}, u32[]{:S(2)}) collective-permute-start(bf16[96,768]{1,0:T(8,128)(2,1)S(1)} %bitcast.17), channel_id=1, source_target_pairs={{0,56},{4,12},{8,0},{12,20},{16,8},{20,28},{24,16},{28,36},{32,24}... | collective-permute-start | bytes 442376 | tf_op jit(solution)/shard_map/ppermute | solution.py:23
  15.0 14.8 %collective-permute-start.1 = (bf16[96,768]{1,0:T(8,128)(2,1)S(1)}, bf16[96,768]{1,0:T(8,128)(2,1)S(1)}, u32[]{:S(2)}, u32[]{:S(2)}) collective-permute-start(bf16[96,768]{1,0:T(8,128)(2,1)S(1)} %bitcast.18), channel_id=1, source_target_pairs={{0,48},{4,20},{8,56},{12,28},{16,0},{20,36},{24,8},{28,44},{32,16}... | collective-permute-start | bytes 442376 | tf_op jit(solution)/shard_map/ppermute | solution.py:23
  20.8 13.4 %collective-permute-start.4 = (bf16[96,768]{1,0:T(8,128)(2,1)S(1)}, bf16[96,768]{1,0:T(8,128)(2,1)S(1)}, u32[]{:S(2)}, u32[]{:S(2)}) collective-permute-start(bf16[96,768]{1,0:T(8,128)(2,1)S(1)} %bitcast.19), channel_id=1, source_target_pairs={{0,16},{4,52},{8,24},{12,60},{16,32},{20,4},{24,40},{28,12},{32,48... | collective-permute-start | bytes 442376 | tf_op jit(solution)/shard_map/ppermute | solution.py:23
  26.7 15.3 %collective-permute-start.6 = (bf16[96,768]{1,0:T(8,128)(2,1)S(1)}, bf16[96,768]{1,0:T(8,128)(2,1)S(1)}, u32[]{:S(2)}, u32[]{:S(2)}) collective-permute-start(bf16[96,768]{1,0:T(8,128)(2,1)S(1)} %bitcast.20), channel_id=1, source_target_pairs={{0,8},{4,60},{8,16},{12,4},{16,24},{20,12},{24,32},{28,20},{32,40}... | collective-permute-start | bytes 442376 | tf_op jit(solution)/shard_map/ppermute | solution.py:23
  29.8 8.8 %collective-permute-start.2 = (bf16[96,768]{1,0:T(8,128)(2,1)S(1)}, bf16[96,768]{1,0:T(8,128)(2,1)S(1)}, u32[]{:S(2)}, u32[]{:S(2)}) collective-permute-start(bf16[96,768]{1,0:T(8,128)(2,1)S(1)} %collective-permute-done.1), channel_id=1, source_target_pairs={{0,56},{4,12},{8,0},{12,20},{16,8},{20,28},{24,16},{28,36},{32,24}... | collective-permute-start | bytes 442376 | tf_op jit(solution)/shard_map/ppermute | solution.py:23
  32.0 8.5 %collective-permute-start.3 = (bf16[96,768]{1,0:T(8,128)(2,1)S(1)}, bf16[96,768]{1,0:T(8,128)(2,1)S(1)}, u32[]{:S(2)}, u32[]{:S(2)}) collective-permute-start(bf16[96,768]{1,0:T(8,128)(2,1)S(1)} %collective-permute-done.1), channel_id=1, source_target_pairs={{0,48},{4,20},{8,56},{12,28},{16,0},{20,36},{24,8},{28,44},{32,16}... | collective-permute-start | bytes 442376 | tf_op jit(solution)/shard_map/ppermute | solution.py:23
  34.3 7.7 %collective-permute-start.5 = (bf16[96,768]{1,0:T(8,128)(2,1)S(1)}, bf16[96,768]{1,0:T(8,128)(2,1)S(1)}, u32[]{:S(2)}, u32[]{:S(2)}) collective-permute-start(bf16[96,768]{1,0:T(8,128)(2,1)S(1)} %collective-permute-done.4), channel_id=1, source_target_pairs={{0,8},{4,60},{8,16},{12,4},{16,24},{20,12},{24,32},{28,20},{32,40}... | collective-permute-start | bytes 442376 | tf_op jit(solution)/shard_map/ppermute | solution.py:23
  42.1 12.0 %collective-permute-start.7 = (bf16[768,768]{1,0:T(8,128)(2,1)S(1)}, bf16[768,768]{1,0:T(8,128)(2,1)S(1)}, u32[]{:S(2)}, u32[]{:S(2)}) collective-permute-start(bf16[768,768]{1,0:T(8,128)(2,1)S(1)} %constant_dynamic-update-slice_fusion.own_ref), channel_id=1, source_target_pairs={{0,4},{4,0},{1,5},{5,1},{2,6},{6,2},{3,7},{7,3},{8,12},{12,8},{9,1... | collective-permute-start | bytes 3538952 | tf_op jit(solution)/shard_map/ppermute | solution.py:163
  55.7 0.8 copy-start
  56.5 4.1 %copy-start.3 = (s32[12,6]{0,1:T(8,128)S(1)}, s32[12,6]{0,1:T(8,128)}, u32[]{:S(2)}) copy-start(s32[12,6]{0,1:T(8,128)} %param.4) | copy-start | bytes 868
  56.5 13.7 %all-to-all-start.1 = ((bf16[4,2,96,384]{3,2,1,0:T(8,128)(2,1)}), bf16[4,2,96,384]{3,2,1,0:T(8,128)(2,1)S(1)}, u32[]{:S(2)}, u32[]{:S(2)}) async-start(bf16[4,2,96,384]{3,2,1,0:T(8,128)(2,1)} %copy-done), calls=%async_computation.1 | async-start | bytes 1179648 | tf_op jit(solution)/shard_map/all_to_all | solution.py:203
  71.1 11.0 %collective-permute-start.8 = (bf16[2,96,384]{2,1,0:T(8,128)(2,1)S(1)}, bf16[2,96,384]{2,1,0:T(8,128)(2,1)S(1)}, u32[]{:S(2)}, u32[]{:S(2)}) collective-permute-start(bf16[2,96,384]{2,1,0:T(8,128)(2,1)S(1)} %shard_map.40.refs_0_), channel_id=1, source_target_pairs={{0,448},{4,68},{64,0},{68,132},{128,64},{132,196},{192,128},{196,2... | collective-permute-start | bytes 442376 | tf_op jit(solution)/shard_map/ppermute | solution.py:23
  74.6 9.1 %collective-permute-start.9 = (bf16[2,96,384]{2,1,0:T(8,128)(2,1)S(1)}, bf16[2,96,384]{2,1,0:T(8,128)(2,1)S(1)}, u32[]{:S(2)}, u32[]{:S(2)}) collective-permute-start(bf16[2,96,384]{2,1,0:T(8,128)(2,1)S(1)} %shard_map.40.refs_0_), channel_id=1, source_target_pairs={{0,384},{4,132},{64,448},{68,196},{128,0},{132,260},{192,64},{196,... | collective-permute-start | bytes 442376 | tf_op jit(solution)/shard_map/ppermute | solution.py:23
  78.6 13.7 %collective-permute-start.11 = (bf16[2,96,384]{2,1,0:T(8,128)(2,1)S(1)}, bf16[2,96,384]{2,1,0:T(8,128)(2,1)S(1)}, u32[]{:S(2)}, u32[]{:S(2)}) collective-permute-start(bf16[2,96,384]{2,1,0:T(8,128)(2,1)S(1)} %shard_map.40.refs_0_), channel_id=1, source_target_pairs={{0,128},{4,388},{64,192},{68,452},{128,256},{132,4},{192,320},{196... | collective-permute-start | bytes 442376 | tf_op jit(solution)/shard_map/ppermute | solution.py:23
  84.5 15.2 %collective-permute-start.10 = (bf16[4,96,384]{2,1,0:T(8,128)(2,1)}, bf16[4,96,384]{2,1,0:T(8,128)(2,1)S(1)}, u32[]{:S(2)}, u32[]{:S(2)}) collective-permute-start(bf16[4,96,384]{2,1,0:T(8,128)(2,1)} %pad_maximum_fusion), channel_id=1, source_target_pairs={{0,384},{4,132},{64,448},{68,196},{128,0},{132,260},{192,64},{196,... | collective-permute-start | bytes 884744 | tf_op jit(solution)/shard_map/ppermute | solution.py:23
  87.5 7.4 %collective-permute-start.13 = (bf16[2,96,384]{2,1,0:T(8,128)(2,1)S(1)}, bf16[2,96,384]{2,1,0:T(8,128)(2,1)S(1)}, u32[]{:S(2)}, u32[]{:S(2)}) collective-permute-start(bf16[2,96,384]{2,1,0:T(8,128)(2,1)S(1)} %shard_map.40.refs_0_), channel_id=1, source_target_pairs={{0,64},{4,452},{64,128},{68,4},{128,192},{132,68},{192,256},{196,1... | collective-permute-start | bytes 442376 | tf_op jit(solution)/shard_map/ppermute | solution.py:23
  92.4 7.3 %collective-permute-start.12 = (bf16[2,96,384]{2,1,0:T(8,128)(2,1)S(1)}, bf16[2,96,384]{2,1,0:T(8,128)(2,1)S(1)}, u32[]{:S(2)}, u32[]{:S(2)}) collective-permute-start(bf16[2,96,384]{2,1,0:T(8,128)(2,1)S(1)} %collective-permute-done.11.refs_5_), channel_id=1, source_target_pairs={{0,64},{4,452},{64,128},{68,4},{128,192},{132,68},{192,256},{196,1... | collective-permute-start | bytes 442376 | tf_op jit(solution)/shard_map/ppermute | solution.py:23
  94.3 5.4 %copy-start.1 = (bf16[768,384]{1,0:T(8,128)(2,1)S(1)}, bf16[768,384]{1,0:T(8,128)(2,1)}, u32[]{:S(2)}) copy-start(bf16[768,384]{1,0:T(8,128)(2,1)} %matrix_ref.1) | copy-start | bytes 1769476
  94.3 5.4 %copy-start.2 = (s32[1,16]{1,0:T(1,128)S(1)}, s32[1,16]{1,0:T(1,128)}, u32[]{:S(2)}) copy-start(s32[1,16]{1,0:T(1,128)} %param.5) | copy-start | bytes 196

commit v13 on v8

--- a/solution.py
+++ b/solution.py
@@ -44,24 +44,19 @@
     total_ref[...] = lax.dot_general(own_ref[...], right, CONTRACT, preferred_element_type=jnp.float32)
 
 
-def square_kernel(place_ref, total_ref, other_ref, right_ref, out_ref, ordered_ref, staged_ref, sems):
-    halves, layers, part, columns = staged_ref.shape
+def square_kernel(place_ref, total_ref, other_ref, right_ref, out_ref, ordered_ref):
+    layers, halves, part, columns = out_ref.shape
     tiles = right_ref.shape[0]
     z, core = place_ref[1], place_ref[2]
     way = 1 - 2 * core
     for offset in range(tiles):
         ordered_ref[offset] = right_ref[lax.rem(z - way * offset + tiles, tiles), 1 - core]
     right = ordered_ref[...].reshape(tiles * part, columns)
-    copies = []
     for half in range(halves):
         rows = pl.ds(half * layers * part, layers * part)
         term = lax.dot_general(other_ref[:, rows], right, CONTRACT, preferred_element_type=jnp.float32)
-        total = (total_ref[rows, :] + term).astype(staged_ref.dtype)
-        staged_ref[half] = total.reshape(layers, part, columns)
-        copies.append(pltpu.make_async_copy(staged_ref.at[half], out_ref.at[:, half], sems.at[half]))
-        copies[-1].start()
-    for copy in copies:
-        copy.wait()
+        total = (total_ref[rows, :] + term).astype(out_ref.dtype)
+        out_ref[:, half] = total.reshape(layers, part, columns)
 
 
 def turn_kernel(own_ref, other_ref, own_turned_ref, other_turned_ref):
@@ -169,12 +164,8 @@
         square_kernel,
         out_shape=jax.ShapeDtypeStruct((layers, halves, part, width), jnp.bfloat16),
         in_specs=[smem] + [vmem] * 3,
-        out_specs=pl.BlockSpec(memory_space=pltpu.HBM),
-        scratch_shapes=[
-            ordered,
-            pltpu.VMEM((halves, layers, part, width), jnp.bfloat16),
-            pltpu.SemaphoreType.DMA((halves,)),
-        ],
+        out_specs=vmem,
+        scratch_shapes=[ordered],
         compiler_params=params,
         cost_estimate=cost,
     )(place, own_total, left_other, right)

time: 131 us -> 131 us (level)
  no operation moved by 1% of the time
where the time goes in v13:
time: 131 us; the launch traced here: 130 us
  starting transfers between devices  72.2 us (55%)
  blocking collectives  26.3 us (20%)
  waiting for transfers between devices  19.4 us (15%)
  Pallas kernels  6.51 us (5%)
  local copies, waits for them, and re-layouts  5.15 us (4%)
    ppermute x14, starting transfers between devices, shifted(): return lax.ppermute(piece, (axis, 'core'), pairs)  50.8 us
    all_to_all x1, blocking collectives, on_device(): lax.all_to_all(outgoing, ('z', 'core'), split_axis=0, concat_axis=0, tile...  14 us
    all_to_all x1, blocking collectives, to_all(): return lax.all_to_all(copies, axis, split_axis=0, concat_axis=0, tiled=True)  12.3 us
    ppermute x1, starting transfers between devices, on_device(): left_other = lax.ppermute(left_own, 'core', [(0, 1), (1, 0)])  9.55 us
    all_to_all x1, waiting for transfers between devices, on_device(): lax.all_to_all(square_part, 'layer', split_axis=0, concat_axis=0, tiled=T...  9.49 us
    ppermute x14, waiting for transfers between devices, shifted(): return lax.ppermute(piece, (axis, 'core'), pairs)  8.93 us
    all_to_all x1, starting transfers between devices, to_all(): return lax.all_to_all(copies, axis, split_axis=0, concat_axis=0, tiled=True)  7.65 us
    all_to_all x1, starting transfers between devices, on_device(): lax.all_to_all(square_part, 'layer', split_axis=0, concat_axis=0, tiled=T...  4.13 us
  transfers between devices with their start and end apart: 17, of which 6 were waited for; matrix products, arithmetic and copies ran while one was open for 1% of the time, Pallas kernels for 2%

profile of v13, /device:TPU:1, one launch (start us, length us, event | category | flops | bytes accessed | tf_op | source)
XLA Modules:
  0.0 130.1 jit_solution(10081675312138972408)
XLA Ops:
  0.0 0.9 dynamic-slice_bitcast_fusion
  0.9 1.2 broadcast_in_dim.14
  2.1 7.7 %all-to-all-start = ((bf16[8,2,96,384]{3,2,1,0:T(8,128)(2,1)}), bf16[8,2,96,384]{3,2,1,0:T(8,128)(2,1)S(1)}, u32[]{:S(2)}, u32[]{:S(2)}) async-start(bf16[8,2,96,384]{3,2,1,0:T(8,128)(2,1)} %broadcast_in_dim.14), calls=%async_computation | async-start | bytes 2359296 | tf_op jit(solution)/shard_map/all_to_all | solution.py:14
  9.8 1.1 constant_dynamic-slice_fusion
  10.9 0.1 copy.8
  11.0 4.0 %collective-permute-start = (bf16[96,768]{1,0:T(8,128)(2,1)S(1)}, bf16[96,768]{1,0:T(8,128)(2,1)S(1)}, u32[]{:S(2)}, u32[]{:S(2)}) collective-permute-start(bf16[96,768]{1,0:T(8,128)(2,1)S(1)} %bitcast.17), channel_id=1, source_target_pairs={{0,56},{4,12},{8,0},{12,20},{16,8},{20,28},{24,16},{28,36},{32,24}... | collective-permute-start | bytes 442376 | tf_op jit(solution)/shard_map/ppermute | solution.py:23
  15.0 5.8 %collective-permute-start.1 = (bf16[96,768]{1,0:T(8,128)(2,1)S(1)}, bf16[96,768]{1,0:T(8,128)(2,1)S(1)}, u32[]{:S(2)}, u32[]{:S(2)}) collective-permute-start(bf16[96,768]{1,0:T(8,128)(2,1)S(1)} %bitcast.18), channel_id=1, source_target_pairs={{0,48},{4,20},{8,56},{12,28},{16,0},{20,36},{24,8},{28,44},{32,16}... | collective-permute-start | bytes 442376 | tf_op jit(solution)/shard_map/ppermute | solution.py:23
  20.8 5.9 %collective-permute-start.4 = (bf16[96,768]{1,0:T(8,128)(2,1)S(1)}, bf16[96,768]{1,0:T(8,128)(2,1)S(1)}, u32[]{:S(2)}, u32[]{:S(2)}) collective-permute-start(bf16[96,768]{1,0:T(8,128)(2,1)S(1)} %bitcast.19), channel_id=1, source_target_pairs={{0,16},{4,52},{8,24},{12,60},{16,32},{20,4},{24,40},{28,12},{32,48... | collective-permute-start | bytes 442376 | tf_op jit(solution)/shard_map/ppermute | solution.py:23
  26.7 3.1 %collective-permute-start.6 = (bf16[96,768]{1,0:T(8,128)(2,1)S(1)}, bf16[96,768]{1,0:T(8,128)(2,1)S(1)}, u32[]{:S(2)}, u32[]{:S(2)}) collective-permute-start(bf16[96,768]{1,0:T(8,128)(2,1)S(1)} %bitcast.20), channel_id=1, source_target_pairs={{0,8},{4,60},{8,16},{12,4},{16,24},{20,12},{24,32},{28,20},{32,40}... | collective-permute-start | bytes 442376 | tf_op jit(solution)/shard_map/ppermute | solution.py:23
  29.8 0.0 collective-permute-done.1
  29.8 2.2 %collective-permute-start.2 = (bf16[96,768]{1,0:T(8,128)(2,1)S(1)}, bf16[96,768]{1,0:T(8,128)(2,1)S(1)}, u32[]{:S(2)}, u32[]{:S(2)}) collective-permute-start(bf16[96,768]{1,0:T(8,128)(2,1)S(1)} %collective-permute-done.1), channel_id=1, source_target_pairs={{0,56},{4,12},{8,0},{12,20},{16,8},{20,28},{24,16},{28,36},{32,24}... | collective-permute-start | bytes 442376 | tf_op jit(solution)/shard_map/ppermute | solution.py:23
  32.0 2.2 %collective-permute-start.3 = (bf16[96,768]{1,0:T(8,128)(2,1)S(1)}, bf16[96,768]{1,0:T(8,128)(2,1)S(1)}, u32[]{:S(2)}, u32[]{:S(2)}) collective-permute-start(bf16[96,768]{1,0:T(8,128)(2,1)S(1)} %collective-permute-done.1), channel_id=1, source_target_pairs={{0,48},{4,20},{8,56},{12,28},{16,0},{20,36},{24,8},{28,44},{32,16}... | collective-permute-start | bytes 442376 | tf_op jit(solution)/shard_map/ppermute | solution.py:23
  34.3 0.0 collective-permute-done.4
  34.3 4.3 %collective-permute-start.5 = (bf16[96,768]{1,0:T(8,128)(2,1)S(1)}, bf16[96,768]{1,0:T(8,128)(2,1)S(1)}, u32[]{:S(2)}, u32[]{:S(2)}) collective-permute-start(bf16[96,768]{1,0:T(8,128)(2,1)S(1)} %collective-permute-done.4), channel_id=1, source_target_pairs={{0,8},{4,60},{8,16},{12,4},{16,24},{20,12},{24,32},{28,20},{32,40}... | collective-permute-start | bytes 442376 | tf_op jit(solution)/shard_map/ppermute | solution.py:23
  38.6 0.1 collective-permute-done.2
  38.6 1.9 %collective-permute-done.3 = bf16[96,768]{1,0:T(8,128)(2,1)S(1)} collective-permute-done((bf16[96,768]{1,0:T(8,128)(2,1)S(1)}, bf16[96,768]{1,0:T(8,128)(2,1)S(1)}, u32[]{:S(2)}, u32[]{:S(2)}) %collective-permute-start.3) | collective-permute-done | bytes 147488 | tf_op jit(solution)/shard_map/ppermute | solution.py:23
  40.5 1.5 %collective-permute-done.5 = bf16[96,768]{1,0:T(8,128)(2,1)S(1)} collective-permute-done((bf16[96,768]{1,0:T(8,128)(2,1)S(1)}, bf16[96,768]{1,0:T(8,128)(2,1)S(1)}, u32[]{:S(2)}, u32[]{:S(2)}) %collective-permute-start.5) | collective-permute-done | bytes 147488 | tf_op jit(solution)/shard_map/ppermute | solution.py:23
  42.1 9.6 %collective-permute-start.7 = (bf16[768,768]{1,0:T(8,128)(2,1)S(1)}, bf16[768,768]{1,0:T(8,128)(2,1)S(1)}, u32[]{:S(2)}, u32[]{:S(2)}) collective-permute-start(bf16[768,768]{1,0:T(8,128)(2,1)S(1)} %constant_dynamic-update-slice_fusion.own_ref), channel_id=1, source_target_pairs={{0,4},{4,0},{1,5},{5,1},{2,6},{6,2},{3,7},{7,3},{8,12},{12,8},{9,1... | collective-permute-start | bytes 3538952 | tf_op jit(solution)/shard_map/ppermute | solution.py:146
  51.6 0.1 pad_add_fusion.place_ref
  51.7 1.4 %shard_map.37.total_ref = f32[768,384]{1,0:T(8,128)S(1)} custom-call(s32[3]{0:T(128)S(1)} %pad_add_fusion.place_ref, bf16[768,768]{1,0:T(8,128)(2,1)S(1)} %constant_dynamic-update-slice_fusion.own_ref, bf16[8,2,96,384]{3,2,1,0:T(8,128)(2,1)S(1)} %all-to-all-done.right_ref), custom_call_target="tpu_custom_call" | custom-call | flops 452984832 | bytes 1769472 | tf_op jit(solution)/shard_map/pallas_call | solution.py:154
  53.1 1.0 collective-permute-done.7.other_ref
  54.1 1.4 %shard_map.38 = bf16[4,2,96,384]{3,2,1,0:T(8,128)(2,1)S(1)} custom-call(s32[3]{0:T(128)S(1)} %pad_add_fusion.place_ref, f32[768,384]{1,0:T(8,128)S(1)} %shard_map.37.total_ref, bf16[768,768]{1,0:T(8,128)(2,1)S(1)} %collective-permute-done.7.other_ref, bf16[8,2,96,384]{3,2,1,0:T(8,128)(2,1)S(1)} %all-to-all-done.right_ref), custom_call_target="tpu_custom_call" | custom-call | flops 452984832 | bytes 1769472 | tf_op jit(solution)/shard_map/pallas_call | solution.py:163
  55.4 0.8 copy-done
  56.3 4.1 %all-to-all-start.1 = ((bf16[4,2,96,384]{3,2,1,0:T(8,128)(2,1)}), bf16[4,2,96,384]{3,2,1,0:T(8,128)(2,1)S(1)}, u32[]{:S(2)}, u32[]{:S(2)}) async-start(bf16[4,2,96,384]{3,2,1,0:T(8,128)(2,1)} %copy-done), calls=%async_computation.1 | async-start | bytes 1179648 | tf_op jit(solution)/shard_map/all_to_all | solution.py:182
  60.4 0.1 copy.7.keep_ref
  60.5 9.5 %all-to-all-done.1.parts_ref = bf16[4,2,96,384]{3,2,1,0:T(8,128)(2,1)S(1)} async-done(((bf16[4,2,96,384]{3,2,1,0:T(8,128)(2,1)}), bf16[4,2,96,384]{3,2,1,0:T(8,128)(2,1)S(1)}, u32[]{:S(2)}, u32[]{:S(2)}) %all-to-all-start.1) | async-done | bytes 589856 | tf_op jit(solution)/shard_map/all_to_all | solution.py:182
  70.0 0.8 shard_map.40.refs_0_
  70.8 4.5 %collective-permute-start.9 = (bf16[2,96,384]{2,1,0:T(8,128)(2,1)S(1)}, bf16[2,96,384]{2,1,0:T(8,128)(2,1)S(1)}, u32[]{:S(2)}, u32[]{:S(2)}) collective-permute-start(bf16[2,96,384]{2,1,0:T(8,128)(2,1)S(1)} %shard_map.40.refs_0_), channel_id=1, source_target_pairs={{0,384},{4,132},{64,448},{68,196},{128,0},{132,260},{192,64},{196,... | collective-permute-start | bytes 442376 | tf_op jit(solution)/shard_map/ppermute | solution.py:23
  75.2 3.1 %collective-permute-start.12 = (bf16[2,96,384]{2,1,0:T(8,128)(2,1)S(1)}, bf16[2,96,384]{2,1,0:T(8,128)(2,1)S(1)}, u32[]{:S(2)}, u32[]{:S(2)}) collective-permute-start(bf16[2,96,384]{2,1,0:T(8,128)(2,1)S(1)} %shard_map.40.refs_0_), channel_id=1, source_target_pairs={{0,128},{4,388},{64,192},{68,452},{128,256},{132,4},{192,320},{196... | collective-permute-start | bytes 442376 | tf_op jit(solution)/shard_map/ppermute | solution.py:23
  78.4 3.4 %collective-permute-start.14 = (bf16[2,96,384]{2,1,0:T(8,128)(2,1)S(1)}, bf16[2,96,384]{2,1,0:T(8,128)(2,1)S(1)}, u32[]{:S(2)}, u32[]{:S(2)}) collective-permute-start(bf16[2,96,384]{2,1,0:T(8,128)(2,1)S(1)} %shard_map.40.refs_0_), channel_id=1, source_target_pairs={{0,64},{4,452},{64,128},{68,4},{128,192},{132,68},{192,256},{196,1... | collective-permute-start | bytes 442376 | tf_op jit(solution)/shard_map/ppermute | solution.py:23
  81.8 1.9 %collective-permute-start.8 = (bf16[2,96,384]{2,1,0:T(8,128)(2,1)S(1)}, bf16[2,96,384]{2,1,0:T(8,128)(2,1)S(1)}, u32[]{:S(2)}, u32[]{:S(2)}) collective-permute-start(bf16[2,96,384]{2,1,0:T(8,128)(2,1)S(1)} %shard_map.40.refs_0_), channel_id=1, source_target_pairs={{0,448},{4,68},{64,0},{68,132},{128,64},{132,196},{192,128},{196,2... | collective-permute-start | bytes 442376 | tf_op jit(solution)/shard_map/ppermute | solution.py:23
  83.7 3.3 %collective-permute-start.10 = (bf16[2,96,384]{2,1,0:T(8,128)(2,1)S(1)}, bf16[2,96,384]{2,1,0:T(8,128)(2,1)S(1)}, u32[]{:S(2)}, u32[]{:S(2)}) collective-permute-start(bf16[2,96,384]{2,1,0:T(8,128)(2,1)S(1)} %collective-permute-done.9.refs_2_), channel_id=1, source_target_pairs={{0,448},{4,68},{64,0},{68,132},{128,64},{132,196},{192,128},{196,2... | collective-permute-start | bytes 442376 | tf_op jit(solution)/shard_map/ppermute | solution.py:23
  87.1 4.9 %collective-permute-start.11 = (bf16[2,96,384]{2,1,0:T(8,128)(2,1)S(1)}, bf16[2,96,384]{2,1,0:T(8,128)(2,1)S(1)}, u32[]{:S(2)}, u32[]{:S(2)}) collective-permute-start(bf16[2,96,384]{2,1,0:T(8,128)(2,1)S(1)} %collective-permute-done.9.refs_2_), channel_id=1, source_target_pairs={{0,384},{4,132},{64,448},{68,196},{128,0},{132,260},{192,64},{196,... | collective-permute-start | bytes 442376 | tf_op jit(solution)/shard_map/ppermute | solution.py:23
  92.0 0.0 collective-permute-done.12.refs_6_
  92.0 2.2 %collective-permute-start.13 = (bf16[2,96,384]{2,1,0:T(8,128)(2,1)S(1)}, bf16[2,96,384]{2,1,0:T(8,128)(2,1)S(1)}, u32[]{:S(2)}, u32[]{:S(2)}) collective-permute-start(bf16[2,96,384]{2,1,0:T(8,128)(2,1)S(1)} %collective-permute-done.12.refs_6_), channel_id=1, source_target_pairs={{0,64},{4,452},{64,128},{68,4},{128,192},{132,68},{192,256},{196,1... | collective-permute-start | bytes 442376 | tf_op jit(solution)/shard_map/ppermute | solution.py:23
  94.2 0.0 copy-start.1
  94.3 0.0 copy-start.2
  94.3 0.7 shard_map.39
  94.9 0.0 collective-permute-done.14.refs_7_
  94.9 0.0 collective-permute-done.8.refs_1_
  95.0 1.2 collective-permute-done.11.refs_4_
  96.2 4.3 %collective-permute-done.13.refs_5_ = bf16[2,96,384]{2,1,0:T(8,128)(2,1)S(1)} collective-permute-done((bf16[2,96,384]{2,1,0:T(8,128)(2,1)S(1)}, bf16[2,96,384]{2,1,0:T(8,128)(2,1)S(1)}, u32[]{:S(2)}, u32[]{:S(2)}) %collective-permute-start.13) | collective-permute-done | bytes 147488 | tf_op jit(solution)/shard_map/ppermute | solution.py:23
  100.5 2.4 %shard_map.41 = bf16[16,32,128]{2,1,0:T(8,128)(2,1)S(1)} custom-call(s32[16]{0:T(128)S(1)} %bitcast.16, s32[3]{0:T(128)S(1)} %pad_add_fusion.place_ref, f32[1]{0:T(128)} %bitcast.4.scale_ref, bf16[768,768]{1,0:T(8,128)(2,1)S(1)} %get-tuple-element.16.own_ref, bf16[768,768]{1,0:T(8,128)(2,1)S(1)} %get-tuple-element.17.other_ref, ...), custom_call_target="tpu_custom_call" | custom-call | tf_op jit(solution)/shard_map/pallas_call | solution.py:195
  102.9 14.0 %all_to_all.20 = bf16[16,32,128]{2,1,0:T(8,128)(2,1)S(1)} all-to-all(bf16[16,32,128]{2,1,0:T(8,128)(2,1)S(1)} %shard_map.41), channel_id=1, replica_groups=mesh['row'=8,'z'=8,'core'=2,'layer'=4] {'z','core'}, dimensions={0} | all-to-all | bytes 262144 | tf_op jit(solution)/shard_map/all_to_all | solution.py:207
  116.9 0.1 broadcast_in_dim.15
  117.0 12.3 %all_to_all.21 = bf16[4,16,32,128]{3,2,1,0:T(8,128)(2,1)S(1)} all-to-all(bf16[4,16,32,128]{3,2,1,0:T(8,128)(2,1)S(1)} %broadcast_in_dim.15), channel_id=1, replica_groups=mesh['row'=8,'z'=8,'core'=2,'layer'=4] {'layer'}, dimensions={0} | all-to-all | bytes 1048576 | tf_op jit(solution)/shard_map/all_to_all | solution.py:14
  129.3 0.1 reduce_sum.12
  129.4 0.7 copy.11
  (18 shorter events, 0.1 us)
Async XLA Ops:
  2.1 40.0 %all-to-all-start = ((bf16[8,2,96,384]{3,2,1,0:T(8,128)(2,1)}), bf16[8,2,96,384]{3,2,1,0:T(8,128)(2,1)S(1)}, u32[]{:S(2)}, u32[]{:S(2)}) async-start(bf16[8,2,96,384]{3,2,1,0:T(8,128)(2,1)} %broadcast_in_dim.14), calls=%async_computation | async-start | bytes 2359296 | tf_op jit(solution)/shard_map/all_to_all | solution.py:14
  11.0 23.2 %collective-permute-start = (bf16[96,768]{1,0:T(8,128)(2,1)S(1)}, bf16[96,768]{1,0:T(8,128)(2,1)S(1)}, u32[]{:S(2)}, u32[]{:S(2)}) collective-permute-start(bf16[96,768]{1,0:T(8,128)(2,1)S(1)} %bitcast.17), channel_id=1, source_target_pairs={{0,56},{4,12},{8,0},{12,20},{16,8},{20,28},{24,16},{28,36},{32,24}... | collective-permute-start | bytes 442376 | tf_op jit(solution)/shard_map/ppermute | solution.py:23
  15.0 14.8 %collective-permute-start.1 = (bf16[96,768]{1,0:T(8,128)(2,1)S(1)}, bf16[96,768]{1,0:T(8,128)(2,1)S(1)}, u32[]{:S(2)}, u32[]{:S(2)}) collective-permute-start(bf16[96,768]{1,0:T(8,128)(2,1)S(1)} %bitcast.18), channel_id=1, source_target_pairs={{0,48},{4,20},{8,56},{12,28},{16,0},{20,36},{24,8},{28,44},{32,16}... | collective-permute-start | bytes 442376 | tf_op jit(solution)/shard_map/ppermute | solution.py:23
  20.8 13.4 %collective-permute-start.4 = (bf16[96,768]{1,0:T(8,128)(2,1)S(1)}, bf16[96,768]{1,0:T(8,128)(2,1)S(1)}, u32[]{:S(2)}, u32[]{:S(2)}) collective-permute-start(bf16[96,768]{1,0:T(8,128)(2,1)S(1)} %bitcast.19), channel_id=1, source_target_pairs={{0,16},{4,52},{8,24},{12,60},{16,32},{20,4},{24,40},{28,12},{32,48... | collective-permute-start | bytes 442376 | tf_op jit(solution)/shard_map/ppermute | solution.py:23
  26.7 15.3 %collective-permute-start.6 = (bf16[96,768]{1,0:T(8,128)(2,1)S(1)}, bf16[96,768]{1,0:T(8,128)(2,1)S(1)}, u32[]{:S(2)}, u32[]{:S(2)}) collective-permute-start(bf16[96,768]{1,0:T(8,128)(2,1)S(1)} %bitcast.20), channel_id=1, source_target_pairs={{0,8},{4,60},{8,16},{12,4},{16,24},{20,12},{24,32},{28,20},{32,40}... | collective-permute-start | bytes 442376 | tf_op jit(solution)/shard_map/ppermute | solution.py:23
  29.8 8.8 %collective-permute-start.2 = (bf16[96,768]{1,0:T(8,128)(2,1)S(1)}, bf16[96,768]{1,0:T(8,128)(2,1)S(1)}, u32[]{:S(2)}, u32[]{:S(2)}) collective-permute-start(bf16[96,768]{1,0:T(8,128)(2,1)S(1)} %collective-permute-done.1), channel_id=1, source_target_pairs={{0,56},{4,12},{8,0},{12,20},{16,8},{20,28},{24,16},{28,36},{32,24}... | collective-permute-start | bytes 442376 | tf_op jit(solution)/shard_map/ppermute | solution.py:23
  32.0 8.5 %collective-permute-start.3 = (bf16[96,768]{1,0:T(8,128)(2,1)S(1)}, bf16[96,768]{1,0:T(8,128)(2,1)S(1)}, u32[]{:S(2)}, u32[]{:S(2)}) collective-permute-start(bf16[96,768]{1,0:T(8,128)(2,1)S(1)} %collective-permute-done.1), channel_id=1, source_target_pairs={{0,48},{4,20},{8,56},{12,28},{16,0},{20,36},{24,8},{28,44},{32,16}... | collective-permute-start | bytes 442376 | tf_op jit(solution)/shard_map/ppermute | solution.py:23
  34.3 7.7 %collective-permute-start.5 = (bf16[96,768]{1,0:T(8,128)(2,1)S(1)}, bf16[96,768]{1,0:T(8,128)(2,1)S(1)}, u32[]{:S(2)}, u32[]{:S(2)}) collective-permute-start(bf16[96,768]{1,0:T(8,128)(2,1)S(1)} %collective-permute-done.4), channel_id=1, source_target_pairs={{0,8},{4,60},{8,16},{12,4},{16,24},{20,12},{24,32},{28,20},{32,40}... | collective-permute-start | bytes 442376 | tf_op jit(solution)/shard_map/ppermute | solution.py:23
  42.1 12.0 %collective-permute-start.7 = (bf16[768,768]{1,0:T(8,128)(2,1)S(1)}, bf16[768,768]{1,0:T(8,128)(2,1)S(1)}, u32[]{:S(2)}, u32[]{:S(2)}) collective-permute-start(bf16[768,768]{1,0:T(8,128)(2,1)S(1)} %constant_dynamic-update-slice_fusion.own_ref), channel_id=1, source_target_pairs={{0,4},{4,0},{1,5},{5,1},{2,6},{6,2},{3,7},{7,3},{8,12},{12,8},{9,1... | collective-permute-start | bytes 3538952 | tf_op jit(solution)/shard_map/ppermute | solution.py:146
  55.4 0.8 copy-start
  56.3 4.1 %copy-start.3 = (s32[12,6]{0,1:T(8,128)S(1)}, s32[12,6]{0,1:T(8,128)}, u32[]{:S(2)}) copy-start(s32[12,6]{0,1:T(8,128)} %param.4) | copy-start | bytes 868
  56.3 13.7 %all-to-all-start.1 = ((bf16[4,2,96,384]{3,2,1,0:T(8,128)(2,1)}), bf16[4,2,96,384]{3,2,1,0:T(8,128)(2,1)S(1)}, u32[]{:S(2)}, u32[]{:S(2)}) async-start(bf16[4,2,96,384]{3,2,1,0:T(8,128)(2,1)} %copy-done), calls=%async_computation.1 | async-start | bytes 1179648 | tf_op jit(solution)/shard_map/all_to_all | solution.py:182
  70.8 12.9 %collective-permute-start.9 = (bf16[2,96,384]{2,1,0:T(8,128)(2,1)S(1)}, bf16[2,96,384]{2,1,0:T(8,128)(2,1)S(1)}, u32[]{:S(2)}, u32[]{:S(2)}) collective-permute-start(bf16[2,96,384]{2,1,0:T(8,128)(2,1)S(1)} %shard_map.40.refs_0_), channel_id=1, source_target_pairs={{0,384},{4,132},{64,448},{68,196},{128,0},{132,260},{192,64},{196,... | collective-permute-start | bytes 442376 | tf_op jit(solution)/shard_map/ppermute | solution.py:23
  75.2 16.8 %collective-permute-start.12 = (bf16[2,96,384]{2,1,0:T(8,128)(2,1)S(1)}, bf16[2,96,384]{2,1,0:T(8,128)(2,1)S(1)}, u32[]{:S(2)}, u32[]{:S(2)}) collective-permute-start(bf16[2,96,384]{2,1,0:T(8,128)(2,1)S(1)} %shard_map.40.refs_0_), channel_id=1, source_target_pairs={{0,128},{4,388},{64,192},{68,452},{128,256},{132,4},{192,320},{196... | collective-permute-start | bytes 442376 | tf_op jit(solution)/shard_map/ppermute | solution.py:23
  78.4 16.6 %collective-permute-start.14 = (bf16[2,96,384]{2,1,0:T(8,128)(2,1)S(1)}, bf16[2,96,384]{2,1,0:T(8,128)(2,1)S(1)}, u32[]{:S(2)}, u32[]{:S(2)}) collective-permute-start(bf16[2,96,384]{2,1,0:T(8,128)(2,1)S(1)} %shard_map.40.refs_0_), channel_id=1, source_target_pairs={{0,64},{4,452},{64,128},{68,4},{128,192},{132,68},{192,256},{196,1... | collective-permute-start | bytes 442376 | tf_op jit(solution)/shard_map/ppermute | solution.py:23
  81.8 13.2 %collective-permute-start.8 = (bf16[2,96,384]{2,1,0:T(8,128)(2,1)S(1)}, bf16[2,96,384]{2,1,0:T(8,128)(2,1)S(1)}, u32[]{:S(2)}, u32[]{:S(2)}) collective-permute-start(bf16[2,96,384]{2,1,0:T(8,128)(2,1)S(1)} %shard_map.40.refs_0_), channel_id=1, source_target_pairs={{0,448},{4,68},{64,0},{68,132},{128,64},{132,196},{192,128},{196,2... | collective-permute-start | bytes 442376 | tf_op jit(solution)/shard_map/ppermute | solution.py:23
  83.7 11.2 %collective-permute-start.10 = (bf16[2,96,384]{2,1,0:T(8,128)(2,1)S(1)}, bf16[2,96,384]{2,1,0:T(8,128)(2,1)S(1)}, u32[]{:S(2)}, u32[]{:S(2)}) collective-permute-start(bf16[2,96,384]{2,1,0:T(8,128)(2,1)S(1)} %collective-permute-done.9.refs_2_), channel_id=1, source_target_pairs={{0,448},{4,68},{64,0},{68,132},{128,64},{132,196},{192,128},{196,2... | collective-permute-start | bytes 442376 | tf_op jit(solution)/shard_map/ppermute | solution.py:23
  87.1 9.1 %collective-permute-start.11 = (bf16[2,96,384]{2,1,0:T(8,128)(2,1)S(1)}, bf16[2,96,384]{2,1,0:T(8,128)(2,1)S(1)}, u32[]{:S(2)}, u32[]{:S(2)}) collective-permute-start(bf16[2,96,384]{2,1,0:T(8,128)(2,1)S(1)} %collective-permute-done.9.refs_2_), channel_id=1, source_target_pairs={{0,384},{4,132},{64,448},{68,196},{128,0},{132,260},{192,64},{196,... | collective-permute-start | bytes 442376 | tf_op jit(solution)/shard_map/ppermute | solution.py:23
  92.0 8.5 %collective-permute-start.13 = (bf16[2,96,384]{2,1,0:T(8,128)(2,1)S(1)}, bf16[2,96,384]{2,1,0:T(8,128)(2,1)S(1)}, u32[]{:S(2)}, u32[]{:S(2)}) collective-permute-start(bf16[2,96,384]{2,1,0:T(8,128)(2,1)S(1)} %collective-permute-done.12.refs_6_), channel_id=1, source_target_pairs={{0,64},{4,452},{64,128},{68,4},{128,192},{132,68},{192,256},{196,1... | collective-permute-start | bytes 442376 | tf_op jit(solution)/shard_map/ppermute | solution.py:23
  94.2 6.3 %copy-start.1 = (bf16[768,384]{1,0:T(8,128)(2,1)S(1)}, bf16[768,384]{1,0:T(8,128)(2,1)}, u32[]{:S(2)}) copy-start(bf16[768,384]{1,0:T(8,128)(2,1)} %matrix_ref.1) | copy-start | bytes 1769476
  94.3 6.2 %copy-start.2 = (s32[1,16]{1,0:T(1,128)S(1)}, s32[1,16]{1,0:T(1,128)}, u32[]{:S(2)}) copy-start(s32[1,16]{1,0:T(1,128)} %param.5) | copy-start | bytes 196
